TPU v7x, 32 devices: a whole 2x2x4 slice. The times are simulated.
32 devices in a mesh: tm: 8 (over y, x, core), unit: 4 (over z).
Axes of the slice: x: 2, y: 2, z: 4, core: 2. Of those that a mesh axis runs over, the one named last changes fastest.
Arguments:
- recording: bfloat16 [65536, 384], P(('tm', 'unit')), may hold values from -6 to 6
- spike_times: int32 [1024], P(('tm', 'unit')), may hold values from 30 to 65505, as said below
- unit_labels: int32 [1024], P(('tm', 'unit')), may hold values from 0 to 255, as said below
- old_templates: bfloat16 [256, 23424], P('unit'), may hold values from -3 to 3
Outputs:
- templates: bfloat16 [256, 23424], P('unit', 'tm')
- scores: float32 [256, 32768], P('unit', 'tm')
Inputs may be any that keep to these rules, and one draw needn't show every extreme that they name: `spike_times`: the spikes lie in blocks of 32, block b on the device of flattened index b over tm and unit; the times of block b lie in b * 2048 + 30 to (b + 1) * 2048 - 31, and both ends are reached in every block. `unit_labels`: labels lie in 0 to 255; the panel of a label is label // 64. In each block of 32 spikes at most 8 labels fall in one panel, and on each index of tm one panel receives exactly 8 from every block of that index.
All inputs are finite; a program needn't handle non-finite values.
Results may differ from a plain program's by a relative error of at most 0.0027.
Values may be sent and summed in bfloat16 or wider, within the bound.
No kernel may reach another device: no remote copies, remote signals or barrier semaphores. Data moves between devices by JAX's collectives and lax.ppermute only.
A program may use at most 64 MiB of HBM per device.

v0:
```python
import jax
import jax.numpy as jnp
from jax import lax
from jax.sharding import PartitionSpec as P

STRIDE = 2
CAP = 8


def from_behind(value, axis, by):
    size = lax.axis_size(axis)
    pairs = [(i, i + by) for i in range(size) if 0 <= i + by < size]
    return lax.ppermute(value, axis, pairs)


def refine(sums, counts, old):
    weight = counts / (counts + 4.0)
    mean = sums / jnp.maximum(counts, 1.0)[:, None]
    base = old.astype(jnp.float32)
    return (base + weight[:, None] * (mean - base)).astype(jnp.bfloat16)


def correlate(extended, kernel_rows, channels, taps):
    kernel = kernel_rows.reshape(kernel_rows.shape[0], channels, taps)
    out = lax.conv_general_dilated(
        extended[None],
        kernel,
        (STRIDE,),
        "VALID",
        dimension_numbers=("NWC", "OIW", "NCW"),
        preferred_element_type=jnp.float32,
    )
    return out[0]


def body(recording, spike_times, unit_labels, old_templates):
    sub_rows, chans = recording.shape
    panel, feat = old_templates.shape
    taps = feat // chans
    half = (taps - 1) // 2
    owners = lax.axis_size("unit")
    tm_count = lax.axis_size("tm")
    spikes = spike_times.shape[0]
    tm_pos = lax.axis_index("tm")
    unit_pos = lax.axis_index("unit")
    scale = 1.0 / jnp.sqrt(jnp.float32(feat))
    flat_pos = tm_pos * owners + unit_pos
    local = spike_times - flat_pos * sub_rows - half
    snips = jax.vmap(lambda s: lax.dynamic_slice(recording, (s, jnp.int32(0)), (taps, chans)))(
        local
    )
    snippet_rows = jnp.transpose(snips, (0, 2, 1)).reshape(spikes, feat)
    owner = unit_labels // panel
    within = unit_labels % panel
    owner_hits = (owner[:, None] == jnp.arange(owners)[None, :]).astype(jnp.int32)
    earlier = jnp.cumsum(owner_hits, axis=0) - owner_hits
    rank = jnp.sum(earlier * owner_hits, axis=1)
    target = owner * CAP + rank
    placing = jnp.arange(owners * CAP)[:, None] == target[None, :]
    send_rows = jnp.dot(
        placing.astype(jnp.bfloat16), snippet_rows, preferred_element_type=jnp.float32
    )
    send_rows = send_rows.astype(jnp.bfloat16).reshape(owners, CAP, feat)
    send_tags = jnp.dot(placing.astype(jnp.float32), within.astype(jnp.float32) + 1.0) - 1.0
    send_tags = send_tags.astype(jnp.bfloat16).reshape(owners, CAP)
    got_rows, got_tags = (
        lax.all_to_all(send_rows, "unit", split_axis=0, concat_axis=0, tiled=True),
        lax.all_to_all(send_tags, "unit", split_axis=0, concat_axis=0, tiled=True),
    )
    matching = (
        got_tags.astype(jnp.float32).reshape(1, -1) == jnp.arange(panel, dtype=jnp.float32)[:, None]
    )
    sums = jnp.dot(
        matching.astype(jnp.bfloat16),
        got_rows.reshape(-1, feat),
        preferred_element_type=jnp.float32,
    )
    counts = jnp.sum(matching.astype(jnp.float32), axis=1)
    whole_slab = lax.all_gather(recording, "unit", axis=0, tiled=True)
    following = from_behind(whole_slab[: taps - 1], "tm", -1)
    extended = jnp.concatenate([whole_slab, following], axis=0)
    share = feat // tm_count
    total_sums, total_counts = lax.psum((sums, counts), "tm")
    refined = refine(total_sums, total_counts, old_templates)
    raw_scores = correlate(extended, refined, chans, taps)
    out_templates = lax.dynamic_slice_in_dim(refined, tm_pos * share, share, 1)
    return (out_templates, raw_scores * scale)


def solution(mesh):
    in_specs = (P(("tm", "unit"), None), P(("tm", "unit")), P(("tm", "unit")), P("unit", None))
    out_specs = (P("unit", "tm"), P("unit", "tm"))
    return jax.shard_map(body, mesh=mesh, in_specs=in_specs, out_specs=out_specs, check_vma=False)
```

profile of v0, /device:TPU:0, one launch (start us, length us, event | category | flops | bytes accessed | tf_op | source)
XLA Modules:
  0.0 392.5 jit_solution(16456514907144105917)
XLA Ops:
  11.1 6.3 %all-to-all-start = ((bf16[4,1,8]{2,1,0:T(2,128)(2,1)}), bf16[4,1,8]{2,1,0:T(2,128)(2,1)S(1)}, u32[]{:S(2)}, u32[]{:S(2)}) async-start(bf16[4,1,8]{2,1,0:T(2,128)(2,1)} %all_to_all.12), calls=%async_computation | async-start | bytes 4096 | tf_op jit(solution)/shard_map/all_to_all | solution.py:68
  18.1 85.5 %while.1 = (s32[]{:T(128)}, bf16[2048,384]{1,0:T(8,128)(2,1)}, s32[32,2]{0,1:T(2,128)S(1)}, bf16[32,61,384]{2,1,0:T(8,128)(2,1)}, s32[]{:T(128)}) while((s32[]{:T(128)}, bf16[2048,384]{1,0:T(8,128)(2,1)}, s32[32,2]{0,1:T(2,128)S(1)}, bf16[32,61,384]{2,1,0:T(8,128)(2,1)}, s32[]{:T(128)}) %tuple.21), condition=%wide.while_cond, body=%wide.while_body.sunk | while | flops 2 | bytes 99417 | solution.py:49
  48.0 2.1 bitcast_dynamic-update-slice_fusion.2
  66.7 2.1 bitcast_dynamic-update-slice_fusion.2
  69.4 2.1 bitcast_dynamic-update-slice_fusion.2
  77.4 2.1 bitcast_dynamic-update-slice_fusion.2
  88.1 2.1 bitcast_dynamic-update-slice_fusion.2
  103.5 3.1 copy.25
  106.6 5.5 %reshape.34 = bf16[32,23424]{1,0:T(8,128)(2,1)} reshape(bf16[32,384,61]{2,1,0:T(8,128)(2,1)S(1)} %copy.25) | data formatting | bytes 2998272 | tf_op jit(solution)/shard_map/reshape | solution.py:52
  112.1 3.0 fusion
  115.2 5.1 %all-to-all-start.1 = ((bf16[4,8,23424]{2,1,0:T(8,128)(2,1)}), bf16[4,8,23424]{2,1,0:T(8,128)(2,1)S(1)}, u32[]{:S(2)}, u32[]{:S(2)}) async-start(bf16[4,8,23424]{2,1,0:T(8,128)(2,1)} %fusion), calls=%async_computation.1 | async-start | bytes 2998272 | tf_op jit(solution)/shard_map/all_to_all | solution.py:67
  120.4 34.7 %all-to-all-done.1 = bf16[4,8,23424]{2,1,0:T(8,128)(2,1)S(1)} async-done(((bf16[4,8,23424]{2,1,0:T(8,128)(2,1)}), bf16[4,8,23424]{2,1,0:T(8,128)(2,1)S(1)}, u32[]{:S(2)}, u32[]{:S(2)}) %all-to-all-start.1) | async-done | bytes 1499168 | tf_op jit(solution)/shard_map/all_to_all | solution.py:67
  155.1 3.6 fusion.12
  159.4 13.2 %psum.14 = f32[64]{0:T(128)S(1)} all-reduce(f32[64]{0:T(128)S(1)} %convert_reduce_fusion), channel_id=1, replica_groups=mesh['tm'=8,'unit'=4] {'tm'}, use_global_device_ids=true, to_apply=%region_3.4 | all-reduce | flops 64 | bytes 512 | tf_op jit(solution)/shard_map/psum | solution.py:83
  172.6 86.6 %all-reduce.3.cloned.1.call-done = f32[64,23424]{1,0:T(8,128)} async-done(((f32[64,23424]{1,0:T(8,128)}), f32[64,23424]{1,0:T(8,128)}) %all-reduce.3.cloned.1.call-update) | async-done | bytes 5996560 | tf_op jit(solution)/shard_map/psum | solution.py:83
  259.2 4.8 %fusion.10 = bf16[64,23424]{1,0:T(8,128)(2,1)S(1)} fusion(bf16[64,23424]{1,0:T(8,128)(2,1)} %param.7, f32[64,23424]{1,0:T(8,128)} %all-reduce.3.cloned.1.call-done, f32[64]{0:T(128)S(1)} %get-tuple-element.19, f32[64]{0:T(128)S(1)} %get-tuple-element.18), kind=kLoop, calls=%fused_computation.16 | loop fusion | flops 8994816 | bytes 11993600 | tf_op jit(solution)/shard_map/convert_element_type | solution.py:20
  263.9 11.2 %all-gather.2.cloned.1.call-done = bf16[8192,384]{1,0:T(8,128)(2,1)} async-done(((bf16[2048,384]{1,0:T(8,128)(2,1)}), bf16[8192,384]{1,0:T(8,128)(2,1)}) %all-gather.2.cloned.1.call-update) | async-done | bytes 6291472 | tf_op jit(solution)/shard_map/all_gather | solution.py:79
  278.1 19.6 %reshape.37 = bf16[64,384,61]{2,1,0:T(8,128)(2,1)} reshape(bf16[64,23424]{1,0:T(8,128)(2,1)S(1)} %fusion.10) | data formatting | bytes 5996544 | tf_op jit(solution)/shard_map/reshape | solution.py:24
  297.7 7.3 %copy.28 = bf16[64,384,61]{1,0,2:T(8,128)(2,1)S(1)} copy(bf16[64,384,61]{2,1,0:T(8,128)(2,1)} %reshape.37) | data formatting | bytes 5996544 | tf_op jit(solution)/shard_map/reshape | solution.py:24
  305.0 10.1 %maximum_bitcast_fusion = bf16[1,8252,384]{2,1,0:T(8,128)(2,1)S(1)} fusion(bf16[60,384]{1,0:T(8,128)(2,1)S(1)} %collective-permute-done, bf16[8192,384]{1,0:T(8,128)(2,1)} %all-gather.2.cloned.1.call-done), kind=kLoop, calls=%fused_computation.14 | loop fusion | flops 12675072 | bytes 12675072 | tf_op jit(solution)/shard_map/broadcast_in_dim | solution.py:26
  315.2 2.6 pad.3
  317.7 5.9 %copy.27 = bf16[1,8,1032,384]{3,1,2,0:T(8,128)(2,1)S(1)} copy(bf16[1,8,1032,384]{3,2,1,0:T(8,128)(2,1)S(1)} %bitcast.41) | data formatting | bytes 12681216 | tf_op jit(solution)/shard_map/conv_general_dilated | solution.py:25
  323.8 56.5 %fusion.4 = f32[8,516,64]{2,0,1:T(8,128)} fusion(bf16[64,384,61]{1,0,2:T(8,128)(2,1)S(1)} %copy.28, bf16[1,7,60,384]{3,1,2,0:T(8,128)(2,1)S(1)} %slice.18, bf16[1,8,1032,384]{3,1,2,0:T(8,128)(2,1)S(1)} %copy.27), kind=kOutput, calls=%fused_computation.10 | convolution fusion | flops 12396994560 | bytes 10718208 | tf_op jit(solution)/shard_map/conv_general_dilated | solution.py:25
  380.2 2.5 copy.29
  (121 shorter events, 85.1 us)
Async XLA Ops:
  11.1 104.1 %all-to-all-start = ((bf16[4,1,8]{2,1,0:T(2,128)(2,1)}), bf16[4,1,8]{2,1,0:T(2,128)(2,1)S(1)}, u32[]{:S(2)}, u32[]{:S(2)}) async-start(bf16[4,1,8]{2,1,0:T(2,128)(2,1)} %all_to_all.12), calls=%async_computation | async-start | bytes 4096 | tf_op jit(solution)/shard_map/all_to_all | solution.py:68
  115.2 39.9 %all-to-all-start.1 = ((bf16[4,8,23424]{2,1,0:T(8,128)(2,1)}), bf16[4,8,23424]{2,1,0:T(8,128)(2,1)S(1)}, u32[]{:S(2)}, u32[]{:S(2)}) async-start(bf16[4,8,23424]{2,1,0:T(8,128)(2,1)} %fusion), calls=%async_computation.1 | async-start | bytes 2998272 | tf_op jit(solution)/shard_map/all_to_all | solution.py:67
  120.3 138.9 %all-reduce.3.cloned.1.call-start = ((), (), s32[]{:S(2)}) async-start(), calls=%async_computation.2 | async-start | bytes 11993088 | tf_op jit(solution)/shard_map/psum | solution.py:83
  158.7 116.4 %all-gather.2.cloned.1.call-start = ((), (), s32[]{:S(2)}) async-start(), calls=%async_computation.3 | async-start | bytes 7864320 | tf_op jit(solution)/shard_map/all_gather | solution.py:79
  275.9 29.1 %collective-permute-start = (bf16[60,384]{1,0:T(8,128)(2,1)S(1)}, bf16[60,384]{1,0:T(8,128)(2,1)S(1)}, u32[]{:S(2)}, u32[]{:S(2)}) collective-permute-start(bf16[60,384]{1,0:T(8,128)(2,1)S(1)} %slice.17), channel_id=1, source_target_pairs={{4,0},{8,4},{12,8},{16,12},{20,16},{24,20},{28,24},{5,1},{9,5},{13... | collective-permute-start | bytes 138248 | tf_op jit(solution)/shard_map/ppermute | solution.py:13
  380.2 2.5 copy-start
Sparse Core Ops, SparseCore 0:
  158.8 100.2 all-reduce.2
Sparse Core Ops, SparseCore 1:
  160.7 114.3 all-gather.1
where the time goes:
time: 396 us; the launch traced here: 393 us
  local copies, waits for them, and re-layouts  137 us (35%)
  waiting for transfers between devices  133 us (34%)
  matrix products  63.9 us (16%)
  other arithmetic  17.5 us (4%)
  between operations  15.6 us (4%)
  blocking collectives  13.2 us (3%)
  starting transfers between devices  12.7 us (3%)
    psum x1, waiting for transfers between devices, body(): total_sums, total_counts = lax.psum((sums, counts), 'tm')  86.6 us
    gather x96, local copies, waits for them, and re-layouts  85.4 us
    conv_general_dilated x1, matrix products, correlate(): lax.conv_general_dilated(extended[None], kernel, (STRIDE,), 'VALID', dime...  56.5 us
    all_to_all x1, waiting for transfers between devices, body(): lax.all_to_all(send_rows, 'unit', split_axis=0, concat_axis=0, tiled=True)  34.7 us
    reshape x2, local copies, waits for them, and re-layouts, correlate(): kernel = kernel_rows.reshape(kernel_rows.shape[0], channels, taps)  26.9 us
    psum x1, blocking collectives, body(): total_sums, total_counts = lax.psum((sums, counts), 'tm')  13.2 us
    all_gather x1, waiting for transfers between devices, body(): whole_slab = lax.all_gather(recording, 'unit', axis=0, tiled=True)  11.2 us
    broadcast_in_dim x1, other arithmetic, correlate(): extended[None]  10.1 us
  transfers between devices with their start and end apart: 5, of which 3 were waited for; matrix products, arithmetic and copies ran while one was open for 33% of the time, Pallas kernels for 0%

commit v1 on v0

v1 whole, which is shorter than its diff:
```python
import functools

import jax
import jax.numpy as jnp
from jax import lax
from jax.experimental import pallas as pl
from jax.experimental.pallas import tpu as pltpu
from jax.sharding import PartitionSpec as P

STRIDE = 2
CAP = 8
FOLD = 4
ROWS = STRIDE * FOLD
AXES = ("tm", "unit")
VMEM_LIMIT = 56 * 1024 * 1024
NT = (((1,), (1,)), ((), ()))


def params():
    return pltpu.CompilerParams(vmem_limit_bytes=VMEM_LIMIT)


def pack_kernel(
    taps, panel, owners, tm_count, tpd, times_ref, labels_ref, base_ref, rec_ref, send_ref, buf, cnt
):
    spikes = times_ref.shape[0]
    sub_rows = rec_ref.shape[0]
    padded = tm_count * tpd
    win = padded + 16
    base = base_ref[0]
    for o in range(owners):
        cnt[o] = 0
    if owners * CAP > spikes:
        buf[...] = jnp.zeros_like(buf)
    tap = lax.broadcasted_iota(jnp.int32, (padded, win), 0)
    col = lax.broadcasted_iota(jnp.int32, (padded, win), 1)
    gap = jnp.where(tap < taps, col - tap, -1)

    def one(s):
        first = times_ref[s] - base
        start = jnp.minimum((first // 16) * 16, sub_rows - win)
        owner = labels_ref[s] // panel
        slot = cnt[owner]
        cnt[owner] = slot + 1
        pick = (gap == first - start).astype(jnp.bfloat16)
        window = rec_ref[pl.ds(pl.multiple_of(start, 16), win), :]
        snip = jnp.dot(pick, window, preferred_element_type=jnp.float32)
        for t in range(tm_count):
            row = (t * owners + owner) * (CAP * tpd) + slot * tpd
            buf[pl.ds(pl.multiple_of(row, tpd), tpd), :] = snip[t * tpd : (t + 1) * tpd]

    def group(g, carry):
        for i in range(8):
            one(g * 8 + i)
        return carry

    lax.fori_loop(0, spikes // 8, group, 0)
    send_ref[...] = buf[...].astype(jnp.bfloat16)


def pack(times, labels, base, rec, taps, panel, owners, tm_count, tpd):
    chans = rec.shape[1]
    rows = owners * tm_count * CAP * tpd
    smem = pl.BlockSpec(memory_space=pltpu.SMEM)
    vmem = pl.BlockSpec(memory_space=pltpu.VMEM)
    return pl.pallas_call(
        functools.partial(pack_kernel, taps, panel, owners, tm_count, tpd),
        out_shape=jax.ShapeDtypeStruct((rows, chans), jnp.bfloat16),
        in_specs=[smem, smem, smem, vmem],
        out_specs=vmem,
        scratch_shapes=[
            pltpu.VMEM((rows, chans), jnp.float32),
            pltpu.SMEM((owners,), jnp.int32),
        ],
        compiler_params=params(),
        cost_estimate=pl.CostEstimate(flops=10**8, bytes_accessed=4 * 10**6, transcendentals=0),
        name="pack",
    )(times, labels, base, rec)


def fold_kernel(rec_ref, out_ref):
    rows, chans = rec_ref.shape
    block = 16 * ROWS
    new = lax.broadcasted_iota(jnp.int32, (block, block), 0)
    old = lax.broadcasted_iota(jnp.int32, (block, block), 1)
    perm = (old == (new % 16) * ROWS + new // 16).astype(jnp.bfloat16)
    for b in range(rows // block):
        part = jnp.dot(perm, rec_ref[b * block : (b + 1) * block, :], preferred_element_type=jnp.float32)
        part = part.astype(jnp.bfloat16)
        for r in range(ROWS):
            out_ref[b * 16 : (b + 1) * 16, r * chans : (r + 1) * chans] = part[r * 16 : (r + 1) * 16]


def fold(rec):
    rows, chans = rec.shape
    vmem = pl.BlockSpec(memory_space=pltpu.VMEM)
    return pl.pallas_call(
        fold_kernel,
        out_shape=jax.ShapeDtypeStruct((rows // ROWS, ROWS * chans), jnp.bfloat16),
        in_specs=[vmem],
        out_specs=vmem,
        compiler_params=params(),
        cost_estimate=pl.CostEstimate(flops=2 * 10**8, bytes_accessed=4 * 10**6, transcendentals=0),
        name="fold",
    )(rec)


def refine_kernel(tpd, key_ref, got_ref, old_ref, out_ref, sums):
    panel = old_ref.shape[0]
    rows, chans = got_ref.shape
    step = min(rows, 2048)
    count = jnp.zeros((panel, 1), jnp.float32)
    for b in range(rows // step):
        key = key_ref[:, b * step : (b + 1) * step]
        wanted = lax.broadcasted_iota(jnp.int32, (tpd * panel, step), 0)
        wanted = (wanted % panel) * tpd + wanted // panel
        hit = (wanted == key).astype(jnp.float32)
        count = count + jnp.sum(hit[:panel], axis=1, keepdims=True)
        part = jnp.dot(
            hit.astype(jnp.bfloat16),
            got_ref[b * step : (b + 1) * step, :],
            preferred_element_type=jnp.float32,
        )
        if b == 0:
            sums[...] = part
        else:
            sums[...] += part
    weight = count / (count + 4.0)
    most = jnp.maximum(count, 1.0)
    for t in range(tpd):
        base = old_ref[:, t * chans : (t + 1) * chans].astype(jnp.float32)
        mean = sums[t * panel : (t + 1) * panel, :] / most
        out_ref[:, t * chans : (t + 1) * chans] = (base + weight * (mean - base)).astype(jnp.bfloat16)


def refine(key, got, old, tpd):
    vmem = pl.BlockSpec(memory_space=pltpu.VMEM)
    panel = old.shape[0]
    return pl.pallas_call(
        functools.partial(refine_kernel, tpd),
        out_shape=jax.ShapeDtypeStruct(old.shape, jnp.bfloat16),
        in_specs=[vmem] * 3,
        out_specs=vmem,
        scratch_shapes=[pltpu.VMEM((tpd * panel, got.shape[1]), jnp.float32)],
        compiler_params=params(),
        cost_estimate=pl.CostEstimate(flops=8 * 10**8, bytes_accessed=3 * 10**6, transcendentals=0),
        name="refine",
    )(key, got, old)


def correlate_kernel(chans, scale, odd_ref, t_ref, e_ref, out_ref, rhs, part, acc):
    blocks, panel, lanes = t_ref.shape
    height = e_ref.shape[0] // 2
    keep = acc.shape[0] // 2
    shift = STRIDE * chans
    for a in range(blocks + 1):
        used = lanes if a < blocks else lanes // 2
        for q in range(FOLD):
            rows = slice(q * panel, (q + 1) * panel)
            cut = q * shift
            if cut > 0:
                low = min(cut, used)
                if a > 0:
                    rhs[rows, 0:low] = t_ref[a - 1, :, lanes - cut : lanes - cut + low]
                else:
                    rhs[rows, 0:low] = jnp.zeros((panel, low), jnp.bfloat16)
            if cut < used:
                if a < blocks:
                    rhs[rows, cut:used] = t_ref[a, :, 0 : used - cut]
                else:
                    rhs[rows, cut:used] = jnp.zeros((panel, used - cut), jnp.bfloat16)
        part[...] = lax.dot_general(
            e_ref[:, 0:used], rhs[:, 0:used], NT, preferred_element_type=jnp.float32
        )
        for h in range(2):
            found = part[h * height + a : h * height + a + keep, :]
            if a == 0:
                acc[h * keep : (h + 1) * keep, :] = found
            else:
                acc[h * keep : (h + 1) * keep, :] += found
    width = 128
    place = lax.broadcasted_iota(jnp.int32, (FOLD * width, FOLD * width), 0)
    lane = lax.broadcasted_iota(jnp.int32, (FOLD * width, FOLD * width), 1)
    weave = (lane == (place % width) * FOLD + place // width).astype(jnp.bfloat16)
    per_half = keep // width
    odd = odd_ref[0]
    for h in range(2):
        side = odd if h == 0 else 1 - odd
        for b in range(per_half):
            first = h * keep + b * width
            turned = acc[first : first + width, :].T * scale
            row = jnp.concatenate([turned[q * panel : (q + 1) * panel] for q in range(FOLD)], axis=1)
            high = row.astype(jnp.bfloat16)
            found = jnp.dot(high, weave, preferred_element_type=jnp.float32)
            if out_ref.dtype == jnp.float32:
                rest = (row - high.astype(jnp.float32)).astype(jnp.bfloat16)
                found = found + jnp.dot(rest, weave, preferred_element_type=jnp.float32)
            at = pl.multiple_of((side * per_half + b) * (FOLD * width), FOLD * width)
            out_ref[:, pl.ds(at, FOLD * width)] = found.astype(out_ref.dtype)


def correlate(odd, t_all, e_two, keep, chans, scale, dtype):
    panel = t_all.shape[1]
    smem = pl.BlockSpec(memory_space=pltpu.SMEM)
    vmem = pl.BlockSpec(memory_space=pltpu.VMEM)
    return pl.pallas_call(
        functools.partial(correlate_kernel, chans, scale),
        out_shape=jax.ShapeDtypeStruct((panel, 2 * keep * FOLD), dtype),
        in_specs=[smem, vmem, vmem],
        out_specs=vmem,
        scratch_shapes=[
            pltpu.VMEM((FOLD * panel, ROWS * chans), jnp.bfloat16),
            pltpu.VMEM((e_two.shape[0], FOLD * panel), jnp.float32),
            pltpu.VMEM((2 * keep, FOLD * panel), jnp.float32),
        ],
        compiler_params=params(),
        cost_estimate=pl.CostEstimate(flops=8 * 10**9, bytes_accessed=8 * 10**6, transcendentals=0),
        name="correlate",
    )(odd, t_all, e_two)


def by_tap(parts, chans):
    count, panel, lanes = parts.shape
    per = ROWS * chans // lanes
    if per == 1:
        return parts
    parts = parts.reshape(count // per, per, panel, lanes)
    return jnp.transpose(parts, (0, 2, 1, 3)).reshape(count // per, panel, per * lanes)


def body(recording, spike_times, unit_labels, old_templates):
    sub_rows, chans = recording.shape
    panel, feat = old_templates.shape
    taps = feat // chans
    half = (taps - 1) // 2
    owners = lax.axis_size("unit")
    tm_count = lax.axis_size("tm")
    devices = owners * tm_count
    spikes = spike_times.shape[0]
    tm_pos = lax.axis_index("tm")
    unit_pos = lax.axis_index("unit")
    flat_pos = tm_pos * owners + unit_pos
    tpd = -(-taps // tm_count)
    padded = tpd * tm_count
    keep = sub_rows // ROWS
    scale = 1.0 / (float(feat) ** 0.5)

    base = (flat_pos * sub_rows + half).astype(jnp.int32).reshape(1)
    groups = padded // ROWS
    send = pack(spike_times, unit_labels, base, recording, taps, panel, owners, groups, ROWS)
    if tpd != ROWS:
        send = send.reshape(groups, owners, CAP, ROWS // tpd, tpd, chans)
        send = jnp.transpose(send, (0, 3, 1, 2, 4, 5))
    got = lax.all_to_all(
        send.reshape(devices, CAP * tpd, chans), AXES, split_axis=0, concat_axis=0, tiled=True
    ).reshape(devices * CAP * tpd, chans)

    labels = lax.all_gather(unit_labels, AXES, axis=0, tiled=True).reshape(devices, spikes)
    mine = labels // panel == unit_pos
    counted = mine.astype(jnp.int32)
    rank = jnp.cumsum(counted, axis=1) - counted
    here = mine[:, :, None] & (rank[:, :, None] == jnp.arange(CAP)[None, None, :])
    within = jnp.sum(jnp.where(here, (labels % panel + 1)[:, :, None], 0), axis=1) - 1
    key = (within[:, :, None] * tpd + jnp.arange(tpd)[None, None, :]).reshape(1, -1)

    cube = old_templates.reshape(panel, chans, taps)
    cube = jnp.pad(cube, ((0, 0), (0, 0), (0, padded - taps)))
    cube = lax.dynamic_slice_in_dim(cube, tm_pos * tpd, tpd, 2)
    old = jnp.transpose(cube, (0, 2, 1)).reshape(panel, tpd * chans)

    folded = fold(recording)
    halo = padded // ROWS
    following = lax.ppermute(folded[:halo], AXES, [(i, i - 1) for i in range(1, devices)])
    spare = jnp.zeros((16 - halo % 16, ROWS * chans), jnp.bfloat16)
    mine_rows = jnp.concatenate([folded, following, spare], axis=0)
    their_rows = lax.ppermute(mine_rows, "unit", [(i, i ^ 1) for i in range(owners)])
    e_two = jnp.concatenate([mine_rows, their_rows], axis=0)

    fresh = refine(key, got, old, tpd)
    odd = (unit_pos % 2).astype(jnp.int32).reshape(1)
    own_panel = lax.all_gather(fresh, "tm", axis=0, tiled=False)
    width = 2 * keep * FOLD
    scores = jnp.zeros((panel, owners // 2 * width), jnp.float32)
    found = []
    for m in range(1, owners // 2):
        ahead = [(i, (i + 2 * m) % owners) for i in range(owners)]
        back = [(j, i) for i, j in ahead]
        other = lax.all_gather(lax.ppermute(fresh, "unit", ahead), "tm", axis=0, tiled=False)
        out = correlate(odd, by_tap(other, chans), e_two, keep, chans, scale, jnp.bfloat16)
        found.append((lax.ppermute(out, "unit", back), ((unit_pos + 2 * m) % owners) // 2))
    found.append((correlate(odd, by_tap(own_panel, chans), e_two, keep, chans, scale, jnp.float32), unit_pos // 2))
    for out, pair in found:
        scores = lax.dynamic_update_slice_in_dim(
            scores, out.astype(jnp.float32), pair * width, 1
        )

    share = chans // tm_count
    part = own_panel.reshape(tm_count, panel, tpd, chans)
    part = lax.dynamic_slice_in_dim(part, tm_pos * share, share, 3)
    part = jnp.transpose(part, (1, 3, 0, 2)).reshape(panel, share, padded)[:, :, :taps]
    return (part.reshape(panel, share * taps), scores)


def solution(mesh):
    in_specs = (P(AXES, None), P(AXES), P(AXES), P("unit", None))
    out_specs = (P("unit", "tm"), P("unit", "tm"))
    return jax.shard_map(body, mesh=mesh, in_specs=in_specs, out_specs=out_specs, check_vma=False)
```

time: 396 us -> 230 us (0.58)
  local copies, waits for them, and re-layouts: 137 us -> 41.4 us
  waiting for transfers between devices: 133 us -> 61.7 us
  matrix products: 63.9 us -> 0 us
  blocking collectives: 13.2 us -> 57.2 us
  Pallas kernels: 0 us -> 36.6 us
  other arithmetic: 17.5 us -> 5.51 us
    psum x1 -> x0, waiting for transfers between devices: 86.6 us -> none  [body(): total_sums, total_counts = lax.psum((sums, counts), 'tm')]
    gather x96 -> x0, local copies, waits for them, and re-layouts: 85.4 us -> none
    ppermute x1 -> x4, waiting for transfers between devices: 0.01 us -> 61 us  [the longest x1 37.8 us: body(): lax.ppermute(mine_rows, 'unit', [(i, i ^ 1) for i in range(owners)])]
    unnamed x0 -> x1, blocking collectives: none -> 57.2 us
    conv_general_dilated x1 -> x0, matrix products: 56.5 us -> none  [correlate(): lax.conv_general_dilated(extended[None], kernel, (STRIDE,), 'VALID', dime...]
    pallas_call x0 -> x5, Pallas kernels: none -> 36.6 us  [the longest x2 25.8 us: correlate(): pl.pallas_call(functools.partial(correlate_kernel, chans, scale), out_sha...]
    all_to_all x2 -> x1, waiting for transfers between devices: 34.7 us -> 0.01 us  [body(): lax.all_to_all(send.reshape(devices, CAP * tpd, chans), AXES, split_axis=...]
    psum x1 -> x0, blocking collectives: 13.2 us -> none  [body(): total_sums, total_counts = lax.psum((sums, counts), 'tm')]
  transfers between devices with their start and end apart: 5 -> 7, of which waited for: 3 -> 3; matrix products, arithmetic and copies ran while one was open for 33% -> 20% of each run, Pallas kernels for 0% -> 13%
where the time goes in v1:
time: 230 us; the launch traced here: 229 us
  waiting for transfers between devices  61.7 us (27%)
  blocking collectives  57.2 us (25%)
  local copies, waits for them, and re-layouts  41.4 us (18%)
  Pallas kernels  36.6 us (16%)
  between operations  14.2 us (6%)
  starting transfers between devices  12.6 us (5%)
  other arithmetic  5.51 us (2%)
    unnamed x1, blocking collectives  57.2 us
    ppermute x1, waiting for transfers between devices, body(): lax.ppermute(mine_rows, 'unit', [(i, i ^ 1) for i in range(owners)])  37.8 us
    pallas_call x2, Pallas kernels, correlate(): pl.pallas_call(functools.partial(correlate_kernel, chans, scale), out_sha...  25.8 us
    reshape x1, local copies, waits for them, and re-layouts, body(): cube = old_templates.reshape(panel, chans, taps)  19.6 us
    ppermute x1, waiting for transfers between devices, body(): lax.ppermute(fresh, 'unit', ahead)  18.5 us
    unnamed x19, local copies, waits for them, and re-layouts  10.4 us
    transpose x1, local copies, waits for them, and re-layouts, body(): old = jnp.transpose(cube, (0, 2, 1)).reshape(panel, tpd * chans)  7.91 us
    all_to_all x1, starting transfers between devices, body(): lax.all_to_all(send.reshape(devices, CAP * tpd, chans), AXES, split_axis=...  7.41 us
  transfers between devices with their start and end apart: 7, of which 3 were waited for; matrix products, arithmetic and copies ran while one was open for 20% of the time, Pallas kernels for 13%

profile of v1, /device:TPU:0, one launch (start us, length us, event | category | flops | bytes accessed | tf_op | source)
XLA Modules:
  0.0 229.3 jit_solution(13499091219962763432)
XLA Ops:
  7.2 4.1 %pack.1 = bf16[2048,384]{1,0:T(8,128)(2,1)} custom-call(s32[32]{0:T(128)} %times_ref.1, s32[32]{0:T(128)} %labels_ref.1, s32[1]{0:T(128)} %bitcast.base_ref, bf16[2048,384]{1,0:T(8,128)(2,1)} %rec_ref.3), custom_call_target="tpu_custom_call" | custom-call | flops 100000000 | bytes 4000000 | tf_op jit(solution)/shard_map/pack/pallas_call | solution.py:66
  11.3 7.4 %all-to-all-start = ((bf16[32,64,384]{2,1,0:T(8,128)(2,1)}), bf16[32,64,384]{2,1,0:T(8,128)(2,1)}, u32[]{:S(2)}, u32[]{:S(2)}) async-start(bf16[32,64,384]{2,1,0:T(8,128)(2,1)} %bitcast.21), calls=%async_computation | async-start | bytes 3145728 | tf_op jit(solution)/shard_map/all_to_all | solution.py:254
  19.0 57.2 %all-reduce.1 = s32[1024]{0:T(1024)S(1)} all-reduce(s32[1024]{0:T(1024)S(1)} %dynamic-update-slice), channel_id=1, replica_groups=mesh['tm'=8,'unit'=4] {'tm','unit'}, use_global_device_ids=true, to_apply=%add.1 | all-reduce | flops 1024 | bytes 8192
  78.0 19.6 %reshape.163 = bf16[64,384,61]{2,1,0:T(8,128)(2,1)} reshape(bf16[64,23424]{1,0:T(8,128)(2,1)S(1)} %copy-done.2) | data formatting | bytes 5996544 | tf_op jit(solution)/shard_map/reshape | solution.py:266
  97.6 7.9 %dynamic-slice_bitcast_fusion = bf16[64,8,384]{1,2,0:T(8,128)(2,1)} fusion(s32[]{:T(128)S(6)} %select_n.63, bf16[64,384,61]{2,1,0:T(8,128)(2,1)} %reshape.163), kind=kLoop, calls=%fused_computation | loop fusion | bytes 3391492 | tf_op jit(solution)/shard_map/transpose | solution.py:269
  105.5 6.1 %copy.15 = bf16[8,8,8,384]{3,1,2,0:T(8,128)(2,1)} copy(bf16[8,8,8,384]{2,3,1,0:T(8,128)(2,1)} %bitcast.20) | data formatting | bytes 786432
  111.6 3.5 %refine.1 = bf16[64,3072]{1,0:T(8,128)(2,1)} custom-call(s32[1,2048]{1,0:T(1,128)} %add.95.key_ref, bf16[2048,384]{1,0:T(8,128)(2,1)} %bitcast.2.got_ref, bf16[64,3072]{1,0:T(8,128)(2,1)} %bitcast.26), custom_call_target="tpu_custom_call" | custom-call | flops 800000000 | bytes 3000000 | tf_op jit(solution)/shard_map/refine/pallas_call | solution.py:139
  115.1 0.8 collective-permute-start
  115.9 18.5 %collective-permute-done = bf16[64,3072]{1,0:T(8,128)(2,1)S(1)} collective-permute-done((bf16[64,3072]{1,0:T(8,128)(2,1)}, bf16[64,3072]{1,0:T(8,128)(2,1)S(1)}, u32[]{:S(2)}, u32[]{:S(2)}) %collective-permute-start) | collective-permute-done | bytes 393248 | tf_op jit(solution)/shard_map/ppermute | solution.py:288
  134.4 0.7 copy-done.5
  135.9 3.1 %fold.1 = bf16[256,3072]{1,0:T(8,128)(2,1)} custom-call(bf16[2048,384]{1,0:T(8,128)(2,1)} %rec_ref.3), custom_call_target="tpu_custom_call" | custom-call | flops 200000000 | bytes 4000000 | tf_op jit(solution)/shard_map/fold/pallas_call | solution.py:97
  139.0 0.9 slice.9
  140.0 1.3 collective-permute-start.1
  141.3 4.7 %collective-permute-done.1 = bf16[8,3072]{1,0:T(8,128)(2,1)S(1)} collective-permute-done((bf16[8,3072]{1,0:T(8,128)(2,1)S(1)}, bf16[8,3072]{1,0:T(8,128)(2,1)S(1)}, u32[]{:S(2)}, u32[]{:S(2)}) %collective-permute-start.1) | collective-permute-done | bytes 49184 | tf_op jit(solution)/shard_map/ppermute | solution.py:273
  145.9 2.7 %pad_maximum_fusion.1 = bf16[272,3072]{1,0:T(8,128)(2,1)} fusion(bf16[8,3072]{1,0:T(8,128)(2,1)S(1)} %broadcast_in_dim.27, bf16[8,3072]{1,0:T(8,128)(2,1)S(1)} %collective-permute-done.1, bf16[256,3072]{1,0:T(8,128)(2,1)} %fold.1), kind=kLoop, calls=%fused_computation.2 | loop fusion | flops 5013504 | bytes 3342336 | tf_op jit(solution)/shard_map/concatenate | solution.py:275
  148.7 37.8 %collective-permute-done.2 = bf16[272,3072]{1,0:T(8,128)(2,1)S(1)} collective-permute-done((bf16[272,3072]{1,0:T(8,128)(2,1)}, bf16[272,3072]{1,0:T(8,128)(2,1)S(1)}, u32[]{:S(2)}, u32[]{:S(2)}) %collective-permute-start.2) | collective-permute-done | bytes 1671200 | tf_op jit(solution)/shard_map/ppermute | solution.py:276
  186.5 1.8 pad_maximum_fusion.e_ref
  188.3 12.6 %correlate.2 = bf16[64,2048]{1,0:T(8,128)(2,1)} custom-call(s32[1]{0:T(128)} %bitcast.6.odd_ref, bf16[8,64,3072]{2,1,0:T(8,128)(2,1)} %bitcast.27, bf16[544,3072]{1,0:T(8,128)(2,1)} %pad_maximum_fusion.e_ref), custom_call_target="tpu_custom_call" | custom-call | flops 8000000000 | bytes 8000000 | tf_op jit(solution)/shard_map/correlate/pallas_call | solution.py:206
  200.9 3.0 %collective-permute-start.3 = (bf16[64,2048]{1,0:T(8,128)(2,1)}, bf16[64,2048]{1,0:T(8,128)(2,1)S(1)}, u32[]{:S(2)}, u32[]{:S(2)}) collective-permute-start(bf16[64,2048]{1,0:T(8,128)(2,1)} %correlate.2), channel_id=1, source_target_pairs={{2,0},{3,1},{0,2},{1,3},{6,4},{7,5},{4,6},{5,7},{10,8},{11,9},{8,1... | collective-permute-start | bytes 786440 | tf_op jit(solution)/shard_map/ppermute | solution.py:290
  204.0 13.2 %correlate.3 = f32[64,2048]{1,0:T(8,128)} custom-call(s32[1]{0:T(128)} %bitcast.6.odd_ref, bf16[8,64,3072]{2,1,0:T(8,128)(2,1)} %bitcast.24, bf16[544,3072]{1,0:T(8,128)(2,1)} %pad_maximum_fusion.e_ref), custom_call_target="tpu_custom_call" | custom-call | flops 8000000000 | bytes 8000000 | tf_op jit(solution)/shard_map/correlate/pallas_call | solution.py:206
  217.2 0.7 copy.16
  218.3 1.6 copy.14
  220.3 1.0 copy.13
  221.5 1.0 copy-done.3
  (37 shorter events, 3.6 us)
Async XLA Ops:
  7.2 11.6 %copy-start.6 = (s32[32]{0:T(128)S(1)}, s32[32]{0:T(128)}, u32[]{:S(2)}) copy-start(s32[32]{0:T(128)} %labels_ref.1) | copy-start | bytes 388
  7.2 70.9 %copy-start.2 = (bf16[64,23424]{1,0:T(8,128)(2,1)S(1)}, bf16[64,23424]{1,0:T(8,128)(2,1)}, u32[]{:S(2)}) copy-start(bf16[64,23424]{1,0:T(8,128)(2,1)} %param.7) | copy-start | bytes 8994820
  11.3 100.3 %all-to-all-start = ((bf16[32,64,384]{2,1,0:T(8,128)(2,1)}), bf16[32,64,384]{2,1,0:T(8,128)(2,1)}, u32[]{:S(2)}, u32[]{:S(2)}) async-start(bf16[32,64,384]{2,1,0:T(8,128)(2,1)} %bitcast.21), calls=%async_computation | async-start | bytes 3145728 | tf_op jit(solution)/shard_map/all_to_all | solution.py:254
  18.7 169.6 %all-gather.7.cloned.1.call-start = ((), (), s32[]{:S(2)}) async-start(), calls=%async_computation.2 | async-start | bytes 3538944 | tf_op jit(solution)/shard_map/all_gather | solution.py:288
  115.1 19.3 %collective-permute-start = (bf16[64,3072]{1,0:T(8,128)(2,1)}, bf16[64,3072]{1,0:T(8,128)(2,1)S(1)}, u32[]{:S(2)}, u32[]{:S(2)}) collective-permute-start(bf16[64,3072]{1,0:T(8,128)(2,1)} %refine.1), channel_id=1, source_target_pairs={{0,2},{1,3},{2,0},{3,1},{4,6},{5,7},{6,4},{7,5},{8,10},{9,11},{10,... | collective-permute-start | bytes 1179656 | tf_op jit(solution)/shard_map/ppermute | solution.py:288
  134.4 0.7 copy-start.5
  135.2 68.8 %all-gather.5.cloned.1.call-start = ((), (), s32[]{:S(2)}) async-start(), calls=%async_computation.1 | async-start | bytes 3538944 | tf_op jit(solution)/shard_map/all_gather | solution.py:281
  139.0 47.4 %copy-start = (bf16[256,3072]{1,0:T(8,128)(2,1)S(1)}, bf16[256,3072]{1,0:T(8,128)(2,1)}, u32[]{:S(2)}) copy-start(bf16[256,3072]{1,0:T(8,128)(2,1)} %fold.1) | copy-start | bytes 4718596
  140.0 6.0 %collective-permute-start.1 = (bf16[8,3072]{1,0:T(8,128)(2,1)S(1)}, bf16[8,3072]{1,0:T(8,128)(2,1)S(1)}, u32[]{:S(2)}, u32[]{:S(2)}) collective-permute-start(bf16[8,3072]{1,0:T(8,128)(2,1)S(1)} %slice.9), channel_id=1, source_target_pairs={{1,0},{2,1},{3,2},{4,3},{5,4},{6,5},{7,6},{8,7},{9,8},{10,9},{11,1... | collective-permute-start | bytes 147464 | tf_op jit(solution)/shard_map/ppermute | solution.py:273
  148.7 37.8 %collective-permute-start.2 = (bf16[272,3072]{1,0:T(8,128)(2,1)}, bf16[272,3072]{1,0:T(8,128)(2,1)S(1)}, u32[]{:S(2)}, u32[]{:S(2)}) collective-permute-start(bf16[272,3072]{1,0:T(8,128)(2,1)} %pad_maximum_fusion.1), channel_id=1, source_target_pairs={{0,1},{1,0},{2,3},{3,2},{4,5},{5,4},{6,7},{7,6},{8,9},{9,8},{10,11... | collective-permute-start | bytes 5013512 | tf_op jit(solution)/shard_map/ppermute | solution.py:276
  200.9 20.3 %collective-permute-start.3 = (bf16[64,2048]{1,0:T(8,128)(2,1)}, bf16[64,2048]{1,0:T(8,128)(2,1)S(1)}, u32[]{:S(2)}, u32[]{:S(2)}) collective-permute-start(bf16[64,2048]{1,0:T(8,128)(2,1)} %correlate.2), channel_id=1, source_target_pairs={{2,0},{3,1},{0,2},{1,3},{6,4},{7,5},{4,6},{5,7},{10,8},{11,9},{8,1... | collective-permute-start | bytes 786440 | tf_op jit(solution)/shard_map/ppermute | solution.py:290
  204.0 13.2 %copy-start.1 = (bf16[512,3072]{1,0:T(8,128)(2,1)S(1)}, bf16[512,3072]{1,0:T(8,128)(2,1)}, u32[]{:S(2)}) copy-start(bf16[512,3072]{1,0:T(8,128)(2,1)} %all-gather.5.cloned.1.call-done) | copy-start | bytes 9437188
  218.3 3.1 %copy-start.4 = (f32[64,2048]{1,0:T(8,128)S(1)}, f32[64,2048]{1,0:T(8,128)}, u32[]{:S(2)}) copy-start(f32[64,2048]{1,0:T(8,128)} %correlate.3) | copy-start | bytes 1572868
  221.4 1.0 copy-start.3
Sparse Core Ops, SparseCore 0:
  135.3 32.3 all-gather.6
  169.5 32.3 all-gather.4

commit v2 on v1

--- a/solution.py
+++ b/solution.py
@@ -148,12 +148,38 @@
     )(key, got, old)
 
 
-def correlate_kernel(chans, scale, odd_ref, t_ref, e_ref, out_ref, rhs, part, acc):
-    blocks, panel, lanes = t_ref.shape
-    height = e_ref.shape[0] // 2
+def correlate_kernel(
+    chans, tpd, scale, place_ref, same_ref, cross_ref, mine_ref, theirs_ref, out_ref, t_buf, e_buf, t_sem, e_sem, rhs, part, acc
+):
+    pairs = same_ref.shape[0]
+    blocks, panel, lanes = t_buf.shape
+    height = mine_ref.shape[0]
     keep = acc.shape[0] // 2
     shift = STRIDE * chans
+    core, odd, pair = place_ref[0], place_ref[1], place_ref[2]
+    e_copies = [
+        pltpu.make_async_copy(ref, e_buf.at[h * height : (h + 1) * height, :], e_sem.at[h])
+        for h, ref in enumerate((mine_ref, theirs_ref))
+    ]
+    t_copies = []
+    for i in range(pairs):
+        for n, ref, side in ((0, same_ref, core), (1, cross_ref, 1 - core)):
+            chunk = 2 * i + side
+            if tpd == ROWS:
+                target = t_buf.at[chunk]
+            else:
+                first = pl.multiple_of(chunk * tpd % ROWS * chans, 128)
+                target = t_buf.at[chunk * tpd // ROWS, :, pl.ds(first, tpd * chans)]
+            t_copies.append(pltpu.make_async_copy(ref.at[i], target, t_sem.at[2 * i + n]))
+    for copy in t_copies[:2] + e_copies + t_copies[2:]:
+        copy.start()
+    for copy in e_copies:
+        copy.wait()
+    waited = 0
     for a in range(blocks + 1):
+        while a < blocks and waited < len(t_copies) and waited // 2 * 2 * tpd < (a + 1) * ROWS:
+            t_copies[waited].wait()
+            waited += 1
         used = lanes if a < blocks else lanes // 2
         for q in range(FOLD):
             rows = slice(q * panel, (q + 1) * panel)
@@ -161,16 +187,16 @@
             if cut > 0:
                 low = min(cut, used)
                 if a > 0:
-                    rhs[rows, 0:low] = t_ref[a - 1, :, lanes - cut : lanes - cut + low]
+                    rhs[rows, 0:low] = t_buf[a - 1, :, lanes - cut : lanes - cut + low]
                 else:
                     rhs[rows, 0:low] = jnp.zeros((panel, low), jnp.bfloat16)
             if cut < used:
                 if a < blocks:
-                    rhs[rows, cut:used] = t_ref[a, :, 0 : used - cut]
+                    rhs[rows, cut:used] = t_buf[a, :, 0 : used - cut]
                 else:
                     rhs[rows, cut:used] = jnp.zeros((panel, used - cut), jnp.bfloat16)
         part[...] = lax.dot_general(
-            e_ref[:, 0:used], rhs[:, 0:used], NT, preferred_element_type=jnp.float32
+            e_buf[:, 0:used], rhs[:, 0:used], NT, preferred_element_type=jnp.float32
         )
         for h in range(2):
             found = part[h * height + a : h * height + a + keep, :]
@@ -183,7 +209,6 @@
     lane = lax.broadcasted_iota(jnp.int32, (FOLD * width, FOLD * width), 1)
     weave = (lane == (place % width) * FOLD + place // width).astype(jnp.bfloat16)
     per_half = keep // width
-    odd = odd_ref[0]
     for h in range(2):
         side = odd if h == 0 else 1 - odd
         for b in range(per_half):
@@ -195,37 +220,41 @@
             if out_ref.dtype == jnp.float32:
                 rest = (row - high.astype(jnp.float32)).astype(jnp.bfloat16)
                 found = found + jnp.dot(rest, weave, preferred_element_type=jnp.float32)
-            at = pl.multiple_of((side * per_half + b) * (FOLD * width), FOLD * width)
+            at = ((2 * pair + side) * per_half + b) * (FOLD * width)
+            at = pl.multiple_of(at, FOLD * width)
             out_ref[:, pl.ds(at, FOLD * width)] = found.astype(out_ref.dtype)
 
 
-def correlate(odd, t_all, e_two, keep, chans, scale, dtype):
-    panel = t_all.shape[1]
-    smem = pl.BlockSpec(memory_space=pltpu.SMEM)
-    vmem = pl.BlockSpec(memory_space=pltpu.VMEM)
+def correlate(place, same, cross, mine, theirs, keep, chans, tpd, scale, width, dtype):
+    panel = same.shape[1]
+    height = mine.shape[0]
+    blocks = 2 * same.shape[0] * tpd // ROWS
+    anywhere = pl.BlockSpec(memory_space=pl.ANY)
     return pl.pallas_call(
-        functools.partial(correlate_kernel, chans, scale),
-        out_shape=jax.ShapeDtypeStruct((panel, 2 * keep * FOLD), dtype),
-        in_specs=[smem, vmem, vmem],
-        out_specs=vmem,
+        functools.partial(correlate_kernel, chans, tpd, scale),
+        out_shape=jax.ShapeDtypeStruct((panel, width), dtype),
+        in_specs=[pl.BlockSpec(memory_space=pltpu.SMEM)] + [anywhere] * 4,
+        out_specs=pl.BlockSpec(memory_space=pltpu.VMEM),
         scratch_shapes=[
+            pltpu.VMEM((blocks, panel, ROWS * chans), jnp.bfloat16),
+            pltpu.VMEM((2 * height, ROWS * chans), jnp.bfloat16),
+            pltpu.SemaphoreType.DMA((2 * same.shape[0],)),
+            pltpu.SemaphoreType.DMA((2,)),
             pltpu.VMEM((FOLD * panel, ROWS * chans), jnp.bfloat16),
-            pltpu.VMEM((e_two.shape[0], FOLD * panel), jnp.float32),
+            pltpu.VMEM((2 * height, FOLD * panel), jnp.float32),
             pltpu.VMEM((2 * keep, FOLD * panel), jnp.float32),
         ],
         compiler_params=params(),
         cost_estimate=pl.CostEstimate(flops=8 * 10**9, bytes_accessed=8 * 10**6, transcendentals=0),
         name="correlate",
-    )(odd, t_all, e_two)
-
-
-def by_tap(parts, chans):
-    count, panel, lanes = parts.shape
-    per = ROWS * chans // lanes
-    if per == 1:
-        return parts
-    parts = parts.reshape(count // per, per, panel, lanes)
-    return jnp.transpose(parts, (0, 2, 1, 3)).reshape(count // per, panel, per * lanes)
+    )(place, same, cross, mine, theirs)
+
+
+def gather_panel(value):
+    size = lax.axis_size("tm")
+    groups = [list(range(c, size, 2)) for c in range(2)]
+    same = lax.all_gather(value, "tm", axis=0, tiled=False, axis_index_groups=groups)
+    return same, lax.ppermute(same, "tm", [(i, i ^ 1) for i in range(size)])
 
 
 def body(recording, spike_times, unit_labels, old_templates):
@@ -255,7 +284,8 @@
         send.reshape(devices, CAP * tpd, chans), AXES, split_axis=0, concat_axis=0, tiled=True
     ).reshape(devices * CAP * tpd, chans)
 
-    labels = lax.all_gather(unit_labels, AXES, axis=0, tiled=True).reshape(devices, spikes)
+    wide = jnp.pad(unit_labels.reshape(1, spikes), ((0, 7), (0, -spikes % 128)))
+    labels = lax.all_gather(wide, AXES, axis=0, tiled=False)[:, 0, :spikes]
     mine = labels // panel == unit_pos
     counted = mine.astype(jnp.int32)
     rank = jnp.cumsum(counted, axis=1) - counted
@@ -268,37 +298,53 @@
     cube = lax.dynamic_slice_in_dim(cube, tm_pos * tpd, tpd, 2)
     old = jnp.transpose(cube, (0, 2, 1)).reshape(panel, tpd * chans)
 
-    folded = fold(recording)
+    folded = fold(lax.optimization_barrier((recording, send))[0])
     halo = padded // ROWS
     following = lax.ppermute(folded[:halo], AXES, [(i, i - 1) for i in range(1, devices)])
     spare = jnp.zeros((16 - halo % 16, ROWS * chans), jnp.bfloat16)
     mine_rows = jnp.concatenate([folded, following, spare], axis=0)
     their_rows = lax.ppermute(mine_rows, "unit", [(i, i ^ 1) for i in range(owners)])
-    e_two = jnp.concatenate([mine_rows, their_rows], axis=0)
+    got, their_rows = lax.optimization_barrier((got, their_rows))
 
     fresh = refine(key, got, old, tpd)
-    odd = (unit_pos % 2).astype(jnp.int32).reshape(1)
-    own_panel = lax.all_gather(fresh, "tm", axis=0, tiled=False)
+    core = tm_pos % 2
+    own = gather_panel(fresh)
     width = 2 * keep * FOLD
-    scores = jnp.zeros((panel, owners // 2 * width), jnp.float32)
+
+    share = chans // tm_count
+    near, far = [
+        lax.dynamic_slice_in_dim(
+            value.reshape(tm_count // 2, panel, tpd, chans), tm_pos * share, share, 3
+        )
+        for value in own
+    ]
+    part = jnp.stack([jnp.where(core == 0, near, far), jnp.where(core == 0, far, near)], axis=1)
+    part = part.reshape(tm_count, panel, tpd, share)
+    part = jnp.transpose(part, (1, 3, 0, 2)).reshape(panel, share, padded)[:, :, :taps]
+    part = part.reshape(panel, share * taps)
+
+    odd = unit_pos % 2
     found = []
     for m in range(1, owners // 2):
         ahead = [(i, (i + 2 * m) % owners) for i in range(owners)]
         back = [(j, i) for i, j in ahead]
-        other = lax.all_gather(lax.ppermute(fresh, "unit", ahead), "tm", axis=0, tiled=False)
-        out = correlate(odd, by_tap(other, chans), e_two, keep, chans, scale, jnp.bfloat16)
+        other = gather_panel(lax.ppermute(fresh, "unit", ahead))
+        if m == 1:
+            part, other = lax.optimization_barrier((part, other))
+        place = jnp.stack([core, odd, 0 * core]).astype(jnp.int32)
+        out = correlate(
+            place, *other, mine_rows, their_rows, keep, chans, tpd, scale, width, jnp.bfloat16
+        )
         found.append((lax.ppermute(out, "unit", back), ((unit_pos + 2 * m) % owners) // 2))
-    found.append((correlate(odd, by_tap(own_panel, chans), e_two, keep, chans, scale, jnp.float32), unit_pos // 2))
+    place = jnp.stack([core, odd, unit_pos // 2]).astype(jnp.int32)
+    scores = correlate(
+        place, *own, mine_rows, their_rows, keep, chans, tpd, scale, owners // 2 * width, jnp.float32
+    )
     for out, pair in found:
         scores = lax.dynamic_update_slice_in_dim(
             scores, out.astype(jnp.float32), pair * width, 1
         )
-
-    share = chans // tm_count
-    part = own_panel.reshape(tm_count, panel, tpd, chans)
-    part = lax.dynamic_slice_in_dim(part, tm_pos * share, share, 3)
-    part = jnp.transpose(part, (1, 3, 0, 2)).reshape(panel, share, padded)[:, :, :taps]
-    return (part.reshape(panel, share * taps), scores)
+    return (part, scores)
 
 
 def solution(mesh):

time: 230 us -> 307 us (1.33)
  blocking collectives: 57.2 us -> 98.6 us
  starting transfers between devices: 12.6 us -> 29.5 us
  waiting for transfers between devices: 61.7 us -> 76.2 us
    all_gather x0 -> x1, blocking collectives: none -> 98.6 us  [body(): labels = lax.all_gather(wide, AXES, axis=0, tiled=False)[:, 0, :spikes]]
    unnamed x1 -> x0, blocking collectives: 57.2 us -> none
    all_gather x2, waiting for transfers between devices: 0.01 us -> 48.5 us  [gather_panel(): lax.all_gather(value, 'tm', axis=0, tiled=False, axis_index_groups=groups)]
    ppermute x1, waiting for transfers between devices: 37.8 us -> 0.01 us  [body(): lax.ppermute(mine_rows, 'unit', [(i, i ^ 1) for i in range(owners)])]
    ppermute x1, starting transfers between devices: 0.01 us -> 18 us  [body(): lax.ppermute(mine_rows, 'unit', [(i, i ^ 1) for i in range(owners)])]
    ppermute x1, waiting for transfers between devices: 4.68 us -> 15.4 us  [body(): lax.ppermute(folded[:halo], AXES, [(i, i - 1) for i in range(1, devices)])]
    ppermute x1 -> x3, waiting for transfers between devices: 18.5 us -> 12.3 us  [the longest x1 12.2 us: body(): other = gather_panel(lax.ppermute(fresh, 'unit', ahead))]
    reshape x3, local copies, waits for them, and re-layouts: 1.35 us -> 4.52 us  [the longest x1 3.25 us: body(): value.reshape(tm_count // 2, panel, tpd, chans)]
  transfers between devices with their start and end apart: 7 -> 9, of which waited for: 3 -> 4; matrix products, arithmetic and copies ran while one was open for 20% -> 16% of each run, Pallas kernels for 13% -> 6%
where the time goes in v2:
time: 307 us
  blocking collectives  98.6 us (32%)
  waiting for transfers between devices  76.2 us (25%)
  local copies, waits for them, and re-layouts  43 us (14%)
  Pallas kernels  38.8 us (13%)
  starting transfers between devices  29.5 us (10%)
  between operations  14.2 us (5%)
  other arithmetic  6.39 us (2%)
    all_gather x1, blocking collectives, body(): labels = lax.all_gather(wide, AXES, axis=0, tiled=False)[:, 0, :spikes]  98.6 us
    all_gather x2, waiting for transfers between devices, gather_panel(): lax.all_gather(value, 'tm', axis=0, tiled=False, axis_index_groups=groups)  48.5 us
    pallas_call x2, Pallas kernels, correlate(): pl.pallas_call(functools.partial(correlate_kernel, chans, tpd, scale), ou...  28.2 us
    reshape x1, local copies, waits for them, and re-layouts, body(): cube = old_templates.reshape(panel, chans, taps)  19.6 us
    ppermute x1, starting transfers between devices, body(): lax.ppermute(mine_rows, 'unit', [(i, i ^ 1) for i in range(owners)])  18 us
    ppermute x1, waiting for transfers between devices, body(): lax.ppermute(folded[:halo], AXES, [(i, i - 1) for i in range(1, devices)])  15.4 us
    ppermute x1, waiting for transfers between devices, body(): other = gather_panel(lax.ppermute(fresh, 'unit', ahead))  12.2 us
    unnamed x9, local copies, waits for them, and re-layouts  8.89 us
  transfers between devices with their start and end apart: 9, of which 4 were waited for; matrix products, arithmetic and copies ran while one was open for 16% of the time, Pallas kernels for 6%

profile of v2, /device:TPU:0, one launch (start us, length us, event | category | flops | bytes accessed | tf_op | source)
XLA Modules:
  0.0 306.7 jit_solution(13706165154526958388)
XLA Ops:
  7.2 4.0 %pack.1 = bf16[2048,384]{1,0:T(8,128)(2,1)} custom-call(s32[32]{0:T(128)} %times_ref.1, s32[32]{0:T(128)} %labels_ref.1, s32[1]{0:T(128)} %bitcast.3.base_ref, bf16[2048,384]{1,0:T(8,128)(2,1)} %rec_ref.2), custom_call_target="tpu_custom_call" | custom-call | flops 100000000 | bytes 4000000 | tf_op jit(solution)/shard_map/pack/pallas_call | solution.py:66
  11.1 7.4 %all-to-all-start = ((bf16[32,64,384]{2,1,0:T(8,128)(2,1)}), bf16[32,64,384]{2,1,0:T(8,128)(2,1)}, u32[]{:S(2)}, u32[]{:S(2)}) async-start(bf16[32,64,384]{2,1,0:T(8,128)(2,1)} %bitcast.38), calls=%async_computation | async-start | bytes 3145728 | tf_op jit(solution)/shard_map/all_to_all | solution.py:283
  18.6 3.1 %fold.1 = bf16[256,3072]{1,0:T(8,128)(2,1)} custom-call(bf16[2048,384]{1,0:T(8,128)(2,1)} %rec_ref.2), custom_call_target="tpu_custom_call" | custom-call | flops 200000000 | bytes 4000000 | tf_op jit(solution)/shard_map/fold/pallas_call | solution.py:97
  21.7 0.8 slice.13
  22.5 1.4 collective-permute-start
  24.1 15.4 %collective-permute-done = bf16[8,3072]{1,0:T(8,128)(2,1)S(1)} collective-permute-done((bf16[8,3072]{1,0:T(8,128)(2,1)S(1)}, bf16[8,3072]{1,0:T(8,128)(2,1)S(1)}, u32[]{:S(2)}, u32[]{:S(2)}) %collective-permute-start) | collective-permute-done | bytes 49184 | tf_op jit(solution)/shard_map/ppermute | solution.py:303
  39.5 3.1 %maximum_maximum_fusion.mine_ref = bf16[272,3072]{1,0:T(8,128)(2,1)} fusion(bf16[8,3072]{1,0:T(8,128)(2,1)S(1)} %collective-permute-done, bf16[256,3072]{1,0:T(8,128)(2,1)} %fold.1, bf16[272]{0:T(512)(128)(2,1)S(1)} %pad.20.clone), kind=kLoop, calls=%fused_computation.1 | loop fusion | flops 5013504 | bytes 3293728 | tf_op jit(solution)/shard_map/concatenate | solution.py:305
  42.6 18.0 %collective-permute-start.1 = (bf16[272,3072]{1,0:T(8,128)(2,1)}, bf16[272,3072]{1,0:T(8,128)(2,1)}, u32[]{:S(2)}, u32[]{:S(2)}) collective-permute-start(bf16[272,3072]{1,0:T(8,128)(2,1)} %maximum_maximum_fusion.mine_ref), channel_id=1, source_target_pairs={{0,1},{1,0},{2,3},{3,2},{4,5},{5,4},{6,7},{7,6},{8,9},{9,8},{10,11... | collective-permute-start | bytes 5013512 | tf_op jit(solution)/shard_map/ppermute | solution.py:306
  60.7 98.6 %all-gather = s32[256,128]{1,0:T(8,128)S(1)} all-gather(s32[8,128]{1,0:T(8,128)S(1)} %pad.8), channel_id=2, replica_groups=mesh['tm'=8,'unit'=4] {'tm','unit'}, dimensions={0}, use_global_device_ids=true | all-gather | bytes 135168 | tf_op jit(solution)/shard_map/all_gather | solution.py:288
  160.9 19.6 %reshape.166 = bf16[64,384,61]{2,1,0:T(8,128)(2,1)} reshape(bf16[64,23424]{1,0:T(8,128)(2,1)S(1)} %copy-done) | data formatting | bytes 5996544 | tf_op jit(solution)/shard_map/reshape | solution.py:296
  180.5 7.9 %dynamic-slice_bitcast_fusion = bf16[64,8,384]{1,2,0:T(8,128)(2,1)} fusion(s32[]{:T(128)S(6)} %select_n.79, bf16[64,384,61]{2,1,0:T(8,128)(2,1)} %reshape.166), kind=kLoop, calls=%fused_computation | loop fusion | bytes 3391492 | tf_op jit(solution)/shard_map/transpose | solution.py:299
  188.4 6.1 %copy.25 = bf16[8,8,8,384]{3,1,2,0:T(8,128)(2,1)} copy(bf16[8,8,8,384]{2,3,1,0:T(8,128)(2,1)} %bitcast.37) | data formatting | bytes 786432
  194.5 3.5 %refine.1 = bf16[64,3072]{1,0:T(8,128)(2,1)} custom-call(s32[1,2048]{1,0:T(1,128)} %add.99.key_ref, bf16[2048,384]{1,0:T(8,128)(2,1)} %bitcast.5.got_ref, bf16[64,3072]{1,0:T(8,128)(2,1)} %bitcast.46), custom_call_target="tpu_custom_call" | custom-call | flops 800000000 | bytes 3000000 | tf_op jit(solution)/shard_map/refine/pallas_call | solution.py:139
  198.2 12.2 %collective-permute-done.3 = bf16[64,3072]{1,0:T(8,128)(2,1)S(1)} collective-permute-done((bf16[64,3072]{1,0:T(8,128)(2,1)}, bf16[64,3072]{1,0:T(8,128)(2,1)S(1)}, u32[]{:S(2)}, u32[]{:S(2)}) %collective-permute-start.3) | collective-permute-done | bytes 393248 | tf_op jit(solution)/shard_map/ppermute | solution.py:331
  210.4 0.7 copy-done.1
  211.2 15.1 %all-gather.6.cloned.1.call-done = bf16[256,3072]{1,0:T(8,128)(2,1)} async-done(((bf16[64,3072]{1,0:T(8,128)(2,1)}), bf16[256,3072]{1,0:T(8,128)(2,1)}) %all-gather.6.cloned.1.call-update) | async-done | bytes 1572880 | tf_op jit(solution)/shard_map/all_gather | solution.py:256
  226.3 33.4 %all-gather.8.cloned.1.call-done = bf16[256,3072]{1,0:T(8,128)(2,1)} async-done(((bf16[64,3072]{1,0:T(8,128)(2,1)}), bf16[256,3072]{1,0:T(8,128)(2,1)}) %all-gather.8.cloned.1.call-update) | async-done | bytes 1572880 | tf_op jit(solution)/shard_map/all_gather | solution.py:256
  260.9 1.7 copy.26
  263.2 3.2 %copy.21 = bf16[4,64,3072]{1,2,0:T(8,128)(2,1)S(1)} copy(bf16[4,64,3072]{2,1,0:T(8,128)(2,1)} %collective-permute-done.2.cross_ref) | data formatting | bytes 3145728 | tf_op jit(solution)/shard_map/reshape | solution.py:317
  267.3 1.0 copy.22
  268.3 13.7 %correlate.3 = bf16[64,2048]{1,0:T(8,128)(2,1)} custom-call(s32[3]{0:T(128)} %pad_add_fusion.2.place_ref, bf16[4,64,3072]{2,1,0:T(8,128)(2,1)} %bitcast.52, bf16[4,64,3072]{2,1,0:T(8,128)(2,1)} %collective-permute-done.4.cross_ref, bf16[272,3072]{1,0:T(8,128)(2,1)} %maximum_maximum_fusion.mine_ref, bf16[272,3072]{1,0:T(8,128)(2,1)} %collective-permute-done.1.theirs_ref), custom_call_target="tpu_custom_call" | custom-call | flops 8000000000 | bytes 8000000 | tf_op jit(solution)/shard_map/correlate/pallas_call | solution.py:233
  282.0 2.5 collective-permute-start.5
  284.5 14.5 %correlate.2 = f32[64,4096]{1,0:T(8,128)} custom-call(s32[3]{0:T(128)} %pad_add_fusion.place_ref, bf16[4,64,3072]{2,1,0:T(8,128)(2,1)} %bitcast.45, bf16[4,64,3072]{2,1,0:T(8,128)(2,1)} %collective-permute-done.2.cross_ref, bf16[272,3072]{1,0:T(8,128)(2,1)} %maximum_maximum_fusion.mine_ref, bf16[272,3072]{1,0:T(8,128)(2,1)} %collective-permute-done.1.theirs_ref), custom_call_target="tpu_custom_call" | custom-call | flops 8000000000 | bytes 8000000 | tf_op jit(solution)/shard_map/correlate/pallas_call | solution.py:233
  299.0 0.8 convert_dynamic-update-slice_fusion
  (36 shorter events, 4.5 us)
Async XLA Ops:
  11.1 183.4 %all-to-all-start = ((bf16[32,64,384]{2,1,0:T(8,128)(2,1)}), bf16[32,64,384]{2,1,0:T(8,128)(2,1)}, u32[]{:S(2)}, u32[]{:S(2)}) async-start(bf16[32,64,384]{2,1,0:T(8,128)(2,1)} %bitcast.38), calls=%async_computation | async-start | bytes 3145728 | tf_op jit(solution)/shard_map/all_to_all | solution.py:283
  18.6 207.8 %all-gather.6.cloned.1.call-start = ((), (), s32[]{:S(2)}) async-start(), calls=%async_computation.1 | async-start | bytes 1966080 | tf_op jit(solution)/shard_map/all_gather | solution.py:256
  22.5 38.1 %copy-start.2 = (s32[32]{0:T(128)S(1)}, s32[32]{0:T(128)}, u32[]{:S(2)}) copy-start(s32[32]{0:T(128)} %labels_ref.1) | copy-start | bytes 388
  22.5 16.9 %collective-permute-start = (bf16[8,3072]{1,0:T(8,128)(2,1)S(1)}, bf16[8,3072]{1,0:T(8,128)(2,1)S(1)}, u32[]{:S(2)}, u32[]{:S(2)}) collective-permute-start(bf16[8,3072]{1,0:T(8,128)(2,1)S(1)} %slice.13), channel_id=1, source_target_pairs={{1,0},{2,1},{3,2},{4,3},{5,4},{6,5},{7,6},{8,7},{9,8},{10,9},{11,1... | collective-permute-start | bytes 147464 | tf_op jit(solution)/shard_map/ppermute | solution.py:303
  24.1 136.9 %copy-start = (bf16[64,23424]{1,0:T(8,128)(2,1)S(1)}, bf16[64,23424]{1,0:T(8,128)(2,1)}, u32[]{:S(2)}) copy-start(bf16[64,23424]{1,0:T(8,128)(2,1)} %param.7) | copy-start | bytes 8994820
  42.6 151.9 %collective-permute-start.1 = (bf16[272,3072]{1,0:T(8,128)(2,1)}, bf16[272,3072]{1,0:T(8,128)(2,1)}, u32[]{:S(2)}, u32[]{:S(2)}) collective-permute-start(bf16[272,3072]{1,0:T(8,128)(2,1)} %maximum_maximum_fusion.mine_ref), channel_id=1, source_target_pairs={{0,1},{1,0},{2,3},{3,2},{4,5},{5,4},{6,7},{7,6},{8,9},{9,8},{10,11... | collective-permute-start | bytes 5013512 | tf_op jit(solution)/shard_map/ppermute | solution.py:306
  198.1 61.7 %all-gather.8.cloned.1.call-start = ((), (), s32[]{:S(2)}) async-start(), calls=%async_computation.2 | async-start | bytes 1966080 | tf_op jit(solution)/shard_map/all_gather | solution.py:256
  198.1 12.3 %collective-permute-start.3 = (bf16[64,3072]{1,0:T(8,128)(2,1)}, bf16[64,3072]{1,0:T(8,128)(2,1)S(1)}, u32[]{:S(2)}, u32[]{:S(2)}) collective-permute-start(bf16[64,3072]{1,0:T(8,128)(2,1)} %refine.1), channel_id=1, source_target_pairs={{0,2},{1,3},{2,0},{3,1},{4,6},{5,7},{6,4},{7,5},{8,10},{9,11},{10,... | collective-permute-start | bytes 1179656 | tf_op jit(solution)/shard_map/ppermute | solution.py:331
  210.4 0.7 copy-start.1
  226.3 36.9 %collective-permute-start.2 = (bf16[4,64,3072]{2,1,0:T(8,128)(2,1)}, bf16[4,64,3072]{2,1,0:T(8,128)(2,1)}, u32[]{:S(2)}, u32[]{:S(2)}) collective-permute-start(bf16[4,64,3072]{2,1,0:T(8,128)(2,1)} %bitcast.43), channel_id=1, source_target_pairs={{0,4},{4,0},{8,12},{12,8},{16,20},{20,16},{24,28},{28,24},{1,5},{5... | collective-permute-start | bytes 4718600 | tf_op jit(solution)/shard_map/ppermute | solution.py:257
  259.7 8.6 %collective-permute-start.4 = (bf16[4,64,3072]{2,1,0:T(8,128)(2,1)}, bf16[4,64,3072]{2,1,0:T(8,128)(2,1)}, u32[]{:S(2)}, u32[]{:S(2)}) collective-permute-start(bf16[4,64,3072]{2,1,0:T(8,128)(2,1)} %bitcast.51), channel_id=1, source_target_pairs={{0,4},{4,0},{8,12},{12,8},{16,20},{20,16},{24,28},{28,24},{1,5},{5... | collective-permute-start | bytes 4718600 | tf_op jit(solution)/shard_map/ppermute | solution.py:257
  282.0 17.0 %collective-permute-start.5 = (bf16[64,2048]{1,0:T(8,128)(2,1)}, bf16[64,2048]{1,0:T(8,128)(2,1)S(1)}, u32[]{:S(2)}, u32[]{:S(2)}) collective-permute-start(bf16[64,2048]{1,0:T(8,128)(2,1)} %correlate.3), channel_id=1, source_target_pairs={{2,0},{3,1},{0,2},{1,3},{6,4},{7,5},{4,6},{5,7},{10,8},{11,9},{8,1... | collective-permute-start | bytes 786440 | tf_op jit(solution)/shard_map/ppermute | solution.py:338
Sparse Core Ops, SparseCore 0:
  198.2 28.0 all-gather.5
  228.7 30.9 all-gather.7

commit v3 on v1

--- a/solution.py
+++ b/solution.py
@@ -148,29 +148,66 @@
     )(key, got, old)
 
 
-def correlate_kernel(chans, scale, odd_ref, t_ref, e_ref, out_ref, rhs, part, acc):
-    blocks, panel, lanes = t_ref.shape
-    height = e_ref.shape[0] // 2
+def correlate_kernel(chans, tpd, scale, masks, place_ref, *refs):
+    count = len(masks)
+    pieces, rest = refs[:count], refs[count:]
+    mine_ref, my_halo, theirs_ref, their_halo, out_ref, rhs, e_buf, t_sem, e_sem, part, acc = rest
+    half_rows = pieces[0].shape[1]
+    panel = 2 * half_rows
+    lanes = tpd * chans
+    chunks = t_sem.shape[0]
+    whole = chunks * lanes
+    height = e_buf.shape[0] // 2
     keep = acc.shape[0] // 2
     shift = STRIDE * chans
-    for a in range(blocks + 1):
-        used = lanes if a < blocks else lanes // 2
-        for q in range(FOLD):
-            rows = slice(q * panel, (q + 1) * panel)
-            cut = q * shift
-            if cut > 0:
-                low = min(cut, used)
-                if a > 0:
-                    rhs[rows, 0:low] = t_ref[a - 1, :, lanes - cut : lanes - cut + low]
-                else:
-                    rhs[rows, 0:low] = jnp.zeros((panel, low), jnp.bfloat16)
-            if cut < used:
-                if a < blocks:
-                    rhs[rows, cut:used] = t_ref[a, :, 0 : used - cut]
-                else:
-                    rhs[rows, cut:used] = jnp.zeros((panel, used - cut), jnp.bfloat16)
+    me, odd, pair = place_ref[0], place_ref[1], place_ref[2]
+
+    def spot(chunk, part_of, q):
+        first = chunk * lanes + q * shift
+        if not isinstance(chunk, int):
+            first = pl.multiple_of(first, 128)
+        return rhs.at[pl.ds(q * panel + part_of * half_rows, half_rows), pl.ds(first, lanes)]
+
+    e_copies = []
+    for n, (body_ref, halo_ref) in enumerate(((mine_ref, my_halo), (theirs_ref, their_halo))):
+        low = n * height
+        e_copies.append(
+            pltpu.make_async_copy(body_ref, e_buf.at[low : low + keep, :], e_sem.at[2 * n])
+        )
+        e_copies.append(
+            pltpu.make_async_copy(halo_ref, e_buf.at[low + keep : low + height, :], e_sem.at[2 * n + 1])
+        )
+    for copy in e_copies:
+        copy.start()
+    for ref, (part_of, items) in zip(pieces, masks):
+        for at, mask in enumerate(items):
+            chunk = jnp.bitwise_xor(me, mask)
+            for q in range(FOLD):
+                sem = t_sem.at[chunk, part_of * FOLD + q]
+                pltpu.make_async_copy(ref.at[at], spot(chunk, part_of, q), sem).start()
+    for q in range(FOLD):
+        rows = slice(q * panel, (q + 1) * panel)
+        if q > 0:
+            rhs[rows, 0 : q * shift] = jnp.zeros((panel, q * shift), jnp.bfloat16)
+        tail = rhs.shape[1] - whole - q * shift
+        if tail > 0:
+            rhs[rows, whole + q * shift :] = jnp.zeros((panel, tail), jnp.bfloat16)
+    for copy in e_copies:
+        copy.wait()
+    depth = ROWS * chans
+    per = depth // lanes
+    for a in range(chunks // per + 1):
+        for chunk in range(a * per, min((a + 1) * per, chunks)):
+            for part_of in range(2):
+                for q in range(FOLD):
+                    sem = t_sem.at[chunk, part_of * FOLD + q]
+                    pltpu.make_async_copy(pieces[0].at[0], spot(chunk, part_of, q), sem).wait()
+        used = min(depth, rhs.shape[1] - a * depth)
         part[...] = lax.dot_general(
-            e_ref[:, 0:used], rhs[:, 0:used], NT, preferred_element_type=jnp.float32
+            e_buf[:, 0:used],
+            rhs[:, a * depth : a * depth + used],
+            NT,
+            preferred_element_type=jnp.float32,
         )
         for h in range(2):
             found = part[h * height + a : h * height + a + keep, :]
@@ -183,7 +220,6 @@
     lane = lax.broadcasted_iota(jnp.int32, (FOLD * width, FOLD * width), 1)
     weave = (lane == (place % width) * FOLD + place // width).astype(jnp.bfloat16)
     per_half = keep // width
-    odd = odd_ref[0]
     for h in range(2):
         side = odd if h == 0 else 1 - odd
         for b in range(per_half):
@@ -195,37 +231,58 @@
             if out_ref.dtype == jnp.float32:
                 rest = (row - high.astype(jnp.float32)).astype(jnp.bfloat16)
                 found = found + jnp.dot(rest, weave, preferred_element_type=jnp.float32)
-            at = pl.multiple_of((side * per_half + b) * (FOLD * width), FOLD * width)
+            at = ((2 * pair + side) * per_half + b) * (FOLD * width)
+            at = pl.multiple_of(at, FOLD * width)
             out_ref[:, pl.ds(at, FOLD * width)] = found.astype(out_ref.dtype)
 
 
-def correlate(odd, t_all, e_two, keep, chans, scale, dtype):
-    panel = t_all.shape[1]
-    smem = pl.BlockSpec(memory_space=pltpu.SMEM)
-    vmem = pl.BlockSpec(memory_space=pltpu.VMEM)
+def correlate(place, gathered, windows, chans, tpd, scale, width, dtype):
+    pieces = [value for value, _, _ in gathered]
+    masks = [(part_of, items) for _, part_of, items in gathered]
+    panel = 2 * pieces[0].shape[1]
+    chunks = sum(len(items) for _, items in masks) // 2
+    keep = windows[0].shape[0]
+    height = keep + windows[1].shape[0]
+    depth = ROWS * chans
+    anywhere = pl.BlockSpec(memory_space=pl.ANY)
     return pl.pallas_call(
-        functools.partial(correlate_kernel, chans, scale),
-        out_shape=jax.ShapeDtypeStruct((panel, 2 * keep * FOLD), dtype),
-        in_specs=[smem, vmem, vmem],
-        out_specs=vmem,
+        functools.partial(correlate_kernel, chans, tpd, scale, masks),
+        out_shape=jax.ShapeDtypeStruct((panel, width), dtype),
+        in_specs=[pl.BlockSpec(memory_space=pltpu.SMEM)] + [anywhere] * (len(pieces) + 4),
+        out_specs=pl.BlockSpec(memory_space=pltpu.VMEM),
         scratch_shapes=[
-            pltpu.VMEM((FOLD * panel, ROWS * chans), jnp.bfloat16),
-            pltpu.VMEM((e_two.shape[0], FOLD * panel), jnp.float32),
+            pltpu.VMEM((FOLD * panel, chunks * tpd * chans + (FOLD - 1) * STRIDE * chans), jnp.bfloat16),
+            pltpu.VMEM((2 * height, depth), jnp.bfloat16),
+            pltpu.SemaphoreType.DMA((chunks, 2 * FOLD)),
+            pltpu.SemaphoreType.DMA((4,)),
+            pltpu.VMEM((2 * height, FOLD * panel), jnp.float32),
             pltpu.VMEM((2 * keep, FOLD * panel), jnp.float32),
         ],
         compiler_params=params(),
-        cost_estimate=pl.CostEstimate(flops=8 * 10**9, bytes_accessed=8 * 10**6, transcendentals=0),
+        cost_estimate=pl.CostEstimate(flops=8 * 10**9, bytes_accessed=16 * 10**6, transcendentals=0),
         name="correlate",
-    )(odd, t_all, e_two)
-
-
-def by_tap(parts, chans):
-    count, panel, lanes = parts.shape
-    per = ROWS * chans // lanes
-    if per == 1:
-        return parts
-    parts = parts.reshape(count // per, per, panel, lanes)
-    return jnp.transpose(parts, (0, 2, 1, 3)).reshape(count // per, panel, per * lanes)
+    )(place, *pieces, *windows)
+
+
+def swap(value, bit):
+    size = lax.axis_size("tm")
+    return lax.ppermute(value, "tm", [(i, i ^ bit) for i in range(size)])
+
+
+def gather_panel(value):
+    bits = []
+    while 2 << len(bits) < lax.axis_size("tm"):
+        bits.append(2 << len(bits))
+    rows = value.shape[0] // 2
+    out = []
+    for part_of, order in enumerate((bits[::-1], bits)):
+        parts = [(value[part_of * rows : (part_of + 1) * rows][None], [0])]
+        for bit in order:
+            held = jnp.concatenate([v for v, _ in parts], axis=0) if len(parts) > 1 else parts[0][0]
+            items = [m for _, ms in parts for m in ms]
+            parts = [(held, items), (swap(held, bit), [m ^ bit for m in items])]
+        out += [(v, part_of, ms) for v, ms in parts]
+    return out + [(swap(v, 1), part_of, [m ^ 1 for m in ms]) for v, part_of, ms in out]
 
 
 def body(recording, spike_times, unit_labels, old_templates):
@@ -251,54 +308,78 @@
     if tpd != ROWS:
         send = send.reshape(groups, owners, CAP, ROWS // tpd, tpd, chans)
         send = jnp.transpose(send, (0, 3, 1, 2, 4, 5))
+    owner = unit_labels // panel
+    hits = (owner[:, None] == jnp.arange(owners)[None, :]).astype(jnp.int32)
+    rank = jnp.sum((jnp.cumsum(hits, axis=0) - hits) * hits, axis=1)
+    placing = jnp.arange(owners * CAP)[:, None] == (owner * CAP + rank)[None, :]
+    tags = jnp.sum(jnp.where(placing, (unit_labels % panel + 1)[None, :], 0), axis=1) - 1
+    tags = jnp.broadcast_to(tags.reshape(1, owners, CAP), (tm_count, owners, CAP))
+    tags = tags.reshape(devices, CAP)
+    tags = lax.all_to_all(tags, AXES, split_axis=0, concat_axis=0, tiled=True)
+    key = (tags[:, :, None] * tpd + jnp.arange(tpd)[None, None, :]).reshape(1, -1)
+    send, key = lax.optimization_barrier((send, key))
     got = lax.all_to_all(
         send.reshape(devices, CAP * tpd, chans), AXES, split_axis=0, concat_axis=0, tiled=True
     ).reshape(devices * CAP * tpd, chans)
-
-    labels = lax.all_gather(unit_labels, AXES, axis=0, tiled=True).reshape(devices, spikes)
-    mine = labels // panel == unit_pos
-    counted = mine.astype(jnp.int32)
-    rank = jnp.cumsum(counted, axis=1) - counted
-    here = mine[:, :, None] & (rank[:, :, None] == jnp.arange(CAP)[None, None, :])
-    within = jnp.sum(jnp.where(here, (labels % panel + 1)[:, :, None], 0), axis=1) - 1
-    key = (within[:, :, None] * tpd + jnp.arange(tpd)[None, None, :]).reshape(1, -1)
 
     cube = old_templates.reshape(panel, chans, taps)
     cube = jnp.pad(cube, ((0, 0), (0, 0), (0, padded - taps)))
     cube = lax.dynamic_slice_in_dim(cube, tm_pos * tpd, tpd, 2)
     old = jnp.transpose(cube, (0, 2, 1)).reshape(panel, tpd * chans)
 
-    folded = fold(recording)
+    folded = fold(lax.optimization_barrier((recording, send))[0])
+    folded, got = lax.optimization_barrier((folded, got))
     halo = padded // ROWS
-    following = lax.ppermute(folded[:halo], AXES, [(i, i - 1) for i in range(1, devices)])
-    spare = jnp.zeros((16 - halo % 16, ROWS * chans), jnp.bfloat16)
-    mine_rows = jnp.concatenate([folded, following, spare], axis=0)
-    their_rows = lax.ppermute(mine_rows, "unit", [(i, i ^ 1) for i in range(owners)])
-    e_two = jnp.concatenate([mine_rows, their_rows], axis=0)
+    head = folded[:halo]
+    follow = lax.ppermute(head, AXES, [(i, i - 1) for i in range(1, devices)])
+    skip = lax.ppermute(head, AXES, [(i, i - 2) for i in range(2, devices, 2)])
+    theirs = lax.ppermute(folded, "unit", [(i, i ^ 1) for i in range(owners)])
+    odd = unit_pos % 2
+    spare = ((0, -halo % 16), (0, 0))
+    windows = (
+        folded,
+        jnp.pad(follow, spare),
+        theirs,
+        jnp.pad(jnp.where(odd == 1, head, skip), spare),
+    )
 
     fresh = refine(key, got, old, tpd)
-    odd = (unit_pos % 2).astype(jnp.int32).reshape(1)
-    own_panel = lax.all_gather(fresh, "tm", axis=0, tiled=False)
+    own = gather_panel(fresh)
     width = 2 * keep * FOLD
-    scores = jnp.zeros((panel, owners // 2 * width), jnp.float32)
+
+    share = chans // tm_count
+    order = []
+    pieces = [[], []]
+    for value, part_of, items in own:
+        value = value.reshape(len(items), panel // 2, tpd, chans)
+        pieces[part_of].append(lax.dynamic_slice_in_dim(value, tm_pos * share, share, 3))
+        order += items if part_of == 0 else []
+    order_b = [m for _, part_of, items in own if part_of == 1 for m in items]
+    part = []
+    for found, masks in ((pieces[0], order), (pieces[1], order_b)):
+        spots = jnp.array([masks.index(m) for m in range(tm_count)])
+        stacked = jnp.concatenate(found, axis=0)
+        picks = spots[jnp.bitwise_xor(jnp.arange(tm_count), tm_pos)]
+        part.append(jnp.take(stacked, picks, axis=0))
+    part = jnp.concatenate(part, axis=1)
+    part = jnp.transpose(part, (1, 3, 0, 2)).reshape(panel, share, padded)[:, :, :taps]
+    part = part.reshape(panel, share * taps)
+
     found = []
     for m in range(1, owners // 2):
         ahead = [(i, (i + 2 * m) % owners) for i in range(owners)]
         back = [(j, i) for i, j in ahead]
-        other = lax.all_gather(lax.ppermute(fresh, "unit", ahead), "tm", axis=0, tiled=False)
-        out = correlate(odd, by_tap(other, chans), e_two, keep, chans, scale, jnp.bfloat16)
+        other = gather_panel(lax.ppermute(fresh, "unit", ahead))
+        place = jnp.stack([tm_pos, odd, 0 * odd]).astype(jnp.int32)
+        out = correlate(place, other, windows, chans, tpd, scale, width, jnp.bfloat16)
         found.append((lax.ppermute(out, "unit", back), ((unit_pos + 2 * m) % owners) // 2))
-    found.append((correlate(odd, by_tap(own_panel, chans), e_two, keep, chans, scale, jnp.float32), unit_pos // 2))
+    place = jnp.stack([tm_pos, odd, unit_pos // 2]).astype(jnp.int32)
+    scores = correlate(place, own, windows, chans, tpd, scale, owners // 2 * width, jnp.float32)
     for out, pair in found:
         scores = lax.dynamic_update_slice_in_dim(
             scores, out.astype(jnp.float32), pair * width, 1
         )
-
-    share = chans // tm_count
-    part = own_panel.reshape(tm_count, panel, tpd, chans)
-    part = lax.dynamic_slice_in_dim(part, tm_pos * share, share, 3)
-    part = jnp.transpose(part, (1, 3, 0, 2)).reshape(panel, share, padded)[:, :, :taps]
-    return (part.reshape(panel, share * taps), scores)
+    return (part, scores)
 
 
 def solution(mesh):

time: 230 us -> 186 us (0.81)
  blocking collectives: 57.2 us -> 0 us
  waiting for transfers between devices: 61.7 us -> 38.4 us
  Pallas kernels: 36.6 us -> 59.6 us
  starting transfers between devices: 12.6 us -> 34.1 us
  between operations: 14.2 us -> 1.17 us
  local copies, waits for them, and re-layouts: 41.4 us -> 44.9 us
    unnamed x1 -> x0, blocking collectives: 57.2 us -> none
    ppermute x3 -> x20, waiting for transfers between devices: 61 us -> 35.4 us  [the longest x16 23.1 us: swap(): return lax.ppermute(value, 'tm', [(i, i ^ bit) for i in range(size)])]
    pallas_call x2, Pallas kernels: 25.8 us -> 48.8 us  [correlate(): pl.pallas_call(functools.partial(correlate_kernel, chans, tpd, scale, mas...]
    ppermute x3 -> x20, starting transfers between devices: 2.06 us -> 22.8 us  [the longest x16 15.8 us: swap(): return lax.ppermute(value, 'tm', [(i, i ^ bit) for i in range(size)])]
    all_to_all x0 -> x1, starting transfers between devices: none -> 7.3 us  [body(): tags = lax.all_to_all(tags, AXES, split_axis=0, concat_axis=0, tiled=True)]
    all_to_all x1, starting transfers between devices: 7.41 us -> 3.42 us  [body(): lax.all_to_all(send.reshape(devices, CAP * tpd, chans), AXES, split_axis=...]
    unnamed x19 -> x35, local copies, waits for them, and re-layouts: 10.4 us -> 6.56 us
    all_to_all x0 -> x1, waiting for transfers between devices: none -> 2.96 us  [body(): tags = lax.all_to_all(tags, AXES, split_axis=0, concat_axis=0, tiled=True)]
  transfers between devices with their start and end apart: 7 -> 23, of which waited for: 3 -> 10; matrix products, arithmetic and copies ran while one was open for 20% -> 26% of each run, Pallas kernels for 13% -> 19%
where the time goes in v3:
time: 186 us
  Pallas kernels  59.6 us (32%)
  local copies, waits for them, and re-layouts  44.9 us (24%)
  waiting for transfers between devices  38.4 us (21%)
  starting transfers between devices  34.1 us (18%)
  other arithmetic  7.38 us (4%)
    pallas_call x2, Pallas kernels, correlate(): pl.pallas_call(functools.partial(correlate_kernel, chans, tpd, scale, mas...  48.8 us
    ppermute x16, waiting for transfers between devices, swap(): return lax.ppermute(value, 'tm', [(i, i ^ bit) for i in range(size)])  23.1 us
    reshape x1, local copies, waits for them, and re-layouts, body(): cube = old_templates.reshape(panel, chans, taps)  19.6 us
    ppermute x16, starting transfers between devices, swap(): return lax.ppermute(value, 'tm', [(i, i ^ bit) for i in range(size)])  15.8 us
    ppermute x1, waiting for transfers between devices, body(): theirs = lax.ppermute(folded, 'unit', [(i, i ^ 1) for i in range(owners)])  8.06 us
    transpose x1, local copies, waits for them, and re-layouts, body(): old = jnp.transpose(cube, (0, 2, 1)).reshape(panel, tpd * chans)  7.9 us
    all_to_all x1, starting transfers between devices, body(): tags = lax.all_to_all(tags, AXES, split_axis=0, concat_axis=0, tiled=True)  7.3 us
    unnamed x35, local copies, waits for them, and re-layouts  6.56 us
  transfers between devices with their start and end apart: 23, of which 10 were waited for; matrix products, arithmetic and copies ran while one was open for 26% of the time, Pallas kernels for 19%

profile of v3, /device:TPU:0, one launch (start us, length us, event | category | flops | bytes accessed | tf_op | source)
XLA Modules:
  0.0 185.6 jit_solution(5012267831517005523)
XLA Ops:
  2.4 7.3 %all-to-all-start = ((s32[32,1,8]{2,1,0:T(1,128)}), s32[32,1,8]{2,1,0:T(1,128)S(1)}, u32[]{:S(2)}, u32[]{:S(2)}) async-start(s32[32,1,8]{2,1,0:T(1,128)} %bitcast.2), calls=%async_computation | async-start | bytes 32768 | tf_op jit(solution)/shard_map/all_to_all | solution.py:318
  9.8 4.1 %pack.1 = bf16[2048,384]{1,0:T(8,128)(2,1)} custom-call(s32[32]{0:T(128)} %times_ref.1, s32[32]{0:T(128)} %labels_ref.1, s32[1]{0:T(128)} %bitcast.1.base_ref, bf16[2048,384]{1,0:T(8,128)(2,1)} %rec_ref.2), custom_call_target="tpu_custom_call" | custom-call | flops 100000000 | bytes 4000000 | tf_op jit(solution)/shard_map/pack/pallas_call | solution.py:66
  13.9 3.0 %all-to-all-done = s32[32,1,8]{2,1,0:T(1,128)S(1)} async-done(((s32[32,1,8]{2,1,0:T(1,128)}), s32[32,1,8]{2,1,0:T(1,128)S(1)}, u32[]{:S(2)}, u32[]{:S(2)}) %all-to-all-start) | async-done | bytes 1056 | tf_op jit(solution)/shard_map/all_to_all | solution.py:318
  17.7 3.4 %all-to-all-start.1 = ((bf16[32,64,384]{2,1,0:T(8,128)(2,1)}), bf16[32,64,384]{2,1,0:T(8,128)(2,1)}, u32[]{:S(2)}, u32[]{:S(2)}) async-start(bf16[32,64,384]{2,1,0:T(8,128)(2,1)} %bitcast.68), calls=%async_computation.1 | async-start | bytes 3145728 | tf_op jit(solution)/shard_map/all_to_all | solution.py:321
  21.2 19.6 %reshape.121 = bf16[64,384,61]{2,1,0:T(8,128)(2,1)} reshape(bf16[64,23424]{1,0:T(8,128)(2,1)S(1)} %copy-done.2) | data formatting | bytes 5996544 | tf_op jit(solution)/shard_map/reshape | solution.py:325
  40.7 7.9 %dynamic-slice_bitcast_fusion = bf16[64,8,384]{1,2,0:T(8,128)(2,1)} fusion(s32[]{:T(128)S(6)} %select_n.78, bf16[64,384,61]{2,1,0:T(8,128)(2,1)} %reshape.121), kind=kLoop, calls=%fused_computation.4 | loop fusion | bytes 3391492 | tf_op jit(solution)/shard_map/transpose | solution.py:328
  48.6 6.1 %copy.21 = bf16[8,8,8,384]{3,1,2,0:T(8,128)(2,1)} copy(bf16[8,8,8,384]{2,3,1,0:T(8,128)(2,1)} %bitcast.67) | data formatting | bytes 786432
  57.4 3.2 %fold.1.refs_8_ = bf16[256,3072]{1,0:T(8,128)(2,1)} custom-call(bf16[2048,384]{1,0:T(8,128)(2,1)} %rec_ref.2), custom_call_target="tpu_custom_call" | custom-call | flops 200000000 | bytes 4000000 | tf_op jit(solution)/shard_map/fold/pallas_call | solution.py:97
  64.1 3.5 %refine.1 = bf16[64,3072]{1,0:T(8,128)(2,1)} custom-call(s32[1,2048]{1,0:T(1,128)} %add.104.key_ref, bf16[2048,384]{1,0:T(8,128)(2,1)} %bitcast.5.got_ref, bf16[64,3072]{1,0:T(8,128)(2,1)} %bitcast.84), custom_call_target="tpu_custom_call" | custom-call | flops 800000000 | bytes 3000000 | tf_op jit(solution)/shard_map/refine/pallas_call | solution.py:139
  68.7 4.4 %collective-permute-start.11 = (bf16[64,3072]{1,0:T(8,128)(2,1)}, bf16[64,3072]{1,0:T(8,128)(2,1)S(1)}, u32[]{:S(2)}, u32[]{:S(2)}) collective-permute-start(bf16[64,3072]{1,0:T(8,128)(2,1)} %refine.1), channel_id=1, source_target_pairs={{0,2},{1,3},{2,0},{3,1},{4,6},{5,7},{6,4},{7,5},{8,10},{9,11},{10,... | collective-permute-start | bytes 1179656 | tf_op jit(solution)/shard_map/ppermute | solution.py:372
  73.1 4.6 %collective-permute-start.4 = (bf16[1,32,3072]{2,1,0:T(8,128)(2,1)S(1)}, bf16[1,32,3072]{2,1,0:T(8,128)(2,1)S(1)}, u32[]{:S(2)}, u32[]{:S(2)}) collective-permute-start(bf16[1,32,3072]{2,1,0:T(8,128)(2,1)S(1)} %get-tuple-element.17), channel_id=1, source_target_pairs={{0,8},{4,12},{8,0},{12,4},{16,24},{20,28},{24,16},{28,20},{1,9},{5... | collective-permute-start | bytes 589832 | tf_op jit(solution)/shard_map/ppermute | solution.py:269
  80.6 2.3 %collective-permute-done.4 = bf16[1,32,3072]{2,1,0:T(8,128)(2,1)S(1)} collective-permute-done((bf16[1,32,3072]{2,1,0:T(8,128)(2,1)S(1)}, bf16[1,32,3072]{2,1,0:T(8,128)(2,1)S(1)}, u32[]{:S(2)}, u32[]{:S(2)}) %collective-permute-start.4) | collective-permute-done | bytes 196640 | tf_op jit(solution)/shard_map/ppermute | solution.py:269
  82.9 3.3 %collective-permute-start.5 = (bf16[2,32,3072]{2,1,0:T(8,128)(2,1)S(1)}, bf16[2,32,3072]{2,1,0:T(8,128)(2,1)S(1)}, u32[]{:S(2)}, u32[]{:S(2)}) collective-permute-start(bf16[2,32,3072]{2,1,0:T(8,128)(2,1)S(1)} %pad_maximum_fusion.3.refs_2_), channel_id=1, source_target_pairs={{0,16},{4,20},{8,24},{12,28},{16,0},{20,4},{24,8},{28,12},{1,17},{... | collective-permute-start | bytes 1179656 | tf_op jit(solution)/shard_map/ppermute | solution.py:269
  86.2 4.3 %collective-permute-done.11 = bf16[64,3072]{1,0:T(8,128)(2,1)S(1)} collective-permute-done((bf16[64,3072]{1,0:T(8,128)(2,1)}, bf16[64,3072]{1,0:T(8,128)(2,1)S(1)}, u32[]{:S(2)}, u32[]{:S(2)}) %collective-permute-start.11) | collective-permute-done | bytes 393248 | tf_op jit(solution)/shard_map/ppermute | solution.py:372
  90.5 2.3 %collective-permute-start.12 = (bf16[1,32,3072]{2,1,0:T(8,128)(2,1)S(1)}, bf16[1,32,3072]{2,1,0:T(8,128)(2,1)S(1)}, u32[]{:S(2)}, u32[]{:S(2)}) collective-permute-start(bf16[1,32,3072]{2,1,0:T(8,128)(2,1)S(1)} %get-tuple-element.14), channel_id=1, source_target_pairs={{0,16},{4,20},{8,24},{12,28},{16,0},{20,4},{24,8},{28,12},{1,17},{... | collective-permute-start | bytes 589832 | tf_op jit(solution)/shard_map/ppermute | solution.py:269
  94.8 2.9 %collective-permute-done.12 = bf16[1,32,3072]{2,1,0:T(8,128)(2,1)S(1)} collective-permute-done((bf16[1,32,3072]{2,1,0:T(8,128)(2,1)S(1)}, bf16[1,32,3072]{2,1,0:T(8,128)(2,1)S(1)}, u32[]{:S(2)}, u32[]{:S(2)}) %collective-permute-start.12) | collective-permute-done | bytes 196640 | tf_op jit(solution)/shard_map/ppermute | solution.py:269
  100.0 5.0 %collective-permute-done.1.refs_1_ = bf16[2,32,3072]{2,1,0:T(8,128)(2,1)S(1)} collective-permute-done((bf16[2,32,3072]{2,1,0:T(8,128)(2,1)S(1)}, bf16[2,32,3072]{2,1,0:T(8,128)(2,1)S(1)}, u32[]{:S(2)}, u32[]{:S(2)}) %collective-permute-start.1) | collective-permute-done | bytes 393248 | tf_op jit(solution)/shard_map/ppermute | solution.py:269
  106.1 3.2 %collective-permute-done.14 = bf16[1,32,3072]{2,1,0:T(8,128)(2,1)S(1)} collective-permute-done((bf16[1,32,3072]{2,1,0:T(8,128)(2,1)S(1)}, bf16[1,32,3072]{2,1,0:T(8,128)(2,1)S(1)}, u32[]{:S(2)}, u32[]{:S(2)}) %collective-permute-start.14) | collective-permute-done | bytes 196640 | tf_op jit(solution)/shard_map/ppermute | solution.py:269
  112.8 3.3 %collective-permute-done.13.refs_1_ = bf16[2,32,3072]{2,1,0:T(8,128)(2,1)} collective-permute-done((bf16[2,32,3072]{2,1,0:T(8,128)(2,1)}, bf16[2,32,3072]{2,1,0:T(8,128)(2,1)}, u32[]{:S(2)}, u32[]{:S(2)}) %collective-permute-start.13) | collective-permute-done | bytes 393248 | tf_op jit(solution)/shard_map/ppermute | solution.py:269
  116.1 5.8 %collective-permute-done.15.refs_3_ = bf16[2,32,3072]{2,1,0:T(8,128)(2,1)} collective-permute-done((bf16[2,32,3072]{2,1,0:T(8,128)(2,1)}, bf16[2,32,3072]{2,1,0:T(8,128)(2,1)}, u32[]{:S(2)}, u32[]{:S(2)}) %collective-permute-start.15) | collective-permute-done | bytes 393248 | tf_op jit(solution)/shard_map/ppermute | solution.py:269
  124.1 1.8 copy.18
  127.2 8.1 %collective-permute-done.9.refs_10_ = bf16[256,3072]{1,0:T(8,128)(2,1)} collective-permute-done((bf16[256,3072]{1,0:T(8,128)(2,1)S(1)}, bf16[256,3072]{1,0:T(8,128)(2,1)}, u32[]{:S(2)}, u32[]{:S(2)}) %collective-permute-start.9) | collective-permute-done | bytes 1572896 | tf_op jit(solution)/shard_map/ppermute | solution.py:336
  135.3 23.7 %correlate.3 = bf16[64,2048]{1,0:T(8,128)(2,1)} custom-call(s32[3]{0:T(128)} %pad_add_fusion.2.place_ref, bf16[2,32,3072]{2,1,0:T(8,128)(2,1)} %pad_maximum_fusion.4.refs_0_, bf16[2,32,3072]{2,1,0:T(8,128)(2,1)} %collective-permute-done.13.refs_1_, bf16[2,32,3072]{2,1,0:T(8,128)(2,1)} %pad_maximum_fusion.5.refs_2_, ...), custom_call_target="tpu_custom_call" | custom-call | flops 8000000000 | bytes 16000000 | tf_op jit(solution)/shard_map/correlate/pallas_call | solution.py:248
  159.7 25.1 %correlate.2 = f32[64,4096]{1,0:T(8,128)} custom-call(s32[3]{0:T(128)} %pad_add_fusion.place_ref, bf16[2,32,3072]{2,1,0:T(8,128)(2,1)} %copy-done.7, bf16[2,32,3072]{2,1,0:T(8,128)(2,1)} %copy-done.8, bf16[2,32,3072]{2,1,0:T(8,128)(2,1)} %copy-done.4, bf16[2,32,3072]{2,1,0:T(8,128)(2,1)} %copy-done.5, bf16[2,32,3072]{2,1,0:T(8,128)(2,1)} %copy-done.9, ...), custom_call_target="tpu_custom_call" | custom-call | flops 8000000000 | bytes 16000000 | tf_op jit(solution)/shard_map/correlate/pallas_call | solution.py:248
  (111 shorter events, 26.3 us)
Async XLA Ops:
  2.4 14.4 %all-to-all-start = ((s32[32,1,8]{2,1,0:T(1,128)}), s32[32,1,8]{2,1,0:T(1,128)S(1)}, u32[]{:S(2)}, u32[]{:S(2)}) async-start(s32[32,1,8]{2,1,0:T(1,128)} %bitcast.2), calls=%async_computation | async-start | bytes 32768 | tf_op jit(solution)/shard_map/all_to_all | solution.py:318
  17.7 42.9 %all-to-all-start.1 = ((bf16[32,64,384]{2,1,0:T(8,128)(2,1)}), bf16[32,64,384]{2,1,0:T(8,128)(2,1)}, u32[]{:S(2)}, u32[]{:S(2)}) async-start(bf16[32,64,384]{2,1,0:T(8,128)(2,1)} %bitcast.68), calls=%async_computation.1 | async-start | bytes 3145728 | tf_op jit(solution)/shard_map/all_to_all | solution.py:321
  61.5 18.4 %collective-permute-start.8 = (bf16[8,3072]{1,0:T(8,128)(2,1)S(1)}, bf16[8,3072]{1,0:T(8,128)(2,1)S(1)}, u32[]{:S(2)}, u32[]{:S(2)}) collective-permute-start(bf16[8,3072]{1,0:T(8,128)(2,1)S(1)} %slice.21), channel_id=1, source_target_pairs={{1,0},{2,1},{3,2},{4,3},{5,4},{6,5},{7,6},{8,7},{9,8},{10,9},{11,1... | collective-permute-start | bytes 147464 | tf_op jit(solution)/shard_map/ppermute | solution.py:334
  62.8 16.5 %collective-permute-start.10 = (bf16[8,3072]{1,0:T(8,128)(2,1)S(1)}, bf16[8,3072]{1,0:T(8,128)(2,1)S(1)}, u32[]{:S(2)}, u32[]{:S(2)}) collective-permute-start(bf16[8,3072]{1,0:T(8,128)(2,1)S(1)} %slice.21), channel_id=1, source_target_pairs={{2,0},{4,2},{6,4},{8,6},{10,8},{12,10},{14,12},{16,14},{18,16},{20... | collective-permute-start | bytes 147464 | tf_op jit(solution)/shard_map/ppermute | solution.py:335
  68.7 21.8 %collective-permute-start.11 = (bf16[64,3072]{1,0:T(8,128)(2,1)}, bf16[64,3072]{1,0:T(8,128)(2,1)S(1)}, u32[]{:S(2)}, u32[]{:S(2)}) collective-permute-start(bf16[64,3072]{1,0:T(8,128)(2,1)} %refine.1), channel_id=1, source_target_pairs={{0,2},{1,3},{2,0},{3,1},{4,6},{5,7},{6,4},{7,5},{8,10},{9,11},{10,... | collective-permute-start | bytes 1179656 | tf_op jit(solution)/shard_map/ppermute | solution.py:372
  73.1 9.7 %collective-permute-start.4 = (bf16[1,32,3072]{2,1,0:T(8,128)(2,1)S(1)}, bf16[1,32,3072]{2,1,0:T(8,128)(2,1)S(1)}, u32[]{:S(2)}, u32[]{:S(2)}) collective-permute-start(bf16[1,32,3072]{2,1,0:T(8,128)(2,1)S(1)} %get-tuple-element.17), channel_id=1, source_target_pairs={{0,8},{4,12},{8,0},{12,4},{16,24},{20,28},{24,16},{28,20},{1,9},{5... | collective-permute-start | bytes 589832 | tf_op jit(solution)/shard_map/ppermute | solution.py:269
  77.7 15.1 %collective-permute-start = (bf16[1,32,3072]{2,1,0:T(8,128)(2,1)S(1)}, bf16[1,32,3072]{2,1,0:T(8,128)(2,1)S(1)}, u32[]{:S(2)}, u32[]{:S(2)}) collective-permute-start(bf16[1,32,3072]{2,1,0:T(8,128)(2,1)S(1)} %get-tuple-element.16), channel_id=1, source_target_pairs={{0,16},{4,20},{8,24},{12,28},{16,0},{20,4},{24,8},{28,12},{1,17},{... | collective-permute-start | bytes 589832 | tf_op jit(solution)/shard_map/ppermute | solution.py:269
  82.9 27.1 %copy-start.4 = (bf16[2,32,3072]{2,1,0:T(8,128)(2,1)}, bf16[2,32,3072]{2,1,0:T(8,128)(2,1)S(1)}, u32[]{:S(2)}) copy-start(bf16[2,32,3072]{2,1,0:T(8,128)(2,1)S(1)} %pad_maximum_fusion.3.refs_2_) | copy-start | bytes 1179652
  82.9 23.2 %collective-permute-start.5 = (bf16[2,32,3072]{2,1,0:T(8,128)(2,1)S(1)}, bf16[2,32,3072]{2,1,0:T(8,128)(2,1)S(1)}, u32[]{:S(2)}, u32[]{:S(2)}) collective-permute-start(bf16[2,32,3072]{2,1,0:T(8,128)(2,1)S(1)} %pad_maximum_fusion.3.refs_2_), channel_id=1, source_target_pairs={{0,16},{4,20},{8,24},{12,28},{16,0},{20,4},{24,8},{28,12},{1,17},{... | collective-permute-start | bytes 1179656 | tf_op jit(solution)/shard_map/ppermute | solution.py:269
  86.2 23.9 %collective-permute-start.6 = (bf16[2,32,3072]{2,1,0:T(8,128)(2,1)S(1)}, bf16[2,32,3072]{2,1,0:T(8,128)(2,1)S(1)}, u32[]{:S(2)}, u32[]{:S(2)}) collective-permute-start(bf16[2,32,3072]{2,1,0:T(8,128)(2,1)S(1)} %pad_maximum_fusion.3.refs_2_), channel_id=1, source_target_pairs={{0,4},{4,0},{8,12},{12,8},{16,20},{20,16},{24,28},{28,24},{1,5},{5... | collective-permute-start | bytes 1179656 | tf_op jit(solution)/shard_map/ppermute | solution.py:269
  90.5 7.2 %collective-permute-start.12 = (bf16[1,32,3072]{2,1,0:T(8,128)(2,1)S(1)}, bf16[1,32,3072]{2,1,0:T(8,128)(2,1)S(1)}, u32[]{:S(2)}, u32[]{:S(2)}) collective-permute-start(bf16[1,32,3072]{2,1,0:T(8,128)(2,1)S(1)} %get-tuple-element.14), channel_id=1, source_target_pairs={{0,16},{4,20},{8,24},{12,28},{16,0},{20,4},{24,8},{28,12},{1,17},{... | collective-permute-start | bytes 589832 | tf_op jit(solution)/shard_map/ppermute | solution.py:269
  92.9 12.1 %collective-permute-start.1 = (bf16[2,32,3072]{2,1,0:T(8,128)(2,1)S(1)}, bf16[2,32,3072]{2,1,0:T(8,128)(2,1)S(1)}, u32[]{:S(2)}, u32[]{:S(2)}) collective-permute-start(bf16[2,32,3072]{2,1,0:T(8,128)(2,1)S(1)} %pad_maximum_fusion.2.refs_0_), channel_id=1, source_target_pairs={{0,8},{4,12},{8,0},{12,4},{16,24},{20,28},{24,16},{28,20},{1,9},{5... | collective-permute-start | bytes 1179656 | tf_op jit(solution)/shard_map/ppermute | solution.py:269
  93.9 6.0 %collective-permute-start.2 = (bf16[2,32,3072]{2,1,0:T(8,128)(2,1)S(1)}, bf16[2,32,3072]{2,1,0:T(8,128)(2,1)S(1)}, u32[]{:S(2)}, u32[]{:S(2)}) collective-permute-start(bf16[2,32,3072]{2,1,0:T(8,128)(2,1)S(1)} %pad_maximum_fusion.2.refs_0_), channel_id=1, source_target_pairs={{0,4},{4,0},{8,12},{12,8},{16,20},{20,16},{24,28},{28,24},{1,5},{5... | collective-permute-start | bytes 1179656 | tf_op jit(solution)/shard_map/ppermute | solution.py:269
  97.7 11.5 %collective-permute-start.14 = (bf16[1,32,3072]{2,1,0:T(8,128)(2,1)S(1)}, bf16[1,32,3072]{2,1,0:T(8,128)(2,1)S(1)}, u32[]{:S(2)}, u32[]{:S(2)}) collective-permute-start(bf16[1,32,3072]{2,1,0:T(8,128)(2,1)S(1)} %get-tuple-element.13), channel_id=1, source_target_pairs={{0,8},{4,12},{8,0},{12,4},{16,24},{20,28},{24,16},{28,20},{1,9},{5... | collective-permute-start | bytes 589832 | tf_op jit(solution)/shard_map/ppermute | solution.py:269
  99.9 35.3 %collective-permute-start.9 = (bf16[256,3072]{1,0:T(8,128)(2,1)S(1)}, bf16[256,3072]{1,0:T(8,128)(2,1)}, u32[]{:S(2)}, u32[]{:S(2)}) collective-permute-start(bf16[256,3072]{1,0:T(8,128)(2,1)S(1)} %copy-done.3), channel_id=1, source_target_pairs={{0,1},{1,0},{2,3},{3,2},{4,5},{5,4},{6,7},{7,6},{8,9},{9,8},{10,11... | collective-permute-start | bytes 4718600 | tf_op jit(solution)/shard_map/ppermute | solution.py:336
  105.1 11.1 %collective-permute-start.13 = (bf16[2,32,3072]{2,1,0:T(8,128)(2,1)}, bf16[2,32,3072]{2,1,0:T(8,128)(2,1)}, u32[]{:S(2)}, u32[]{:S(2)}) collective-permute-start(bf16[2,32,3072]{2,1,0:T(8,128)(2,1)} %pad_maximum_fusion.4.refs_0_), channel_id=1, source_target_pairs={{0,8},{4,12},{8,0},{12,4},{16,24},{20,28},{24,16},{28,20},{1,9},{5... | collective-permute-start | bytes 1179656 | tf_op jit(solution)/shard_map/ppermute | solution.py:269
  106.0 5.1 %collective-permute-start.3 = (bf16[2,32,3072]{2,1,0:T(8,128)(2,1)S(1)}, bf16[2,32,3072]{2,1,0:T(8,128)(2,1)S(1)}, u32[]{:S(2)}, u32[]{:S(2)}) collective-permute-start(bf16[2,32,3072]{2,1,0:T(8,128)(2,1)S(1)} %collective-permute-done.1.refs_1_), channel_id=1, source_target_pairs={{0,4},{4,0},{8,12},{12,8},{16,20},{20,16},{24,28},{28,24},{1,5},{5... | collective-permute-start | bytes 1179656 | tf_op jit(solution)/shard_map/ppermute | solution.py:269
  109.2 1.7 collective-permute-start.7
  110.0 11.9 %collective-permute-start.15 = (bf16[2,32,3072]{2,1,0:T(8,128)(2,1)}, bf16[2,32,3072]{2,1,0:T(8,128)(2,1)}, u32[]{:S(2)}, u32[]{:S(2)}) collective-permute-start(bf16[2,32,3072]{2,1,0:T(8,128)(2,1)} %pad_maximum_fusion.5.refs_2_), channel_id=1, source_target_pairs={{0,16},{4,20},{8,24},{12,28},{16,0},{20,4},{24,8},{28,12},{1,17},{... | collective-permute-start | bytes 1179656 | tf_op jit(solution)/shard_map/ppermute | solution.py:269
  110.9 16.3 %collective-permute-start.16 = (bf16[2,32,3072]{2,1,0:T(8,128)(2,1)}, bf16[2,32,3072]{2,1,0:T(8,128)(2,1)}, u32[]{:S(2)}, u32[]{:S(2)}) collective-permute-start(bf16[2,32,3072]{2,1,0:T(8,128)(2,1)} %pad_maximum_fusion.4.refs_0_), channel_id=1, source_target_pairs={{0,4},{4,0},{8,12},{12,8},{16,20},{20,16},{24,28},{28,24},{1,5},{5... | collective-permute-start | bytes 1179656 | tf_op jit(solution)/shard_map/ppermute | solution.py:269
  111.2 16.0 %collective-permute-start.18 = (bf16[2,32,3072]{2,1,0:T(8,128)(2,1)}, bf16[2,32,3072]{2,1,0:T(8,128)(2,1)}, u32[]{:S(2)}, u32[]{:S(2)}) collective-permute-start(bf16[2,32,3072]{2,1,0:T(8,128)(2,1)} %pad_maximum_fusion.5.refs_2_), channel_id=1, source_target_pairs={{0,4},{4,0},{8,12},{12,8},{16,20},{20,16},{24,28},{28,24},{1,5},{5... | collective-permute-start | bytes 1179656 | tf_op jit(solution)/shard_map/ppermute | solution.py:269
  116.1 11.1 %collective-permute-start.17 = (bf16[2,32,3072]{2,1,0:T(8,128)(2,1)}, bf16[2,32,3072]{2,1,0:T(8,128)(2,1)}, u32[]{:S(2)}, u32[]{:S(2)}) collective-permute-start(bf16[2,32,3072]{2,1,0:T(8,128)(2,1)} %collective-permute-done.13.refs_1_), channel_id=1, source_target_pairs={{0,4},{4,0},{8,12},{12,8},{16,20},{20,16},{24,28},{28,24},{1,5},{5... | collective-permute-start | bytes 1179656 | tf_op jit(solution)/shard_map/ppermute | solution.py:269
  121.9 5.3 %collective-permute-start.19 = (bf16[2,32,3072]{2,1,0:T(8,128)(2,1)}, bf16[2,32,3072]{2,1,0:T(8,128)(2,1)}, u32[]{:S(2)}, u32[]{:S(2)}) collective-permute-start(bf16[2,32,3072]{2,1,0:T(8,128)(2,1)} %collective-permute-done.15.refs_3_), channel_id=1, source_target_pairs={{0,4},{4,0},{8,12},{12,8},{16,20},{20,16},{24,28},{28,24},{1,5},{5... | collective-permute-start | bytes 1179656 | tf_op jit(solution)/shard_map/ppermute | solution.py:269
  159.0 25.8 %collective-permute-start.20 = (bf16[64,2048]{1,0:T(8,128)(2,1)}, bf16[64,2048]{1,0:T(8,128)(2,1)S(1)}, u32[]{:S(2)}, u32[]{:S(2)}) collective-permute-start(bf16[64,2048]{1,0:T(8,128)(2,1)} %correlate.3), channel_id=1, source_target_pairs={{2,0},{3,1},{0,2},{1,3},{6,4},{7,5},{4,6},{5,7},{10,8},{11,9},{8,1... | collective-permute-start | bytes 786440 | tf_op jit(solution)/shard_map/ppermute | solution.py:375
  (11 other events, 89.0 us)

commit v4 on v3

--- a/solution.py
+++ b/solution.py
@@ -78,31 +78,35 @@
     )(times, labels, base, rec)
 
 
-def fold_kernel(rec_ref, out_ref):
+def fold_kernel(rec_ref, halo_ref, out_ref):
     rows, chans = rec_ref.shape
+    extra = halo_ref.shape[0]
     block = 16 * ROWS
     new = lax.broadcasted_iota(jnp.int32, (block, block), 0)
     old = lax.broadcasted_iota(jnp.int32, (block, block), 1)
     perm = (old == (new % 16) * ROWS + new // 16).astype(jnp.bfloat16)
-    for b in range(rows // block):
-        part = jnp.dot(perm, rec_ref[b * block : (b + 1) * block, :], preferred_element_type=jnp.float32)
+    for b in range(rows // block + 1):
+        if b < rows // block:
+            part = jnp.dot(perm, rec_ref[b * block : (b + 1) * block, :], preferred_element_type=jnp.float32)
+        else:
+            part = jnp.dot(perm[:, :extra], halo_ref[...], preferred_element_type=jnp.float32)
         part = part.astype(jnp.bfloat16)
         for r in range(ROWS):
             out_ref[b * 16 : (b + 1) * 16, r * chans : (r + 1) * chans] = part[r * 16 : (r + 1) * 16]
 
 
-def fold(rec):
+def fold(rec, halo):
     rows, chans = rec.shape
     vmem = pl.BlockSpec(memory_space=pltpu.VMEM)
     return pl.pallas_call(
         fold_kernel,
-        out_shape=jax.ShapeDtypeStruct((rows // ROWS, ROWS * chans), jnp.bfloat16),
-        in_specs=[vmem],
+        out_shape=jax.ShapeDtypeStruct((rows // ROWS + 16, ROWS * chans), jnp.bfloat16),
+        in_specs=[vmem, vmem],
         out_specs=vmem,
         compiler_params=params(),
         cost_estimate=pl.CostEstimate(flops=2 * 10**8, bytes_accessed=4 * 10**6, transcendentals=0),
         name="fold",
-    )(rec)
+    )(rec, halo)
 
 
 def refine_kernel(tpd, key_ref, got_ref, old_ref, out_ref, sums):
@@ -151,66 +155,65 @@
 def correlate_kernel(chans, tpd, scale, masks, place_ref, *refs):
     count = len(masks)
     pieces, rest = refs[:count], refs[count:]
-    mine_ref, my_halo, theirs_ref, their_halo, out_ref, rhs, e_buf, t_sem, e_sem, part, acc = rest
+    mine_ref, theirs_ref, out_ref, t_buf, e_buf, t_sem, e_sem, rhs, part, acc = rest
     half_rows = pieces[0].shape[1]
-    panel = 2 * half_rows
     lanes = tpd * chans
     chunks = t_sem.shape[0]
-    whole = chunks * lanes
+    blocks, panel, depth = t_buf.shape
+    per = depth // lanes
     height = e_buf.shape[0] // 2
     keep = acc.shape[0] // 2
     shift = STRIDE * chans
     me, odd, pair = place_ref[0], place_ref[1], place_ref[2]
 
-    def spot(chunk, part_of, q):
-        first = chunk * lanes + q * shift
+    def spot(chunk, part_of):
+        rows = pl.ds(part_of * half_rows, half_rows)
+        if per == 1:
+            return t_buf.at[chunk, rows]
+        first = chunk % per * lanes
         if not isinstance(chunk, int):
             first = pl.multiple_of(first, 128)
-        return rhs.at[pl.ds(q * panel + part_of * half_rows, half_rows), pl.ds(first, lanes)]
-
-    e_copies = []
-    for n, (body_ref, halo_ref) in enumerate(((mine_ref, my_halo), (theirs_ref, their_halo))):
-        low = n * height
-        e_copies.append(
-            pltpu.make_async_copy(body_ref, e_buf.at[low : low + keep, :], e_sem.at[2 * n])
-        )
-        e_copies.append(
-            pltpu.make_async_copy(halo_ref, e_buf.at[low + keep : low + height, :], e_sem.at[2 * n + 1])
-        )
+        return t_buf.at[chunk // per, rows, pl.ds(first, lanes)]
+
+    e_copies = [
+        pltpu.make_async_copy(ref, e_buf.at[n * height : (n + 1) * height, :], e_sem.at[n])
+        for n, ref in enumerate((mine_ref, theirs_ref))
+    ]
     for copy in e_copies:
         copy.start()
     for ref, (part_of, items) in zip(pieces, masks):
         for at, mask in enumerate(items):
             chunk = jnp.bitwise_xor(me, mask)
-            for q in range(FOLD):
-                sem = t_sem.at[chunk, part_of * FOLD + q]
-                pltpu.make_async_copy(ref.at[at], spot(chunk, part_of, q), sem).start()
-    for q in range(FOLD):
-        rows = slice(q * panel, (q + 1) * panel)
-        if q > 0:
-            rhs[rows, 0 : q * shift] = jnp.zeros((panel, q * shift), jnp.bfloat16)
-        tail = rhs.shape[1] - whole - q * shift
-        if tail > 0:
-            rhs[rows, whole + q * shift :] = jnp.zeros((panel, tail), jnp.bfloat16)
+            pltpu.make_async_copy(ref.at[at], spot(chunk, part_of), t_sem.at[chunk, part_of]).start()
     for copy in e_copies:
         copy.wait()
-    depth = ROWS * chans
-    per = depth // lanes
-    for a in range(chunks // per + 1):
-        for chunk in range(a * per, min((a + 1) * per, chunks)):
-            for part_of in range(2):
-                for q in range(FOLD):
-                    sem = t_sem.at[chunk, part_of * FOLD + q]
-                    pltpu.make_async_copy(pieces[0].at[0], spot(chunk, part_of, q), sem).wait()
-        used = min(depth, rhs.shape[1] - a * depth)
-        part[...] = lax.dot_general(
-            e_buf[:, 0:used],
-            rhs[:, a * depth : a * depth + used],
-            NT,
-            preferred_element_type=jnp.float32,
+    for a in range(blocks + 1):
+        if a < blocks:
+            for chunk in range(a * per, (a + 1) * per):
+                for part_of in range(2):
+                    sem = t_sem.at[chunk, part_of]
+                    pltpu.make_async_copy(pieces[0].at[0], spot(chunk, part_of), sem).wait()
+        used = depth if a < blocks else depth // 2
+        turn = a % 2
+        for q in range(FOLD):
+            rows = slice(q * panel, (q + 1) * panel)
+            cut = q * shift
+            low = min(cut, used)
+            if low > 0:
+                if a > 0:
+                    rhs[turn, rows, 0:low] = t_buf[a - 1, :, depth - cut : depth - cut + low]
+                else:
+                    rhs[turn, rows, 0:low] = jnp.zeros((panel, low), jnp.bfloat16)
+            if cut < used:
+                if a < blocks:
+                    rhs[turn, rows, cut:used] = t_buf[a, :, 0 : used - cut]
+                else:
+                    rhs[turn, rows, cut:used] = jnp.zeros((panel, used - cut), jnp.bfloat16)
+        part[turn] = lax.dot_general(
+            e_buf[:, 0:used], rhs[turn, :, 0:used], NT, preferred_element_type=jnp.float32
         )
         for h in range(2):
-            found = part[h * height + a : h * height + a + keep, :]
+            found = part[turn, h * height + a : h * height + a + keep, :]
             if a == 0:
                 acc[h * keep : (h + 1) * keep, :] = found
             else:
@@ -241,25 +244,26 @@
     masks = [(part_of, items) for _, part_of, items in gathered]
     panel = 2 * pieces[0].shape[1]
     chunks = sum(len(items) for _, items in masks) // 2
-    keep = windows[0].shape[0]
-    height = keep + windows[1].shape[0]
+    height = windows[0].shape[0]
+    keep = height - 16
     depth = ROWS * chans
     anywhere = pl.BlockSpec(memory_space=pl.ANY)
     return pl.pallas_call(
         functools.partial(correlate_kernel, chans, tpd, scale, masks),
         out_shape=jax.ShapeDtypeStruct((panel, width), dtype),
-        in_specs=[pl.BlockSpec(memory_space=pltpu.SMEM)] + [anywhere] * (len(pieces) + 4),
+        in_specs=[pl.BlockSpec(memory_space=pltpu.SMEM)] + [anywhere] * (len(pieces) + 2),
         out_specs=pl.BlockSpec(memory_space=pltpu.VMEM),
         scratch_shapes=[
-            pltpu.VMEM((FOLD * panel, chunks * tpd * chans + (FOLD - 1) * STRIDE * chans), jnp.bfloat16),
+            pltpu.VMEM((chunks * tpd // ROWS, panel, depth), jnp.bfloat16),
             pltpu.VMEM((2 * height, depth), jnp.bfloat16),
-            pltpu.SemaphoreType.DMA((chunks, 2 * FOLD)),
-            pltpu.SemaphoreType.DMA((4,)),
-            pltpu.VMEM((2 * height, FOLD * panel), jnp.float32),
+            pltpu.SemaphoreType.DMA((chunks, 2)),
+            pltpu.SemaphoreType.DMA((2,)),
+            pltpu.VMEM((2, FOLD * panel, depth), jnp.bfloat16),
+            pltpu.VMEM((2, 2 * height, FOLD * panel), jnp.float32),
             pltpu.VMEM((2 * keep, FOLD * panel), jnp.float32),
         ],
         compiler_params=params(),
-        cost_estimate=pl.CostEstimate(flops=8 * 10**9, bytes_accessed=16 * 10**6, transcendentals=0),
+        cost_estimate=pl.CostEstimate(flops=8 * 10**9, bytes_accessed=8 * 10**6, transcendentals=0),
         name="correlate",
     )(place, *pieces, *windows)
 
@@ -327,23 +331,16 @@
     cube = lax.dynamic_slice_in_dim(cube, tm_pos * tpd, tpd, 2)
     old = jnp.transpose(cube, (0, 2, 1)).reshape(panel, tpd * chans)
 
-    folded = fold(lax.optimization_barrier((recording, send))[0])
-    folded, got = lax.optimization_barrier((folded, got))
-    halo = padded // ROWS
-    head = folded[:halo]
+    head = recording[:padded]
     follow = lax.ppermute(head, AXES, [(i, i - 1) for i in range(1, devices)])
     skip = lax.ppermute(head, AXES, [(i, i - 2) for i in range(2, devices, 2)])
-    theirs = lax.ppermute(folded, "unit", [(i, i ^ 1) for i in range(owners)])
+    theirs = lax.ppermute(recording, "unit", [(i, i ^ 1) for i in range(owners)])
+    got, theirs, follow, skip = lax.optimization_barrier((got, theirs, follow, skip))
     odd = unit_pos % 2
-    spare = ((0, -halo % 16), (0, 0))
-    windows = (
-        folded,
-        jnp.pad(follow, spare),
-        theirs,
-        jnp.pad(jnp.where(odd == 1, head, skip), spare),
-    )
 
     fresh = refine(key, got, old, tpd)
+    late, theirs, fresh = lax.optimization_barrier((recording, theirs, fresh))
+    windows = (fold(late, follow), fold(theirs, jnp.where(odd == 1, head, skip)))
     own = gather_panel(fresh)
     width = 2 * keep * FOLD
 

time: 186 us -> 200 us (1.075)
  waiting for transfers between devices: 38.4 us -> 66.2 us
  starting transfers between devices: 34.1 us -> 26.9 us
  Pallas kernels: 59.6 us -> 56.3 us
  other arithmetic: 7.38 us -> 4.25 us
    ppermute x1, waiting for transfers between devices: 0.01 us -> 22.4 us  [body(): follow = lax.ppermute(head, AXES, [(i, i - 1) for i in range(1, devices)])]
    ppermute x1, waiting for transfers between devices: 0.01 us -> 12.1 us  [body(): lax.ppermute(out, 'unit', back)]
    ppermute x1, waiting for transfers between devices: 8.06 us -> 0.01 us  [body(): lax.ppermute(recording, 'unit', [(i, i ^ 1) for i in range(owners)])]
    pallas_call x2, Pallas kernels: 48.8 us -> 41.8 us  [correlate(): pl.pallas_call(functools.partial(correlate_kernel, chans, tpd, scale, mas...]
    ppermute x1, waiting for transfers between devices: 4.32 us -> 10.1 us  [body(): other = gather_panel(lax.ppermute(fresh, 'unit', ahead))]
    ppermute x16, starting transfers between devices: 15.8 us -> 10.4 us  [swap(): return lax.ppermute(value, 'tm', [(i, i ^ bit) for i in range(size)])]
    ppermute x16, waiting for transfers between devices: 23.1 us -> 18.5 us  [swap(): return lax.ppermute(value, 'tm', [(i, i ^ bit) for i in range(size)])]
    pallas_call x1 -> x2, Pallas kernels: 3.16 us -> 6.39 us  [fold(): pl.pallas_call(fold_kernel, out_shape=jax.ShapeDtypeStruct((rows // ROWS...]
  transfers between devices with their start and end apart: 23 -> 23, of which waited for: 10 -> 9; matrix products, arithmetic and copies ran while one was open for 26% -> 22% of each run, Pallas kernels for 19% -> 16%
where the time goes in v4:
time: 200 us
  waiting for transfers between devices  66.2 us (33%)
  Pallas kernels  56.3 us (28%)
  local copies, waits for them, and re-layouts  44.6 us (22%)
  starting transfers between devices  26.9 us (13%)
  other arithmetic  4.25 us (2%)
    pallas_call x2, Pallas kernels, correlate(): pl.pallas_call(functools.partial(correlate_kernel, chans, tpd, scale, mas...  41.8 us
    ppermute x1, waiting for transfers between devices, body(): follow = lax.ppermute(head, AXES, [(i, i - 1) for i in range(1, devices)])  22.4 us
    reshape x1, local copies, waits for them, and re-layouts, body(): cube = old_templates.reshape(panel, chans, taps)  20.6 us
    ppermute x16, waiting for transfers between devices, swap(): return lax.ppermute(value, 'tm', [(i, i ^ bit) for i in range(size)])  18.5 us
    ppermute x1, waiting for transfers between devices, body(): lax.ppermute(out, 'unit', back)  12.1 us
    ppermute x16, starting transfers between devices, swap(): return lax.ppermute(value, 'tm', [(i, i ^ bit) for i in range(size)])  10.4 us
    ppermute x1, waiting for transfers between devices, body(): other = gather_panel(lax.ppermute(fresh, 'unit', ahead))  10.1 us
    transpose x1, local copies, waits for them, and re-layouts, body(): old = jnp.transpose(cube, (0, 2, 1)).reshape(panel, tpd * chans)  7.93 us
  transfers between devices with their start and end apart: 23, of which 9 were waited for; matrix products, arithmetic and copies ran while one was open for 22% of the time, Pallas kernels for 16%

profile of v4, /device:TPU:0, one launch (start us, length us, event | category | flops | bytes accessed | tf_op | source)
XLA Modules:
  0.0 199.5 jit_solution(2119661984560915919)
XLA Ops:
  2.4 7.3 %all-to-all-start = ((s32[32,1,8]{2,1,0:T(1,128)}), s32[32,1,8]{2,1,0:T(1,128)S(1)}, u32[]{:S(2)}, u32[]{:S(2)}) async-start(s32[32,1,8]{2,1,0:T(1,128)} %bitcast.2), calls=%async_computation | async-start | bytes 32768 | tf_op jit(solution)/shard_map/all_to_all | solution.py:322
  9.8 4.0 %pack.1 = bf16[2048,384]{1,0:T(8,128)(2,1)} custom-call(s32[32]{0:T(128)} %times_ref.1, s32[32]{0:T(128)} %labels_ref.1, s32[1]{0:T(128)} %bitcast.1.base_ref, bf16[2048,384]{1,0:T(8,128)(2,1)} %rec_ref.2), custom_call_target="tpu_custom_call" | custom-call | flops 100000000 | bytes 4000000 | tf_op jit(solution)/shard_map/pack/pallas_call | solution.py:66
  13.7 3.1 %all-to-all-done = s32[32,1,8]{2,1,0:T(1,128)S(1)} async-done(((s32[32,1,8]{2,1,0:T(1,128)}), s32[32,1,8]{2,1,0:T(1,128)S(1)}, u32[]{:S(2)}, u32[]{:S(2)}) %all-to-all-start) | async-done | bytes 1056 | tf_op jit(solution)/shard_map/all_to_all | solution.py:322
  17.7 3.4 %all-to-all-start.1 = ((bf16[32,64,384]{2,1,0:T(8,128)(2,1)}), bf16[32,64,384]{2,1,0:T(8,128)(2,1)}, u32[]{:S(2)}, u32[]{:S(2)}) async-start(bf16[32,64,384]{2,1,0:T(8,128)(2,1)} %bitcast.68), calls=%async_computation.1 | async-start | bytes 3145728 | tf_op jit(solution)/shard_map/all_to_all | solution.py:325
  21.1 1.7 collective-permute-start
  25.4 20.6 %reshape.121 = bf16[64,384,61]{2,1,0:T(8,128)(2,1)} reshape(bf16[64,23424]{1,0:T(8,128)(2,1)} %param.11) | data formatting | bytes 5996544 | tf_op jit(solution)/shard_map/reshape | solution.py:329
  48.1 7.9 %dynamic-slice_bitcast_fusion = bf16[64,8,384]{1,2,0:T(8,128)(2,1)} fusion(s32[]{:T(128)S(6)} %select_n.78, bf16[64,384,61]{2,1,0:T(8,128)(2,1)} %reshape.121), kind=kLoop, calls=%fused_computation.4 | loop fusion | bytes 3391492 | tf_op jit(solution)/shard_map/transpose | solution.py:332
  56.7 6.1 %copy.21 = bf16[8,8,8,384]{3,1,2,0:T(8,128)(2,1)} copy(bf16[8,8,8,384]{2,3,1,0:T(8,128)(2,1)} %bitcast.67) | data formatting | bytes 786432
  62.8 22.4 %collective-permute-done.1.halo_ref = bf16[64,384]{1,0:T(8,128)(2,1)S(1)} collective-permute-done((bf16[64,384]{1,0:T(8,128)(2,1)S(1)}, bf16[64,384]{1,0:T(8,128)(2,1)S(1)}, u32[]{:S(2)}, u32[]{:S(2)}) %collective-permute-start.1) | collective-permute-done | bytes 49184 | tf_op jit(solution)/shard_map/ppermute | solution.py:335
  85.2 4.1 %refine.1 = bf16[64,3072]{1,0:T(8,128)(2,1)} custom-call(s32[1,2048]{1,0:T(1,128)} %add.100.key_ref, bf16[2048,384]{1,0:T(8,128)(2,1)} %bitcast.5.got_ref, bf16[64,3072]{1,0:T(8,128)(2,1)} %bitcast.84), custom_call_target="tpu_custom_call" | custom-call | flops 800000000 | bytes 3000000 | tf_op jit(solution)/shard_map/refine/pallas_call | solution.py:143
  94.7 2.2 %collective-permute-done.7 = bf16[1,32,3072]{2,1,0:T(8,128)(2,1)S(1)} collective-permute-done((bf16[1,32,3072]{2,1,0:T(8,128)(2,1)S(1)}, bf16[1,32,3072]{2,1,0:T(8,128)(2,1)S(1)}, u32[]{:S(2)}, u32[]{:S(2)}) %collective-permute-start.7) | collective-permute-done | bytes 196640 | tf_op jit(solution)/shard_map/ppermute | solution.py:273
  98.5 2.4 %collective-permute-done.3 = bf16[1,32,3072]{2,1,0:T(8,128)(2,1)S(1)} collective-permute-done((bf16[1,32,3072]{2,1,0:T(8,128)(2,1)S(1)}, bf16[1,32,3072]{2,1,0:T(8,128)(2,1)S(1)}, u32[]{:S(2)}, u32[]{:S(2)}) %collective-permute-start.3) | collective-permute-done | bytes 196640 | tf_op jit(solution)/shard_map/ppermute | solution.py:273
  101.6 10.1 %collective-permute-done.11 = bf16[64,3072]{1,0:T(8,128)(2,1)S(1)} collective-permute-done((bf16[64,3072]{1,0:T(8,128)(2,1)}, bf16[64,3072]{1,0:T(8,128)(2,1)S(1)}, u32[]{:S(2)}, u32[]{:S(2)}) %collective-permute-start.11) | collective-permute-done | bytes 393248 | tf_op jit(solution)/shard_map/ppermute | solution.py:369
  113.0 3.2 %fold.2.refs_8_ = bf16[272,3072]{1,0:T(8,128)(2,1)} custom-call(bf16[2048,384]{1,0:T(8,128)(2,1)} %rec_ref.2, bf16[64,384]{1,0:T(8,128)(2,1)} %copy-done.14), custom_call_target="tpu_custom_call" | custom-call | flops 200000000 | bytes 4000000 | tf_op jit(solution)/shard_map/fold/pallas_call | solution.py:101
  116.2 3.2 %fold.3.refs_9_ = bf16[272,3072]{1,0:T(8,128)(2,1)} custom-call(bf16[2048,384]{1,0:T(8,128)(2,1)} %copy-done.3, bf16[64,384]{1,0:T(8,128)(2,1)} %broadcast_select_fusion.2.halo_ref), custom_call_target="tpu_custom_call" | custom-call | flops 200000000 | bytes 4000000 | tf_op jit(solution)/shard_map/fold/pallas_call | solution.py:101
  120.0 1.7 collective-permute-start.14
  122.2 5.6 %collective-permute-done.14 = bf16[1,32,3072]{2,1,0:T(8,128)(2,1)S(1)} collective-permute-done((bf16[1,32,3072]{2,1,0:T(8,128)(2,1)S(1)}, bf16[1,32,3072]{2,1,0:T(8,128)(2,1)S(1)}, u32[]{:S(2)}, u32[]{:S(2)}) %collective-permute-start.14) | collective-permute-done | bytes 196640 | tf_op jit(solution)/shard_map/ppermute | solution.py:273
  127.9 1.6 collective-permute-start.15
  130.9 4.4 %collective-permute-done.13.refs_1_ = bf16[2,32,3072]{2,1,0:T(8,128)(2,1)S(1)} collective-permute-done((bf16[2,32,3072]{2,1,0:T(8,128)(2,1)S(1)}, bf16[2,32,3072]{2,1,0:T(8,128)(2,1)S(1)}, u32[]{:S(2)}, u32[]{:S(2)}) %collective-permute-start.13) | collective-permute-done | bytes 393248 | tf_op jit(solution)/shard_map/ppermute | solution.py:273
  135.6 3.8 %collective-permute-done.15.refs_3_ = bf16[2,32,3072]{2,1,0:T(8,128)(2,1)S(1)} collective-permute-done((bf16[2,32,3072]{2,1,0:T(8,128)(2,1)S(1)}, bf16[2,32,3072]{2,1,0:T(8,128)(2,1)S(1)}, u32[]{:S(2)}, u32[]{:S(2)}) %collective-permute-start.15) | collective-permute-done | bytes 393248 | tf_op jit(solution)/shard_map/ppermute | solution.py:273
  139.5 21.5 %correlate.2 = f32[64,4096]{1,0:T(8,128)} custom-call(s32[3]{0:T(128)} %pad_add_fusion.place_ref, bf16[2,32,3072]{2,1,0:T(8,128)(2,1)} %copy-done.6, bf16[2,32,3072]{2,1,0:T(8,128)(2,1)} %copy-done.7, bf16[2,32,3072]{2,1,0:T(8,128)(2,1)} %copy-done.4, bf16[2,32,3072]{2,1,0:T(8,128)(2,1)} %copy-done.5, bf16[2,32,3072]{2,1,0:T(8,128)(2,1)} %copy-done.11, ...), custom_call_target="tpu_custom_call" | custom-call | flops 8000000000 | bytes 8000000 | tf_op jit(solution)/shard_map/correlate/pallas_call | solution.py:251
  162.7 20.3 %correlate.3 = bf16[64,2048]{1,0:T(8,128)(2,1)} custom-call(s32[3]{0:T(128)} %pad_add_fusion.2.place_ref, bf16[2,32,3072]{2,1,0:T(8,128)(2,1)} %copy-done.8, bf16[2,32,3072]{2,1,0:T(8,128)(2,1)} %copy-done.17, bf16[2,32,3072]{2,1,0:T(8,128)(2,1)} %copy-done.9, bf16[2,32,3072]{2,1,0:T(8,128)(2,1)} %copy-done.18, ...), custom_call_target="tpu_custom_call" | custom-call | flops 8000000000 | bytes 8000000 | tf_op jit(solution)/shard_map/correlate/pallas_call | solution.py:251
  183.5 1.6 copy.18
  186.4 12.1 %collective-permute-done.20 = bf16[64,2048]{1,0:T(8,128)(2,1)S(1)} collective-permute-done((bf16[64,2048]{1,0:T(8,128)(2,1)}, bf16[64,2048]{1,0:T(8,128)(2,1)S(1)}, u32[]{:S(2)}, u32[]{:S(2)}) %collective-permute-start.20) | collective-permute-done | bytes 262176 | tf_op jit(solution)/shard_map/ppermute | solution.py:372
  (124 shorter events, 23.8 us)
Async XLA Ops:
  2.4 14.4 %all-to-all-start = ((s32[32,1,8]{2,1,0:T(1,128)}), s32[32,1,8]{2,1,0:T(1,128)S(1)}, u32[]{:S(2)}, u32[]{:S(2)}) async-start(s32[32,1,8]{2,1,0:T(1,128)} %bitcast.2), calls=%async_computation | async-start | bytes 32768 | tf_op jit(solution)/shard_map/all_to_all | solution.py:322
  17.7 67.5 %all-to-all-start.1 = ((bf16[32,64,384]{2,1,0:T(8,128)(2,1)}), bf16[32,64,384]{2,1,0:T(8,128)(2,1)}, u32[]{:S(2)}, u32[]{:S(2)}) async-start(bf16[32,64,384]{2,1,0:T(8,128)(2,1)} %bitcast.68), calls=%async_computation.1 | async-start | bytes 3145728 | tf_op jit(solution)/shard_map/all_to_all | solution.py:325
  21.1 64.1 %collective-permute-start = (bf16[2048,384]{1,0:T(8,128)(2,1)S(1)}, bf16[2048,384]{1,0:T(8,128)(2,1)S(1)}, u32[]{:S(2)}, u32[]{:S(2)}) collective-permute-start(bf16[2048,384]{1,0:T(8,128)(2,1)S(1)} %copy-done.2), channel_id=1, source_target_pairs={{0,1},{1,0},{2,3},{3,2},{4,5},{5,4},{6,7},{7,6},{8,9},{9,8},{10,11... | collective-permute-start | bytes 4718600 | tf_op jit(solution)/shard_map/ppermute | solution.py:337
  22.8 62.3 %collective-permute-start.1 = (bf16[64,384]{1,0:T(8,128)(2,1)S(1)}, bf16[64,384]{1,0:T(8,128)(2,1)S(1)}, u32[]{:S(2)}, u32[]{:S(2)}) collective-permute-start(bf16[64,384]{1,0:T(8,128)(2,1)S(1)} %slice.18), channel_id=1, source_target_pairs={{1,0},{2,1},{3,2},{4,3},{5,4},{6,5},{7,6},{8,7},{9,8},{10,9},{11,1... | collective-permute-start | bytes 147464 | tf_op jit(solution)/shard_map/ppermute | solution.py:335
  24.1 61.1 %collective-permute-start.2 = (bf16[64,384]{1,0:T(8,128)(2,1)S(1)}, bf16[64,384]{1,0:T(8,128)(2,1)S(1)}, u32[]{:S(2)}, u32[]{:S(2)}) collective-permute-start(bf16[64,384]{1,0:T(8,128)(2,1)S(1)} %slice.18), channel_id=1, source_target_pairs={{2,0},{4,2},{6,4},{8,6},{10,8},{12,10},{14,12},{16,14},{18,16},{20... | collective-permute-start | bytes 147464 | tf_op jit(solution)/shard_map/ppermute | solution.py:336
  90.4 6.5 %collective-permute-start.7 = (bf16[1,32,3072]{2,1,0:T(8,128)(2,1)S(1)}, bf16[1,32,3072]{2,1,0:T(8,128)(2,1)S(1)}, u32[]{:S(2)}, u32[]{:S(2)}) collective-permute-start(bf16[1,32,3072]{2,1,0:T(8,128)(2,1)S(1)} %get-tuple-element.25), channel_id=1, source_target_pairs={{0,8},{4,12},{8,0},{12,4},{16,24},{20,28},{24,16},{28,20},{1,9},{5... | collective-permute-start | bytes 589832 | tf_op jit(solution)/shard_map/ppermute | solution.py:273
  91.7 20.0 %collective-permute-start.11 = (bf16[64,3072]{1,0:T(8,128)(2,1)}, bf16[64,3072]{1,0:T(8,128)(2,1)S(1)}, u32[]{:S(2)}, u32[]{:S(2)}) collective-permute-start(bf16[64,3072]{1,0:T(8,128)(2,1)} %refine.1), channel_id=1, source_target_pairs={{0,2},{1,3},{2,0},{3,1},{4,6},{5,7},{6,4},{7,5},{8,10},{9,11},{10,... | collective-permute-start | bytes 1179656 | tf_op jit(solution)/shard_map/ppermute | solution.py:369
  93.2 7.8 %collective-permute-start.3 = (bf16[1,32,3072]{2,1,0:T(8,128)(2,1)S(1)}, bf16[1,32,3072]{2,1,0:T(8,128)(2,1)S(1)}, u32[]{:S(2)}, u32[]{:S(2)}) collective-permute-start(bf16[1,32,3072]{2,1,0:T(8,128)(2,1)S(1)} %get-tuple-element.24), channel_id=1, source_target_pairs={{0,16},{4,20},{8,24},{12,28},{16,0},{20,4},{24,8},{28,12},{1,17},{... | collective-permute-start | bytes 589832 | tf_op jit(solution)/shard_map/ppermute | solution.py:273
  97.0 24.8 %collective-permute-start.8 = (bf16[2,32,3072]{2,1,0:T(8,128)(2,1)S(1)}, bf16[2,32,3072]{2,1,0:T(8,128)(2,1)S(1)}, u32[]{:S(2)}, u32[]{:S(2)}) collective-permute-start(bf16[2,32,3072]{2,1,0:T(8,128)(2,1)S(1)} %pad_maximum_fusion.3.refs_2_), channel_id=1, source_target_pairs={{0,16},{4,20},{8,24},{12,28},{16,0},{20,4},{24,8},{28,12},{1,17},{... | collective-permute-start | bytes 1179656 | tf_op jit(solution)/shard_map/ppermute | solution.py:273
  101.0 21.2 %collective-permute-start.4 = (bf16[2,32,3072]{2,1,0:T(8,128)(2,1)S(1)}, bf16[2,32,3072]{2,1,0:T(8,128)(2,1)S(1)}, u32[]{:S(2)}, u32[]{:S(2)}) collective-permute-start(bf16[2,32,3072]{2,1,0:T(8,128)(2,1)S(1)} %pad_maximum_fusion.2.refs_0_), channel_id=1, source_target_pairs={{0,8},{4,12},{8,0},{12,4},{16,24},{20,28},{24,16},{28,20},{1,9},{5... | collective-permute-start | bytes 1179656 | tf_op jit(solution)/shard_map/ppermute | solution.py:273
  111.7 8.2 %collective-permute-start.12 = (bf16[1,32,3072]{2,1,0:T(8,128)(2,1)S(1)}, bf16[1,32,3072]{2,1,0:T(8,128)(2,1)S(1)}, u32[]{:S(2)}, u32[]{:S(2)}) collective-permute-start(bf16[1,32,3072]{2,1,0:T(8,128)(2,1)S(1)} %get-tuple-element.22), channel_id=1, source_target_pairs={{0,16},{4,20},{8,24},{12,28},{16,0},{20,4},{24,8},{28,12},{1,17},{... | collective-permute-start | bytes 589832 | tf_op jit(solution)/shard_map/ppermute | solution.py:273
  119.4 8.5 %collective-permute-start.9 = (bf16[2,32,3072]{2,1,0:T(8,128)(2,1)S(1)}, bf16[2,32,3072]{2,1,0:T(8,128)(2,1)S(1)}, u32[]{:S(2)}, u32[]{:S(2)}) collective-permute-start(bf16[2,32,3072]{2,1,0:T(8,128)(2,1)S(1)} %pad_maximum_fusion.3.refs_2_), channel_id=1, source_target_pairs={{0,4},{4,0},{8,12},{12,8},{16,20},{20,16},{24,28},{28,24},{1,5},{5... | collective-permute-start | bytes 1179656 | tf_op jit(solution)/shard_map/ppermute | solution.py:273
  119.4 10.4 %collective-permute-start.5 = (bf16[2,32,3072]{2,1,0:T(8,128)(2,1)S(1)}, bf16[2,32,3072]{2,1,0:T(8,128)(2,1)S(1)}, u32[]{:S(2)}, u32[]{:S(2)}) collective-permute-start(bf16[2,32,3072]{2,1,0:T(8,128)(2,1)S(1)} %pad_maximum_fusion.2.refs_0_), channel_id=1, source_target_pairs={{0,4},{4,0},{8,12},{12,8},{16,20},{20,16},{24,28},{28,24},{1,5},{5... | collective-permute-start | bytes 1179656 | tf_op jit(solution)/shard_map/ppermute | solution.py:273
  120.0 7.8 %collective-permute-start.14 = (bf16[1,32,3072]{2,1,0:T(8,128)(2,1)S(1)}, bf16[1,32,3072]{2,1,0:T(8,128)(2,1)S(1)}, u32[]{:S(2)}, u32[]{:S(2)}) collective-permute-start(bf16[1,32,3072]{2,1,0:T(8,128)(2,1)S(1)} %get-tuple-element.21), channel_id=1, source_target_pairs={{0,8},{4,12},{8,0},{12,4},{16,24},{20,28},{24,16},{28,20},{1,9},{5... | collective-permute-start | bytes 589832 | tf_op jit(solution)/shard_map/ppermute | solution.py:273
  121.8 13.6 %collective-permute-start.13 = (bf16[2,32,3072]{2,1,0:T(8,128)(2,1)S(1)}, bf16[2,32,3072]{2,1,0:T(8,128)(2,1)S(1)}, u32[]{:S(2)}, u32[]{:S(2)}) collective-permute-start(bf16[2,32,3072]{2,1,0:T(8,128)(2,1)S(1)} %pad_maximum_fusion.4.refs_0_), channel_id=1, source_target_pairs={{0,8},{4,12},{8,0},{12,4},{16,24},{20,28},{24,16},{28,20},{1,9},{5... | collective-permute-start | bytes 1179656 | tf_op jit(solution)/shard_map/ppermute | solution.py:273
  122.2 8.2 %collective-permute-start.10 = (bf16[2,32,3072]{2,1,0:T(8,128)(2,1)S(1)}, bf16[2,32,3072]{2,1,0:T(8,128)(2,1)S(1)}, u32[]{:S(2)}, u32[]{:S(2)}) collective-permute-start(bf16[2,32,3072]{2,1,0:T(8,128)(2,1)S(1)} %collective-permute-done.8.refs_3_), channel_id=1, source_target_pairs={{0,4},{4,0},{8,12},{12,8},{16,20},{20,16},{24,28},{28,24},{1,5},{5... | collective-permute-start | bytes 1179656 | tf_op jit(solution)/shard_map/ppermute | solution.py:273
  127.8 3.0 %collective-permute-start.6 = (bf16[2,32,3072]{2,1,0:T(8,128)(2,1)S(1)}, bf16[2,32,3072]{2,1,0:T(8,128)(2,1)S(1)}, u32[]{:S(2)}, u32[]{:S(2)}) collective-permute-start(bf16[2,32,3072]{2,1,0:T(8,128)(2,1)S(1)} %collective-permute-done.4.refs_1_), channel_id=1, source_target_pairs={{0,4},{4,0},{8,12},{12,8},{16,20},{20,16},{24,28},{28,24},{1,5},{5... | collective-permute-start | bytes 1179656 | tf_op jit(solution)/shard_map/ppermute | solution.py:273
  127.9 11.6 %collective-permute-start.15 = (bf16[2,32,3072]{2,1,0:T(8,128)(2,1)S(1)}, bf16[2,32,3072]{2,1,0:T(8,128)(2,1)S(1)}, u32[]{:S(2)}, u32[]{:S(2)}) collective-permute-start(bf16[2,32,3072]{2,1,0:T(8,128)(2,1)S(1)} %pad_maximum_fusion.5.refs_2_), channel_id=1, source_target_pairs={{0,16},{4,20},{8,24},{12,28},{16,0},{20,4},{24,8},{28,12},{1,17},{... | collective-permute-start | bytes 1179656 | tf_op jit(solution)/shard_map/ppermute | solution.py:273
  129.8 32.9 %collective-permute-start.16 = (bf16[2,32,3072]{2,1,0:T(8,128)(2,1)S(1)}, bf16[2,32,3072]{2,1,0:T(8,128)(2,1)}, u32[]{:S(2)}, u32[]{:S(2)}) collective-permute-start(bf16[2,32,3072]{2,1,0:T(8,128)(2,1)S(1)} %pad_maximum_fusion.4.refs_0_), channel_id=1, source_target_pairs={{0,4},{4,0},{8,12},{12,8},{16,20},{20,16},{24,28},{28,24},{1,5},{5... | collective-permute-start | bytes 1179656 | tf_op jit(solution)/shard_map/ppermute | solution.py:273
  130.4 32.3 %collective-permute-start.18 = (bf16[2,32,3072]{2,1,0:T(8,128)(2,1)S(1)}, bf16[2,32,3072]{2,1,0:T(8,128)(2,1)}, u32[]{:S(2)}, u32[]{:S(2)}) collective-permute-start(bf16[2,32,3072]{2,1,0:T(8,128)(2,1)S(1)} %pad_maximum_fusion.5.refs_2_), channel_id=1, source_target_pairs={{0,4},{4,0},{8,12},{12,8},{16,20},{20,16},{24,28},{28,24},{1,5},{5... | collective-permute-start | bytes 1179656 | tf_op jit(solution)/shard_map/ppermute | solution.py:273
  135.3 25.6 %copy-start.17 = (bf16[2,32,3072]{2,1,0:T(8,128)(2,1)}, bf16[2,32,3072]{2,1,0:T(8,128)(2,1)S(1)}, u32[]{:S(2)}) copy-start(bf16[2,32,3072]{2,1,0:T(8,128)(2,1)S(1)} %collective-permute-done.13.refs_1_) | copy-start | bytes 1179652
  135.3 27.4 %collective-permute-start.17 = (bf16[2,32,3072]{2,1,0:T(8,128)(2,1)S(1)}, bf16[2,32,3072]{2,1,0:T(8,128)(2,1)}, u32[]{:S(2)}, u32[]{:S(2)}) collective-permute-start(bf16[2,32,3072]{2,1,0:T(8,128)(2,1)S(1)} %collective-permute-done.13.refs_1_), channel_id=1, source_target_pairs={{0,4},{4,0},{8,12},{12,8},{16,20},{20,16},{24,28},{28,24},{1,5},{5... | collective-permute-start | bytes 1179656 | tf_op jit(solution)/shard_map/ppermute | solution.py:273
  139.4 23.3 %collective-permute-start.19 = (bf16[2,32,3072]{2,1,0:T(8,128)(2,1)S(1)}, bf16[2,32,3072]{2,1,0:T(8,128)(2,1)}, u32[]{:S(2)}, u32[]{:S(2)}) collective-permute-start(bf16[2,32,3072]{2,1,0:T(8,128)(2,1)S(1)} %collective-permute-done.15.refs_3_), channel_id=1, source_target_pairs={{0,4},{4,0},{8,12},{12,8},{16,20},{20,16},{24,28},{28,24},{1,5},{5... | collective-permute-start | bytes 1179656 | tf_op jit(solution)/shard_map/ppermute | solution.py:273
  183.1 15.4 %collective-permute-start.20 = (bf16[64,2048]{1,0:T(8,128)(2,1)}, bf16[64,2048]{1,0:T(8,128)(2,1)S(1)}, u32[]{:S(2)}, u32[]{:S(2)}) collective-permute-start(bf16[64,2048]{1,0:T(8,128)(2,1)} %correlate.3), channel_id=1, source_target_pairs={{2,0},{3,1},{0,2},{1,3},{6,4},{7,5},{4,6},{5,7},{10,8},{11,9},{8,1... | collective-permute-start | bytes 786440 | tf_op jit(solution)/shard_map/ppermute | solution.py:372
  (18 other events, 180.8 us)

commit v5 on v4

--- a/solution.py
+++ b/solution.py
@@ -78,35 +78,37 @@
     )(times, labels, base, rec)
 
 
-def fold_kernel(rec_ref, halo_ref, out_ref):
-    rows, chans = rec_ref.shape
-    extra = halo_ref.shape[0]
+def fold_kernel(*refs):
+    out_ref = refs[-1]
+    chans = refs[0].shape[1]
     block = 16 * ROWS
     new = lax.broadcasted_iota(jnp.int32, (block, block), 0)
     old = lax.broadcasted_iota(jnp.int32, (block, block), 1)
     perm = (old == (new % 16) * ROWS + new // 16).astype(jnp.bfloat16)
-    for b in range(rows // block + 1):
-        if b < rows // block:
-            part = jnp.dot(perm, rec_ref[b * block : (b + 1) * block, :], preferred_element_type=jnp.float32)
-        else:
-            part = jnp.dot(perm[:, :extra], halo_ref[...], preferred_element_type=jnp.float32)
-        part = part.astype(jnp.bfloat16)
-        for r in range(ROWS):
-            out_ref[b * 16 : (b + 1) * 16, r * chans : (r + 1) * chans] = part[r * 16 : (r + 1) * 16]
-
-
-def fold(rec, halo):
-    rows, chans = rec.shape
+    at = 0
+    for ref in refs[:-1]:
+        for low in range(0, ref.shape[0], block):
+            size = min(block, ref.shape[0] - low)
+            part = jnp.dot(perm[:, :size], ref[low : low + size, :], preferred_element_type=jnp.float32)
+            part = part.astype(jnp.bfloat16)
+            for r in range(ROWS):
+                out_ref[at : at + 16, r * chans : (r + 1) * chans] = part[r * 16 : (r + 1) * 16]
+            at += 16
+
+
+def fold(*parts):
+    chans = parts[0].shape[1]
+    blocks = sum(-(-p.shape[0] // (16 * ROWS)) for p in parts)
     vmem = pl.BlockSpec(memory_space=pltpu.VMEM)
     return pl.pallas_call(
         fold_kernel,
-        out_shape=jax.ShapeDtypeStruct((rows // ROWS + 16, ROWS * chans), jnp.bfloat16),
-        in_specs=[vmem, vmem],
+        out_shape=jax.ShapeDtypeStruct((blocks * 16, ROWS * chans), jnp.bfloat16),
+        in_specs=[vmem] * len(parts),
         out_specs=vmem,
         compiler_params=params(),
         cost_estimate=pl.CostEstimate(flops=2 * 10**8, bytes_accessed=4 * 10**6, transcendentals=0),
         name="fold",
-    )(rec, halo)
+    )(*parts)
 
 
 def refine_kernel(tpd, key_ref, got_ref, old_ref, out_ref, sums):
@@ -155,7 +157,7 @@
 def correlate_kernel(chans, tpd, scale, masks, place_ref, *refs):
     count = len(masks)
     pieces, rest = refs[:count], refs[count:]
-    mine_ref, theirs_ref, out_ref, t_buf, e_buf, t_sem, e_sem, rhs, part, acc = rest
+    mine_ref, early_ref, late_ref, out_ref, t_buf, e_buf, t_sem, e_sem, rhs, part, acc = rest
     half_rows = pieces[0].shape[1]
     lanes = tpd * chans
     chunks = t_sem.shape[0]
@@ -175,10 +177,12 @@
             first = pl.multiple_of(first, 128)
         return t_buf.at[chunk // per, rows, pl.ds(first, lanes)]
 
-    e_copies = [
-        pltpu.make_async_copy(ref, e_buf.at[n * height : (n + 1) * height, :], e_sem.at[n])
-        for n, ref in enumerate((mine_ref, theirs_ref))
-    ]
+    e_copies = []
+    low = 0
+    for n, ref in enumerate((mine_ref, early_ref, late_ref)):
+        size = ref.shape[0]
+        e_copies.append(pltpu.make_async_copy(ref, e_buf.at[low : low + size, :], e_sem.at[n]))
+        low += size
     for copy in e_copies:
         copy.start()
     for ref, (part_of, items) in zip(pieces, masks):
@@ -194,26 +198,25 @@
                     sem = t_sem.at[chunk, part_of]
                     pltpu.make_async_copy(pieces[0].at[0], spot(chunk, part_of), sem).wait()
         used = depth if a < blocks else depth // 2
-        turn = a % 2
         for q in range(FOLD):
             rows = slice(q * panel, (q + 1) * panel)
             cut = q * shift
             low = min(cut, used)
             if low > 0:
                 if a > 0:
-                    rhs[turn, rows, 0:low] = t_buf[a - 1, :, depth - cut : depth - cut + low]
+                    rhs[rows, 0:low] = t_buf[a - 1, :, depth - cut : depth - cut + low]
                 else:
-                    rhs[turn, rows, 0:low] = jnp.zeros((panel, low), jnp.bfloat16)
+                    rhs[rows, 0:low] = jnp.zeros((panel, low), jnp.bfloat16)
             if cut < used:
                 if a < blocks:
-                    rhs[turn, rows, cut:used] = t_buf[a, :, 0 : used - cut]
+                    rhs[rows, cut:used] = t_buf[a, :, 0 : used - cut]
                 else:
-                    rhs[turn, rows, cut:used] = jnp.zeros((panel, used - cut), jnp.bfloat16)
-        part[turn] = lax.dot_general(
-            e_buf[:, 0:used], rhs[turn, :, 0:used], NT, preferred_element_type=jnp.float32
+                    rhs[rows, cut:used] = jnp.zeros((panel, used - cut), jnp.bfloat16)
+        part[...] = lax.dot_general(
+            e_buf[:, 0:used], rhs[:, 0:used], NT, preferred_element_type=jnp.float32
         )
         for h in range(2):
-            found = part[turn, h * height + a : h * height + a + keep, :]
+            found = part[h * height + a : h * height + a + keep, :]
             if a == 0:
                 acc[h * keep : (h + 1) * keep, :] = found
             else:
@@ -251,15 +254,15 @@
     return pl.pallas_call(
         functools.partial(correlate_kernel, chans, tpd, scale, masks),
         out_shape=jax.ShapeDtypeStruct((panel, width), dtype),
-        in_specs=[pl.BlockSpec(memory_space=pltpu.SMEM)] + [anywhere] * (len(pieces) + 2),
+        in_specs=[pl.BlockSpec(memory_space=pltpu.SMEM)] + [anywhere] * (len(pieces) + 3),
         out_specs=pl.BlockSpec(memory_space=pltpu.VMEM),
         scratch_shapes=[
             pltpu.VMEM((chunks * tpd // ROWS, panel, depth), jnp.bfloat16),
             pltpu.VMEM((2 * height, depth), jnp.bfloat16),
             pltpu.SemaphoreType.DMA((chunks, 2)),
-            pltpu.SemaphoreType.DMA((2,)),
-            pltpu.VMEM((2, FOLD * panel, depth), jnp.bfloat16),
-            pltpu.VMEM((2, 2 * height, FOLD * panel), jnp.float32),
+            pltpu.SemaphoreType.DMA((3,)),
+            pltpu.VMEM((FOLD * panel, depth), jnp.bfloat16),
+            pltpu.VMEM((2 * height, FOLD * panel), jnp.float32),
             pltpu.VMEM((2 * keep, FOLD * panel), jnp.float32),
         ],
         compiler_params=params(),
@@ -321,26 +324,30 @@
     tags = tags.reshape(devices, CAP)
     tags = lax.all_to_all(tags, AXES, split_axis=0, concat_axis=0, tiled=True)
     key = (tags[:, :, None] * tpd + jnp.arange(tpd)[None, None, :]).reshape(1, -1)
-    send, key = lax.optimization_barrier((send, key))
+    pairs = [(i, i ^ 1) for i in range(owners)]
+    first = sub_rows * 7 // 16 // (16 * ROWS) * (16 * ROWS)
+    early = lax.ppermute(recording[:first], "unit", pairs)
+    send, key, early, before = lax.optimization_barrier((send, key, early, old_templates))
     got = lax.all_to_all(
         send.reshape(devices, CAP * tpd, chans), AXES, split_axis=0, concat_axis=0, tiled=True
     ).reshape(devices * CAP * tpd, chans)
 
-    cube = old_templates.reshape(panel, chans, taps)
+    cube = before.reshape(panel, chans, taps)
     cube = jnp.pad(cube, ((0, 0), (0, 0), (0, padded - taps)))
     cube = lax.dynamic_slice_in_dim(cube, tm_pos * tpd, tpd, 2)
     old = jnp.transpose(cube, (0, 2, 1)).reshape(panel, tpd * chans)
 
-    head = recording[:padded]
+    got, rest = lax.optimization_barrier((got, recording))
+    head = rest[:padded]
     follow = lax.ppermute(head, AXES, [(i, i - 1) for i in range(1, devices)])
     skip = lax.ppermute(head, AXES, [(i, i - 2) for i in range(2, devices, 2)])
-    theirs = lax.ppermute(recording, "unit", [(i, i ^ 1) for i in range(owners)])
-    got, theirs, follow, skip = lax.optimization_barrier((got, theirs, follow, skip))
+    late = lax.ppermute(rest[first:], "unit", pairs)
     odd = unit_pos % 2
 
     fresh = refine(key, got, old, tpd)
-    late, theirs, fresh = lax.optimization_barrier((recording, theirs, fresh))
-    windows = (fold(late, follow), fold(theirs, jnp.where(odd == 1, head, skip)))
+    early, rest, fresh = lax.optimization_barrier((early, rest, fresh))
+    mine = fold(rest, follow)
+    early = fold(early)
     own = gather_panel(fresh)
     width = 2 * keep * FOLD
 
@@ -366,11 +373,20 @@
     for m in range(1, owners // 2):
         ahead = [(i, (i + 2 * m) % owners) for i in range(owners)]
         back = [(j, i) for i, j in ahead]
-        other = gather_panel(lax.ppermute(fresh, "unit", ahead))
+        chunk = lax.ppermute(fresh, "unit", ahead)
+        if m == 1:
+            chunk, mine, early = lax.optimization_barrier((chunk, mine, early))
+        other = gather_panel(chunk)
+        if m == 1:
+            windows = (mine, early, fold(late, jnp.where(odd == 1, head, skip)))
+            tied = lax.optimization_barrier((part, *[v for v, _, _ in other]))
+            part = tied[0]
+            other = [(v, n, ms) for v, (_, n, ms) in zip(tied[1:], other)]
         place = jnp.stack([tm_pos, odd, 0 * odd]).astype(jnp.int32)
         out = correlate(place, other, windows, chans, tpd, scale, width, jnp.bfloat16)
         found.append((lax.ppermute(out, "unit", back), ((unit_pos + 2 * m) % owners) // 2))
     place = jnp.stack([tm_pos, odd, unit_pos // 2]).astype(jnp.int32)
+    place, _ = lax.optimization_barrier((place, out))
     scores = correlate(place, own, windows, chans, tpd, scale, owners // 2 * width, jnp.float32)
     for out, pair in found:
         scores = lax.dynamic_update_slice_in_dim(

time: 200 us -> 179 us (0.90)
  waiting for transfers between devices: 66.2 us -> 28 us
  starting transfers between devices: 26.9 us -> 38.8 us
  local copies, waits for them, and re-layouts: 44.6 us -> 46.9 us
  other arithmetic: 4.25 us -> 6.46 us
    ppermute x1, waiting for transfers between devices: 22.4 us -> 0.01 us  [body(): follow = lax.ppermute(head, AXES, [(i, i - 1) for i in range(1, devices)])]
    ppermute x1, waiting for transfers between devices: 12.1 us -> 0.01 us  [body(): lax.ppermute(out, 'unit', back)]
    ppermute x2 -> x3, waiting for transfers between devices: 10.1 us -> 3.52 us  [the longest x1 1.8 us: body(): chunk = lax.ppermute(fresh, 'unit', ahead)]
    ppermute x1, starting transfers between devices: 0.07 us -> 6.22 us  [body(): lax.ppermute(out, 'unit', back)]
    all_to_all x1, waiting for transfers between devices: 3.11 us -> 9.25 us  [body(): tags = lax.all_to_all(tags, AXES, split_axis=0, concat_axis=0, tiled=True)]
    ppermute x2 -> x3, starting transfers between devices: 3.17 us -> 8.47 us  [the longest x1 3.61 us: body(): chunk = lax.ppermute(fresh, 'unit', ahead)]
    ppermute x16, waiting for transfers between devices: 18.5 us -> 15.1 us  [swap(): return lax.ppermute(value, 'tm', [(i, i ^ bit) for i in range(size)])]
    ppermute x16, starting transfers between devices: 10.4 us -> 13.1 us  [swap(): return lax.ppermute(value, 'tm', [(i, i ^ bit) for i in range(size)])]
  transfers between devices with their start and end apart: 23 -> 24, of which waited for: 9 -> 7; matrix products, arithmetic and copies ran while one was open for 22% -> 27% of each run, Pallas kernels for 16% -> 19%
where the time goes in v5:
time: 179 us
  Pallas kernels  57.3 us (32%)
  local copies, waits for them, and re-layouts  46.9 us (26%)
  starting transfers between devices  38.8 us (22%)
  waiting for transfers between devices  28 us (16%)
  other arithmetic  6.46 us (4%)
    pallas_call x2, Pallas kernels, correlate(): pl.pallas_call(functools.partial(correlate_kernel, chans, tpd, scale, mas...  41.8 us
    reshape x1, local copies, waits for them, and re-layouts, body(): cube = before.reshape(panel, chans, taps)  19.6 us
    ppermute x16, waiting for transfers between devices, swap(): return lax.ppermute(value, 'tm', [(i, i ^ bit) for i in range(size)])  15.1 us
    ppermute x16, starting transfers between devices, swap(): return lax.ppermute(value, 'tm', [(i, i ^ bit) for i in range(size)])  13.1 us
    all_to_all x1, waiting for transfers between devices, body(): tags = lax.all_to_all(tags, AXES, split_axis=0, concat_axis=0, tiled=True)  9.25 us
    unnamed x45, local copies, waits for them, and re-layouts  8.61 us
    pallas_call x3, Pallas kernels, fold(): pl.pallas_call(fold_kernel, out_shape=jax.ShapeDtypeStruct((blocks * 16,...  8.03 us
    transpose x1, local copies, waits for them, and re-layouts, body(): old = jnp.transpose(cube, (0, 2, 1)).reshape(panel, tpd * chans)  7.92 us
  transfers between devices with their start and end apart: 24, of which 7 were waited for; matrix products, arithmetic and copies ran while one was open for 27% of the time, Pallas kernels for 19%

profile of v5, /device:TPU:0, one launch (start us, length us, event | category | flops | bytes accessed | tf_op | source)
XLA Modules:
  0.0 178.8 jit_solution(13270940735025177217)
XLA Ops:
  0.6 2.0 %slice.24 = bf16[896,384]{1,0:T(8,128)(2,1)} slice(bf16[2048,384]{1,0:T(8,128)(2,1)} %refs_0_), slice={[0:896], [0:384]} | slice | bytes 1376256 | tf_op jit(solution)/shard_map/slice | solution.py:329
  2.6 3.0 %collective-permute-start = (bf16[896,384]{1,0:T(8,128)(2,1)}, bf16[896,384]{1,0:T(8,128)(2,1)}, u32[]{:S(2)}, u32[]{:S(2)}) collective-permute-start(bf16[896,384]{1,0:T(8,128)(2,1)} %slice.24), channel_id=1, source_target_pairs={{0,1},{1,0},{2,3},{3,2},{4,5},{5,4},{6,7},{7,6},{8,9},{9,8},{10,11... | collective-permute-start | bytes 2064392 | tf_op jit(solution)/shard_map/ppermute | solution.py:329
  7.5 4.8 %all-to-all-start = ((s32[32,1,8]{2,1,0:T(1,128)}), s32[32,1,8]{2,1,0:T(1,128)S(1)}, u32[]{:S(2)}, u32[]{:S(2)}) async-start(s32[32,1,8]{2,1,0:T(1,128)} %bitcast.2), calls=%async_computation | async-start | bytes 32768 | tf_op jit(solution)/shard_map/all_to_all | solution.py:325
  12.4 4.0 %pack.1 = bf16[2048,384]{1,0:T(8,128)(2,1)} custom-call(s32[32]{0:T(128)} %times_ref.1, s32[32]{0:T(128)} %labels_ref.1, s32[1]{0:T(128)} %bitcast.1.base_ref, bf16[2048,384]{1,0:T(8,128)(2,1)} %refs_0_), custom_call_target="tpu_custom_call" | custom-call | flops 100000000 | bytes 4000000 | tf_op jit(solution)/shard_map/pack/pallas_call | solution.py:66
  16.3 9.2 %all-to-all-done = s32[32,1,8]{2,1,0:T(1,128)S(1)} async-done(((s32[32,1,8]{2,1,0:T(1,128)}), s32[32,1,8]{2,1,0:T(1,128)S(1)}, u32[]{:S(2)}, u32[]{:S(2)}) %all-to-all-start) | async-done | bytes 1056 | tf_op jit(solution)/shard_map/all_to_all | solution.py:325
  26.4 3.4 %all-to-all-start.1 = ((bf16[32,64,384]{2,1,0:T(8,128)(2,1)}), bf16[32,64,384]{2,1,0:T(8,128)(2,1)}, u32[]{:S(2)}, u32[]{:S(2)}) async-start(bf16[32,64,384]{2,1,0:T(8,128)(2,1)} %bitcast.68), calls=%async_computation.1 | async-start | bytes 3145728 | tf_op jit(solution)/shard_map/all_to_all | solution.py:331
  32.6 19.6 %reshape.121 = bf16[64,384,61]{2,1,0:T(8,128)(2,1)} reshape(bf16[64,23424]{1,0:T(8,128)(2,1)S(1)} %copy-done.3) | data formatting | bytes 5996544 | tf_op jit(solution)/shard_map/reshape | solution.py:335
  52.1 7.9 %dynamic-slice_bitcast_fusion = bf16[64,8,384]{1,2,0:T(8,128)(2,1)} fusion(s32[]{:T(128)S(6)} %select_n.78, bf16[64,384,61]{2,1,0:T(8,128)(2,1)} %reshape.121), kind=kLoop, calls=%fused_computation.4 | loop fusion | bytes 3391492 | tf_op jit(solution)/shard_map/transpose | solution.py:338
  60.1 6.2 %copy.21 = bf16[8,8,8,384]{3,1,2,0:T(8,128)(2,1)} copy(bf16[8,8,8,384]{2,3,1,0:T(8,128)(2,1)} %bitcast.67) | data formatting | bytes 786432
  66.3 3.5 %refine.1 = bf16[64,3072]{1,0:T(8,128)(2,1)} custom-call(s32[1,2048]{1,0:T(1,128)} %add.100.key_ref, bf16[2048,384]{1,0:T(8,128)(2,1)} %bitcast.5.got_ref, bf16[64,3072]{1,0:T(8,128)(2,1)} %bitcast.84), custom_call_target="tpu_custom_call" | custom-call | flops 800000000 | bytes 3000000 | tf_op jit(solution)/shard_map/refine/pallas_call | solution.py:145
  72.2 3.6 %collective-permute-start.9 = (bf16[64,3072]{1,0:T(8,128)(2,1)}, bf16[64,3072]{1,0:T(8,128)(2,1)S(1)}, u32[]{:S(2)}, u32[]{:S(2)}) collective-permute-start(bf16[64,3072]{1,0:T(8,128)(2,1)} %refine.1), channel_id=1, source_target_pairs={{0,2},{1,3},{2,0},{3,1},{4,6},{5,7},{6,4},{7,5},{8,10},{9,11},{10,... | collective-permute-start | bytes 1179656 | tf_op jit(solution)/shard_map/ppermute | solution.py:376
  77.4 2.3 %collective-permute-start.5 = (bf16[1,32,3072]{2,1,0:T(8,128)(2,1)S(1)}, bf16[1,32,3072]{2,1,0:T(8,128)(2,1)S(1)}, u32[]{:S(2)}, u32[]{:S(2)}) collective-permute-start(bf16[1,32,3072]{2,1,0:T(8,128)(2,1)S(1)} %get-tuple-element.51), channel_id=1, source_target_pairs={{0,8},{4,12},{8,0},{12,4},{16,24},{20,28},{24,16},{28,20},{1,9},{5... | collective-permute-start | bytes 589832 | tf_op jit(solution)/shard_map/ppermute | solution.py:276
  81.2 2.3 %fold.4.refs_9_ = bf16[112,3072]{1,0:T(8,128)(2,1)} custom-call(bf16[896,384]{1,0:T(8,128)(2,1)} %collective-permute-done.refs_0_), custom_call_target="tpu_custom_call" | custom-call | flops 200000000 | bytes 4000000 | tf_op jit(solution)/shard_map/fold/pallas_call | solution.py:103
  83.7 1.8 %collective-permute-start.19 = (bf16[1152,384]{1,0:T(8,128)(2,1)S(1)}, bf16[1152,384]{1,0:T(8,128)(2,1)S(1)}, u32[]{:S(2)}, u32[]{:S(2)}) collective-permute-start(bf16[1152,384]{1,0:T(8,128)(2,1)S(1)} %slice.31), channel_id=1, source_target_pairs={{0,1},{1,0},{2,3},{3,2},{4,5},{5,4},{6,7},{7,6},{8,9},{9,8},{10,11... | collective-permute-start | bytes 2654216 | tf_op jit(solution)/shard_map/ppermute | solution.py:344
  86.8 3.2 %fold.3.refs_8_ = bf16[272,3072]{1,0:T(8,128)(2,1)} custom-call(bf16[2048,384]{1,0:T(8,128)(2,1)} %refs_0_, bf16[64,384]{1,0:T(8,128)(2,1)} %copy-done.13), custom_call_target="tpu_custom_call" | custom-call | flops 200000000 | bytes 4000000 | tf_op jit(solution)/shard_map/fold/pallas_call | solution.py:103
  90.0 2.1 %collective-permute-start.2 = (bf16[2,32,3072]{2,1,0:T(8,128)(2,1)S(1)}, bf16[2,32,3072]{2,1,0:T(8,128)(2,1)S(1)}, u32[]{:S(2)}, u32[]{:S(2)}) collective-permute-start(bf16[2,32,3072]{2,1,0:T(8,128)(2,1)S(1)} %pad_maximum_fusion.2.refs_0_), channel_id=1, source_target_pairs={{0,8},{4,12},{8,0},{12,4},{16,24},{20,28},{24,16},{28,20},{1,9},{5... | collective-permute-start | bytes 1179656 | tf_op jit(solution)/shard_map/ppermute | solution.py:276
  96.6 5.0 %collective-permute-done.2.refs_1_ = bf16[2,32,3072]{2,1,0:T(8,128)(2,1)S(1)} collective-permute-done((bf16[2,32,3072]{2,1,0:T(8,128)(2,1)S(1)}, bf16[2,32,3072]{2,1,0:T(8,128)(2,1)S(1)}, u32[]{:S(2)}, u32[]{:S(2)}) %collective-permute-start.2) | collective-permute-done | bytes 393248 | tf_op jit(solution)/shard_map/ppermute | solution.py:276
  104.5 5.0 %collective-permute-done.6.refs_3_ = bf16[2,32,3072]{2,1,0:T(8,128)(2,1)S(1)} collective-permute-done((bf16[2,32,3072]{2,1,0:T(8,128)(2,1)S(1)}, bf16[2,32,3072]{2,1,0:T(8,128)(2,1)S(1)}, u32[]{:S(2)}, u32[]{:S(2)}) %collective-permute-start.6) | collective-permute-done | bytes 393248 | tf_op jit(solution)/shard_map/ppermute | solution.py:276
  114.6 2.5 %fold.5.refs_10_ = bf16[160,3072]{1,0:T(8,128)(2,1)} custom-call(bf16[1152,384]{1,0:T(8,128)(2,1)} %copy-done.4, bf16[64,384]{1,0:T(8,128)(2,1)} %broadcast_select_fusion.2.refs_1_), custom_call_target="tpu_custom_call" | custom-call | flops 200000000 | bytes 4000000 | tf_op jit(solution)/shard_map/fold/pallas_call | solution.py:103
  119.5 5.1 %collective-permute-done.14.refs_3_ = bf16[2,32,3072]{2,1,0:T(8,128)(2,1)} collective-permute-done((bf16[2,32,3072]{2,1,0:T(8,128)(2,1)}, bf16[2,32,3072]{2,1,0:T(8,128)(2,1)}, u32[]{:S(2)}, u32[]{:S(2)}) %collective-permute-start.14) | collective-permute-done | bytes 393248 | tf_op jit(solution)/shard_map/ppermute | solution.py:276
  125.7 1.9 %copy.18 = bf16[64,48,8,8]{0,3,2,1:T(8,128)(2,1)S(1)} copy(bf16[64,48,8,8]{1,3,0,2:T(8,128)(2,1)S(1)} %maximum_bitcast_fusion) | data formatting | bytes 786432 | tf_op jit(solution)/shard_map/transpose | solution.py:369
  129.9 20.3 %correlate.2 = bf16[64,2048]{1,0:T(8,128)(2,1)} custom-call(s32[3]{0:T(128)} %pad_add_fusion.2.place_ref, bf16[2,32,3072]{2,1,0:T(8,128)(2,1)} %pad_maximum_fusion.4.refs_0_, bf16[2,32,3072]{2,1,0:T(8,128)(2,1)} %collective-permute-done.12.refs_1_, bf16[2,32,3072]{2,1,0:T(8,128)(2,1)} %pad_maximum_fusion.5.refs_2_, ...), custom_call_target="tpu_custom_call" | custom-call | flops 8000000000 | bytes 8000000 | tf_op jit(solution)/shard_map/correlate/pallas_call | solution.py:254
  150.2 6.2 %collective-permute-start.21 = (bf16[64,2048]{1,0:T(8,128)(2,1)}, bf16[64,2048]{1,0:T(8,128)(2,1)S(1)}, u32[]{:S(2)}, u32[]{:S(2)}) collective-permute-start(bf16[64,2048]{1,0:T(8,128)(2,1)} %correlate.2), channel_id=1, source_target_pairs={{2,0},{3,1},{0,2},{1,3},{6,4},{7,5},{4,6},{5,7},{10,8},{11,9},{8,1... | collective-permute-start | bytes 786440 | tf_op jit(solution)/shard_map/ppermute | solution.py:387
  156.5 21.5 %correlate.3 = f32[64,4096]{1,0:T(8,128)} custom-call(s32[3]{0:T(128)} %pad_add_fusion.place_ref, bf16[2,32,3072]{2,1,0:T(8,128)(2,1)} %copy-done.5, bf16[2,32,3072]{2,1,0:T(8,128)(2,1)} %copy-done.6, bf16[2,32,3072]{2,1,0:T(8,128)(2,1)} %copy-done.8, bf16[2,32,3072]{2,1,0:T(8,128)(2,1)} %copy-done.9, bf16[2,32,3072]{2,1,0:T(8,128)(2,1)} %copy-done.7, ...), custom_call_target="tpu_custom_call" | custom-call | flops 8000000000 | bytes 8000000 | tf_op jit(solution)/shard_map/correlate/pallas_call | solution.py:254
  (125 shorter events, 31.0 us)
Async XLA Ops:
  2.6 23.8 %collective-permute-start = (bf16[896,384]{1,0:T(8,128)(2,1)}, bf16[896,384]{1,0:T(8,128)(2,1)}, u32[]{:S(2)}, u32[]{:S(2)}) collective-permute-start(bf16[896,384]{1,0:T(8,128)(2,1)} %slice.24), channel_id=1, source_target_pairs={{0,1},{1,0},{2,3},{3,2},{4,5},{5,4},{6,7},{7,6},{8,9},{9,8},{10,11... | collective-permute-start | bytes 2064392 | tf_op jit(solution)/shard_map/ppermute | solution.py:329
  7.5 18.1 %all-to-all-start = ((s32[32,1,8]{2,1,0:T(1,128)}), s32[32,1,8]{2,1,0:T(1,128)S(1)}, u32[]{:S(2)}, u32[]{:S(2)}) async-start(s32[32,1,8]{2,1,0:T(1,128)} %bitcast.2), calls=%async_computation | async-start | bytes 32768 | tf_op jit(solution)/shard_map/all_to_all | solution.py:325
  26.4 39.9 %all-to-all-start.1 = ((bf16[32,64,384]{2,1,0:T(8,128)(2,1)}), bf16[32,64,384]{2,1,0:T(8,128)(2,1)}, u32[]{:S(2)}, u32[]{:S(2)}) async-start(bf16[32,64,384]{2,1,0:T(8,128)(2,1)} %bitcast.68), calls=%async_computation.1 | async-start | bytes 3145728 | tf_op jit(solution)/shard_map/all_to_all | solution.py:331
  69.8 13.9 %collective-permute-start.20 = (bf16[64,384]{1,0:T(8,128)(2,1)S(1)}, bf16[64,384]{1,0:T(8,128)(2,1)S(1)}, u32[]{:S(2)}, u32[]{:S(2)}) collective-permute-start(bf16[64,384]{1,0:T(8,128)(2,1)S(1)} %slice.28), channel_id=1, source_target_pairs={{2,0},{4,2},{6,4},{8,6},{10,8},{12,10},{14,12},{16,14},{18,16},{20... | collective-permute-start | bytes 147464 | tf_op jit(solution)/shard_map/ppermute | solution.py:343
  72.2 21.8 %collective-permute-start.9 = (bf16[64,3072]{1,0:T(8,128)(2,1)}, bf16[64,3072]{1,0:T(8,128)(2,1)S(1)}, u32[]{:S(2)}, u32[]{:S(2)}) collective-permute-start(bf16[64,3072]{1,0:T(8,128)(2,1)} %refine.1), channel_id=1, source_target_pairs={{0,2},{1,3},{2,0},{3,1},{4,6},{5,7},{6,4},{7,5},{8,10},{9,11},{10,... | collective-permute-start | bytes 1179656 | tf_op jit(solution)/shard_map/ppermute | solution.py:376
  75.8 10.3 %collective-permute-start.10 = (bf16[64,384]{1,0:T(8,128)(2,1)S(1)}, bf16[64,384]{1,0:T(8,128)(2,1)S(1)}, u32[]{:S(2)}, u32[]{:S(2)}) collective-permute-start(bf16[64,384]{1,0:T(8,128)(2,1)S(1)} %slice.28), channel_id=1, source_target_pairs={{1,0},{2,1},{3,2},{4,3},{5,4},{6,5},{7,6},{8,7},{9,8},{10,9},{11,1... | collective-permute-start | bytes 147464 | tf_op jit(solution)/shard_map/ppermute | solution.py:342
  77.4 18.4 %collective-permute-start.5 = (bf16[1,32,3072]{2,1,0:T(8,128)(2,1)S(1)}, bf16[1,32,3072]{2,1,0:T(8,128)(2,1)S(1)}, u32[]{:S(2)}, u32[]{:S(2)}) collective-permute-start(bf16[1,32,3072]{2,1,0:T(8,128)(2,1)S(1)} %get-tuple-element.51), channel_id=1, source_target_pairs={{0,8},{4,12},{8,0},{12,4},{16,24},{20,28},{24,16},{28,20},{1,9},{5... | collective-permute-start | bytes 589832 | tf_op jit(solution)/shard_map/ppermute | solution.py:276
  79.6 10.3 %collective-permute-start.1 = (bf16[1,32,3072]{2,1,0:T(8,128)(2,1)S(1)}, bf16[1,32,3072]{2,1,0:T(8,128)(2,1)S(1)}, u32[]{:S(2)}, u32[]{:S(2)}) collective-permute-start(bf16[1,32,3072]{2,1,0:T(8,128)(2,1)S(1)} %get-tuple-element.50), channel_id=1, source_target_pairs={{0,16},{4,20},{8,24},{12,28},{16,0},{20,4},{24,8},{28,12},{1,17},{... | collective-permute-start | bytes 589832 | tf_op jit(solution)/shard_map/ppermute | solution.py:276
  83.7 29.3 %collective-permute-start.19 = (bf16[1152,384]{1,0:T(8,128)(2,1)S(1)}, bf16[1152,384]{1,0:T(8,128)(2,1)S(1)}, u32[]{:S(2)}, u32[]{:S(2)}) collective-permute-start(bf16[1152,384]{1,0:T(8,128)(2,1)S(1)} %slice.31), channel_id=1, source_target_pairs={{0,1},{1,0},{2,3},{3,2},{4,5},{5,4},{6,7},{7,6},{8,9},{9,8},{10,11... | collective-permute-start | bytes 2654216 | tf_op jit(solution)/shard_map/ppermute | solution.py:344
  90.0 11.5 %collective-permute-start.2 = (bf16[2,32,3072]{2,1,0:T(8,128)(2,1)S(1)}, bf16[2,32,3072]{2,1,0:T(8,128)(2,1)S(1)}, u32[]{:S(2)}, u32[]{:S(2)}) collective-permute-start(bf16[2,32,3072]{2,1,0:T(8,128)(2,1)S(1)} %pad_maximum_fusion.2.refs_0_), channel_id=1, source_target_pairs={{0,8},{4,12},{8,0},{12,4},{16,24},{20,28},{24,16},{28,20},{1,9},{5... | collective-permute-start | bytes 1179656 | tf_op jit(solution)/shard_map/ppermute | solution.py:276
  92.2 4.3 %collective-permute-start.3 = (bf16[2,32,3072]{2,1,0:T(8,128)(2,1)S(1)}, bf16[2,32,3072]{2,1,0:T(8,128)(2,1)S(1)}, u32[]{:S(2)}, u32[]{:S(2)}) collective-permute-start(bf16[2,32,3072]{2,1,0:T(8,128)(2,1)S(1)} %pad_maximum_fusion.2.refs_0_), channel_id=1, source_target_pairs={{0,4},{4,0},{8,12},{12,8},{16,20},{20,16},{24,28},{28,24},{1,5},{5... | collective-permute-start | bytes 1179656 | tf_op jit(solution)/shard_map/ppermute | solution.py:276
  94.0 9.1 %collective-permute-start.11 = (bf16[1,32,3072]{2,1,0:T(8,128)(2,1)S(1)}, bf16[1,32,3072]{2,1,0:T(8,128)(2,1)S(1)}, u32[]{:S(2)}, u32[]{:S(2)}) collective-permute-start(bf16[1,32,3072]{2,1,0:T(8,128)(2,1)S(1)} %get-tuple-element.48), channel_id=1, source_target_pairs={{0,16},{4,20},{8,24},{12,28},{16,0},{20,4},{24,8},{28,12},{1,17},{... | collective-permute-start | bytes 589832 | tf_op jit(solution)/shard_map/ppermute | solution.py:276
  95.8 13.7 %collective-permute-start.6 = (bf16[2,32,3072]{2,1,0:T(8,128)(2,1)S(1)}, bf16[2,32,3072]{2,1,0:T(8,128)(2,1)S(1)}, u32[]{:S(2)}, u32[]{:S(2)}) collective-permute-start(bf16[2,32,3072]{2,1,0:T(8,128)(2,1)S(1)} %pad_maximum_fusion.3.refs_2_), channel_id=1, source_target_pairs={{0,16},{4,20},{8,24},{12,28},{16,0},{20,4},{24,8},{28,12},{1,17},{... | collective-permute-start | bytes 1179656 | tf_op jit(solution)/shard_map/ppermute | solution.py:276
  96.4 14.5 %collective-permute-start.7 = (bf16[2,32,3072]{2,1,0:T(8,128)(2,1)S(1)}, bf16[2,32,3072]{2,1,0:T(8,128)(2,1)S(1)}, u32[]{:S(2)}, u32[]{:S(2)}) collective-permute-start(bf16[2,32,3072]{2,1,0:T(8,128)(2,1)S(1)} %pad_maximum_fusion.3.refs_2_), channel_id=1, source_target_pairs={{0,4},{4,0},{8,12},{12,8},{16,20},{20,16},{24,28},{28,24},{1,5},{5... | collective-permute-start | bytes 1179656 | tf_op jit(solution)/shard_map/ppermute | solution.py:276
  101.6 7.9 %collective-permute-start.13 = (bf16[1,32,3072]{2,1,0:T(8,128)(2,1)S(1)}, bf16[1,32,3072]{2,1,0:T(8,128)(2,1)S(1)}, u32[]{:S(2)}, u32[]{:S(2)}) collective-permute-start(bf16[1,32,3072]{2,1,0:T(8,128)(2,1)S(1)} %get-tuple-element.47), channel_id=1, source_target_pairs={{0,8},{4,12},{8,0},{12,4},{16,24},{20,28},{24,16},{28,20},{1,9},{5... | collective-permute-start | bytes 589832 | tf_op jit(solution)/shard_map/ppermute | solution.py:276
  103.9 14.9 %collective-permute-start.12 = (bf16[2,32,3072]{2,1,0:T(8,128)(2,1)}, bf16[2,32,3072]{2,1,0:T(8,128)(2,1)}, u32[]{:S(2)}, u32[]{:S(2)}) collective-permute-start(bf16[2,32,3072]{2,1,0:T(8,128)(2,1)} %pad_maximum_fusion.4.refs_0_), channel_id=1, source_target_pairs={{0,8},{4,12},{8,0},{12,4},{16,24},{20,28},{24,16},{28,20},{1,9},{5... | collective-permute-start | bytes 1179656 | tf_op jit(solution)/shard_map/ppermute | solution.py:276
  109.5 7.8 %collective-permute-start.4 = (bf16[2,32,3072]{2,1,0:T(8,128)(2,1)S(1)}, bf16[2,32,3072]{2,1,0:T(8,128)(2,1)S(1)}, u32[]{:S(2)}, u32[]{:S(2)}) collective-permute-start(bf16[2,32,3072]{2,1,0:T(8,128)(2,1)S(1)} %collective-permute-done.2.refs_1_), channel_id=1, source_target_pairs={{0,4},{4,0},{8,12},{12,8},{16,20},{20,16},{24,28},{28,24},{1,5},{5... | collective-permute-start | bytes 1179656 | tf_op jit(solution)/shard_map/ppermute | solution.py:276
  109.5 7.7 %collective-permute-start.8 = (bf16[2,32,3072]{2,1,0:T(8,128)(2,1)S(1)}, bf16[2,32,3072]{2,1,0:T(8,128)(2,1)S(1)}, u32[]{:S(2)}, u32[]{:S(2)}) collective-permute-start(bf16[2,32,3072]{2,1,0:T(8,128)(2,1)S(1)} %collective-permute-done.6.refs_3_), channel_id=1, source_target_pairs={{0,4},{4,0},{8,12},{12,8},{16,20},{20,16},{24,28},{28,24},{1,5},{5... | collective-permute-start | bytes 1179656 | tf_op jit(solution)/shard_map/ppermute | solution.py:276
  111.0 17.9 %collective-permute-start.15 = (bf16[2,32,3072]{2,1,0:T(8,128)(2,1)}, bf16[2,32,3072]{2,1,0:T(8,128)(2,1)S(1)}, u32[]{:S(2)}, u32[]{:S(2)}) collective-permute-start(bf16[2,32,3072]{2,1,0:T(8,128)(2,1)} %pad_maximum_fusion.4.refs_0_), channel_id=1, source_target_pairs={{0,4},{4,0},{8,12},{12,8},{16,20},{20,16},{24,28},{28,24},{1,5},{5... | collective-permute-start | bytes 1179656 | tf_op jit(solution)/shard_map/ppermute | solution.py:276
  112.9 11.7 %collective-permute-start.14 = (bf16[2,32,3072]{2,1,0:T(8,128)(2,1)}, bf16[2,32,3072]{2,1,0:T(8,128)(2,1)}, u32[]{:S(2)}, u32[]{:S(2)}) collective-permute-start(bf16[2,32,3072]{2,1,0:T(8,128)(2,1)} %pad_maximum_fusion.5.refs_2_), channel_id=1, source_target_pairs={{0,16},{4,20},{8,24},{12,28},{16,0},{20,4},{24,8},{28,12},{1,17},{... | collective-permute-start | bytes 1179656 | tf_op jit(solution)/shard_map/ppermute | solution.py:276
  117.2 11.7 %collective-permute-start.17 = (bf16[2,32,3072]{2,1,0:T(8,128)(2,1)}, bf16[2,32,3072]{2,1,0:T(8,128)(2,1)S(1)}, u32[]{:S(2)}, u32[]{:S(2)}) collective-permute-start(bf16[2,32,3072]{2,1,0:T(8,128)(2,1)} %pad_maximum_fusion.5.refs_2_), channel_id=1, source_target_pairs={{0,4},{4,0},{8,12},{12,8},{16,20},{20,16},{24,28},{28,24},{1,5},{5... | collective-permute-start | bytes 1179656 | tf_op jit(solution)/shard_map/ppermute | solution.py:276
  118.8 10.0 %collective-permute-start.16 = (bf16[2,32,3072]{2,1,0:T(8,128)(2,1)}, bf16[2,32,3072]{2,1,0:T(8,128)(2,1)S(1)}, u32[]{:S(2)}, u32[]{:S(2)}) collective-permute-start(bf16[2,32,3072]{2,1,0:T(8,128)(2,1)} %collective-permute-done.12.refs_1_), channel_id=1, source_target_pairs={{0,4},{4,0},{8,12},{12,8},{16,20},{20,16},{24,28},{28,24},{1,5},{5... | collective-permute-start | bytes 1179656 | tf_op jit(solution)/shard_map/ppermute | solution.py:276
  124.6 4.3 %collective-permute-start.18 = (bf16[2,32,3072]{2,1,0:T(8,128)(2,1)}, bf16[2,32,3072]{2,1,0:T(8,128)(2,1)}, u32[]{:S(2)}, u32[]{:S(2)}) collective-permute-start(bf16[2,32,3072]{2,1,0:T(8,128)(2,1)} %collective-permute-done.14.refs_3_), channel_id=1, source_target_pairs={{0,4},{4,0},{8,12},{12,8},{16,20},{20,16},{24,28},{28,24},{1,5},{5... | collective-permute-start | bytes 1179656 | tf_op jit(solution)/shard_map/ppermute | solution.py:276
  150.2 27.7 %collective-permute-start.21 = (bf16[64,2048]{1,0:T(8,128)(2,1)}, bf16[64,2048]{1,0:T(8,128)(2,1)S(1)}, u32[]{:S(2)}, u32[]{:S(2)}) collective-permute-start(bf16[64,2048]{1,0:T(8,128)(2,1)} %correlate.2), channel_id=1, source_target_pairs={{2,0},{3,1},{0,2},{1,3},{6,4},{7,5},{4,6},{5,7},{10,8},{11,9},{8,1... | collective-permute-start | bytes 786440 | tf_op jit(solution)/shard_map/ppermute | solution.py:387
  (17 other events, 151.8 us)

commit v6 on v5

--- a/solution.py
+++ b/solution.py
@@ -12,12 +12,12 @@
 FOLD = 4
 ROWS = STRIDE * FOLD
 AXES = ("tm", "unit")
-VMEM_LIMIT = 56 * 1024 * 1024
+MIB = 1024 * 1024
 NT = (((1,), (1,)), ((), ()))
 
 
-def params():
-    return pltpu.CompilerParams(vmem_limit_bytes=VMEM_LIMIT)
+def params(mib):
+    return pltpu.CompilerParams(vmem_limit_bytes=mib * MIB)
 
 
 def pack_kernel(
@@ -72,7 +72,7 @@
             pltpu.VMEM((rows, chans), jnp.float32),
             pltpu.SMEM((owners,), jnp.int32),
         ],
-        compiler_params=params(),
+        compiler_params=params(24),
         cost_estimate=pl.CostEstimate(flops=10**8, bytes_accessed=4 * 10**6, transcendentals=0),
         name="pack",
     )(times, labels, base, rec)
@@ -105,7 +105,7 @@
         out_shape=jax.ShapeDtypeStruct((blocks * 16, ROWS * chans), jnp.bfloat16),
         in_specs=[vmem] * len(parts),
         out_specs=vmem,
-        compiler_params=params(),
+        compiler_params=params(14),
         cost_estimate=pl.CostEstimate(flops=2 * 10**8, bytes_accessed=4 * 10**6, transcendentals=0),
         name="fold",
     )(*parts)
@@ -148,7 +148,7 @@
         in_specs=[vmem] * 3,
         out_specs=vmem,
         scratch_shapes=[pltpu.VMEM((tpd * panel, got.shape[1]), jnp.float32)],
-        compiler_params=params(),
+        compiler_params=params(32),
         cost_estimate=pl.CostEstimate(flops=8 * 10**8, bytes_accessed=3 * 10**6, transcendentals=0),
         name="refine",
     )(key, got, old)
@@ -157,46 +157,30 @@
 def correlate_kernel(chans, tpd, scale, masks, place_ref, *refs):
     count = len(masks)
     pieces, rest = refs[:count], refs[count:]
-    mine_ref, early_ref, late_ref, out_ref, t_buf, e_buf, t_sem, e_sem, rhs, part, acc = rest
+    mine_ref, early_ref, late_ref, out_ref, t_buf, e_buf, rhs, part, acc = rest
     half_rows = pieces[0].shape[1]
     lanes = tpd * chans
-    chunks = t_sem.shape[0]
     blocks, panel, depth = t_buf.shape
     per = depth // lanes
     height = e_buf.shape[0] // 2
     keep = acc.shape[0] // 2
     shift = STRIDE * chans
     me, odd, pair = place_ref[0], place_ref[1], place_ref[2]
-
-    def spot(chunk, part_of):
-        rows = pl.ds(part_of * half_rows, half_rows)
-        if per == 1:
-            return t_buf.at[chunk, rows]
-        first = chunk % per * lanes
-        if not isinstance(chunk, int):
-            first = pl.multiple_of(first, 128)
-        return t_buf.at[chunk // per, rows, pl.ds(first, lanes)]
-
-    e_copies = []
-    low = 0
-    for n, ref in enumerate((mine_ref, early_ref, late_ref)):
-        size = ref.shape[0]
-        e_copies.append(pltpu.make_async_copy(ref, e_buf.at[low : low + size, :], e_sem.at[n]))
-        low += size
-    for copy in e_copies:
-        copy.start()
+    early = early_ref.shape[0]
+    e_buf[0:keep, :] = mine_ref[...]
+    e_buf[keep:height, :] = late_ref[0 : height - keep, :]
+    e_buf[height : height + early, :] = early_ref[...]
+    e_buf[height + early :, :] = late_ref[height - keep :, :]
     for ref, (part_of, items) in zip(pieces, masks):
+        rows = slice(part_of * half_rows, (part_of + 1) * half_rows)
         for at, mask in enumerate(items):
             chunk = jnp.bitwise_xor(me, mask)
-            pltpu.make_async_copy(ref.at[at], spot(chunk, part_of), t_sem.at[chunk, part_of]).start()
-    for copy in e_copies:
-        copy.wait()
+            if per == 1:
+                t_buf[chunk, rows, :] = ref[at]
+            else:
+                first = pl.multiple_of(chunk % per * lanes, 128)
+                t_buf[chunk // per, rows, pl.ds(first, lanes)] = ref[at]
     for a in range(blocks + 1):
-        if a < blocks:
-            for chunk in range(a * per, (a + 1) * per):
-                for part_of in range(2):
-                    sem = t_sem.at[chunk, part_of]
-                    pltpu.make_async_copy(pieces[0].at[0], spot(chunk, part_of), sem).wait()
         used = depth if a < blocks else depth // 2
         for q in range(FOLD):
             rows = slice(q * panel, (q + 1) * panel)
@@ -247,25 +231,23 @@
     masks = [(part_of, items) for _, part_of, items in gathered]
     panel = 2 * pieces[0].shape[1]
     chunks = sum(len(items) for _, items in masks) // 2
-    height = windows[0].shape[0]
-    keep = height - 16
+    keep = windows[0].shape[0]
+    height = keep + 16
     depth = ROWS * chans
-    anywhere = pl.BlockSpec(memory_space=pl.ANY)
+    vmem = pl.BlockSpec(memory_space=pltpu.VMEM)
     return pl.pallas_call(
         functools.partial(correlate_kernel, chans, tpd, scale, masks),
         out_shape=jax.ShapeDtypeStruct((panel, width), dtype),
-        in_specs=[pl.BlockSpec(memory_space=pltpu.SMEM)] + [anywhere] * (len(pieces) + 3),
-        out_specs=pl.BlockSpec(memory_space=pltpu.VMEM),
+        in_specs=[pl.BlockSpec(memory_space=pltpu.SMEM)] + [vmem] * (len(pieces) + 3),
+        out_specs=vmem,
         scratch_shapes=[
             pltpu.VMEM((chunks * tpd // ROWS, panel, depth), jnp.bfloat16),
             pltpu.VMEM((2 * height, depth), jnp.bfloat16),
-            pltpu.SemaphoreType.DMA((chunks, 2)),
-            pltpu.SemaphoreType.DMA((3,)),
             pltpu.VMEM((FOLD * panel, depth), jnp.bfloat16),
             pltpu.VMEM((2 * height, FOLD * panel), jnp.float32),
             pltpu.VMEM((2 * keep, FOLD * panel), jnp.float32),
         ],
-        compiler_params=params(),
+        compiler_params=params(30),
         cost_estimate=pl.CostEstimate(flops=8 * 10**9, bytes_accessed=8 * 10**6, transcendentals=0),
         name="correlate",
     )(place, *pieces, *windows)
@@ -325,7 +307,7 @@
     tags = lax.all_to_all(tags, AXES, split_axis=0, concat_axis=0, tiled=True)
     key = (tags[:, :, None] * tpd + jnp.arange(tpd)[None, None, :]).reshape(1, -1)
     pairs = [(i, i ^ 1) for i in range(owners)]
-    first = sub_rows * 7 // 16 // (16 * ROWS) * (16 * ROWS)
+    first = sub_rows // 4 // (16 * ROWS) * (16 * ROWS)
     early = lax.ppermute(recording[:first], "unit", pairs)
     send, key, early, before = lax.optimization_barrier((send, key, early, old_templates))
     got = lax.all_to_all(
@@ -346,7 +328,7 @@
 
     fresh = refine(key, got, old, tpd)
     early, rest, fresh = lax.optimization_barrier((early, rest, fresh))
-    mine = fold(rest, follow)
+    mine = fold(rest)
     early = fold(early)
     own = gather_panel(fresh)
     width = 2 * keep * FOLD
@@ -378,7 +360,7 @@
             chunk, mine, early = lax.optimization_barrier((chunk, mine, early))
         other = gather_panel(chunk)
         if m == 1:
-            windows = (mine, early, fold(late, jnp.where(odd == 1, head, skip)))
+            windows = (mine, early, fold(follow, late, jnp.where(odd == 1, head, skip)))
             tied = lax.optimization_barrier((part, *[v for v, _, _ in other]))
             part = tied[0]
             other = [(v, n, ms) for v, (_, n, ms) in zip(tied[1:], other)]

time: 179 us -> 167 us (0.933)
  Pallas kernels: 57.3 us -> 28 us
  local copies, waits for them, and re-layouts: 46.9 us -> 61 us
  other arithmetic: 6.46 us -> 17.2 us
  waiting for transfers between devices: 28 us -> 22.3 us
  starting transfers between devices: 38.8 us -> 36 us
    pallas_call x2, Pallas kernels: 41.8 us -> 21.6 us  [correlate(): pl.pallas_call(functools.partial(correlate_kernel, chans, tpd, scale, mas...]
    ppermute x16, waiting for transfers between devices: 15.1 us -> 4.8 us  [swap(): return lax.ppermute(value, 'tm', [(i, i ^ bit) for i in range(size)])]
    all_to_all x1, waiting for transfers between devices: 9.25 us -> 0.01 us  [body(): tags = lax.all_to_all(tags, AXES, split_axis=0, concat_axis=0, tiled=True)]
    ppermute x1, waiting for transfers between devices: 1.8 us -> 9.19 us  [body(): chunk = lax.ppermute(fresh, 'unit', ahead)]
    ppermute x1, starting transfers between devices: 6.22 us -> 0.07 us  [body(): lax.ppermute(out, 'unit', back)]
    pallas_call x3, Pallas kernels: 8.03 us -> 2.13 us  [fold(): pl.pallas_call(fold_kernel, out_shape=jax.ShapeDtypeStruct((blocks * 16,...]
    ppermute x1, waiting for transfers between devices: 0.01 us -> 4.23 us  [body(): lax.ppermute(out, 'unit', back)]
    unnamed x45 -> x61, local copies, waits for them, and re-layouts: 8.61 us -> 12.4 us
  transfers between devices with their start and end apart: 24 -> 24, of which waited for: 7 -> 7; matrix products, arithmetic and copies ran while one was open for 27% -> 42% of each run, Pallas kernels for 19% -> 10%
where the time goes in v6:
time: 167 us; the launch traced here: 166 us
  local copies, waits for them, and re-layouts  61 us (37%)
  starting transfers between devices  36 us (22%)
  Pallas kernels  28 us (17%)
  waiting for transfers between devices  22.3 us (13%)
  other arithmetic  17.2 us (10%)
    pallas_call x2, Pallas kernels, correlate(): pl.pallas_call(functools.partial(correlate_kernel, chans, tpd, scale, mas...  21.6 us
    reshape x1, local copies, waits for them, and re-layouts, body(): cube = before.reshape(panel, chans, taps)  20.6 us
    ppermute x16, starting transfers between devices, swap(): return lax.ppermute(value, 'tm', [(i, i ^ bit) for i in range(size)])  13.3 us
    unnamed x61, local copies, waits for them, and re-layouts  12.4 us
    ppermute x1, waiting for transfers between devices, body(): chunk = lax.ppermute(fresh, 'unit', ahead)  9.19 us
    transpose x1, local copies, waits for them, and re-layouts, body(): old = jnp.transpose(cube, (0, 2, 1)).reshape(panel, tpd * chans)  7.96 us
    all_to_all x1, starting transfers between devices, body(): tags = lax.all_to_all(tags, AXES, split_axis=0, concat_axis=0, tiled=True)  7.3 us
    all_to_all x1, starting transfers between devices, body(): lax.all_to_all(send.reshape(devices, CAP * tpd, chans), AXES, split_axis=...  5.6 us
  transfers between devices with their start and end apart: 24, of which 7 were waited for; matrix products, arithmetic and copies ran while one was open for 42% of the time, Pallas kernels for 10%

profile of v6, /device:TPU:0, one launch (start us, length us, event | category | flops | bytes accessed | tf_op | source)
XLA Modules:
  0.0 165.9 jit_solution(7568195770917099738)
XLA Ops:
  2.4 7.3 %all-to-all-start = ((s32[32,1,8]{2,1,0:T(1,128)}), s32[32,1,8]{2,1,0:T(1,128)S(1)}, u32[]{:S(2)}, u32[]{:S(2)}) async-start(s32[32,1,8]{2,1,0:T(1,128)} %bitcast.2), calls=%async_computation | async-start | bytes 32768 | tf_op jit(solution)/shard_map/all_to_all | solution.py:307
  10.8 1.8 %collective-permute-start = (bf16[512,384]{1,0:T(8,128)(2,1)S(1)}, bf16[512,384]{1,0:T(8,128)(2,1)S(1)}, u32[]{:S(2)}, u32[]{:S(2)}) collective-permute-start(bf16[512,384]{1,0:T(8,128)(2,1)S(1)} %slice.24), channel_id=1, source_target_pairs={{0,1},{1,0},{2,3},{3,2},{4,5},{5,4},{6,7},{7,6},{8,9},{9,8},{10,11... | collective-permute-start | bytes 1179656 | tf_op jit(solution)/shard_map/ppermute | solution.py:311
  15.4 3.0 %pack.1 = bf16[2048,384]{1,0:T(8,128)(2,1)} custom-call(s32[32]{0:T(128)S(1)} %copy-done.21, s32[32]{0:T(128)S(1)} %copy-done.20, s32[1]{0:T(128)} %bitcast.1.base_ref, bf16[2048,384]{1,0:T(8,128)(2,1)S(1)} %copy-done), custom_call_target="tpu_custom_call" | custom-call | flops 100000000 | bytes 4000000 | tf_op jit(solution)/shard_map/pack/pallas_call | solution.py:66
  18.6 3.6 %collective-permute-done.refs_0_ = bf16[512,384]{1,0:T(8,128)(2,1)S(1)} collective-permute-done((bf16[512,384]{1,0:T(8,128)(2,1)S(1)}, bf16[512,384]{1,0:T(8,128)(2,1)S(1)}, u32[]{:S(2)}, u32[]{:S(2)}) %collective-permute-start) | collective-permute-done | bytes 393248 | tf_op jit(solution)/shard_map/ppermute | solution.py:311
  23.0 5.6 %all-to-all-start.1 = ((bf16[32,64,384]{2,1,0:T(8,128)(2,1)}), bf16[32,64,384]{2,1,0:T(8,128)(2,1)S(1)}, u32[]{:S(2)}, u32[]{:S(2)}) async-start(bf16[32,64,384]{2,1,0:T(8,128)(2,1)} %bitcast.4), calls=%async_computation.1 | async-start | bytes 3145728 | tf_op jit(solution)/shard_map/all_to_all | solution.py:313
  31.2 20.6 %reshape.121 = bf16[64,384,61]{2,1,0:T(8,128)(2,1)} reshape(bf16[64,23424]{1,0:T(8,128)(2,1)} %param.11) | data formatting | bytes 5996544 | tf_op jit(solution)/shard_map/reshape | solution.py:317
  51.8 8.0 %dynamic-slice_bitcast_fusion = bf16[64,8,384]{1,2,0:T(8,128)(2,1)} fusion(s32[]{:T(128)S(6)} %select_n.78, bf16[64,384,61]{2,1,0:T(8,128)(2,1)} %reshape.121), kind=kLoop, calls=%fused_computation.4 | loop fusion | bytes 3391492 | tf_op jit(solution)/shard_map/transpose | solution.py:320
  59.7 5.2 %copy.21 = bf16[8,8,8,384]{3,1,2,0:T(8,128)(2,1)S(1)} copy(bf16[8,8,8,384]{2,3,1,0:T(8,128)(2,1)} %bitcast.75) | data formatting | bytes 786432
  70.3 2.4 %collective-permute-start.9 = (bf16[64,3072]{1,0:T(8,128)(2,1)}, bf16[64,3072]{1,0:T(8,128)(2,1)S(1)}, u32[]{:S(2)}, u32[]{:S(2)}) collective-permute-start(bf16[64,3072]{1,0:T(8,128)(2,1)} %copy-done.18), channel_id=1, source_target_pairs={{0,2},{1,3},{2,0},{3,1},{4,6},{5,7},{6,4},{7,5},{8,10},{9,11},{10,... | collective-permute-start | bytes 1179656 | tf_op jit(solution)/shard_map/ppermute | solution.py:358
  82.5 9.2 %collective-permute-done.9 = bf16[64,3072]{1,0:T(8,128)(2,1)S(1)} collective-permute-done((bf16[64,3072]{1,0:T(8,128)(2,1)}, bf16[64,3072]{1,0:T(8,128)(2,1)S(1)}, u32[]{:S(2)}, u32[]{:S(2)}) %collective-permute-start.9) | collective-permute-done | bytes 393248 | tf_op jit(solution)/shard_map/ppermute | solution.py:358
  97.8 2.7 %collective-permute-start.19 = (bf16[1536,384]{1,0:T(8,128)(2,1)}, bf16[1536,384]{1,0:T(8,128)(2,1)S(1)}, u32[]{:S(2)}, u32[]{:S(2)}) collective-permute-start(bf16[1536,384]{1,0:T(8,128)(2,1)} %slice.31), channel_id=1, source_target_pairs={{0,1},{1,0},{2,3},{3,2},{4,5},{5,4},{6,7},{7,6},{8,9},{9,8},{10,11... | collective-permute-start | bytes 3538952 | tf_op jit(solution)/shard_map/ppermute | solution.py:326
  103.6 3.3 %collective-permute-done.6.refs_3_ = bf16[2,32,3072]{2,1,0:T(8,128)(2,1)S(1)} collective-permute-done((bf16[2,32,3072]{2,1,0:T(8,128)(2,1)S(1)}, bf16[2,32,3072]{2,1,0:T(8,128)(2,1)S(1)}, u32[]{:S(2)}, u32[]{:S(2)}) %collective-permute-start.6) | collective-permute-done | bytes 393248 | tf_op jit(solution)/shard_map/ppermute | solution.py:258
  110.8 3.0 %collective-permute-start.13 = (bf16[2,32,3072]{2,1,0:T(8,128)(2,1)}, bf16[2,32,3072]{2,1,0:T(8,128)(2,1)}, u32[]{:S(2)}, u32[]{:S(2)}) collective-permute-start(bf16[2,32,3072]{2,1,0:T(8,128)(2,1)} %pad_maximum_fusion.5.refs_2_), channel_id=1, source_target_pairs={{0,16},{4,20},{8,24},{12,28},{16,0},{20,4},{24,8},{28,12},{1,17},{... | collective-permute-start | bytes 1179656 | tf_op jit(solution)/shard_map/ppermute | solution.py:258
  116.5 2.5 %gather_fusion.3 = bf16[8,32,8,48]{3,2,1,0:T(8,128)(2,1)} fusion(bf16[8,32,8,48]{3,2,1,0:T(8,128)(2,1)} %pad_maximum_fusion.1, s32[1024]{0:T(1024)S(1)} %pad_clamp_fusion), kind=kCustom, calls=%fused_computation.1.clone | custom fusion | bytes 393248 | tf_op jit(solution)/shard_map/jit(_take)/gather | solution.py:349
  118.9 2.0 %broadcast_select_fusion = bf16[8,32,8,48]{3,2,1,0:T(8,128)(2,1)} fusion(bf16[8,32,8,48]{3,2,1,0:T(8,128)(2,1)} %gather_fusion.3, pred[8]{0:T(512)(128)(4,1)} %get-tuple-element.57), kind=kLoop, calls=%fused_computation.9 | loop fusion | flops 98304 | bytes 393224 | tf_op jit(solution)/shard_map/jit(_take)/select_n | solution.py:349
  120.9 2.0 %pad_maximum_fusion = bf16[8,32,8,48]{3,2,1,0:T(8,128)(2,1)} fusion(bf16[2,32,8,48]{3,2,1,0:T(8,128)(2,1)} %get-tuple-element.64, bf16[2,32,8,48]{3,2,1,0:T(8,128)(2,1)} %get-tuple-element.65, bf16[2,32,8,48]{3,2,1,0:T(8,128)(2,1)} %get-tuple-element.66, bf16[2,32,8,48]{3,2,1,0:T(8,128)(2,1)} %get-tuple-element.60), kind=kLoop, calls=%fused_computation.6 | loop fusion | flops 294912 | bytes 393216 | tf_op jit(solution)/shard_map/concatenate | solution.py:347
  122.9 2.4 %gather_fusion.2 = bf16[8,32,8,48]{3,2,1,0:T(8,128)(2,1)} fusion(bf16[8,32,8,48]{3,2,1,0:T(8,128)(2,1)} %pad_maximum_fusion, s32[1024]{0:T(1024)S(1)} %pad_clamp_fusion.1), kind=kCustom, calls=%fused_computation.clone | custom fusion | bytes 393248 | tf_op jit(solution)/shard_map/jit(_take)/gather | solution.py:349
  127.1 2.2 %maximum_bitcast_fusion = bf16[64,48,8,8]{1,3,0,2:T(8,128)(2,1)} fusion(bf16[8,32,8,48]{3,2,1,0:T(8,128)(2,1)} %broadcast_select_fusion, bf16[8,32,8,48]{3,2,1,0:T(8,128)(2,1)S(1)} %broadcast_select_fusion.1), kind=kLoop, calls=%fused_computation.5 | loop fusion | flops 196608 | bytes 786432 | tf_op jit(solution)/shard_map/transpose | solution.py:351
  129.3 3.3 %copy.18 = bf16[64,48,8,8]{0,3,2,1:T(8,128)(2,1)} copy(bf16[64,48,8,8]{1,3,0,2:T(8,128)(2,1)} %maximum_bitcast_fusion) | data formatting | bytes 786432 | tf_op jit(solution)/shard_map/transpose | solution.py:351
  132.6 2.2 %reshape.169 = bf16[64,2928]{0,1:T(8,128)(2,1)} reshape(bf16[64,48,61]{0,2,1:T(8,128)(2,1)} %bitcast.76) | data formatting | bytes 749568 | tf_op jit(solution)/shard_map/reshape | solution.py:352
  134.8 2.1 %copy.20 = bf16[64,2928]{1,0:T(8,128)(2,1)} copy(bf16[64,2928]{0,1:T(8,128)(2,1)} %reshape.169) | data formatting | bytes 749568 | tf_op jit(solution)/shard_map/reshape | solution.py:352
  139.1 10.7 %correlate.2 = bf16[64,2048]{1,0:T(8,128)(2,1)S(1)} custom-call(s32[3]{0:T(128)S(1)} %pad_add_fusion.2.place_ref, bf16[2,32,3072]{2,1,0:T(8,128)(2,1)} %pad_maximum_fusion.4.refs_0_, bf16[2,32,3072]{2,1,0:T(8,128)(2,1)} %collective-permute-done.11.refs_1_, bf16[2,32,3072]{2,1,0:T(8,128)(2,1)} %pad_maximum_fusion.5.refs_2_, ...), custom_call_target="tpu_custom_call" | custom-call | flops 8000000000 | bytes 8000000 | tf_op jit(solution)/shard_map/correlate/pallas_call | solution.py:238
  150.0 10.9 %correlate.3 = f32[64,4096]{1,0:T(8,128)} custom-call(s32[3]{0:T(128)S(1)} %pad_add_fusion.place_ref, bf16[2,32,3072]{2,1,0:T(8,128)(2,1)S(1)} %copy-done.5, bf16[2,32,3072]{2,1,0:T(8,128)(2,1)S(1)} %copy-done.7, bf16[2,32,3072]{2,1,0:T(8,128)(2,1)S(1)} %copy-done.11, bf16[2,32,3072]{2,1,0:T(8,128)(2,1)S(1)} %collective-permute-done.6.refs_3_, ...), custom_call_target="tpu_custom_call" | custom-call | flops 8000000000 | bytes 8000000 | tf_op jit(solution)/shard_map/correlate/pallas_call | solution.py:238
  160.9 4.2 %collective-permute-done.21 = bf16[64,2048]{1,0:T(8,128)(2,1)S(1)} collective-permute-done((bf16[64,2048]{1,0:T(8,128)(2,1)S(1)}, bf16[64,2048]{1,0:T(8,128)(2,1)S(1)}, u32[]{:S(2)}, u32[]{:S(2)}) %collective-permute-start.21) | collective-permute-done | bytes 262176 | tf_op jit(solution)/shard_map/ppermute | solution.py:369
  (141 shorter events, 44.5 us)
Async XLA Ops:
  2.4 15.9 %all-to-all-start = ((s32[32,1,8]{2,1,0:T(1,128)}), s32[32,1,8]{2,1,0:T(1,128)S(1)}, u32[]{:S(2)}, u32[]{:S(2)}) async-start(s32[32,1,8]{2,1,0:T(1,128)} %bitcast.2), calls=%async_computation | async-start | bytes 32768 | tf_op jit(solution)/shard_map/all_to_all | solution.py:307
  10.8 11.5 %collective-permute-start = (bf16[512,384]{1,0:T(8,128)(2,1)S(1)}, bf16[512,384]{1,0:T(8,128)(2,1)S(1)}, u32[]{:S(2)}, u32[]{:S(2)}) collective-permute-start(bf16[512,384]{1,0:T(8,128)(2,1)S(1)} %slice.24), channel_id=1, source_target_pairs={{0,1},{1,0},{2,3},{3,2},{4,5},{5,4},{6,7},{7,6},{8,9},{9,8},{10,11... | collective-permute-start | bytes 1179656 | tf_op jit(solution)/shard_map/ppermute | solution.py:311
  23.0 41.9 %all-to-all-start.1 = ((bf16[32,64,384]{2,1,0:T(8,128)(2,1)}), bf16[32,64,384]{2,1,0:T(8,128)(2,1)S(1)}, u32[]{:S(2)}, u32[]{:S(2)}) async-start(bf16[32,64,384]{2,1,0:T(8,128)(2,1)} %bitcast.4), calls=%async_computation.1 | async-start | bytes 3145728 | tf_op jit(solution)/shard_map/all_to_all | solution.py:313
  67.8 10.5 %collective-permute-start.1 = (bf16[1,32,3072]{2,1,0:T(8,128)(2,1)}, bf16[1,32,3072]{2,1,0:T(8,128)(2,1)}, u32[]{:S(2)}, u32[]{:S(2)}) collective-permute-start(bf16[1,32,3072]{2,1,0:T(8,128)(2,1)} %get-tuple-element.50), channel_id=1, source_target_pairs={{0,16},{4,20},{8,24},{12,28},{16,0},{20,4},{24,8},{28,12},{1,17},{... | collective-permute-start | bytes 589832 | tf_op jit(solution)/shard_map/ppermute | solution.py:258
  70.3 21.4 %collective-permute-start.9 = (bf16[64,3072]{1,0:T(8,128)(2,1)}, bf16[64,3072]{1,0:T(8,128)(2,1)S(1)}, u32[]{:S(2)}, u32[]{:S(2)}) collective-permute-start(bf16[64,3072]{1,0:T(8,128)(2,1)} %copy-done.18), channel_id=1, source_target_pairs={{0,2},{1,3},{2,0},{3,1},{4,6},{5,7},{6,4},{7,5},{8,10},{9,11},{10,... | collective-permute-start | bytes 1179656 | tf_op jit(solution)/shard_map/ppermute | solution.py:358
  74.5 6.6 %collective-permute-start.5 = (bf16[1,32,3072]{2,1,0:T(8,128)(2,1)}, bf16[1,32,3072]{2,1,0:T(8,128)(2,1)S(1)}, u32[]{:S(2)}, u32[]{:S(2)}) collective-permute-start(bf16[1,32,3072]{2,1,0:T(8,128)(2,1)} %get-tuple-element.51), channel_id=1, source_target_pairs={{0,8},{4,12},{8,0},{12,4},{16,24},{20,28},{24,16},{28,20},{1,9},{5... | collective-permute-start | bytes 589832 | tf_op jit(solution)/shard_map/ppermute | solution.py:258
  76.0 16.6 %collective-permute-start.20 = (bf16[64,384]{1,0:T(8,128)(2,1)}, bf16[64,384]{1,0:T(8,128)(2,1)S(1)}, u32[]{:S(2)}, u32[]{:S(2)}) collective-permute-start(bf16[64,384]{1,0:T(8,128)(2,1)} %slice.30), channel_id=1, source_target_pairs={{2,0},{4,2},{6,4},{8,6},{10,8},{12,10},{14,12},{16,14},{18,16},{20... | collective-permute-start | bytes 147464 | tf_op jit(solution)/shard_map/ppermute | solution.py:325
  79.4 21.2 %collective-permute-start.2 = (bf16[2,32,3072]{2,1,0:T(8,128)(2,1)S(1)}, bf16[2,32,3072]{2,1,0:T(8,128)(2,1)S(1)}, u32[]{:S(2)}, u32[]{:S(2)}) collective-permute-start(bf16[2,32,3072]{2,1,0:T(8,128)(2,1)S(1)} %pad_maximum_fusion.2.refs_0_), channel_id=1, source_target_pairs={{0,8},{4,12},{8,0},{12,4},{16,24},{20,28},{24,16},{28,20},{1,9},{5... | collective-permute-start | bytes 1179656 | tf_op jit(solution)/shard_map/ppermute | solution.py:258
  81.0 16.8 %collective-permute-start.3 = (bf16[2,32,3072]{2,1,0:T(8,128)(2,1)S(1)}, bf16[2,32,3072]{2,1,0:T(8,128)(2,1)S(1)}, u32[]{:S(2)}, u32[]{:S(2)}) collective-permute-start(bf16[2,32,3072]{2,1,0:T(8,128)(2,1)S(1)} %pad_maximum_fusion.2.refs_0_), channel_id=1, source_target_pairs={{0,4},{4,0},{8,12},{12,8},{16,20},{20,16},{24,28},{28,24},{1,5},{5... | collective-permute-start | bytes 1179656 | tf_op jit(solution)/shard_map/ppermute | solution.py:258
  82.1 14.2 %collective-permute-start.7 = (bf16[2,32,3072]{2,1,0:T(8,128)(2,1)S(1)}, bf16[2,32,3072]{2,1,0:T(8,128)(2,1)S(1)}, u32[]{:S(2)}, u32[]{:S(2)}) collective-permute-start(bf16[2,32,3072]{2,1,0:T(8,128)(2,1)S(1)} %pad_maximum_fusion.3.refs_2_), channel_id=1, source_target_pairs={{0,4},{4,0},{8,12},{12,8},{16,20},{20,16},{24,28},{28,24},{1,5},{5... | collective-permute-start | bytes 1179656 | tf_op jit(solution)/shard_map/ppermute | solution.py:258
  91.8 10.3 %collective-permute-start.10 = (bf16[1,32,3072]{2,1,0:T(8,128)(2,1)S(1)}, bf16[1,32,3072]{2,1,0:T(8,128)(2,1)S(1)}, u32[]{:S(2)}, u32[]{:S(2)}) collective-permute-start(bf16[1,32,3072]{2,1,0:T(8,128)(2,1)S(1)} %get-tuple-element.48), channel_id=1, source_target_pairs={{0,16},{4,20},{8,24},{12,28},{16,0},{20,4},{24,8},{28,12},{1,17},{... | collective-permute-start | bytes 589832 | tf_op jit(solution)/shard_map/ppermute | solution.py:258
  93.3 13.6 %collective-permute-start.6 = (bf16[2,32,3072]{2,1,0:T(8,128)(2,1)S(1)}, bf16[2,32,3072]{2,1,0:T(8,128)(2,1)S(1)}, u32[]{:S(2)}, u32[]{:S(2)}) collective-permute-start(bf16[2,32,3072]{2,1,0:T(8,128)(2,1)S(1)} %pad_maximum_fusion.3.refs_2_), channel_id=1, source_target_pairs={{0,16},{4,20},{8,24},{12,28},{16,0},{20,4},{24,8},{28,12},{1,17},{... | collective-permute-start | bytes 1179656 | tf_op jit(solution)/shard_map/ppermute | solution.py:258
  96.3 29.1 %collective-permute-start.18 = (bf16[64,384]{1,0:T(8,128)(2,1)}, bf16[64,384]{1,0:T(8,128)(2,1)}, u32[]{:S(2)}, u32[]{:S(2)}) collective-permute-start(bf16[64,384]{1,0:T(8,128)(2,1)} %slice.30), channel_id=1, source_target_pairs={{1,0},{2,1},{3,2},{4,3},{5,4},{6,5},{7,6},{8,7},{9,8},{10,9},{11,1... | collective-permute-start | bytes 147464 | tf_op jit(solution)/shard_map/ppermute | solution.py:324
  97.8 39.1 %collective-permute-start.19 = (bf16[1536,384]{1,0:T(8,128)(2,1)}, bf16[1536,384]{1,0:T(8,128)(2,1)S(1)}, u32[]{:S(2)}, u32[]{:S(2)}) collective-permute-start(bf16[1536,384]{1,0:T(8,128)(2,1)} %slice.31), channel_id=1, source_target_pairs={{0,1},{1,0},{2,3},{3,2},{4,5},{5,4},{6,7},{7,6},{8,9},{9,8},{10,11... | collective-permute-start | bytes 3538952 | tf_op jit(solution)/shard_map/ppermute | solution.py:326
  100.6 7.6 %collective-permute-start.12 = (bf16[1,32,3072]{2,1,0:T(8,128)(2,1)S(1)}, bf16[1,32,3072]{2,1,0:T(8,128)(2,1)S(1)}, u32[]{:S(2)}, u32[]{:S(2)}) collective-permute-start(bf16[1,32,3072]{2,1,0:T(8,128)(2,1)S(1)} %get-tuple-element.47), channel_id=1, source_target_pairs={{0,8},{4,12},{8,0},{12,4},{16,24},{20,28},{24,16},{28,20},{1,9},{5... | collective-permute-start | bytes 589832 | tf_op jit(solution)/shard_map/ppermute | solution.py:258
  102.9 22.5 %collective-permute-start.11 = (bf16[2,32,3072]{2,1,0:T(8,128)(2,1)}, bf16[2,32,3072]{2,1,0:T(8,128)(2,1)}, u32[]{:S(2)}, u32[]{:S(2)}) collective-permute-start(bf16[2,32,3072]{2,1,0:T(8,128)(2,1)} %pad_maximum_fusion.4.refs_0_), channel_id=1, source_target_pairs={{0,8},{4,12},{8,0},{12,4},{16,24},{20,28},{24,16},{28,20},{1,9},{5... | collective-permute-start | bytes 1179656 | tf_op jit(solution)/shard_map/ppermute | solution.py:258
  106.9 3.9 %collective-permute-start.4 = (bf16[2,32,3072]{2,1,0:T(8,128)(2,1)S(1)}, bf16[2,32,3072]{2,1,0:T(8,128)(2,1)S(1)}, u32[]{:S(2)}, u32[]{:S(2)}) collective-permute-start(bf16[2,32,3072]{2,1,0:T(8,128)(2,1)S(1)} %collective-permute-done.2.refs_1_), channel_id=1, source_target_pairs={{0,4},{4,0},{8,12},{12,8},{16,20},{20,16},{24,28},{28,24},{1,5},{5... | collective-permute-start | bytes 1179656 | tf_op jit(solution)/shard_map/ppermute | solution.py:258
  108.3 2.4 %collective-permute-start.8 = (bf16[2,32,3072]{2,1,0:T(8,128)(2,1)S(1)}, bf16[2,32,3072]{2,1,0:T(8,128)(2,1)S(1)}, u32[]{:S(2)}, u32[]{:S(2)}) collective-permute-start(bf16[2,32,3072]{2,1,0:T(8,128)(2,1)S(1)} %collective-permute-done.6.refs_3_), channel_id=1, source_target_pairs={{0,4},{4,0},{8,12},{12,8},{16,20},{20,16},{24,28},{28,24},{1,5},{5... | collective-permute-start | bytes 1179656 | tf_op jit(solution)/shard_map/ppermute | solution.py:258
  110.6 28.5 %collective-permute-start.14 = (bf16[2,32,3072]{2,1,0:T(8,128)(2,1)}, bf16[2,32,3072]{2,1,0:T(8,128)(2,1)}, u32[]{:S(2)}, u32[]{:S(2)}) collective-permute-start(bf16[2,32,3072]{2,1,0:T(8,128)(2,1)} %pad_maximum_fusion.4.refs_0_), channel_id=1, source_target_pairs={{0,4},{4,0},{8,12},{12,8},{16,20},{20,16},{24,28},{28,24},{1,5},{5... | collective-permute-start | bytes 1179656 | tf_op jit(solution)/shard_map/ppermute | solution.py:258
  110.8 15.1 %collective-permute-start.13 = (bf16[2,32,3072]{2,1,0:T(8,128)(2,1)}, bf16[2,32,3072]{2,1,0:T(8,128)(2,1)}, u32[]{:S(2)}, u32[]{:S(2)}) collective-permute-start(bf16[2,32,3072]{2,1,0:T(8,128)(2,1)} %pad_maximum_fusion.5.refs_2_), channel_id=1, source_target_pairs={{0,16},{4,20},{8,24},{12,28},{16,0},{20,4},{24,8},{28,12},{1,17},{... | collective-permute-start | bytes 1179656 | tf_op jit(solution)/shard_map/ppermute | solution.py:258
  125.3 13.8 %collective-permute-start.16 = (bf16[2,32,3072]{2,1,0:T(8,128)(2,1)}, bf16[2,32,3072]{2,1,0:T(8,128)(2,1)}, u32[]{:S(2)}, u32[]{:S(2)}) collective-permute-start(bf16[2,32,3072]{2,1,0:T(8,128)(2,1)} %pad_maximum_fusion.5.refs_2_), channel_id=1, source_target_pairs={{0,4},{4,0},{8,12},{12,8},{16,20},{20,16},{24,28},{28,24},{1,5},{5... | collective-permute-start | bytes 1179656 | tf_op jit(solution)/shard_map/ppermute | solution.py:258
  125.3 13.8 %collective-permute-start.15 = (bf16[2,32,3072]{2,1,0:T(8,128)(2,1)}, bf16[2,32,3072]{2,1,0:T(8,128)(2,1)}, u32[]{:S(2)}, u32[]{:S(2)}) collective-permute-start(bf16[2,32,3072]{2,1,0:T(8,128)(2,1)} %collective-permute-done.11.refs_1_), channel_id=1, source_target_pairs={{0,4},{4,0},{8,12},{12,8},{16,20},{20,16},{24,28},{28,24},{1,5},{5... | collective-permute-start | bytes 1179656 | tf_op jit(solution)/shard_map/ppermute | solution.py:258
  125.8 13.3 %collective-permute-start.17 = (bf16[2,32,3072]{2,1,0:T(8,128)(2,1)}, bf16[2,32,3072]{2,1,0:T(8,128)(2,1)}, u32[]{:S(2)}, u32[]{:S(2)}) collective-permute-start(bf16[2,32,3072]{2,1,0:T(8,128)(2,1)} %collective-permute-done.13.refs_3_), channel_id=1, source_target_pairs={{0,4},{4,0},{8,12},{12,8},{16,20},{20,16},{24,28},{28,24},{1,5},{5... | collective-permute-start | bytes 1179656 | tf_op jit(solution)/shard_map/ppermute | solution.py:258
  149.9 15.2 %collective-permute-start.21 = (bf16[64,2048]{1,0:T(8,128)(2,1)S(1)}, bf16[64,2048]{1,0:T(8,128)(2,1)S(1)}, u32[]{:S(2)}, u32[]{:S(2)}) collective-permute-start(bf16[64,2048]{1,0:T(8,128)(2,1)S(1)} %correlate.2), channel_id=1, source_target_pairs={{2,0},{3,1},{0,2},{1,3},{6,4},{7,5},{4,6},{5,7},{10,8},{11,9},{8,1... | collective-permute-start | bytes 786440 | tf_op jit(solution)/shard_map/ppermute | solution.py:369
  (25 other events, 176.7 us)

commit v7 on v6

--- a/solution.py
+++ b/solution.py
@@ -154,10 +154,11 @@
     )(key, got, old)
 
 
-def correlate_kernel(chans, tpd, scale, masks, place_ref, *refs):
+def correlate_kernel(chans, tpd, scale, masks, share, place_ref, *refs):
     count = len(masks)
     pieces, rest = refs[:count], refs[count:]
-    mine_ref, early_ref, late_ref, out_ref, t_buf, e_buf, rhs, part, acc = rest
+    mine_ref, early_ref, late_ref, out_ref = rest[:4]
+    t_buf, e_buf, rhs, part, acc = rest[-5:]
     half_rows = pieces[0].shape[1]
     lanes = tpd * chans
     blocks, panel, depth = t_buf.shape
@@ -180,6 +181,17 @@
             else:
                 first = pl.multiple_of(chunk % per * lanes, 128)
                 t_buf[chunk // per, rows, pl.ds(first, lanes)] = ref[at]
+    if share:
+        pick_ref = rest[4]
+        wide = pick_ref.shape[2]
+        channel = lax.broadcasted_iota(jnp.int32, (chans, wide), 0)
+        lane = lax.broadcasted_iota(jnp.int32, (chans, wide), 1)
+        pick = ((channel == me * share + lane) & (lane < share)).astype(jnp.bfloat16)
+        for b in range(blocks):
+            for r in range(ROWS):
+                taken = t_buf[b, :, r * chans : (r + 1) * chans]
+                taken = jnp.dot(taken, pick, preferred_element_type=jnp.float32)
+                pick_ref[b * ROWS + r] = taken.astype(jnp.bfloat16)
     for a in range(blocks + 1):
         used = depth if a < blocks else depth // 2
         for q in range(FOLD):
@@ -226,7 +238,7 @@
             out_ref[:, pl.ds(at, FOLD * width)] = found.astype(out_ref.dtype)
 
 
-def correlate(place, gathered, windows, chans, tpd, scale, width, dtype):
+def correlate(place, gathered, windows, chans, tpd, scale, width, dtype, share=0):
     pieces = [value for value, _, _ in gathered]
     masks = [(part_of, items) for _, part_of, items in gathered]
     panel = 2 * pieces[0].shape[1]
@@ -235,11 +247,15 @@
     height = keep + 16
     depth = ROWS * chans
     vmem = pl.BlockSpec(memory_space=pltpu.VMEM)
+    outs = [
+        jax.ShapeDtypeStruct((panel, width), dtype),
+        jax.ShapeDtypeStruct((chunks * tpd, panel, -(-share // 128) * 128), jnp.bfloat16),
+    ]
     return pl.pallas_call(
-        functools.partial(correlate_kernel, chans, tpd, scale, masks),
-        out_shape=jax.ShapeDtypeStruct((panel, width), dtype),
+        functools.partial(correlate_kernel, chans, tpd, scale, masks, share),
+        out_shape=outs if share else outs[0],
         in_specs=[pl.BlockSpec(memory_space=pltpu.SMEM)] + [vmem] * (len(pieces) + 3),
-        out_specs=vmem,
+        out_specs=[vmem] * 2 if share else vmem,
         scratch_shapes=[
             pltpu.VMEM((chunks * tpd // ROWS, panel, depth), jnp.bfloat16),
             pltpu.VMEM((2 * height, depth), jnp.bfloat16),
@@ -258,7 +274,7 @@
     return lax.ppermute(value, "tm", [(i, i ^ bit) for i in range(size)])
 
 
-def gather_panel(value):
+def gather_panel(value, beside=None):
     bits = []
     while 2 << len(bits) < lax.axis_size("tm"):
         bits.append(2 << len(bits))
@@ -271,7 +287,10 @@
             items = [m for _, ms in parts for m in ms]
             parts = [(held, items), (swap(held, bit), [m ^ bit for m in items])]
         out += [(v, part_of, ms) for v, ms in parts]
-    return out + [(swap(v, 1), part_of, [m ^ 1 for m in ms]) for v, part_of, ms in out]
+    if beside is not None:
+        beside, *tied = lax.optimization_barrier((beside, *[v for v, _, _ in out]))
+        out = [(v, n, ms) for v, (_, n, ms) in zip(tied, out)]
+    return beside, out + [(swap(v, 1), part_of, [m ^ 1 for m in ms]) for v, part_of, ms in out]
 
 
 def body(recording, spike_times, unit_labels, old_templates):
@@ -306,10 +325,7 @@
     tags = tags.reshape(devices, CAP)
     tags = lax.all_to_all(tags, AXES, split_axis=0, concat_axis=0, tiled=True)
     key = (tags[:, :, None] * tpd + jnp.arange(tpd)[None, None, :]).reshape(1, -1)
-    pairs = [(i, i ^ 1) for i in range(owners)]
-    first = sub_rows // 4 // (16 * ROWS) * (16 * ROWS)
-    early = lax.ppermute(recording[:first], "unit", pairs)
-    send, key, early, before = lax.optimization_barrier((send, key, early, old_templates))
+    send, key, before = lax.optimization_barrier((send, key, old_templates))
     got = lax.all_to_all(
         send.reshape(devices, CAP * tpd, chans), AXES, split_axis=0, concat_axis=0, tiled=True
     ).reshape(devices * CAP * tpd, chans)
@@ -323,33 +339,17 @@
     head = rest[:padded]
     follow = lax.ppermute(head, AXES, [(i, i - 1) for i in range(1, devices)])
     skip = lax.ppermute(head, AXES, [(i, i - 2) for i in range(2, devices, 2)])
+    pairs = [(i, i ^ 1) for i in range(owners)]
+    first = sub_rows * 5 // 16 // (16 * ROWS) * (16 * ROWS)
+    early = lax.ppermute(rest[:first], "unit", pairs)
     late = lax.ppermute(rest[first:], "unit", pairs)
     odd = unit_pos % 2
 
     fresh = refine(key, got, old, tpd)
-    early, rest, fresh = lax.optimization_barrier((early, rest, fresh))
+    rest, fresh = lax.optimization_barrier((rest, fresh))
     mine = fold(rest)
-    early = fold(early)
-    own = gather_panel(fresh)
+    _, own = gather_panel(fresh)
     width = 2 * keep * FOLD
-
-    share = chans // tm_count
-    order = []
-    pieces = [[], []]
-    for value, part_of, items in own:
-        value = value.reshape(len(items), panel // 2, tpd, chans)
-        pieces[part_of].append(lax.dynamic_slice_in_dim(value, tm_pos * share, share, 3))
-        order += items if part_of == 0 else []
-    order_b = [m for _, part_of, items in own if part_of == 1 for m in items]
-    part = []
-    for found, masks in ((pieces[0], order), (pieces[1], order_b)):
-        spots = jnp.array([masks.index(m) for m in range(tm_count)])
-        stacked = jnp.concatenate(found, axis=0)
-        picks = spots[jnp.bitwise_xor(jnp.arange(tm_count), tm_pos)]
-        part.append(jnp.take(stacked, picks, axis=0))
-    part = jnp.concatenate(part, axis=1)
-    part = jnp.transpose(part, (1, 3, 0, 2)).reshape(panel, share, padded)[:, :, :taps]
-    part = part.reshape(panel, share * taps)
 
     found = []
     for m in range(1, owners // 2):
@@ -358,22 +358,24 @@
         chunk = lax.ppermute(fresh, "unit", ahead)
         if m == 1:
             chunk, mine, early = lax.optimization_barrier((chunk, mine, early))
-        other = gather_panel(chunk)
-        if m == 1:
-            windows = (mine, early, fold(follow, late, jnp.where(odd == 1, head, skip)))
-            tied = lax.optimization_barrier((part, *[v for v, _, _ in other]))
-            part = tied[0]
-            other = [(v, n, ms) for v, (_, n, ms) in zip(tied[1:], other)]
+            late, other = gather_panel(chunk, late)
+            windows = (mine, fold(early), fold(follow, late, jnp.where(odd == 1, head, skip)))
+        else:
+            _, other = gather_panel(chunk)
         place = jnp.stack([tm_pos, odd, 0 * odd]).astype(jnp.int32)
         out = correlate(place, other, windows, chans, tpd, scale, width, jnp.bfloat16)
         found.append((lax.ppermute(out, "unit", back), ((unit_pos + 2 * m) % owners) // 2))
     place = jnp.stack([tm_pos, odd, unit_pos // 2]).astype(jnp.int32)
     place, _ = lax.optimization_barrier((place, out))
-    scores = correlate(place, own, windows, chans, tpd, scale, owners // 2 * width, jnp.float32)
+    share = chans // tm_count
+    scores, part = correlate(
+        place, own, windows, chans, tpd, scale, owners // 2 * width, jnp.float32, share
+    )
     for out, pair in found:
         scores = lax.dynamic_update_slice_in_dim(
             scores, out.astype(jnp.float32), pair * width, 1
         )
+    part = jnp.transpose(part[:taps, :, :share], (1, 2, 0)).reshape(panel, share * taps)
     return (part, scores)
 
 

time: 167 us -> 165 us (0.988)
  waiting for transfers between devices: 22.3 us -> 47.3 us
  local copies, waits for them, and re-layouts: 61 us -> 45.2 us
  other arithmetic: 17.2 us -> 6.58 us
  Pallas kernels: 28 us -> 31.4 us
  starting transfers between devices: 36 us -> 32.7 us
    all_to_all x1, waiting for transfers between devices: 0.01 us -> 15.2 us  [body(): lax.all_to_all(send.reshape(devices, CAP * tpd, chans), AXES, split_axis=...]
    ppermute x1, waiting for transfers between devices: 9.19 us -> 17.6 us  [body(): chunk = lax.ppermute(fresh, 'unit', ahead)]
    ppermute x16, waiting for transfers between devices: 4.8 us -> 11.7 us  [swap(): return lax.ppermute(value, 'tm', [(i, i ^ bit) for i in range(size)])]
    gather x4 -> x0, local copies, waits for them, and re-layouts: 6.18 us -> none  [the longest x2 4.89 us: body(): part.append(jnp.take(stacked, picks, axis=0))]
    ppermute x1, waiting for transfers between devices: 4.23 us -> 0.01 us  [body(): lax.ppermute(out, 'unit', back)]
    ppermute x1, waiting for transfers between devices: 3.63 us -> 0.01 us  [body(): early = lax.ppermute(rest[:first], 'unit', pairs)]
    select_n x5 -> x1, other arithmetic: 4.26 us -> 0.81 us  [body(): jnp.where(odd == 1, head, skip)]
    concatenate x2 -> x0, other arithmetic: 2.93 us -> none  [body(): stacked = jnp.concatenate(found, axis=0)]
  transfers between devices with their start and end apart: 24 -> 24, of which waited for: 7 -> 8; matrix products, arithmetic and copies ran while one was open for 42% -> 26% of each run, Pallas kernels for 10% -> 19%
where the time goes in v7:
time: 165 us; the launch traced here: 164 us
  waiting for transfers between devices  47.3 us (29%)
  local copies, waits for them, and re-layouts  45.2 us (27%)
  starting transfers between devices  32.7 us (20%)
  Pallas kernels  31.4 us (19%)
  other arithmetic  6.58 us (4%)
    pallas_call x2, Pallas kernels, correlate(): pl.pallas_call(functools.partial(correlate_kernel, chans, tpd, scale, mas...  23.4 us
    reshape x1, local copies, waits for them, and re-layouts, body(): cube = before.reshape(panel, chans, taps)  20.7 us
    ppermute x1, waiting for transfers between devices, body(): chunk = lax.ppermute(fresh, 'unit', ahead)  17.6 us
    all_to_all x1, waiting for transfers between devices, body(): lax.all_to_all(send.reshape(devices, CAP * tpd, chans), AXES, split_axis=...  15.2 us
    ppermute x16, starting transfers between devices, swap(): return lax.ppermute(value, 'tm', [(i, i ^ bit) for i in range(size)])  14.1 us
    ppermute x16, waiting for transfers between devices, swap(): return lax.ppermute(value, 'tm', [(i, i ^ bit) for i in range(size)])  11.7 us
    unnamed x17, local copies, waits for them, and re-layouts  10.3 us
    transpose x1, local copies, waits for them, and re-layouts, body(): old = jnp.transpose(cube, (0, 2, 1)).reshape(panel, tpd * chans)  7.88 us
  transfers between devices with their start and end apart: 24, of which 8 were waited for; matrix products, arithmetic and copies ran while one was open for 26% of the time, Pallas kernels for 19%

profile of v7, /device:TPU:0, one launch (start us, length us, event | category | flops | bytes accessed | tf_op | source)
XLA Modules:
  0.0 164.0 jit_solution(9992634926837200022)
XLA Ops:
  2.4 7.3 %all-to-all-start = ((s32[32,1,8]{2,1,0:T(1,128)}), s32[32,1,8]{2,1,0:T(1,128)S(1)}, u32[]{:S(2)}, u32[]{:S(2)}) async-start(s32[32,1,8]{2,1,0:T(1,128)} %bitcast.4), calls=%async_computation | async-start | bytes 32768 | tf_op jit(solution)/shard_map/all_to_all | solution.py:326
  12.5 3.1 %pack.1 = bf16[2048,384]{1,0:T(8,128)(2,1)} custom-call(s32[32]{0:T(128)S(1)} %copy-done.5, s32[32]{0:T(128)S(1)} %copy-done.4, s32[1]{0:T(128)} %bitcast.3.base_ref, bf16[2048,384]{1,0:T(8,128)(2,1)S(1)} %copy-done), custom_call_target="tpu_custom_call" | custom-call | flops 100000000 | bytes 4000000 | tf_op jit(solution)/shard_map/pack/pallas_call | solution.py:66
  17.1 4.6 %all-to-all-start.1 = ((bf16[32,64,384]{2,1,0:T(8,128)(2,1)}), bf16[32,64,384]{2,1,0:T(8,128)(2,1)S(1)}, u32[]{:S(2)}, u32[]{:S(2)}) async-start(bf16[32,64,384]{2,1,0:T(8,128)(2,1)} %bitcast.6), calls=%async_computation.1 | async-start | bytes 3145728 | tf_op jit(solution)/shard_map/all_to_all | solution.py:329
  21.7 20.7 %reshape.71 = bf16[64,384,61]{2,1,0:T(8,128)(2,1)} reshape(bf16[64,23424]{1,0:T(8,128)(2,1)} %param.7) | data formatting | bytes 5996544 | tf_op jit(solution)/shard_map/reshape | solution.py:333
  42.4 15.2 %all-to-all-done.1 = bf16[32,64,384]{2,1,0:T(8,128)(2,1)S(1)} async-done(((bf16[32,64,384]{2,1,0:T(8,128)(2,1)}), bf16[32,64,384]{2,1,0:T(8,128)(2,1)S(1)}, u32[]{:S(2)}, u32[]{:S(2)}) %all-to-all-start.1) | async-done | bytes 1572896 | tf_op jit(solution)/shard_map/all_to_all | solution.py:329
  58.4 3.4 %collective-permute-start.2 = (bf16[640,384]{1,0:T(8,128)(2,1)}, bf16[640,384]{1,0:T(8,128)(2,1)}, u32[]{:S(2)}, u32[]{:S(2)}) collective-permute-start(bf16[640,384]{1,0:T(8,128)(2,1)} %slice.25), channel_id=1, source_target_pairs={{0,1},{1,0},{2,3},{3,2},{4,5},{5,4},{6,7},{7,6},{8,9},{9,8},{10,11... | collective-permute-start | bytes 1474568 | tf_op jit(solution)/shard_map/ppermute | solution.py:344
  61.9 7.9 %dynamic-slice_bitcast_fusion = bf16[64,8,384]{1,2,0:T(8,128)(2,1)} fusion(s32[]{:T(128)S(6)} %select_n.52, bf16[64,384,61]{2,1,0:T(8,128)(2,1)} %reshape.71), kind=kLoop, calls=%fused_computation | loop fusion | bytes 3391492 | tf_op jit(solution)/shard_map/transpose | solution.py:336
  69.8 5.2 %copy.13 = bf16[8,8,8,384]{3,1,2,0:T(8,128)(2,1)S(1)} copy(bf16[8,8,8,384]{2,3,1,0:T(8,128)(2,1)} %bitcast.25) | data formatting | bytes 786432
  77.3 17.6 %collective-permute-done.1 = bf16[64,3072]{1,0:T(8,128)(2,1)S(1)} collective-permute-done((bf16[64,3072]{1,0:T(8,128)(2,1)S(1)}, bf16[64,3072]{1,0:T(8,128)(2,1)S(1)}, u32[]{:S(2)}, u32[]{:S(2)}) %collective-permute-start.1) | collective-permute-done | bytes 393248 | tf_op jit(solution)/shard_map/ppermute | solution.py:358
  94.9 1.5 collective-permute-start.5
  98.8 1.7 %collective-permute-start.13 = (bf16[1,32,3072]{2,1,0:T(8,128)(2,1)}, bf16[1,32,3072]{2,1,0:T(8,128)(2,1)}, u32[]{:S(2)}, u32[]{:S(2)}) collective-permute-start(bf16[1,32,3072]{2,1,0:T(8,128)(2,1)} %get-tuple-element.39), channel_id=1, source_target_pairs={{0,16},{4,20},{8,24},{12,28},{16,0},{20,4},{24,8},{28,12},{1,17},{... | collective-permute-start | bytes 589832 | tf_op jit(solution)/shard_map/ppermute | solution.py:274
  102.6 1.8 %collective-permute-start.6 = (bf16[2,32,3072]{2,1,0:T(8,128)(2,1)}, bf16[2,32,3072]{2,1,0:T(8,128)(2,1)}, u32[]{:S(2)}, u32[]{:S(2)}) collective-permute-start(bf16[2,32,3072]{2,1,0:T(8,128)(2,1)} %pad_maximum_fusion.1.refs_2_), channel_id=1, source_target_pairs={{0,16},{4,20},{8,24},{12,28},{16,0},{20,4},{24,8},{28,12},{1,17},{... | collective-permute-start | bytes 1179656 | tf_op jit(solution)/shard_map/ppermute | solution.py:274
  104.4 6.7 %collective-permute-done.3 = bf16[1,32,3072]{2,1,0:T(8,128)(2,1)S(1)} collective-permute-done((bf16[1,32,3072]{2,1,0:T(8,128)(2,1)S(1)}, bf16[1,32,3072]{2,1,0:T(8,128)(2,1)S(1)}, u32[]{:S(2)}, u32[]{:S(2)}) %collective-permute-start.3) | collective-permute-done | bytes 196640 | tf_op jit(solution)/shard_map/ppermute | solution.py:274
  111.8 1.5 collective-permute-start.4
  113.4 1.5 collective-permute-start.16
  116.2 3.4 %collective-permute-done.6.refs_3_ = bf16[2,32,3072]{2,1,0:T(8,128)(2,1)} collective-permute-done((bf16[2,32,3072]{2,1,0:T(8,128)(2,1)}, bf16[2,32,3072]{2,1,0:T(8,128)(2,1)}, u32[]{:S(2)}, u32[]{:S(2)}) %collective-permute-start.6) | collective-permute-done | bytes 393248 | tf_op jit(solution)/shard_map/ppermute | solution.py:274
  119.6 1.5 collective-permute-start.11
  121.1 1.8 %pad_maximum_fusion.2.refs_0_ = bf16[2,32,3072]{2,1,0:T(8,128)(2,1)} fusion(bf16[1,32,3072]{2,1,0:T(8,128)(2,1)} %collective-permute-done.13, bf16[1,32,3072]{2,1,0:T(8,128)(2,1)} %get-tuple-element.39), kind=kLoop, calls=%fused_computation.5 | loop fusion | flops 196608 | bytes 786432 | tf_op jit(solution)/shard_map/concatenate | solution.py:286
  122.9 2.1 %collective-permute-start.14 = (bf16[2,32,3072]{2,1,0:T(8,128)(2,1)}, bf16[2,32,3072]{2,1,0:T(8,128)(2,1)}, u32[]{:S(2)}, u32[]{:S(2)}) collective-permute-start(bf16[2,32,3072]{2,1,0:T(8,128)(2,1)} %pad_maximum_fusion.2.refs_0_), channel_id=1, source_target_pairs={{0,8},{4,12},{8,0},{12,4},{16,24},{20,28},{24,16},{28,20},{1,9},{5... | collective-permute-start | bytes 1179656 | tf_op jit(solution)/shard_map/ppermute | solution.py:274
  125.0 1.5 collective-permute-done.refs_1_
  131.3 1.7 %fold.5.refs_10_ = bf16[208,3072]{1,0:T(8,128)(2,1)S(1)} custom-call(bf16[64,384]{1,0:T(8,128)(2,1)S(1)} %copy-done.3, bf16[1408,384]{1,0:T(8,128)(2,1)} %collective-permute-done.refs_1_, bf16[64,384]{1,0:T(8,128)(2,1)S(1)} %broadcast_select_fusion.refs_2_), custom_call_target="tpu_custom_call" | custom-call | flops 200000000 | bytes 4000000 | tf_op jit(solution)/shard_map/fold/pallas_call | solution.py:103
  133.6 1.5 collective-permute-start.19
  135.7 10.6 %correlate.2 = bf16[64,2048]{1,0:T(8,128)(2,1)S(1)} custom-call(s32[3]{0:T(128)S(1)} %pad_add_fusion.2.place_ref, bf16[2,32,3072]{2,1,0:T(8,128)(2,1)} %pad_maximum_fusion.refs_0_, bf16[2,32,3072]{2,1,0:T(8,128)(2,1)} %collective-permute-done.4.refs_1_, bf16[2,32,3072]{2,1,0:T(8,128)(2,1)} %pad_maximum_fusion.1.refs_2_, ...), custom_call_target="tpu_custom_call" | custom-call | flops 8000000000 | bytes 8000000 | tf_op jit(solution)/shard_map/correlate/pallas_call | solution.py:254
  146.4 12.9 %correlate.3 = (f32[64,4096]{1,0:T(8,128)}, bf16[64,64,128]{2,1,0:T(8,128)(2,1)S(1)}) custom-call(s32[3]{0:T(128)S(1)} %pad_add_fusion.place_ref, bf16[2,32,3072]{2,1,0:T(8,128)(2,1)} %pad_maximum_fusion.2.refs_0_, bf16[2,32,3072]{2,1,0:T(8,128)(2,1)} %collective-permute-done.14.refs_1_, bf16[2,32,3072]{2,1,0:T(8,128)(2,1)S(1)} %pad_maximum_fusion.3.refs_2_, ...), custom_call_target="tpu_custom_call" | custom-call | flops 8000000000 | bytes 8000000 | tf_op jit(solution)/shard_map/correlate/pallas_call | solution.py:254
  (78 shorter events, 26.5 us)
Async XLA Ops:
  2.4 14.4 %all-to-all-start = ((s32[32,1,8]{2,1,0:T(1,128)}), s32[32,1,8]{2,1,0:T(1,128)S(1)}, u32[]{:S(2)}, u32[]{:S(2)}) async-start(s32[32,1,8]{2,1,0:T(1,128)} %bitcast.4), calls=%async_computation | async-start | bytes 32768 | tf_op jit(solution)/shard_map/all_to_all | solution.py:326
  17.1 40.5 %all-to-all-start.1 = ((bf16[32,64,384]{2,1,0:T(8,128)(2,1)}), bf16[32,64,384]{2,1,0:T(8,128)(2,1)S(1)}, u32[]{:S(2)}, u32[]{:S(2)}) async-start(bf16[32,64,384]{2,1,0:T(8,128)(2,1)} %bitcast.6), calls=%async_computation.1 | async-start | bytes 3145728 | tf_op jit(solution)/shard_map/all_to_all | solution.py:329
  58.4 36.4 %collective-permute-start.2 = (bf16[640,384]{1,0:T(8,128)(2,1)}, bf16[640,384]{1,0:T(8,128)(2,1)}, u32[]{:S(2)}, u32[]{:S(2)}) collective-permute-start(bf16[640,384]{1,0:T(8,128)(2,1)} %slice.25), channel_id=1, source_target_pairs={{0,1},{1,0},{2,3},{3,2},{4,5},{5,4},{6,7},{7,6},{8,9},{9,8},{10,11... | collective-permute-start | bytes 1474568 | tf_op jit(solution)/shard_map/ppermute | solution.py:344
  76.2 18.6 %collective-permute-start.1 = (bf16[64,3072]{1,0:T(8,128)(2,1)S(1)}, bf16[64,3072]{1,0:T(8,128)(2,1)S(1)}, u32[]{:S(2)}, u32[]{:S(2)}) collective-permute-start(bf16[64,3072]{1,0:T(8,128)(2,1)S(1)} %refine.1), channel_id=1, source_target_pairs={{0,2},{1,3},{2,0},{3,1},{4,6},{5,7},{6,4},{7,5},{8,10},{9,11},{10,... | collective-permute-start | bytes 1179656 | tf_op jit(solution)/shard_map/ppermute | solution.py:358
  94.9 6.9 %collective-permute-start.5 = (bf16[1,32,3072]{2,1,0:T(8,128)(2,1)S(1)}, bf16[1,32,3072]{2,1,0:T(8,128)(2,1)S(1)}, u32[]{:S(2)}, u32[]{:S(2)}) collective-permute-start(bf16[1,32,3072]{2,1,0:T(8,128)(2,1)S(1)} %get-tuple-element.40), channel_id=1, source_target_pairs={{0,8},{4,12},{8,0},{12,4},{16,24},{20,28},{24,16},{28,20},{1,9},{5... | collective-permute-start | bytes 589832 | tf_op jit(solution)/shard_map/ppermute | solution.py:274
  98.2 15.1 %collective-permute-start.15 = (bf16[1,32,3072]{2,1,0:T(8,128)(2,1)S(1)}, bf16[1,32,3072]{2,1,0:T(8,128)(2,1)S(1)}, u32[]{:S(2)}, u32[]{:S(2)}) collective-permute-start(bf16[1,32,3072]{2,1,0:T(8,128)(2,1)S(1)} %get-tuple-element.38), channel_id=1, source_target_pairs={{0,8},{4,12},{8,0},{12,4},{16,24},{20,28},{24,16},{28,20},{1,9},{5... | collective-permute-start | bytes 589832 | tf_op jit(solution)/shard_map/ppermute | solution.py:274
  98.8 16.1 %collective-permute-start.13 = (bf16[1,32,3072]{2,1,0:T(8,128)(2,1)}, bf16[1,32,3072]{2,1,0:T(8,128)(2,1)}, u32[]{:S(2)}, u32[]{:S(2)}) collective-permute-start(bf16[1,32,3072]{2,1,0:T(8,128)(2,1)} %get-tuple-element.39), channel_id=1, source_target_pairs={{0,16},{4,20},{8,24},{12,28},{16,0},{20,4},{24,8},{28,12},{1,17},{... | collective-permute-start | bytes 589832 | tf_op jit(solution)/shard_map/ppermute | solution.py:274
  100.5 26.0 %collective-permute-start = (bf16[1408,384]{1,0:T(8,128)(2,1)}, bf16[1408,384]{1,0:T(8,128)(2,1)}, u32[]{:S(2)}, u32[]{:S(2)}) collective-permute-start(bf16[1408,384]{1,0:T(8,128)(2,1)} %slice.24), channel_id=1, source_target_pairs={{0,1},{1,0},{2,3},{3,2},{4,5},{5,4},{6,7},{7,6},{8,9},{9,8},{10,11... | collective-permute-start | bytes 3244040 | tf_op jit(solution)/shard_map/ppermute | solution.py:345
  100.5 10.5 %collective-permute-start.3 = (bf16[1,32,3072]{2,1,0:T(8,128)(2,1)S(1)}, bf16[1,32,3072]{2,1,0:T(8,128)(2,1)S(1)}, u32[]{:S(2)}, u32[]{:S(2)}) collective-permute-start(bf16[1,32,3072]{2,1,0:T(8,128)(2,1)S(1)} %get-tuple-element.41), channel_id=1, source_target_pairs={{0,16},{4,20},{8,24},{12,28},{16,0},{20,4},{24,8},{28,12},{1,17},{... | collective-permute-start | bytes 589832 | tf_op jit(solution)/shard_map/ppermute | solution.py:274
  102.6 17.0 %collective-permute-start.6 = (bf16[2,32,3072]{2,1,0:T(8,128)(2,1)}, bf16[2,32,3072]{2,1,0:T(8,128)(2,1)}, u32[]{:S(2)}, u32[]{:S(2)}) collective-permute-start(bf16[2,32,3072]{2,1,0:T(8,128)(2,1)} %pad_maximum_fusion.1.refs_2_), channel_id=1, source_target_pairs={{0,16},{4,20},{8,24},{12,28},{16,0},{20,4},{24,8},{28,12},{1,17},{... | collective-permute-start | bytes 1179656 | tf_op jit(solution)/shard_map/ppermute | solution.py:274
  111.8 11.0 %collective-permute-start.4 = (bf16[2,32,3072]{2,1,0:T(8,128)(2,1)}, bf16[2,32,3072]{2,1,0:T(8,128)(2,1)}, u32[]{:S(2)}, u32[]{:S(2)}) collective-permute-start(bf16[2,32,3072]{2,1,0:T(8,128)(2,1)} %pad_maximum_fusion.refs_0_), channel_id=1, source_target_pairs={{0,8},{4,12},{8,0},{12,4},{16,24},{20,28},{24,16},{28,20},{1,9},{5... | collective-permute-start | bytes 1179656 | tf_op jit(solution)/shard_map/ppermute | solution.py:274
  113.4 14.6 %collective-permute-start.16 = (bf16[2,32,3072]{2,1,0:T(8,128)(2,1)S(1)}, bf16[2,32,3072]{2,1,0:T(8,128)(2,1)}, u32[]{:S(2)}, u32[]{:S(2)}) collective-permute-start(bf16[2,32,3072]{2,1,0:T(8,128)(2,1)S(1)} %pad_maximum_fusion.3.refs_2_), channel_id=1, source_target_pairs={{0,16},{4,20},{8,24},{12,28},{16,0},{20,4},{24,8},{28,12},{1,17},{... | collective-permute-start | bytes 1179656 | tf_op jit(solution)/shard_map/ppermute | solution.py:274
  114.9 12.0 %collective-permute-start.12 = (bf16[64,384]{1,0:T(8,128)(2,1)S(1)}, bf16[64,384]{1,0:T(8,128)(2,1)}, u32[]{:S(2)}, u32[]{:S(2)}) collective-permute-start(bf16[64,384]{1,0:T(8,128)(2,1)S(1)} %slice.28), channel_id=1, source_target_pairs={{2,0},{4,2},{6,4},{8,6},{10,8},{12,10},{14,12},{16,14},{18,16},{20... | collective-permute-start | bytes 147464 | tf_op jit(solution)/shard_map/ppermute | solution.py:341
  119.6 7.5 %collective-permute-start.11 = (bf16[64,384]{1,0:T(8,128)(2,1)S(1)}, bf16[64,384]{1,0:T(8,128)(2,1)S(1)}, u32[]{:S(2)}, u32[]{:S(2)}) collective-permute-start(bf16[64,384]{1,0:T(8,128)(2,1)S(1)} %slice.28), channel_id=1, source_target_pairs={{1,0},{2,1},{3,2},{4,3},{5,4},{6,5},{7,6},{8,7},{9,8},{10,9},{11,1... | collective-permute-start | bytes 147464 | tf_op jit(solution)/shard_map/ppermute | solution.py:340
  122.9 10.7 %collective-permute-start.14 = (bf16[2,32,3072]{2,1,0:T(8,128)(2,1)}, bf16[2,32,3072]{2,1,0:T(8,128)(2,1)}, u32[]{:S(2)}, u32[]{:S(2)}) collective-permute-start(bf16[2,32,3072]{2,1,0:T(8,128)(2,1)} %pad_maximum_fusion.2.refs_0_), channel_id=1, source_target_pairs={{0,8},{4,12},{8,0},{12,4},{16,24},{20,28},{24,16},{28,20},{1,9},{5... | collective-permute-start | bytes 1179656 | tf_op jit(solution)/shard_map/ppermute | solution.py:274
  126.5 8.6 %collective-permute-start.10 = (bf16[2,32,3072]{2,1,0:T(8,128)(2,1)}, bf16[2,32,3072]{2,1,0:T(8,128)(2,1)}, u32[]{:S(2)}, u32[]{:S(2)}) collective-permute-start(bf16[2,32,3072]{2,1,0:T(8,128)(2,1)} %collective-permute-done.6.refs_3_), channel_id=1, source_target_pairs={{0,4},{4,0},{8,12},{12,8},{16,20},{20,16},{24,28},{28,24},{1,5},{5... | collective-permute-start | bytes 1179656 | tf_op jit(solution)/shard_map/ppermute | solution.py:274
  126.8 8.3 %collective-permute-start.7 = (bf16[2,32,3072]{2,1,0:T(8,128)(2,1)}, bf16[2,32,3072]{2,1,0:T(8,128)(2,1)}, u32[]{:S(2)}, u32[]{:S(2)}) collective-permute-start(bf16[2,32,3072]{2,1,0:T(8,128)(2,1)} %pad_maximum_fusion.refs_0_), channel_id=1, source_target_pairs={{0,4},{4,0},{8,12},{12,8},{16,20},{20,16},{24,28},{28,24},{1,5},{5... | collective-permute-start | bytes 1179656 | tf_op jit(solution)/shard_map/ppermute | solution.py:274
  127.7 7.9 %collective-permute-start.8 = (bf16[2,32,3072]{2,1,0:T(8,128)(2,1)}, bf16[2,32,3072]{2,1,0:T(8,128)(2,1)}, u32[]{:S(2)}, u32[]{:S(2)}) collective-permute-start(bf16[2,32,3072]{2,1,0:T(8,128)(2,1)} %collective-permute-done.4.refs_1_), channel_id=1, source_target_pairs={{0,4},{4,0},{8,12},{12,8},{16,20},{20,16},{24,28},{28,24},{1,5},{5... | collective-permute-start | bytes 1179656 | tf_op jit(solution)/shard_map/ppermute | solution.py:274
  128.0 7.7 %collective-permute-start.9 = (bf16[2,32,3072]{2,1,0:T(8,128)(2,1)}, bf16[2,32,3072]{2,1,0:T(8,128)(2,1)}, u32[]{:S(2)}, u32[]{:S(2)}) collective-permute-start(bf16[2,32,3072]{2,1,0:T(8,128)(2,1)} %pad_maximum_fusion.1.refs_2_), channel_id=1, source_target_pairs={{0,4},{4,0},{8,12},{12,8},{16,20},{20,16},{24,28},{28,24},{1,5},{5... | collective-permute-start | bytes 1179656 | tf_op jit(solution)/shard_map/ppermute | solution.py:274
  133.6 12.7 %collective-permute-start.19 = (bf16[2,32,3072]{2,1,0:T(8,128)(2,1)S(1)}, bf16[2,32,3072]{2,1,0:T(8,128)(2,1)S(1)}, u32[]{:S(2)}, u32[]{:S(2)}) collective-permute-start(bf16[2,32,3072]{2,1,0:T(8,128)(2,1)S(1)} %pad_maximum_fusion.3.refs_2_), channel_id=1, source_target_pairs={{0,4},{4,0},{8,12},{12,8},{16,20},{20,16},{24,28},{28,24},{1,5},{5... | collective-permute-start | bytes 1179656 | tf_op jit(solution)/shard_map/ppermute | solution.py:274
  135.1 11.3 %collective-permute-start.17 = (bf16[2,32,3072]{2,1,0:T(8,128)(2,1)}, bf16[2,32,3072]{2,1,0:T(8,128)(2,1)S(1)}, u32[]{:S(2)}, u32[]{:S(2)}) collective-permute-start(bf16[2,32,3072]{2,1,0:T(8,128)(2,1)} %pad_maximum_fusion.2.refs_0_), channel_id=1, source_target_pairs={{0,4},{4,0},{8,12},{12,8},{16,20},{20,16},{24,28},{28,24},{1,5},{5... | collective-permute-start | bytes 1179656 | tf_op jit(solution)/shard_map/ppermute | solution.py:274
  135.1 11.3 %collective-permute-start.20 = (bf16[2,32,3072]{2,1,0:T(8,128)(2,1)}, bf16[2,32,3072]{2,1,0:T(8,128)(2,1)S(1)}, u32[]{:S(2)}, u32[]{:S(2)}) collective-permute-start(bf16[2,32,3072]{2,1,0:T(8,128)(2,1)} %collective-permute-done.16.refs_3_), channel_id=1, source_target_pairs={{0,4},{4,0},{8,12},{12,8},{16,20},{20,16},{24,28},{28,24},{1,5},{5... | collective-permute-start | bytes 1179656 | tf_op jit(solution)/shard_map/ppermute | solution.py:274
  135.6 10.8 %collective-permute-start.18 = (bf16[2,32,3072]{2,1,0:T(8,128)(2,1)}, bf16[2,32,3072]{2,1,0:T(8,128)(2,1)S(1)}, u32[]{:S(2)}, u32[]{:S(2)}) collective-permute-start(bf16[2,32,3072]{2,1,0:T(8,128)(2,1)} %collective-permute-done.14.refs_1_), channel_id=1, source_target_pairs={{0,4},{4,0},{8,12},{12,8},{16,20},{20,16},{24,28},{28,24},{1,5},{5... | collective-permute-start | bytes 1179656 | tf_op jit(solution)/shard_map/ppermute | solution.py:274
  146.3 15.8 %collective-permute-start.21 = (bf16[64,2048]{1,0:T(8,128)(2,1)S(1)}, bf16[64,2048]{1,0:T(8,128)(2,1)}, u32[]{:S(2)}, u32[]{:S(2)}) collective-permute-start(bf16[64,2048]{1,0:T(8,128)(2,1)S(1)} %correlate.2), channel_id=1, source_target_pairs={{2,0},{3,1},{0,2},{1,3},{6,4},{7,5},{4,6},{5,7},{10,8},{11,9},{8,1... | collective-permute-start | bytes 786440 | tf_op jit(solution)/shard_map/ppermute | solution.py:367
  (8 other events, 43.8 us)

commit v8 on v6

--- a/solution.py
+++ b/solution.py
@@ -152,6 +152,41 @@
         cost_estimate=pl.CostEstimate(flops=8 * 10**8, bytes_accessed=3 * 10**6, transcendentals=0),
         name="refine",
     )(key, got, old)
+
+
+def extract_kernel(chans, tpd, share, masks, place_ref, *refs):
+    pieces, out_ref = refs[:-1], refs[-1]
+    half_rows = pieces[0].shape[1]
+    wide = out_ref.shape[2]
+    me = place_ref[0]
+    channel = lax.broadcasted_iota(jnp.int32, (chans, wide), 0)
+    lane = lax.broadcasted_iota(jnp.int32, (chans, wide), 1)
+    pick = ((channel == me * share + lane) & (lane < share)).astype(jnp.bfloat16)
+    for ref, (part_of, items) in zip(pieces, masks):
+        rows = slice(part_of * half_rows, (part_of + 1) * half_rows)
+        for at, mask in enumerate(items):
+            first = jnp.bitwise_xor(me, mask) * tpd
+            for t in range(tpd):
+                taken = jnp.dot(
+                    ref[at, :, t * chans : (t + 1) * chans], pick, preferred_element_type=jnp.float32
+                )
+                out_ref[first + t, rows, :] = taken.astype(jnp.bfloat16)
+
+
+def extract(me, gathered, chans, tpd, share):
+    pieces = [value for value, _, _ in gathered]
+    masks = [(part_of, items) for _, part_of, items in gathered]
+    taps = sum(len(items) for _, items in masks) // 2 * tpd
+    vmem = pl.BlockSpec(memory_space=pltpu.VMEM)
+    return pl.pallas_call(
+        functools.partial(extract_kernel, chans, tpd, share, masks),
+        out_shape=jax.ShapeDtypeStruct((taps, 2 * pieces[0].shape[1], -(-share // 128) * 128), jnp.bfloat16),
+        in_specs=[pl.BlockSpec(memory_space=pltpu.SMEM)] + [vmem] * len(pieces),
+        out_specs=vmem,
+        compiler_params=params(14),
+        cost_estimate=pl.CostEstimate(flops=4 * 10**8, bytes_accessed=4 * 10**6, transcendentals=0),
+        name="extract",
+    )(me, *pieces)
 
 
 def correlate_kernel(chans, tpd, scale, masks, place_ref, *refs):
@@ -258,7 +293,7 @@
     return lax.ppermute(value, "tm", [(i, i ^ bit) for i in range(size)])
 
 
-def gather_panel(value):
+def spread(value):
     bits = []
     while 2 << len(bits) < lax.axis_size("tm"):
         bits.append(2 << len(bits))
@@ -271,7 +306,17 @@
             items = [m for _, ms in parts for m in ms]
             parts = [(held, items), (swap(held, bit), [m ^ bit for m in items])]
         out += [(v, part_of, ms) for v, ms in parts]
-    return out + [(swap(v, 1), part_of, [m ^ 1 for m in ms]) for v, part_of, ms in out]
+    return out
+
+
+def across(parts):
+    return parts + [(swap(v, 1), part_of, [m ^ 1 for m in ms]) for v, part_of, ms in parts]
+
+
+def tie(parts, *beside):
+    done = lax.optimization_barrier((*beside, *[v for v, _, _ in parts]))
+    tied = [(v, n, ms) for v, (_, n, ms) in zip(done[len(beside) :], parts)]
+    return tied, *done[: len(beside)]
 
 
 def body(recording, spike_times, unit_labels, old_templates):
@@ -306,10 +351,7 @@
     tags = tags.reshape(devices, CAP)
     tags = lax.all_to_all(tags, AXES, split_axis=0, concat_axis=0, tiled=True)
     key = (tags[:, :, None] * tpd + jnp.arange(tpd)[None, None, :]).reshape(1, -1)
-    pairs = [(i, i ^ 1) for i in range(owners)]
-    first = sub_rows // 4 // (16 * ROWS) * (16 * ROWS)
-    early = lax.ppermute(recording[:first], "unit", pairs)
-    send, key, early, before = lax.optimization_barrier((send, key, early, old_templates))
+    send, key, before = lax.optimization_barrier((send, key, old_templates))
     got = lax.all_to_all(
         send.reshape(devices, CAP * tpd, chans), AXES, split_axis=0, concat_axis=0, tiled=True
     ).reshape(devices * CAP * tpd, chans)
@@ -319,37 +361,22 @@
     cube = lax.dynamic_slice_in_dim(cube, tm_pos * tpd, tpd, 2)
     old = jnp.transpose(cube, (0, 2, 1)).reshape(panel, tpd * chans)
 
-    got, rest = lax.optimization_barrier((got, recording))
+    got, rest, old = lax.optimization_barrier((got, recording, old))
     head = rest[:padded]
     follow = lax.ppermute(head, AXES, [(i, i - 1) for i in range(1, devices)])
     skip = lax.ppermute(head, AXES, [(i, i - 2) for i in range(2, devices, 2)])
+    pairs = [(i, i ^ 1) for i in range(owners)]
+    first = sub_rows // 2 // (16 * ROWS) * (16 * ROWS)
+    early = lax.ppermute(rest[:first], "unit", pairs)
     late = lax.ppermute(rest[first:], "unit", pairs)
     odd = unit_pos % 2
 
     fresh = refine(key, got, old, tpd)
-    early, rest, fresh = lax.optimization_barrier((early, rest, fresh))
+    rest, fresh = lax.optimization_barrier((rest, fresh))
     mine = fold(rest)
-    early = fold(early)
-    own = gather_panel(fresh)
+    own = spread(fresh)
+    share = chans // tm_count
     width = 2 * keep * FOLD
-
-    share = chans // tm_count
-    order = []
-    pieces = [[], []]
-    for value, part_of, items in own:
-        value = value.reshape(len(items), panel // 2, tpd, chans)
-        pieces[part_of].append(lax.dynamic_slice_in_dim(value, tm_pos * share, share, 3))
-        order += items if part_of == 0 else []
-    order_b = [m for _, part_of, items in own if part_of == 1 for m in items]
-    part = []
-    for found, masks in ((pieces[0], order), (pieces[1], order_b)):
-        spots = jnp.array([masks.index(m) for m in range(tm_count)])
-        stacked = jnp.concatenate(found, axis=0)
-        picks = spots[jnp.bitwise_xor(jnp.arange(tm_count), tm_pos)]
-        part.append(jnp.take(stacked, picks, axis=0))
-    part = jnp.concatenate(part, axis=1)
-    part = jnp.transpose(part, (1, 3, 0, 2)).reshape(panel, share, padded)[:, :, :taps]
-    part = part.reshape(panel, share * taps)
 
     found = []
     for m in range(1, owners // 2):
@@ -357,13 +384,15 @@
         back = [(j, i) for i, j in ahead]
         chunk = lax.ppermute(fresh, "unit", ahead)
         if m == 1:
-            chunk, mine, early = lax.optimization_barrier((chunk, mine, early))
-        other = gather_panel(chunk)
-        if m == 1:
-            windows = (mine, early, fold(follow, late, jnp.where(odd == 1, head, skip)))
-            tied = lax.optimization_barrier((part, *[v for v, _, _ in other]))
-            part = tied[0]
-            other = [(v, n, ms) for v, (_, n, ms) in zip(tied[1:], other)]
+            own, chunk, mine, early = tie(own, chunk, mine, early)
+            own = across(own)
+            part = extract(tm_pos.astype(jnp.int32).reshape(1), own, chans, tpd, share)
+            part = jnp.transpose(part[:taps, :, :share], (1, 2, 0)).reshape(panel, share * taps)
+            other, late, part = tie(spread(chunk), late, part)
+            windows = (mine, fold(early), fold(follow, late, jnp.where(odd == 1, head, skip)))
+        else:
+            other = spread(chunk)
+        other = across(other)
         place = jnp.stack([tm_pos, odd, 0 * odd]).astype(jnp.int32)
         out = correlate(place, other, windows, chans, tpd, scale, width, jnp.bfloat16)
         found.append((lax.ppermute(out, "unit", back), ((unit_pos + 2 * m) % owners) // 2))

time: 167 us -> 160 us (0.958)
  waiting for transfers between devices: 22.3 us -> 38.6 us
  other arithmetic: 17.2 us -> 4.68 us
  local copies, waits for them, and re-layouts: 61 us -> 52.1 us
  starting transfers between devices: 36 us -> 30.4 us
  Pallas kernels: 28 us -> 32.6 us
    ppermute x1, waiting for transfers between devices: 3.63 us -> 11.4 us  [body(): early = lax.ppermute(rest[:first], 'unit', pairs)]
    gather x4 -> x0, local copies, waits for them, and re-layouts: 6.18 us -> none  [the longest x2 4.89 us: body(): part.append(jnp.take(stacked, picks, axis=0))]
    concatenate x7 -> x4, other arithmetic: 7.34 us -> 1.67 us  [spread(): jnp.concatenate([v for v, _ in parts], axis=0)]
    ppermute x1, waiting for transfers between devices: 0.49 us -> 5.82 us  [body(): skip = lax.ppermute(head, AXES, [(i, i - 2) for i in range(2, devices, 2)])]
    ppermute x1, waiting for transfers between devices: 4.23 us -> 0.61 us  [body(): lax.ppermute(out, 'unit', back)]
    pallas_call x0 -> x1, Pallas kernels: none -> 3.53 us  [extract(): pl.pallas_call(functools.partial(extract_kernel, chans, tpd, share, masks...]
    ppermute x16, starting transfers between devices: 13.3 us -> 9.75 us  [swap(): return lax.ppermute(value, 'tm', [(i, i ^ bit) for i in range(size)])]
    select_n x5 -> x1, other arithmetic: 4.26 us -> 0.82 us  [body(): jnp.where(odd == 1, head, skip)]
  transfers between devices with their start and end apart: 24 -> 24, of which waited for: 7 -> 11; matrix products, arithmetic and copies ran while one was open for 42% -> 28% of each run, Pallas kernels for 10% -> 13%
where the time goes in v8:
time: 160 us; the launch traced here: 159 us
  local copies, waits for them, and re-layouts  52.1 us (33%)
  waiting for transfers between devices  38.6 us (24%)
  Pallas kernels  32.6 us (20%)
  starting transfers between devices  30.4 us (19%)
  other arithmetic  4.68 us (3%)
    pallas_call x2, Pallas kernels, correlate(): pl.pallas_call(functools.partial(correlate_kernel, chans, tpd, scale, mas...  22.2 us
    reshape x1, local copies, waits for them, and re-layouts, body(): cube = before.reshape(panel, chans, taps)  20.6 us
    unnamed x37, local copies, waits for them, and re-layouts  14.5 us
    ppermute x1, waiting for transfers between devices, body(): early = lax.ppermute(rest[:first], 'unit', pairs)  11.4 us
    ppermute x16, starting transfers between devices, swap(): return lax.ppermute(value, 'tm', [(i, i ^ bit) for i in range(size)])  9.75 us
    ppermute x1, waiting for transfers between devices, body(): chunk = lax.ppermute(fresh, 'unit', ahead)  8.8 us
    transpose x1, local copies, waits for them, and re-layouts, body(): old = jnp.transpose(cube, (0, 2, 1)).reshape(panel, tpd * chans)  7.9 us
    all_to_all x1, starting transfers between devices, body(): tags = lax.all_to_all(tags, AXES, split_axis=0, concat_axis=0, tiled=True)  7.3 us
  transfers between devices with their start and end apart: 24, of which 11 were waited for; matrix products, arithmetic and copies ran while one was open for 28% of the time, Pallas kernels for 13%

profile of v8, /device:TPU:0, one launch (start us, length us, event | category | flops | bytes accessed | tf_op | source)
XLA Modules:
  0.0 159.4 jit_solution(12775306414237476883)
XLA Ops:
  2.4 7.3 %all-to-all-start = ((s32[32,1,8]{2,1,0:T(1,128)}), s32[32,1,8]{2,1,0:T(1,128)S(1)}, u32[]{:S(2)}, u32[]{:S(2)}) async-start(s32[32,1,8]{2,1,0:T(1,128)} %bitcast.1), calls=%async_computation | async-start | bytes 32768 | tf_op jit(solution)/shard_map/all_to_all | solution.py:352
  9.8 1.4 copy-done
  12.5 3.1 %pack.1 = bf16[2048,384]{1,0:T(8,128)(2,1)} custom-call(s32[32]{0:T(128)S(1)} %copy-done.17, s32[32]{0:T(128)S(1)} %copy-done.16, s32[1]{0:T(128)} %bitcast.base_ref, bf16[2048,384]{1,0:T(8,128)(2,1)S(1)} %copy-done), custom_call_target="tpu_custom_call" | custom-call | flops 100000000 | bytes 4000000 | tf_op jit(solution)/shard_map/pack/pallas_call | solution.py:66
  17.1 4.5 %all-to-all-start.1 = ((bf16[32,64,384]{2,1,0:T(8,128)(2,1)}), bf16[32,64,384]{2,1,0:T(8,128)(2,1)S(1)}, u32[]{:S(2)}, u32[]{:S(2)}) async-start(bf16[32,64,384]{2,1,0:T(8,128)(2,1)} %bitcast.3), calls=%async_computation.1 | async-start | bytes 3145728 | tf_op jit(solution)/shard_map/all_to_all | solution.py:355
  21.6 20.6 %reshape.74 = bf16[64,384,61]{2,1,0:T(8,128)(2,1)} reshape(bf16[64,23424]{1,0:T(8,128)(2,1)} %param.7) | data formatting | bytes 5996544 | tf_op jit(solution)/shard_map/reshape | solution.py:359
  42.3 7.9 %dynamic-slice_bitcast_fusion = bf16[64,8,384]{1,2,0:T(8,128)(2,1)} fusion(s32[]{:T(128)S(6)} %select_n.50, bf16[64,384,61]{2,1,0:T(8,128)(2,1)} %reshape.74), kind=kLoop, calls=%fused_computation | loop fusion | bytes 3391492 | tf_op jit(solution)/shard_map/transpose | solution.py:362
  50.2 5.2 %copy.13 = bf16[8,8,8,384]{3,1,2,0:T(8,128)(2,1)S(1)} copy(bf16[8,8,8,384]{2,3,1,0:T(8,128)(2,1)} %bitcast.25) | data formatting | bytes 786432
  55.4 2.2 %all-to-all-done.1 = bf16[32,64,384]{2,1,0:T(8,128)(2,1)S(1)} async-done(((bf16[32,64,384]{2,1,0:T(8,128)(2,1)}), bf16[32,64,384]{2,1,0:T(8,128)(2,1)S(1)}, u32[]{:S(2)}, u32[]{:S(2)}) %all-to-all-start.1) | async-done | bytes 1572896 | tf_op jit(solution)/shard_map/all_to_all | solution.py:355
  58.9 2.6 %collective-permute-start.1 = (bf16[64,3072]{1,0:T(8,128)(2,1)S(1)}, bf16[64,3072]{1,0:T(8,128)(2,1)S(1)}, u32[]{:S(2)}, u32[]{:S(2)}) collective-permute-start(bf16[64,3072]{1,0:T(8,128)(2,1)S(1)} %refine.1), channel_id=1, source_target_pairs={{0,2},{1,3},{2,0},{3,1},{4,6},{5,7},{6,4},{7,5},{8,10},{9,11},{10,... | collective-permute-start | bytes 1179656 | tf_op jit(solution)/shard_map/ppermute | solution.py:385
  61.5 1.5 collective-permute-start.5
  65.9 2.4 %collective-permute-done.5 = bf16[1,32,3072]{2,1,0:T(8,128)(2,1)S(1)} collective-permute-done((bf16[1,32,3072]{2,1,0:T(8,128)(2,1)S(1)}, bf16[1,32,3072]{2,1,0:T(8,128)(2,1)S(1)}, u32[]{:S(2)}, u32[]{:S(2)}) %collective-permute-start.5) | collective-permute-done | bytes 196640 | tf_op jit(solution)/shard_map/ppermute | solution.py:293
  71.2 8.8 %collective-permute-done.1 = bf16[64,3072]{1,0:T(8,128)(2,1)S(1)} collective-permute-done((bf16[64,3072]{1,0:T(8,128)(2,1)S(1)}, bf16[64,3072]{1,0:T(8,128)(2,1)S(1)}, u32[]{:S(2)}, u32[]{:S(2)}) %collective-permute-start.1) | collective-permute-done | bytes 393248 | tf_op jit(solution)/shard_map/ppermute | solution.py:385
  80.0 11.4 %collective-permute-done.2.refs_0_ = bf16[1024,384]{1,0:T(8,128)(2,1)S(1)} collective-permute-done((bf16[1024,384]{1,0:T(8,128)(2,1)S(1)}, bf16[1024,384]{1,0:T(8,128)(2,1)S(1)}, u32[]{:S(2)}, u32[]{:S(2)}) %collective-permute-start.2) | collective-permute-done | bytes 786464 | tf_op jit(solution)/shard_map/ppermute | solution.py:370
  93.8 3.4 %collective-permute-done.13 = bf16[1,32,3072]{2,1,0:T(8,128)(2,1)S(1)} collective-permute-done((bf16[1,32,3072]{2,1,0:T(8,128)(2,1)S(1)}, bf16[1,32,3072]{2,1,0:T(8,128)(2,1)S(1)}, u32[]{:S(2)}, u32[]{:S(2)}) %collective-permute-start.13) | collective-permute-done | bytes 196640 | tf_op jit(solution)/shard_map/ppermute | solution.py:293
  106.7 3.5 %extract.1 = bf16[64,64,128]{2,1,0:T(8,128)(2,1)S(1)} custom-call(s32[1]{0:T(128)} %bitcast.6.place_ref, bf16[2,32,3072]{2,1,0:T(8,128)(2,1)S(1)} %copy-done.3, bf16[2,32,3072]{2,1,0:T(8,128)(2,1)} %collective-permute-done.4.refs_1_, bf16[2,32,3072]{2,1,0:T(8,128)(2,1)S(1)} %pad_maximum_fusion.1.refs_2_, bf16[2,32,3072]{2,1,0:T(8,128)(2,1)S(1)} %copy-done.8, ...), custom_call_target="tpu_custom_call" | custom-call | flops 400000000 | bytes 4000000 | tf_op jit(solution)/shard_map/extract/pallas_call | solution.py:181
  111.2 2.9 %copy.12 = bf16[64,48,61]{2,1,0:T(8,128)(2,1)} copy(bf16[64,48,61]{1,0,2:T(8,128)(2,1)} %slice_bitcast_fusion) | data formatting | bytes 749568 | tf_op jit(solution)/shard_map/transpose | solution.py:390
  114.2 2.6 %reshape.77 = bf16[64,2928]{1,0:T(8,128)(2,1)} reshape(bf16[64,48,61]{2,1,0:T(8,128)(2,1)} %copy.12) | data formatting | bytes 749568 | tf_op jit(solution)/shard_map/reshape | solution.py:390
  119.9 5.8 %collective-permute-done.20 = bf16[64,384]{1,0:T(8,128)(2,1)} collective-permute-done((bf16[64,384]{1,0:T(8,128)(2,1)}, bf16[64,384]{1,0:T(8,128)(2,1)}, u32[]{:S(2)}, u32[]{:S(2)}) %collective-permute-start.20) | collective-permute-done | bytes 49184 | tf_op jit(solution)/shard_map/ppermute | solution.py:367
  125.7 1.5 collective-permute-start.19
  129.5 2.4 %collective-permute-done.19.refs_0_ = bf16[64,384]{1,0:T(8,128)(2,1)S(1)} collective-permute-done((bf16[64,384]{1,0:T(8,128)(2,1)}, bf16[64,384]{1,0:T(8,128)(2,1)S(1)}, u32[]{:S(2)}, u32[]{:S(2)}) %collective-permute-start.19) | collective-permute-done | bytes 49184 | tf_op jit(solution)/shard_map/ppermute | solution.py:366
  131.9 1.5 fold.5.refs_10_
  133.5 10.7 %correlate.2 = bf16[64,2048]{1,0:T(8,128)(2,1)S(1)} custom-call(s32[3]{0:T(128)S(1)} %pad_add_fusion.2.place_ref, bf16[2,32,3072]{2,1,0:T(8,128)(2,1)} %pad_maximum_fusion.2.refs_0_, bf16[2,32,3072]{2,1,0:T(8,128)(2,1)} %collective-permute-done.12.refs_1_, bf16[2,32,3072]{2,1,0:T(8,128)(2,1)} %pad_maximum_fusion.3.refs_2_, ...), custom_call_target="tpu_custom_call" | custom-call | flops 8000000000 | bytes 8000000 | tf_op jit(solution)/shard_map/correlate/pallas_call | solution.py:273
  144.2 2.1 %collective-permute-start.21 = (bf16[64,2048]{1,0:T(8,128)(2,1)S(1)}, bf16[64,2048]{1,0:T(8,128)(2,1)S(1)}, u32[]{:S(2)}, u32[]{:S(2)}) collective-permute-start(bf16[64,2048]{1,0:T(8,128)(2,1)S(1)} %correlate.2), channel_id=1, source_target_pairs={{2,0},{3,1},{0,2},{1,3},{6,4},{7,5},{4,6},{5,7},{10,8},{11,9},{8,1... | collective-permute-start | bytes 786440 | tf_op jit(solution)/shard_map/ppermute | solution.py:398
  146.3 11.6 %correlate.3 = f32[64,4096]{1,0:T(8,128)} custom-call(s32[3]{0:T(128)S(1)} %pad_add_fusion.place_ref, bf16[2,32,3072]{2,1,0:T(8,128)(2,1)S(1)} %copy-done.4, bf16[2,32,3072]{2,1,0:T(8,128)(2,1)} %collective-permute-done.4.refs_1_, bf16[2,32,3072]{2,1,0:T(8,128)(2,1)S(1)} %pad_maximum_fusion.1.refs_2_, bf16[2,32,3072]{2,1,0:T(8,128)(2,1)S(1)} %copy-done.9, ...), custom_call_target="tpu_custom_call" | custom-call | flops 8000000000 | bytes 8000000 | tf_op jit(solution)/shard_map/correlate/pallas_call | solution.py:273
  (98 shorter events, 31.5 us)
Async XLA Ops:
  2.4 14.4 %all-to-all-start = ((s32[32,1,8]{2,1,0:T(1,128)}), s32[32,1,8]{2,1,0:T(1,128)S(1)}, u32[]{:S(2)}, u32[]{:S(2)}) async-start(s32[32,1,8]{2,1,0:T(1,128)} %bitcast.1), calls=%async_computation | async-start | bytes 32768 | tf_op jit(solution)/shard_map/all_to_all | solution.py:352
  17.1 40.5 %all-to-all-start.1 = ((bf16[32,64,384]{2,1,0:T(8,128)(2,1)}), bf16[32,64,384]{2,1,0:T(8,128)(2,1)S(1)}, u32[]{:S(2)}, u32[]{:S(2)}) async-start(bf16[32,64,384]{2,1,0:T(8,128)(2,1)} %bitcast.3), calls=%async_computation.1 | async-start | bytes 3145728 | tf_op jit(solution)/shard_map/all_to_all | solution.py:355
  58.9 21.0 %collective-permute-start.1 = (bf16[64,3072]{1,0:T(8,128)(2,1)S(1)}, bf16[64,3072]{1,0:T(8,128)(2,1)S(1)}, u32[]{:S(2)}, u32[]{:S(2)}) collective-permute-start(bf16[64,3072]{1,0:T(8,128)(2,1)S(1)} %refine.1), channel_id=1, source_target_pairs={{0,2},{1,3},{2,0},{3,1},{4,6},{5,7},{6,4},{7,5},{8,10},{9,11},{10,... | collective-permute-start | bytes 1179656 | tf_op jit(solution)/shard_map/ppermute | solution.py:385
  61.5 6.8 %collective-permute-start.5 = (bf16[1,32,3072]{2,1,0:T(8,128)(2,1)S(1)}, bf16[1,32,3072]{2,1,0:T(8,128)(2,1)S(1)}, u32[]{:S(2)}, u32[]{:S(2)}) collective-permute-start(bf16[1,32,3072]{2,1,0:T(8,128)(2,1)S(1)} %get-tuple-element.50), channel_id=1, source_target_pairs={{0,8},{4,12},{8,0},{12,4},{16,24},{20,28},{24,16},{28,20},{1,9},{5... | collective-permute-start | bytes 589832 | tf_op jit(solution)/shard_map/ppermute | solution.py:293
  63.0 6.5 %collective-permute-start.3 = (bf16[1,32,3072]{2,1,0:T(8,128)(2,1)S(1)}, bf16[1,32,3072]{2,1,0:T(8,128)(2,1)S(1)}, u32[]{:S(2)}, u32[]{:S(2)}) collective-permute-start(bf16[1,32,3072]{2,1,0:T(8,128)(2,1)S(1)} %get-tuple-element.51), channel_id=1, source_target_pairs={{0,16},{4,20},{8,24},{12,28},{16,0},{20,4},{24,8},{28,12},{1,17},{... | collective-permute-start | bytes 589832 | tf_op jit(solution)/shard_map/ppermute | solution.py:293
  64.5 26.8 %collective-permute-start.2 = (bf16[1024,384]{1,0:T(8,128)(2,1)S(1)}, bf16[1024,384]{1,0:T(8,128)(2,1)S(1)}, u32[]{:S(2)}, u32[]{:S(2)}) collective-permute-start(bf16[1024,384]{1,0:T(8,128)(2,1)S(1)} %get-tuple-element.46), channel_id=1, source_target_pairs={{0,1},{1,0},{2,3},{3,2},{4,5},{5,4},{6,7},{7,6},{8,9},{9,8},{10,11... | collective-permute-start | bytes 2359304 | tf_op jit(solution)/shard_map/ppermute | solution.py:370
  68.4 11.6 %collective-permute-start.6 = (bf16[2,32,3072]{2,1,0:T(8,128)(2,1)S(1)}, bf16[2,32,3072]{2,1,0:T(8,128)(2,1)S(1)}, u32[]{:S(2)}, u32[]{:S(2)}) collective-permute-start(bf16[2,32,3072]{2,1,0:T(8,128)(2,1)S(1)} %pad_maximum_fusion.1.refs_2_), channel_id=1, source_target_pairs={{0,16},{4,20},{8,24},{12,28},{16,0},{20,4},{24,8},{28,12},{1,17},{... | collective-permute-start | bytes 1179656 | tf_op jit(solution)/shard_map/ppermute | solution.py:293
  69.5 10.4 %collective-permute-start.4 = (bf16[2,32,3072]{2,1,0:T(8,128)(2,1)S(1)}, bf16[2,32,3072]{2,1,0:T(8,128)(2,1)}, u32[]{:S(2)}, u32[]{:S(2)}) collective-permute-start(bf16[2,32,3072]{2,1,0:T(8,128)(2,1)S(1)} %pad_maximum_fusion.refs_0_), channel_id=1, source_target_pairs={{0,8},{4,12},{8,0},{12,4},{16,24},{20,28},{24,16},{28,20},{1,9},{5... | collective-permute-start | bytes 1179656 | tf_op jit(solution)/shard_map/ppermute | solution.py:293
  91.4 5.7 %collective-permute-start.13 = (bf16[1,32,3072]{2,1,0:T(8,128)(2,1)S(1)}, bf16[1,32,3072]{2,1,0:T(8,128)(2,1)S(1)}, u32[]{:S(2)}, u32[]{:S(2)}) collective-permute-start(bf16[1,32,3072]{2,1,0:T(8,128)(2,1)S(1)} %get-tuple-element.48), channel_id=1, source_target_pairs={{0,8},{4,12},{8,0},{12,4},{16,24},{20,28},{24,16},{28,20},{1,9},{5... | collective-permute-start | bytes 589832 | tf_op jit(solution)/shard_map/ppermute | solution.py:293
  92.4 24.4 %collective-permute-start = (bf16[1024,384]{1,0:T(8,128)(2,1)}, bf16[1024,384]{1,0:T(8,128)(2,1)}, u32[]{:S(2)}, u32[]{:S(2)}) collective-permute-start(bf16[1024,384]{1,0:T(8,128)(2,1)} %get-tuple-element.47), channel_id=1, source_target_pairs={{0,1},{1,0},{2,3},{3,2},{4,5},{5,4},{6,7},{7,6},{8,9},{9,8},{10,11... | collective-permute-start | bytes 2359304 | tf_op jit(solution)/shard_map/ppermute | solution.py:371
  92.4 5.7 %collective-permute-start.11 = (bf16[1,32,3072]{2,1,0:T(8,128)(2,1)S(1)}, bf16[1,32,3072]{2,1,0:T(8,128)(2,1)S(1)}, u32[]{:S(2)}, u32[]{:S(2)}) collective-permute-start(bf16[1,32,3072]{2,1,0:T(8,128)(2,1)S(1)} %get-tuple-element.49), channel_id=1, source_target_pairs={{0,16},{4,20},{8,24},{12,28},{16,0},{20,4},{24,8},{28,12},{1,17},{... | collective-permute-start | bytes 589832 | tf_op jit(solution)/shard_map/ppermute | solution.py:293
  93.3 6.0 %collective-permute-start.10 = (bf16[2,32,3072]{2,1,0:T(8,128)(2,1)S(1)}, bf16[2,32,3072]{2,1,0:T(8,128)(2,1)S(1)}, u32[]{:S(2)}, u32[]{:S(2)}) collective-permute-start(bf16[2,32,3072]{2,1,0:T(8,128)(2,1)S(1)} %collective-permute-done.6.refs_3_), channel_id=1, source_target_pairs={{0,4},{4,0},{8,12},{12,8},{16,20},{20,16},{24,28},{28,24},{1,5},{5... | collective-permute-start | bytes 1179656 | tf_op jit(solution)/shard_map/ppermute | solution.py:293
  93.3 7.9 %collective-permute-start.7 = (bf16[2,32,3072]{2,1,0:T(8,128)(2,1)S(1)}, bf16[2,32,3072]{2,1,0:T(8,128)(2,1)S(1)}, u32[]{:S(2)}, u32[]{:S(2)}) collective-permute-start(bf16[2,32,3072]{2,1,0:T(8,128)(2,1)S(1)} %pad_maximum_fusion.refs_0_), channel_id=1, source_target_pairs={{0,4},{4,0},{8,12},{12,8},{16,20},{20,16},{24,28},{28,24},{1,5},{5... | collective-permute-start | bytes 1179656 | tf_op jit(solution)/shard_map/ppermute | solution.py:293
  97.2 5.5 %collective-permute-start.8 = (bf16[2,32,3072]{2,1,0:T(8,128)(2,1)}, bf16[2,32,3072]{2,1,0:T(8,128)(2,1)}, u32[]{:S(2)}, u32[]{:S(2)}) collective-permute-start(bf16[2,32,3072]{2,1,0:T(8,128)(2,1)} %collective-permute-done.4.refs_1_), channel_id=1, source_target_pairs={{0,4},{4,0},{8,12},{12,8},{16,20},{20,16},{24,28},{28,24},{1,5},{5... | collective-permute-start | bytes 1179656 | tf_op jit(solution)/shard_map/ppermute | solution.py:293
  98.0 4.6 %collective-permute-start.9 = (bf16[2,32,3072]{2,1,0:T(8,128)(2,1)S(1)}, bf16[2,32,3072]{2,1,0:T(8,128)(2,1)}, u32[]{:S(2)}, u32[]{:S(2)}) collective-permute-start(bf16[2,32,3072]{2,1,0:T(8,128)(2,1)S(1)} %pad_maximum_fusion.1.refs_2_), channel_id=1, source_target_pairs={{0,4},{4,0},{8,12},{12,8},{16,20},{20,16},{24,28},{28,24},{1,5},{5... | collective-permute-start | bytes 1179656 | tf_op jit(solution)/shard_map/ppermute | solution.py:293
  100.0 16.7 %collective-permute-start.14 = (bf16[2,32,3072]{2,1,0:T(8,128)(2,1)}, bf16[2,32,3072]{2,1,0:T(8,128)(2,1)}, u32[]{:S(2)}, u32[]{:S(2)}) collective-permute-start(bf16[2,32,3072]{2,1,0:T(8,128)(2,1)} %pad_maximum_fusion.3.refs_2_), channel_id=1, source_target_pairs={{0,16},{4,20},{8,24},{12,28},{16,0},{20,4},{24,8},{28,12},{1,17},{... | collective-permute-start | bytes 1179656 | tf_op jit(solution)/shard_map/ppermute | solution.py:293
  102.0 14.8 %collective-permute-start.12 = (bf16[2,32,3072]{2,1,0:T(8,128)(2,1)}, bf16[2,32,3072]{2,1,0:T(8,128)(2,1)}, u32[]{:S(2)}, u32[]{:S(2)}) collective-permute-start(bf16[2,32,3072]{2,1,0:T(8,128)(2,1)} %pad_maximum_fusion.2.refs_0_), channel_id=1, source_target_pairs={{0,8},{4,12},{8,0},{12,4},{16,24},{20,28},{24,16},{28,20},{1,9},{5... | collective-permute-start | bytes 1179656 | tf_op jit(solution)/shard_map/ppermute | solution.py:293
  116.7 16.7 %collective-permute-start.15 = (bf16[2,32,3072]{2,1,0:T(8,128)(2,1)}, bf16[2,32,3072]{2,1,0:T(8,128)(2,1)}, u32[]{:S(2)}, u32[]{:S(2)}) collective-permute-start(bf16[2,32,3072]{2,1,0:T(8,128)(2,1)} %pad_maximum_fusion.2.refs_0_), channel_id=1, source_target_pairs={{0,4},{4,0},{8,12},{12,8},{16,20},{20,16},{24,28},{28,24},{1,5},{5... | collective-permute-start | bytes 1179656 | tf_op jit(solution)/shard_map/ppermute | solution.py:293
  116.8 16.7 %collective-permute-start.16 = (bf16[2,32,3072]{2,1,0:T(8,128)(2,1)}, bf16[2,32,3072]{2,1,0:T(8,128)(2,1)}, u32[]{:S(2)}, u32[]{:S(2)}) collective-permute-start(bf16[2,32,3072]{2,1,0:T(8,128)(2,1)} %collective-permute-done.12.refs_1_), channel_id=1, source_target_pairs={{0,4},{4,0},{8,12},{12,8},{16,20},{20,16},{24,28},{28,24},{1,5},{5... | collective-permute-start | bytes 1179656 | tf_op jit(solution)/shard_map/ppermute | solution.py:293
  117.3 16.2 %collective-permute-start.17 = (bf16[2,32,3072]{2,1,0:T(8,128)(2,1)}, bf16[2,32,3072]{2,1,0:T(8,128)(2,1)}, u32[]{:S(2)}, u32[]{:S(2)}) collective-permute-start(bf16[2,32,3072]{2,1,0:T(8,128)(2,1)} %pad_maximum_fusion.3.refs_2_), channel_id=1, source_target_pairs={{0,4},{4,0},{8,12},{12,8},{16,20},{20,16},{24,28},{28,24},{1,5},{5... | collective-permute-start | bytes 1179656 | tf_op jit(solution)/shard_map/ppermute | solution.py:293
  117.4 16.1 %collective-permute-start.18 = (bf16[2,32,3072]{2,1,0:T(8,128)(2,1)}, bf16[2,32,3072]{2,1,0:T(8,128)(2,1)}, u32[]{:S(2)}, u32[]{:S(2)}) collective-permute-start(bf16[2,32,3072]{2,1,0:T(8,128)(2,1)} %collective-permute-done.14.refs_3_), channel_id=1, source_target_pairs={{0,4},{4,0},{8,12},{12,8},{16,20},{20,16},{24,28},{28,24},{1,5},{5... | collective-permute-start | bytes 1179656 | tf_op jit(solution)/shard_map/ppermute | solution.py:293
  118.5 7.2 %collective-permute-start.20 = (bf16[64,384]{1,0:T(8,128)(2,1)}, bf16[64,384]{1,0:T(8,128)(2,1)}, u32[]{:S(2)}, u32[]{:S(2)}) collective-permute-start(bf16[64,384]{1,0:T(8,128)(2,1)} %slice.31), channel_id=1, source_target_pairs={{2,0},{4,2},{6,4},{8,6},{10,8},{12,10},{14,12},{16,14},{18,16},{20... | collective-permute-start | bytes 147464 | tf_op jit(solution)/shard_map/ppermute | solution.py:367
  125.7 6.2 %collective-permute-start.19 = (bf16[64,384]{1,0:T(8,128)(2,1)}, bf16[64,384]{1,0:T(8,128)(2,1)S(1)}, u32[]{:S(2)}, u32[]{:S(2)}) collective-permute-start(bf16[64,384]{1,0:T(8,128)(2,1)} %slice.31), channel_id=1, source_target_pairs={{1,0},{2,1},{3,2},{4,3},{5,4},{6,5},{7,6},{8,7},{9,8},{10,9},{11,1... | collective-permute-start | bytes 147464 | tf_op jit(solution)/shard_map/ppermute | solution.py:366
  144.2 14.3 %collective-permute-start.21 = (bf16[64,2048]{1,0:T(8,128)(2,1)S(1)}, bf16[64,2048]{1,0:T(8,128)(2,1)S(1)}, u32[]{:S(2)}, u32[]{:S(2)}) collective-permute-start(bf16[64,2048]{1,0:T(8,128)(2,1)S(1)} %correlate.2), channel_id=1, source_target_pairs={{2,0},{3,1},{0,2},{1,3},{6,4},{7,5},{4,6},{5,7},{10,8},{11,9},{8,1... | collective-permute-start | bytes 786440 | tf_op jit(solution)/shard_map/ppermute | solution.py:398
  (18 other events, 128.5 us)

commit v9 on v8

--- a/solution.py
+++ b/solution.py
@@ -351,7 +351,11 @@
     tags = tags.reshape(devices, CAP)
     tags = lax.all_to_all(tags, AXES, split_axis=0, concat_axis=0, tiled=True)
     key = (tags[:, :, None] * tpd + jnp.arange(tpd)[None, None, :]).reshape(1, -1)
-    send, key, before = lax.optimization_barrier((send, key, old_templates))
+    send, key, before, ahead_rows = lax.optimization_barrier((send, key, old_templates, recording))
+    pairs = [(i, i ^ 1) for i in range(owners)]
+    unit_rows = 16 * ROWS
+    cuts = [0, *(sub_rows * n // 16 // unit_rows * unit_rows for n in (4, 9)), sub_rows]
+    ahead_rows = lax.ppermute(ahead_rows[: cuts[1]], "unit", pairs)
     got = lax.all_to_all(
         send.reshape(devices, CAP * tpd, chans), AXES, split_axis=0, concat_axis=0, tiled=True
     ).reshape(devices * CAP * tpd, chans)
@@ -361,14 +365,12 @@
     cube = lax.dynamic_slice_in_dim(cube, tm_pos * tpd, tpd, 2)
     old = jnp.transpose(cube, (0, 2, 1)).reshape(panel, tpd * chans)
 
-    got, rest, old = lax.optimization_barrier((got, recording, old))
+    got, rest, old, ahead_rows = lax.optimization_barrier((got, recording, old, ahead_rows))
     head = rest[:padded]
     follow = lax.ppermute(head, AXES, [(i, i - 1) for i in range(1, devices)])
     skip = lax.ppermute(head, AXES, [(i, i - 2) for i in range(2, devices, 2)])
-    pairs = [(i, i ^ 1) for i in range(owners)]
-    first = sub_rows // 2 // (16 * ROWS) * (16 * ROWS)
-    early = lax.ppermute(rest[:first], "unit", pairs)
-    late = lax.ppermute(rest[first:], "unit", pairs)
+    early = lax.ppermute(rest[cuts[1] : cuts[2]], "unit", pairs)
+    late = lax.ppermute(rest[cuts[2] :], "unit", pairs)
     odd = unit_pos % 2
 
     fresh = refine(key, got, old, tpd)
@@ -384,12 +386,12 @@
         back = [(j, i) for i, j in ahead]
         chunk = lax.ppermute(fresh, "unit", ahead)
         if m == 1:
-            own, chunk, mine, early = tie(own, chunk, mine, early)
+            own, chunk, mine, early, follow, skip = tie(own, chunk, mine, early, follow, skip)
             own = across(own)
             part = extract(tm_pos.astype(jnp.int32).reshape(1), own, chans, tpd, share)
             part = jnp.transpose(part[:taps, :, :share], (1, 2, 0)).reshape(panel, share * taps)
             other, late, part = tie(spread(chunk), late, part)
-            windows = (mine, fold(early), fold(follow, late, jnp.where(odd == 1, head, skip)))
+            windows = (mine, fold(ahead_rows, early), fold(follow, late, jnp.where(odd == 1, head, skip)))
         else:
             other = spread(chunk)
         other = across(other)

time: 160 us -> 156 us (0.975)
  waiting for transfers between devices: 38.6 us -> 30.2 us
  local copies, waits for them, and re-layouts: 52.1 us -> 56.6 us
    ppermute x1, waiting for transfers between devices: 2.4 us -> 14.6 us  [body(): follow = lax.ppermute(head, AXES, [(i, i - 1) for i in range(1, devices)])]
    ppermute x2 -> x3, waiting for transfers between devices: 11.4 us -> 0.01 us  [the longest x1 0.01 us: body(): early = lax.ppermute(rest[cuts[1]:cuts[2]], 'unit', pairs)]
    ppermute x1, waiting for transfers between devices: 8.8 us -> 0.01 us  [body(): chunk = lax.ppermute(fresh, 'unit', ahead)]
    unnamed x37 -> x49, local copies, waits for them, and re-layouts: 14.5 us -> 18.9 us
    all_to_all x1, waiting for transfers between devices: 2.2 us -> 0.01 us  [body(): lax.all_to_all(send.reshape(devices, CAP * tpd, chans), AXES, split_axis=...]
    ppermute x1, waiting for transfers between devices: 0.61 us -> 2.21 us  [body(): lax.ppermute(out, 'unit', back)]
  transfers between devices with their start and end apart: 24 -> 25, of which waited for: 11 -> 8; matrix products, arithmetic and copies ran while one was open for 28% -> 29% of each run, Pallas kernels for 13% -> 13%
where the time goes in v9:
time: 156 us; the launch traced here: 155 us
  local copies, waits for them, and re-layouts  56.6 us (36%)
  Pallas kernels  32.8 us (21%)
  waiting for transfers between devices  30.2 us (19%)
  starting transfers between devices  29.5 us (19%)
  other arithmetic  4.68 us (3%)
    pallas_call x2, Pallas kernels, correlate(): pl.pallas_call(functools.partial(correlate_kernel, chans, tpd, scale, mas...  22.5 us
    reshape x1, local copies, waits for them, and re-layouts, body(): cube = before.reshape(panel, chans, taps)  20.6 us
    unnamed x49, local copies, waits for them, and re-layouts  18.9 us
    ppermute x1, waiting for transfers between devices, body(): follow = lax.ppermute(head, AXES, [(i, i - 1) for i in range(1, devices)])  14.6 us
    ppermute x16, starting transfers between devices, swap(): return lax.ppermute(value, 'tm', [(i, i ^ bit) for i in range(size)])  9.37 us
    transpose x1, local copies, waits for them, and re-layouts, body(): old = jnp.transpose(cube, (0, 2, 1)).reshape(panel, tpd * chans)  7.93 us
    all_to_all x1, starting transfers between devices, body(): tags = lax.all_to_all(tags, AXES, split_axis=0, concat_axis=0, tiled=True)  7.3 us
    ppermute x16, waiting for transfers between devices, swap(): return lax.ppermute(value, 'tm', [(i, i ^ bit) for i in range(size)])  7.24 us
  transfers between devices with their start and end apart: 25, of which 8 were waited for; matrix products, arithmetic and copies ran while one was open for 29% of the time, Pallas kernels for 13%

profile of v9, /device:TPU:0, one launch (start us, length us, event | category | flops | bytes accessed | tf_op | source)
XLA Modules:
  0.0 154.8 jit_solution(14553357838243192803)
XLA Ops:
  2.4 7.3 %all-to-all-start = ((s32[32,1,8]{2,1,0:T(1,128)}), s32[32,1,8]{2,1,0:T(1,128)S(1)}, u32[]{:S(2)}, u32[]{:S(2)}) async-start(s32[32,1,8]{2,1,0:T(1,128)} %bitcast.1), calls=%async_computation | async-start | bytes 32768 | tf_op jit(solution)/shard_map/all_to_all | solution.py:352
  9.8 1.4 copy-done
  12.5 3.1 %pack.1 = bf16[2048,384]{1,0:T(8,128)(2,1)} custom-call(s32[32]{0:T(128)S(1)} %copy-done.22, s32[32]{0:T(128)S(1)} %copy-done.21, s32[1]{0:T(128)} %bitcast.base_ref, bf16[2048,384]{1,0:T(8,128)(2,1)S(1)} %copy-done), custom_call_target="tpu_custom_call" | custom-call | flops 100000000 | bytes 4000000 | tf_op jit(solution)/shard_map/pack/pallas_call | solution.py:66
  17.1 4.6 %all-to-all-start.1 = ((bf16[32,64,384]{2,1,0:T(8,128)(2,1)}), bf16[32,64,384]{2,1,0:T(8,128)(2,1)S(1)}, u32[]{:S(2)}, u32[]{:S(2)}) async-start(bf16[32,64,384]{2,1,0:T(8,128)(2,1)} %bitcast.3), calls=%async_computation.1 | async-start | bytes 3145728 | tf_op jit(solution)/shard_map/all_to_all | solution.py:359
  22.5 1.8 %collective-permute-start = (bf16[512,384]{1,0:T(8,128)(2,1)}, bf16[512,384]{1,0:T(8,128)(2,1)S(1)}, u32[]{:S(2)}, u32[]{:S(2)}) collective-permute-start(bf16[512,384]{1,0:T(8,128)(2,1)} %slice.27), channel_id=1, source_target_pairs={{0,1},{1,0},{2,3},{3,2},{4,5},{5,4},{6,7},{7,6},{8,9},{9,8},{10,11... | collective-permute-start | bytes 1179656 | tf_op jit(solution)/shard_map/ppermute | solution.py:358
  24.2 20.6 %reshape.74 = bf16[64,384,61]{2,1,0:T(8,128)(2,1)} reshape(bf16[64,23424]{1,0:T(8,128)(2,1)} %param.7) | data formatting | bytes 5996544 | tf_op jit(solution)/shard_map/reshape | solution.py:363
  44.8 7.9 %dynamic-slice_bitcast_fusion = bf16[64,8,384]{1,2,0:T(8,128)(2,1)} fusion(s32[]{:T(128)S(6)} %select_n.50, bf16[64,384,61]{2,1,0:T(8,128)(2,1)} %reshape.74), kind=kLoop, calls=%fused_computation | loop fusion | bytes 3391492 | tf_op jit(solution)/shard_map/transpose | solution.py:366
  52.8 6.1 %copy.13 = bf16[8,8,8,384]{3,1,2,0:T(8,128)(2,1)} copy(bf16[8,8,8,384]{2,3,1,0:T(8,128)(2,1)} %bitcast.25) | data formatting | bytes 786432
  61.3 1.5 collective-permute-start.8
  62.9 2.4 %collective-permute-start.2 = (bf16[64,3072]{1,0:T(8,128)(2,1)S(1)}, bf16[64,3072]{1,0:T(8,128)(2,1)S(1)}, u32[]{:S(2)}, u32[]{:S(2)}) collective-permute-start(bf16[64,3072]{1,0:T(8,128)(2,1)S(1)} %refine.1), channel_id=1, source_target_pairs={{0,2},{1,3},{2,0},{3,1},{4,6},{5,7},{6,4},{7,5},{8,10},{9,11},{10,... | collective-permute-start | bytes 1179656 | tf_op jit(solution)/shard_map/ppermute | solution.py:387
  65.4 1.6 %collective-permute-start.6 = (bf16[1,32,3072]{2,1,0:T(8,128)(2,1)S(1)}, bf16[1,32,3072]{2,1,0:T(8,128)(2,1)S(1)}, u32[]{:S(2)}, u32[]{:S(2)}) collective-permute-start(bf16[1,32,3072]{2,1,0:T(8,128)(2,1)S(1)} %get-tuple-element.57), channel_id=1, source_target_pairs={{0,16},{4,20},{8,24},{12,28},{16,0},{20,4},{24,8},{28,12},{1,17},{... | collective-permute-start | bytes 589832 | tf_op jit(solution)/shard_map/ppermute | solution.py:293
  68.5 1.6 %collective-permute-start.9 = (bf16[2,32,3072]{2,1,0:T(8,128)(2,1)S(1)}, bf16[2,32,3072]{2,1,0:T(8,128)(2,1)}, u32[]{:S(2)}, u32[]{:S(2)}) collective-permute-start(bf16[2,32,3072]{2,1,0:T(8,128)(2,1)S(1)} %pad_maximum_fusion.1.refs_2_), channel_id=1, source_target_pairs={{0,16},{4,20},{8,24},{12,28},{16,0},{20,4},{24,8},{28,12},{1,17},{... | collective-permute-start | bytes 1179656 | tf_op jit(solution)/shard_map/ppermute | solution.py:293
  70.1 2.3 %collective-permute-done.6 = bf16[1,32,3072]{2,1,0:T(8,128)(2,1)S(1)} collective-permute-done((bf16[1,32,3072]{2,1,0:T(8,128)(2,1)S(1)}, bf16[1,32,3072]{2,1,0:T(8,128)(2,1)S(1)}, u32[]{:S(2)}, u32[]{:S(2)}) %collective-permute-start.6) | collective-permute-done | bytes 196640 | tf_op jit(solution)/shard_map/ppermute | solution.py:293
  73.8 14.6 %collective-permute-done.4.refs_0_ = bf16[64,384]{1,0:T(8,128)(2,1)S(1)} collective-permute-done((bf16[64,384]{1,0:T(8,128)(2,1)S(1)}, bf16[64,384]{1,0:T(8,128)(2,1)S(1)}, u32[]{:S(2)}, u32[]{:S(2)}) %collective-permute-start.4) | collective-permute-done | bytes 49184 | tf_op jit(solution)/shard_map/ppermute | solution.py:370
  89.1 1.5 collective-permute-start.5
  91.1 4.8 %collective-permute-done.5 = bf16[64,384]{1,0:T(8,128)(2,1)S(1)} collective-permute-done((bf16[64,384]{1,0:T(8,128)(2,1)S(1)}, bf16[64,384]{1,0:T(8,128)(2,1)S(1)}, u32[]{:S(2)}, u32[]{:S(2)}) %collective-permute-start.5) | collective-permute-done | bytes 49184 | tf_op jit(solution)/shard_map/ppermute | solution.py:371
  98.6 3.1 %collective-permute-done.16 = bf16[1,32,3072]{2,1,0:T(8,128)(2,1)S(1)} collective-permute-done((bf16[1,32,3072]{2,1,0:T(8,128)(2,1)S(1)}, bf16[1,32,3072]{2,1,0:T(8,128)(2,1)S(1)}, u32[]{:S(2)}, u32[]{:S(2)}) %collective-permute-start.16) | collective-permute-done | bytes 196640 | tf_op jit(solution)/shard_map/ppermute | solution.py:293
  111.5 3.5 %extract.1 = bf16[64,64,128]{2,1,0:T(8,128)(2,1)S(1)} custom-call(s32[1]{0:T(128)} %bitcast.6.place_ref, bf16[2,32,3072]{2,1,0:T(8,128)(2,1)S(1)} %copy-done.3, bf16[2,32,3072]{2,1,0:T(8,128)(2,1)S(1)} %copy-done.10, bf16[2,32,3072]{2,1,0:T(8,128)(2,1)S(1)} %pad_maximum_fusion.1.refs_2_, bf16[2,32,3072]{2,1,0:T(8,128)(2,1)} %collective-permute-done.9.refs_3_, ...), custom_call_target="tpu_custom_call" | custom-call | flops 400000000 | bytes 4000000 | tf_op jit(solution)/shard_map/extract/pallas_call | solution.py:181
  116.0 3.0 %copy.12 = bf16[64,48,61]{2,1,0:T(8,128)(2,1)} copy(bf16[64,48,61]{1,0,2:T(8,128)(2,1)} %slice_bitcast_fusion) | data formatting | bytes 749568 | tf_op jit(solution)/shard_map/transpose | solution.py:392
  119.0 2.6 %reshape.77 = bf16[64,2928]{1,0:T(8,128)(2,1)} reshape(bf16[64,48,61]{2,1,0:T(8,128)(2,1)} %copy.12) | data formatting | bytes 749568 | tf_op jit(solution)/shard_map/reshape | solution.py:392
  126.9 1.5 fold.5.refs_10_
  128.4 10.7 %correlate.2 = bf16[64,2048]{1,0:T(8,128)(2,1)S(1)} custom-call(s32[3]{0:T(128)S(1)} %pad_add_fusion.2.place_ref, bf16[2,32,3072]{2,1,0:T(8,128)(2,1)} %pad_maximum_fusion.2.refs_0_, bf16[2,32,3072]{2,1,0:T(8,128)(2,1)} %collective-permute-done.15.refs_1_, bf16[2,32,3072]{2,1,0:T(8,128)(2,1)} %pad_maximum_fusion.3.refs_2_, ...), custom_call_target="tpu_custom_call" | custom-call | flops 8000000000 | bytes 8000000 | tf_op jit(solution)/shard_map/correlate/pallas_call | solution.py:273
  139.9 11.8 %correlate.3 = f32[64,4096]{1,0:T(8,128)} custom-call(s32[3]{0:T(128)S(1)} %pad_add_fusion.place_ref, bf16[2,32,3072]{2,1,0:T(8,128)(2,1)S(1)} %copy-done.4, bf16[2,32,3072]{2,1,0:T(8,128)(2,1)S(1)} %copy-done.11, bf16[2,32,3072]{2,1,0:T(8,128)(2,1)S(1)} %pad_maximum_fusion.1.refs_2_, bf16[2,32,3072]{2,1,0:T(8,128)(2,1)} %collective-permute-done.9.refs_3_, ...), custom_call_target="tpu_custom_call" | custom-call | flops 8000000000 | bytes 8000000 | tf_op jit(solution)/shard_map/correlate/pallas_call | solution.py:273
  151.8 2.2 %collective-permute-done.22 = bf16[64,2048]{1,0:T(8,128)(2,1)S(1)} collective-permute-done((bf16[64,2048]{1,0:T(8,128)(2,1)S(1)}, bf16[64,2048]{1,0:T(8,128)(2,1)S(1)}, u32[]{:S(2)}, u32[]{:S(2)}) %collective-permute-start.22) | collective-permute-done | bytes 262176 | tf_op jit(solution)/shard_map/ppermute | solution.py:400
  (114 shorter events, 32.4 us)
Async XLA Ops:
  2.4 14.4 %all-to-all-start = ((s32[32,1,8]{2,1,0:T(1,128)}), s32[32,1,8]{2,1,0:T(1,128)S(1)}, u32[]{:S(2)}, u32[]{:S(2)}) async-start(s32[32,1,8]{2,1,0:T(1,128)} %bitcast.1), calls=%async_computation | async-start | bytes 32768 | tf_op jit(solution)/shard_map/all_to_all | solution.py:352
  17.1 41.8 %all-to-all-start.1 = ((bf16[32,64,384]{2,1,0:T(8,128)(2,1)}), bf16[32,64,384]{2,1,0:T(8,128)(2,1)S(1)}, u32[]{:S(2)}, u32[]{:S(2)}) async-start(bf16[32,64,384]{2,1,0:T(8,128)(2,1)} %bitcast.3), calls=%async_computation.1 | async-start | bytes 3145728 | tf_op jit(solution)/shard_map/all_to_all | solution.py:359
  22.5 36.4 %collective-permute-start = (bf16[512,384]{1,0:T(8,128)(2,1)}, bf16[512,384]{1,0:T(8,128)(2,1)S(1)}, u32[]{:S(2)}, u32[]{:S(2)}) collective-permute-start(bf16[512,384]{1,0:T(8,128)(2,1)} %slice.27), channel_id=1, source_target_pairs={{0,1},{1,0},{2,3},{3,2},{4,5},{5,4},{6,7},{7,6},{8,9},{9,8},{10,11... | collective-permute-start | bytes 1179656 | tf_op jit(solution)/shard_map/ppermute | solution.py:358
  61.3 7.1 %collective-permute-start.8 = (bf16[1,32,3072]{2,1,0:T(8,128)(2,1)S(1)}, bf16[1,32,3072]{2,1,0:T(8,128)(2,1)S(1)}, u32[]{:S(2)}, u32[]{:S(2)}) collective-permute-start(bf16[1,32,3072]{2,1,0:T(8,128)(2,1)S(1)} %get-tuple-element.56), channel_id=1, source_target_pairs={{0,8},{4,12},{8,0},{12,4},{16,24},{20,28},{24,16},{28,20},{1,9},{5... | collective-permute-start | bytes 589832 | tf_op jit(solution)/shard_map/ppermute | solution.py:293
  62.9 33.1 %collective-permute-start.2 = (bf16[64,3072]{1,0:T(8,128)(2,1)S(1)}, bf16[64,3072]{1,0:T(8,128)(2,1)S(1)}, u32[]{:S(2)}, u32[]{:S(2)}) collective-permute-start(bf16[64,3072]{1,0:T(8,128)(2,1)S(1)} %refine.1), channel_id=1, source_target_pairs={{0,2},{1,3},{2,0},{3,1},{4,6},{5,7},{6,4},{7,5},{8,10},{9,11},{10,... | collective-permute-start | bytes 1179656 | tf_op jit(solution)/shard_map/ppermute | solution.py:387
  65.4 7.0 %collective-permute-start.6 = (bf16[1,32,3072]{2,1,0:T(8,128)(2,1)S(1)}, bf16[1,32,3072]{2,1,0:T(8,128)(2,1)S(1)}, u32[]{:S(2)}, u32[]{:S(2)}) collective-permute-start(bf16[1,32,3072]{2,1,0:T(8,128)(2,1)S(1)} %get-tuple-element.57), channel_id=1, source_target_pairs={{0,16},{4,20},{8,24},{12,28},{16,0},{20,4},{24,8},{28,12},{1,17},{... | collective-permute-start | bytes 589832 | tf_op jit(solution)/shard_map/ppermute | solution.py:293
  66.9 29.0 %collective-permute-start.3 = (bf16[640,384]{1,0:T(8,128)(2,1)S(1)}, bf16[640,384]{1,0:T(8,128)(2,1)S(1)}, u32[]{:S(2)}, u32[]{:S(2)}) collective-permute-start(bf16[640,384]{1,0:T(8,128)(2,1)S(1)} %slice.29), channel_id=1, source_target_pairs={{0,1},{1,0},{2,3},{3,2},{4,5},{5,4},{6,7},{7,6},{8,9},{9,8},{10,11... | collective-permute-start | bytes 1474568 | tf_op jit(solution)/shard_map/ppermute | solution.py:372
  68.5 27.5 %collective-permute-start.9 = (bf16[2,32,3072]{2,1,0:T(8,128)(2,1)S(1)}, bf16[2,32,3072]{2,1,0:T(8,128)(2,1)}, u32[]{:S(2)}, u32[]{:S(2)}) collective-permute-start(bf16[2,32,3072]{2,1,0:T(8,128)(2,1)S(1)} %pad_maximum_fusion.1.refs_2_), channel_id=1, source_target_pairs={{0,16},{4,20},{8,24},{12,28},{16,0},{20,4},{24,8},{28,12},{1,17},{... | collective-permute-start | bytes 1179656 | tf_op jit(solution)/shard_map/ppermute | solution.py:293
  72.5 23.5 %collective-permute-start.7 = (bf16[2,32,3072]{2,1,0:T(8,128)(2,1)S(1)}, bf16[2,32,3072]{2,1,0:T(8,128)(2,1)S(1)}, u32[]{:S(2)}, u32[]{:S(2)}) collective-permute-start(bf16[2,32,3072]{2,1,0:T(8,128)(2,1)S(1)} %pad_maximum_fusion.refs_0_), channel_id=1, source_target_pairs={{0,8},{4,12},{8,0},{12,4},{16,24},{20,28},{24,16},{28,20},{1,9},{5... | collective-permute-start | bytes 1179656 | tf_op jit(solution)/shard_map/ppermute | solution.py:293
  72.5 15.9 %collective-permute-start.4 = (bf16[64,384]{1,0:T(8,128)(2,1)S(1)}, bf16[64,384]{1,0:T(8,128)(2,1)S(1)}, u32[]{:S(2)}, u32[]{:S(2)}) collective-permute-start(bf16[64,384]{1,0:T(8,128)(2,1)S(1)} %slice.30), channel_id=1, source_target_pairs={{1,0},{2,1},{3,2},{4,3},{5,4},{6,5},{7,6},{8,7},{9,8},{10,9},{11,1... | collective-permute-start | bytes 147464 | tf_op jit(solution)/shard_map/ppermute | solution.py:370
  89.1 6.9 %collective-permute-start.5 = (bf16[64,384]{1,0:T(8,128)(2,1)S(1)}, bf16[64,384]{1,0:T(8,128)(2,1)S(1)}, u32[]{:S(2)}, u32[]{:S(2)}) collective-permute-start(bf16[64,384]{1,0:T(8,128)(2,1)S(1)} %slice.30), channel_id=1, source_target_pairs={{2,0},{4,2},{6,4},{8,6},{10,8},{12,10},{14,12},{16,14},{18,16},{20... | collective-permute-start | bytes 147464 | tf_op jit(solution)/shard_map/ppermute | solution.py:371
  96.0 5.7 %collective-permute-start.16 = (bf16[1,32,3072]{2,1,0:T(8,128)(2,1)S(1)}, bf16[1,32,3072]{2,1,0:T(8,128)(2,1)S(1)}, u32[]{:S(2)}, u32[]{:S(2)}) collective-permute-start(bf16[1,32,3072]{2,1,0:T(8,128)(2,1)S(1)} %get-tuple-element.54), channel_id=1, source_target_pairs={{0,8},{4,12},{8,0},{12,4},{16,24},{20,28},{24,16},{28,20},{1,9},{5... | collective-permute-start | bytes 589832 | tf_op jit(solution)/shard_map/ppermute | solution.py:293
  97.6 24.0 %collective-permute-start.1 = (bf16[896,384]{1,0:T(8,128)(2,1)}, bf16[896,384]{1,0:T(8,128)(2,1)}, u32[]{:S(2)}, u32[]{:S(2)}) collective-permute-start(bf16[896,384]{1,0:T(8,128)(2,1)} %slice.28), channel_id=1, source_target_pairs={{0,1},{1,0},{2,3},{3,2},{4,5},{5,4},{6,7},{7,6},{8,9},{9,8},{10,11... | collective-permute-start | bytes 2064392 | tf_op jit(solution)/shard_map/ppermute | solution.py:373
  97.6 5.7 %collective-permute-start.14 = (bf16[1,32,3072]{2,1,0:T(8,128)(2,1)S(1)}, bf16[1,32,3072]{2,1,0:T(8,128)(2,1)S(1)}, u32[]{:S(2)}, u32[]{:S(2)}) collective-permute-start(bf16[1,32,3072]{2,1,0:T(8,128)(2,1)S(1)} %get-tuple-element.55), channel_id=1, source_target_pairs={{0,16},{4,20},{8,24},{12,28},{16,0},{20,4},{24,8},{28,12},{1,17},{... | collective-permute-start | bytes 589832 | tf_op jit(solution)/shard_map/ppermute | solution.py:293
  98.1 5.9 %collective-permute-start.10 = (bf16[2,32,3072]{2,1,0:T(8,128)(2,1)S(1)}, bf16[2,32,3072]{2,1,0:T(8,128)(2,1)S(1)}, u32[]{:S(2)}, u32[]{:S(2)}) collective-permute-start(bf16[2,32,3072]{2,1,0:T(8,128)(2,1)S(1)} %pad_maximum_fusion.refs_0_), channel_id=1, source_target_pairs={{0,4},{4,0},{8,12},{12,8},{16,20},{20,16},{24,28},{28,24},{1,5},{5... | collective-permute-start | bytes 1179656 | tf_op jit(solution)/shard_map/ppermute | solution.py:293
  98.1 7.2 %collective-permute-start.11 = (bf16[2,32,3072]{2,1,0:T(8,128)(2,1)S(1)}, bf16[2,32,3072]{2,1,0:T(8,128)(2,1)S(1)}, u32[]{:S(2)}, u32[]{:S(2)}) collective-permute-start(bf16[2,32,3072]{2,1,0:T(8,128)(2,1)S(1)} %collective-permute-done.7.refs_1_), channel_id=1, source_target_pairs={{0,4},{4,0},{8,12},{12,8},{16,20},{20,16},{24,28},{28,24},{1,5},{5... | collective-permute-start | bytes 1179656 | tf_op jit(solution)/shard_map/ppermute | solution.py:293
  101.8 5.7 %collective-permute-start.12 = (bf16[2,32,3072]{2,1,0:T(8,128)(2,1)S(1)}, bf16[2,32,3072]{2,1,0:T(8,128)(2,1)}, u32[]{:S(2)}, u32[]{:S(2)}) collective-permute-start(bf16[2,32,3072]{2,1,0:T(8,128)(2,1)S(1)} %pad_maximum_fusion.1.refs_2_), channel_id=1, source_target_pairs={{0,4},{4,0},{8,12},{12,8},{16,20},{20,16},{24,28},{28,24},{1,5},{5... | collective-permute-start | bytes 1179656 | tf_op jit(solution)/shard_map/ppermute | solution.py:293
  104.8 16.8 %collective-permute-start.17 = (bf16[2,32,3072]{2,1,0:T(8,128)(2,1)}, bf16[2,32,3072]{2,1,0:T(8,128)(2,1)}, u32[]{:S(2)}, u32[]{:S(2)}) collective-permute-start(bf16[2,32,3072]{2,1,0:T(8,128)(2,1)} %pad_maximum_fusion.3.refs_2_), channel_id=1, source_target_pairs={{0,16},{4,20},{8,24},{12,28},{16,0},{20,4},{24,8},{28,12},{1,17},{... | collective-permute-start | bytes 1179656 | tf_op jit(solution)/shard_map/ppermute | solution.py:293
  106.1 15.5 %collective-permute-start.15 = (bf16[2,32,3072]{2,1,0:T(8,128)(2,1)}, bf16[2,32,3072]{2,1,0:T(8,128)(2,1)}, u32[]{:S(2)}, u32[]{:S(2)}) collective-permute-start(bf16[2,32,3072]{2,1,0:T(8,128)(2,1)} %pad_maximum_fusion.2.refs_0_), channel_id=1, source_target_pairs={{0,8},{4,12},{8,0},{12,4},{16,24},{20,28},{24,16},{28,20},{1,9},{5... | collective-permute-start | bytes 1179656 | tf_op jit(solution)/shard_map/ppermute | solution.py:293
  121.6 6.8 %collective-permute-start.18 = (bf16[2,32,3072]{2,1,0:T(8,128)(2,1)}, bf16[2,32,3072]{2,1,0:T(8,128)(2,1)}, u32[]{:S(2)}, u32[]{:S(2)}) collective-permute-start(bf16[2,32,3072]{2,1,0:T(8,128)(2,1)} %pad_maximum_fusion.2.refs_0_), channel_id=1, source_target_pairs={{0,4},{4,0},{8,12},{12,8},{16,20},{20,16},{24,28},{28,24},{1,5},{5... | collective-permute-start | bytes 1179656 | tf_op jit(solution)/shard_map/ppermute | solution.py:293
  121.7 6.7 %collective-permute-start.19 = (bf16[2,32,3072]{2,1,0:T(8,128)(2,1)}, bf16[2,32,3072]{2,1,0:T(8,128)(2,1)}, u32[]{:S(2)}, u32[]{:S(2)}) collective-permute-start(bf16[2,32,3072]{2,1,0:T(8,128)(2,1)} %collective-permute-done.15.refs_1_), channel_id=1, source_target_pairs={{0,4},{4,0},{8,12},{12,8},{16,20},{20,16},{24,28},{28,24},{1,5},{5... | collective-permute-start | bytes 1179656 | tf_op jit(solution)/shard_map/ppermute | solution.py:293
  122.2 6.2 %collective-permute-start.20 = (bf16[2,32,3072]{2,1,0:T(8,128)(2,1)}, bf16[2,32,3072]{2,1,0:T(8,128)(2,1)}, u32[]{:S(2)}, u32[]{:S(2)}) collective-permute-start(bf16[2,32,3072]{2,1,0:T(8,128)(2,1)} %pad_maximum_fusion.3.refs_2_), channel_id=1, source_target_pairs={{0,4},{4,0},{8,12},{12,8},{16,20},{20,16},{24,28},{28,24},{1,5},{5... | collective-permute-start | bytes 1179656 | tf_op jit(solution)/shard_map/ppermute | solution.py:293
  122.2 6.2 %collective-permute-start.21 = (bf16[2,32,3072]{2,1,0:T(8,128)(2,1)}, bf16[2,32,3072]{2,1,0:T(8,128)(2,1)}, u32[]{:S(2)}, u32[]{:S(2)}) collective-permute-start(bf16[2,32,3072]{2,1,0:T(8,128)(2,1)} %collective-permute-done.17.refs_3_), channel_id=1, source_target_pairs={{0,4},{4,0},{8,12},{12,8},{16,20},{20,16},{24,28},{28,24},{1,5},{5... | collective-permute-start | bytes 1179656 | tf_op jit(solution)/shard_map/ppermute | solution.py:293
  139.1 14.9 %collective-permute-start.22 = (bf16[64,2048]{1,0:T(8,128)(2,1)S(1)}, bf16[64,2048]{1,0:T(8,128)(2,1)S(1)}, u32[]{:S(2)}, u32[]{:S(2)}) collective-permute-start(bf16[64,2048]{1,0:T(8,128)(2,1)S(1)} %correlate.2), channel_id=1, source_target_pairs={{2,0},{3,1},{0,2},{1,3},{6,4},{7,5},{4,6},{5,7},{10,8},{11,9},{8,1... | collective-permute-start | bytes 786440 | tf_op jit(solution)/shard_map/ppermute | solution.py:400
  (25 other events, 138.1 us)

commit v10 on v9

--- a/solution.py
+++ b/solution.py
@@ -72,7 +72,7 @@
             pltpu.VMEM((rows, chans), jnp.float32),
             pltpu.SMEM((owners,), jnp.int32),
         ],
-        compiler_params=params(24),
+        compiler_params=params(16),
         cost_estimate=pl.CostEstimate(flops=10**8, bytes_accessed=4 * 10**6, transcendentals=0),
         name="pack",
     )(times, labels, base, rec)
@@ -148,7 +148,7 @@
         in_specs=[vmem] * 3,
         out_specs=vmem,
         scratch_shapes=[pltpu.VMEM((tpd * panel, got.shape[1]), jnp.float32)],
-        compiler_params=params(32),
+        compiler_params=params(20),
         cost_estimate=pl.CostEstimate(flops=8 * 10**8, bytes_accessed=3 * 10**6, transcendentals=0),
         name="refine",
     )(key, got, old)
@@ -282,7 +282,7 @@
             pltpu.VMEM((2 * height, FOLD * panel), jnp.float32),
             pltpu.VMEM((2 * keep, FOLD * panel), jnp.float32),
         ],
-        compiler_params=params(30),
+        compiler_params=params(22),
         cost_estimate=pl.CostEstimate(flops=8 * 10**9, bytes_accessed=8 * 10**6, transcendentals=0),
         name="correlate",
     )(place, *pieces, *windows)
@@ -366,12 +366,13 @@
     old = jnp.transpose(cube, (0, 2, 1)).reshape(panel, tpd * chans)
 
     got, rest, old, ahead_rows = lax.optimization_barrier((got, recording, old, ahead_rows))
-    head = rest[:padded]
-    follow = lax.ppermute(head, AXES, [(i, i - 1) for i in range(1, devices)])
-    skip = lax.ppermute(head, AXES, [(i, i - 2) for i in range(2, devices, 2)])
+    odd = unit_pos % 2
+    head, held = rest[:padded], ahead_rows[:padded]
+    beyond = lax.ppermute(
+        jnp.where(odd == 1, held, head), AXES, [(i, i - 2) for i in range(2, devices)]
+    )
     early = lax.ppermute(rest[cuts[1] : cuts[2]], "unit", pairs)
     late = lax.ppermute(rest[cuts[2] :], "unit", pairs)
-    odd = unit_pos % 2
 
     fresh = refine(key, got, old, tpd)
     rest, fresh = lax.optimization_barrier((rest, fresh))
@@ -386,12 +387,13 @@
         back = [(j, i) for i, j in ahead]
         chunk = lax.ppermute(fresh, "unit", ahead)
         if m == 1:
-            own, chunk, mine, early, follow, skip = tie(own, chunk, mine, early, follow, skip)
-            own = across(own)
+            own, chunk, mine, early = tie(across(own), chunk, mine, early)
             part = extract(tm_pos.astype(jnp.int32).reshape(1), own, chans, tpd, share)
             part = jnp.transpose(part[:taps, :, :share], (1, 2, 0)).reshape(panel, share * taps)
-            other, late, part = tie(spread(chunk), late, part)
-            windows = (mine, fold(ahead_rows, early), fold(follow, late, jnp.where(odd == 1, head, skip)))
+            other, late, part, beyond = tie(spread(chunk), late, part, beyond)
+            windows = (mine, fold(ahead_rows, early), fold(
+                jnp.where(odd == 1, beyond, held), late, jnp.where(odd == 1, head, beyond)
+            ))
         else:
             other = spread(chunk)
         other = across(other)

time: 156 us -> 156 us (level)
  starting transfers between devices: 29.5 us -> 34.1 us
  waiting for transfers between devices: 30.2 us -> 26.2 us
  other arithmetic: 4.68 us -> 8.04 us
  Pallas kernels: 32.8 us -> 30.9 us
  local copies, waits for them, and re-layouts: 56.6 us -> 54.9 us
    ppermute x2 -> x1, waiting for transfers between devices: 19.4 us -> 0.01 us  [body(): lax.ppermute(jnp.where(odd == 1, held, head), AXES, [(i, i - 2) for i in...]
    ppermute x1, waiting for transfers between devices: 0.01 us -> 9.01 us  [body(): chunk = lax.ppermute(fresh, 'unit', ahead)]
    ppermute x1, waiting for transfers between devices: 0.01 us -> 7.66 us  [body(): early = lax.ppermute(rest[cuts[1]:cuts[2]], 'unit', pairs)]
    ppermute x16, starting transfers between devices: 9.37 us -> 13.9 us  [swap(): return lax.ppermute(value, 'tm', [(i, i ^ bit) for i in range(size)])]
    unnamed x49 -> x61, local copies, waits for them, and re-layouts: 18.9 us -> 16.5 us
    concatenate x4, other arithmetic: 1.67 us -> 3.61 us  [spread(): jnp.concatenate([v for v, _ in parts], axis=0)]
  transfers between devices with their start and end apart: 25 -> 24, of which waited for: 8 -> 7; matrix products, arithmetic and copies ran while one was open for 29% -> 32% of each run, Pallas kernels for 13% -> 12%
where the time goes in v10:
time: 156 us; the launch traced here: 155 us
  local copies, waits for them, and re-layouts  54.9 us (35%)
  starting transfers between devices  34.1 us (22%)
  Pallas kernels  30.9 us (20%)
  waiting for transfers between devices  26.2 us (17%)
  other arithmetic  8.04 us (5%)
    pallas_call x2, Pallas kernels, correlate(): pl.pallas_call(functools.partial(correlate_kernel, chans, tpd, scale, mas...  21.8 us
    reshape x1, local copies, waits for them, and re-layouts, body(): cube = before.reshape(panel, chans, taps)  20.6 us
    unnamed x61, local copies, waits for them, and re-layouts  16.5 us
    ppermute x16, starting transfers between devices, swap(): return lax.ppermute(value, 'tm', [(i, i ^ bit) for i in range(size)])  13.9 us
    ppermute x1, waiting for transfers between devices, body(): chunk = lax.ppermute(fresh, 'unit', ahead)  9.01 us
    transpose x1, local copies, waits for them, and re-layouts, body(): old = jnp.transpose(cube, (0, 2, 1)).reshape(panel, tpd * chans)  7.96 us
    ppermute x1, waiting for transfers between devices, body(): early = lax.ppermute(rest[cuts[1]:cuts[2]], 'unit', pairs)  7.66 us
    all_to_all x1, starting transfers between devices, body(): tags = lax.all_to_all(tags, AXES, split_axis=0, concat_axis=0, tiled=True)  7.3 us
  transfers between devices with their start and end apart: 24, of which 7 were waited for; matrix products, arithmetic and copies ran while one was open for 32% of the time, Pallas kernels for 12%

profile of v10, /device:TPU:0, one launch (start us, length us, event | category | flops | bytes accessed | tf_op | source)
XLA Modules:
  0.0 155.2 jit_solution(17608235885944741658)
XLA Ops:
  2.4 7.3 %all-to-all-start = ((s32[32,1,8]{2,1,0:T(1,128)}), s32[32,1,8]{2,1,0:T(1,128)S(1)}, u32[]{:S(2)}, u32[]{:S(2)}) async-start(s32[32,1,8]{2,1,0:T(1,128)} %bitcast.1), calls=%async_computation | async-start | bytes 32768 | tf_op jit(solution)/shard_map/all_to_all | solution.py:352
  12.5 3.0 %pack.1 = bf16[2048,384]{1,0:T(8,128)(2,1)} custom-call(s32[32]{0:T(128)S(1)} %copy-done.29, s32[32]{0:T(128)S(1)} %copy-done.28, s32[1]{0:T(128)} %bitcast.base_ref, bf16[2048,384]{1,0:T(8,128)(2,1)S(1)} %copy-done), custom_call_target="tpu_custom_call" | custom-call | flops 100000000 | bytes 4000000 | tf_op jit(solution)/shard_map/pack/pallas_call | solution.py:66
  17.1 4.5 %all-to-all-start.1 = ((bf16[32,64,384]{2,1,0:T(8,128)(2,1)}), bf16[32,64,384]{2,1,0:T(8,128)(2,1)S(1)}, u32[]{:S(2)}, u32[]{:S(2)}) async-start(bf16[32,64,384]{2,1,0:T(8,128)(2,1)} %bitcast.3), calls=%async_computation.1 | async-start | bytes 3145728 | tf_op jit(solution)/shard_map/all_to_all | solution.py:359
  22.4 1.8 %collective-permute-start = (bf16[512,384]{1,0:T(8,128)(2,1)}, bf16[512,384]{1,0:T(8,128)(2,1)S(1)}, u32[]{:S(2)}, u32[]{:S(2)}) collective-permute-start(bf16[512,384]{1,0:T(8,128)(2,1)} %slice.30), channel_id=1, source_target_pairs={{0,1},{1,0},{2,3},{3,2},{4,5},{5,4},{6,7},{7,6},{8,9},{9,8},{10,11... | collective-permute-start | bytes 1179656 | tf_op jit(solution)/shard_map/ppermute | solution.py:358
  24.2 20.6 %reshape.74 = bf16[64,384,61]{2,1,0:T(8,128)(2,1)} reshape(bf16[64,23424]{1,0:T(8,128)(2,1)} %param.7) | data formatting | bytes 5996544 | tf_op jit(solution)/shard_map/reshape | solution.py:363
  44.8 8.0 %dynamic-slice_bitcast_fusion = bf16[64,8,384]{1,2,0:T(8,128)(2,1)} fusion(s32[]{:T(128)S(6)} %select_n.58, bf16[64,384,61]{2,1,0:T(8,128)(2,1)} %reshape.74), kind=kLoop, calls=%fused_computation | loop fusion | bytes 3391492 | tf_op jit(solution)/shard_map/transpose | solution.py:366
  52.7 6.1 %copy.13 = bf16[8,8,8,384]{3,1,2,0:T(8,128)(2,1)} copy(bf16[8,8,8,384]{2,3,1,0:T(8,128)(2,1)} %bitcast.25) | data formatting | bytes 786432
  61.9 1.5 collective-permute-start.6
  63.4 2.4 %collective-permute-start.2 = (bf16[64,3072]{1,0:T(8,128)(2,1)S(1)}, bf16[64,3072]{1,0:T(8,128)(2,1)S(1)}, u32[]{:S(2)}, u32[]{:S(2)}) collective-permute-start(bf16[64,3072]{1,0:T(8,128)(2,1)S(1)} %refine.1), channel_id=1, source_target_pairs={{0,2},{1,3},{2,0},{3,1},{4,6},{5,7},{6,4},{7,5},{8,10},{9,11},{10,... | collective-permute-start | bytes 1179656 | tf_op jit(solution)/shard_map/ppermute | solution.py:388
  68.7 1.5 collective-permute-start.7
  70.2 3.4 %collective-permute-done.4 = bf16[1,32,3072]{2,1,0:T(8,128)(2,1)S(1)} collective-permute-done((bf16[1,32,3072]{2,1,0:T(8,128)(2,1)S(1)}, bf16[1,32,3072]{2,1,0:T(8,128)(2,1)S(1)}, u32[]{:S(2)}, u32[]{:S(2)}) %collective-permute-start.4) | collective-permute-done | bytes 196640 | tf_op jit(solution)/shard_map/ppermute | solution.py:293
  74.5 9.0 %collective-permute-done.2 = bf16[64,3072]{1,0:T(8,128)(2,1)S(1)} collective-permute-done((bf16[64,3072]{1,0:T(8,128)(2,1)S(1)}, bf16[64,3072]{1,0:T(8,128)(2,1)S(1)}, u32[]{:S(2)}, u32[]{:S(2)}) %collective-permute-start.2) | collective-permute-done | bytes 393248 | tf_op jit(solution)/shard_map/ppermute | solution.py:388
  84.7 7.7 %collective-permute-done.3.refs_1_ = bf16[640,384]{1,0:T(8,128)(2,1)S(1)} collective-permute-done((bf16[640,384]{1,0:T(8,128)(2,1)S(1)}, bf16[640,384]{1,0:T(8,128)(2,1)S(1)}, u32[]{:S(2)}, u32[]{:S(2)}) %collective-permute-start.3) | collective-permute-done | bytes 491552 | tf_op jit(solution)/shard_map/ppermute | solution.py:374
  100.9 2.4 %collective-permute-done.15 = bf16[1,32,3072]{2,1,0:T(8,128)(2,1)} collective-permute-done((bf16[1,32,3072]{2,1,0:T(8,128)(2,1)}, bf16[1,32,3072]{2,1,0:T(8,128)(2,1)}, u32[]{:S(2)}, u32[]{:S(2)}) %collective-permute-start.15) | collective-permute-done | bytes 196640 | tf_op jit(solution)/shard_map/ppermute | solution.py:293
  103.3 1.8 %pad_maximum_fusion.3.refs_2_ = bf16[2,32,3072]{2,1,0:T(8,128)(2,1)} fusion(bf16[1,32,3072]{2,1,0:T(8,128)(2,1)} %collective-permute-done.15, bf16[1,32,3072]{2,1,0:T(8,128)(2,1)} %get-tuple-element.60), kind=kLoop, calls=%fused_computation.6 | loop fusion | flops 196608 | bytes 786432 | tf_op jit(solution)/shard_map/concatenate | solution.py:305
  106.4 1.7 %pad_maximum_fusion.2.refs_0_ = bf16[2,32,3072]{2,1,0:T(8,128)(2,1)} fusion(bf16[1,32,3072]{2,1,0:T(8,128)(2,1)S(1)} %collective-permute-done.13, bf16[1,32,3072]{2,1,0:T(8,128)(2,1)} %get-tuple-element.61), kind=kLoop, calls=%fused_computation.5 | loop fusion | flops 196608 | bytes 786432 | tf_op jit(solution)/shard_map/concatenate | solution.py:305
  108.2 1.7 %collective-permute-start.14 = (bf16[2,32,3072]{2,1,0:T(8,128)(2,1)}, bf16[2,32,3072]{2,1,0:T(8,128)(2,1)}, u32[]{:S(2)}, u32[]{:S(2)}) collective-permute-start(bf16[2,32,3072]{2,1,0:T(8,128)(2,1)} %pad_maximum_fusion.2.refs_0_), channel_id=1, source_target_pairs={{0,8},{4,12},{8,0},{12,4},{16,24},{20,28},{24,16},{28,20},{1,9},{5... | collective-permute-start | bytes 1179656 | tf_op jit(solution)/shard_map/ppermute | solution.py:293
  112.9 2.3 %extract.1 = bf16[64,64,128]{2,1,0:T(8,128)(2,1)S(1)} custom-call(s32[1]{0:T(128)} %bitcast.6.place_ref, bf16[2,32,3072]{2,1,0:T(8,128)(2,1)S(1)} %copy-done.3, bf16[2,32,3072]{2,1,0:T(8,128)(2,1)S(1)} %copy-done.13, bf16[2,32,3072]{2,1,0:T(8,128)(2,1)S(1)} %pad_maximum_fusion.1.refs_2_, bf16[2,32,3072]{2,1,0:T(8,128)(2,1)S(1)} %copy-done.10, ...), custom_call_target="tpu_custom_call" | custom-call | flops 400000000 | bytes 4000000 | tf_op jit(solution)/shard_map/extract/pallas_call | solution.py:181
  116.2 3.0 %copy.12 = bf16[64,48,61]{2,1,0:T(8,128)(2,1)} copy(bf16[64,48,61]{1,0,2:T(8,128)(2,1)} %slice_bitcast_fusion) | data formatting | bytes 749568 | tf_op jit(solution)/shard_map/transpose | solution.py:392
  119.2 2.6 %reshape.77 = bf16[64,2928]{1,0:T(8,128)(2,1)} reshape(bf16[64,48,61]{2,1,0:T(8,128)(2,1)} %copy.12) | data formatting | bytes 749568 | tf_op jit(solution)/shard_map/reshape | solution.py:392
  121.7 2.1 %collective-permute-start.17 = (bf16[2,32,3072]{2,1,0:T(8,128)(2,1)}, bf16[2,32,3072]{2,1,0:T(8,128)(2,1)}, u32[]{:S(2)}, u32[]{:S(2)}) collective-permute-start(bf16[2,32,3072]{2,1,0:T(8,128)(2,1)} %pad_maximum_fusion.2.refs_0_), channel_id=1, source_target_pairs={{0,4},{4,0},{8,12},{12,8},{16,20},{20,16},{24,28},{28,24},{1,5},{5... | collective-permute-start | bytes 1179656 | tf_op jit(solution)/shard_map/ppermute | solution.py:293
  129.4 10.7 %correlate.2 = bf16[64,2048]{1,0:T(8,128)(2,1)S(1)} custom-call(s32[3]{0:T(128)S(1)} %pad_add_fusion.2.place_ref, bf16[2,32,3072]{2,1,0:T(8,128)(2,1)} %pad_maximum_fusion.2.refs_0_, bf16[2,32,3072]{2,1,0:T(8,128)(2,1)} %collective-permute-done.14.refs_1_, bf16[2,32,3072]{2,1,0:T(8,128)(2,1)} %pad_maximum_fusion.3.refs_2_, ...), custom_call_target="tpu_custom_call" | custom-call | flops 8000000000 | bytes 8000000 | tf_op jit(solution)/shard_map/correlate/pallas_call | solution.py:273
  140.1 2.1 %collective-permute-start.21 = (bf16[64,2048]{1,0:T(8,128)(2,1)S(1)}, bf16[64,2048]{1,0:T(8,128)(2,1)S(1)}, u32[]{:S(2)}, u32[]{:S(2)}) collective-permute-start(bf16[64,2048]{1,0:T(8,128)(2,1)S(1)} %correlate.2), channel_id=1, source_target_pairs={{2,0},{3,1},{0,2},{1,3},{6,4},{7,5},{4,6},{5,7},{10,8},{11,9},{8,1... | collective-permute-start | bytes 786440 | tf_op jit(solution)/shard_map/ppermute | solution.py:402
  142.2 11.1 %correlate.3 = f32[64,4096]{1,0:T(8,128)} custom-call(s32[3]{0:T(128)S(1)} %pad_add_fusion.place_ref, bf16[2,32,3072]{2,1,0:T(8,128)(2,1)S(1)} %copy-done.4, bf16[2,32,3072]{2,1,0:T(8,128)(2,1)S(1)} %copy-done.14, bf16[2,32,3072]{2,1,0:T(8,128)(2,1)S(1)} %pad_maximum_fusion.1.refs_2_, bf16[2,32,3072]{2,1,0:T(8,128)(2,1)S(1)} %copy-done.11, ...), custom_call_target="tpu_custom_call" | custom-call | flops 8000000000 | bytes 8000000 | tf_op jit(solution)/shard_map/correlate/pallas_call | solution.py:273
  (124 shorter events, 35.8 us)
Async XLA Ops:
  2.4 14.4 %all-to-all-start = ((s32[32,1,8]{2,1,0:T(1,128)}), s32[32,1,8]{2,1,0:T(1,128)S(1)}, u32[]{:S(2)}, u32[]{:S(2)}) async-start(s32[32,1,8]{2,1,0:T(1,128)} %bitcast.1), calls=%async_computation | async-start | bytes 32768 | tf_op jit(solution)/shard_map/all_to_all | solution.py:352
  17.1 41.7 %all-to-all-start.1 = ((bf16[32,64,384]{2,1,0:T(8,128)(2,1)}), bf16[32,64,384]{2,1,0:T(8,128)(2,1)S(1)}, u32[]{:S(2)}, u32[]{:S(2)}) async-start(bf16[32,64,384]{2,1,0:T(8,128)(2,1)} %bitcast.3), calls=%async_computation.1 | async-start | bytes 3145728 | tf_op jit(solution)/shard_map/all_to_all | solution.py:359
  22.4 36.4 %collective-permute-start = (bf16[512,384]{1,0:T(8,128)(2,1)}, bf16[512,384]{1,0:T(8,128)(2,1)S(1)}, u32[]{:S(2)}, u32[]{:S(2)}) collective-permute-start(bf16[512,384]{1,0:T(8,128)(2,1)} %slice.30), channel_id=1, source_target_pairs={{0,1},{1,0},{2,3},{3,2},{4,5},{5,4},{6,7},{7,6},{8,9},{9,8},{10,11... | collective-permute-start | bytes 1179656 | tf_op jit(solution)/shard_map/ppermute | solution.py:358
  61.9 6.7 %collective-permute-start.6 = (bf16[1,32,3072]{2,1,0:T(8,128)(2,1)S(1)}, bf16[1,32,3072]{2,1,0:T(8,128)(2,1)S(1)}, u32[]{:S(2)}, u32[]{:S(2)}) collective-permute-start(bf16[1,32,3072]{2,1,0:T(8,128)(2,1)S(1)} %get-tuple-element.62), channel_id=1, source_target_pairs={{0,8},{4,12},{8,0},{12,4},{16,24},{20,28},{24,16},{28,20},{1,9},{5... | collective-permute-start | bytes 589832 | tf_op jit(solution)/shard_map/ppermute | solution.py:293
  63.4 20.0 %collective-permute-start.2 = (bf16[64,3072]{1,0:T(8,128)(2,1)S(1)}, bf16[64,3072]{1,0:T(8,128)(2,1)S(1)}, u32[]{:S(2)}, u32[]{:S(2)}) collective-permute-start(bf16[64,3072]{1,0:T(8,128)(2,1)S(1)} %refine.1), channel_id=1, source_target_pairs={{0,2},{1,3},{2,0},{3,1},{4,6},{5,7},{6,4},{7,5},{8,10},{9,11},{10,... | collective-permute-start | bytes 1179656 | tf_op jit(solution)/shard_map/ppermute | solution.py:388
  65.9 7.8 %collective-permute-start.4 = (bf16[1,32,3072]{2,1,0:T(8,128)(2,1)S(1)}, bf16[1,32,3072]{2,1,0:T(8,128)(2,1)S(1)}, u32[]{:S(2)}, u32[]{:S(2)}) collective-permute-start(bf16[1,32,3072]{2,1,0:T(8,128)(2,1)S(1)} %get-tuple-element.63), channel_id=1, source_target_pairs={{0,16},{4,20},{8,24},{12,28},{16,0},{20,4},{24,8},{28,12},{1,17},{... | collective-permute-start | bytes 589832 | tf_op jit(solution)/shard_map/ppermute | solution.py:293
  68.7 14.8 %collective-permute-start.7 = (bf16[2,32,3072]{2,1,0:T(8,128)(2,1)S(1)}, bf16[2,32,3072]{2,1,0:T(8,128)(2,1)S(1)}, u32[]{:S(2)}, u32[]{:S(2)}) collective-permute-start(bf16[2,32,3072]{2,1,0:T(8,128)(2,1)S(1)} %pad_maximum_fusion.1.refs_2_), channel_id=1, source_target_pairs={{0,16},{4,20},{8,24},{12,28},{16,0},{20,4},{24,8},{28,12},{1,17},{... | collective-permute-start | bytes 1179656 | tf_op jit(solution)/shard_map/ppermute | solution.py:293
  73.7 10.3 %collective-permute-start.5 = (bf16[2,32,3072]{2,1,0:T(8,128)(2,1)S(1)}, bf16[2,32,3072]{2,1,0:T(8,128)(2,1)S(1)}, u32[]{:S(2)}, u32[]{:S(2)}) collective-permute-start(bf16[2,32,3072]{2,1,0:T(8,128)(2,1)S(1)} %pad_maximum_fusion.refs_0_), channel_id=1, source_target_pairs={{0,8},{4,12},{8,0},{12,4},{16,24},{20,28},{24,16},{28,20},{1,9},{5... | collective-permute-start | bytes 1179656 | tf_op jit(solution)/shard_map/ppermute | solution.py:293
  73.8 18.5 %collective-permute-start.3 = (bf16[640,384]{1,0:T(8,128)(2,1)S(1)}, bf16[640,384]{1,0:T(8,128)(2,1)S(1)}, u32[]{:S(2)}, u32[]{:S(2)}) collective-permute-start(bf16[640,384]{1,0:T(8,128)(2,1)S(1)} %slice.32), channel_id=1, source_target_pairs={{0,1},{1,0},{2,3},{3,2},{4,5},{5,4},{6,7},{7,6},{8,9},{9,8},{10,11... | collective-permute-start | bytes 1474568 | tf_op jit(solution)/shard_map/ppermute | solution.py:374
  74.5 18.7 %collective-permute-start.10 = (bf16[2,32,3072]{2,1,0:T(8,128)(2,1)S(1)}, bf16[2,32,3072]{2,1,0:T(8,128)(2,1)S(1)}, u32[]{:S(2)}, u32[]{:S(2)}) collective-permute-start(bf16[2,32,3072]{2,1,0:T(8,128)(2,1)S(1)} %pad_maximum_fusion.1.refs_2_), channel_id=1, source_target_pairs={{0,4},{4,0},{8,12},{12,8},{16,20},{20,16},{24,28},{28,24},{1,5},{5... | collective-permute-start | bytes 1179656 | tf_op jit(solution)/shard_map/ppermute | solution.py:293
  83.5 10.4 %collective-permute-start.8 = (bf16[2,32,3072]{2,1,0:T(8,128)(2,1)S(1)}, bf16[2,32,3072]{2,1,0:T(8,128)(2,1)S(1)}, u32[]{:S(2)}, u32[]{:S(2)}) collective-permute-start(bf16[2,32,3072]{2,1,0:T(8,128)(2,1)S(1)} %pad_maximum_fusion.refs_0_), channel_id=1, source_target_pairs={{0,4},{4,0},{8,12},{12,8},{16,20},{20,16},{24,28},{28,24},{1,5},{5... | collective-permute-start | bytes 1179656 | tf_op jit(solution)/shard_map/ppermute | solution.py:293
  83.5 11.2 %collective-permute-start.11 = (bf16[2,32,3072]{2,1,0:T(8,128)(2,1)S(1)}, bf16[2,32,3072]{2,1,0:T(8,128)(2,1)S(1)}, u32[]{:S(2)}, u32[]{:S(2)}) collective-permute-start(bf16[2,32,3072]{2,1,0:T(8,128)(2,1)S(1)} %collective-permute-done.7.refs_3_), channel_id=1, source_target_pairs={{0,4},{4,0},{8,12},{12,8},{16,20},{20,16},{24,28},{28,24},{1,5},{5... | collective-permute-start | bytes 1179656 | tf_op jit(solution)/shard_map/ppermute | solution.py:293
  84.0 11.4 %collective-permute-start.9 = (bf16[2,32,3072]{2,1,0:T(8,128)(2,1)S(1)}, bf16[2,32,3072]{2,1,0:T(8,128)(2,1)S(1)}, u32[]{:S(2)}, u32[]{:S(2)}) collective-permute-start(bf16[2,32,3072]{2,1,0:T(8,128)(2,1)S(1)} %collective-permute-done.5.refs_1_), channel_id=1, source_target_pairs={{0,4},{4,0},{8,12},{12,8},{16,20},{20,16},{24,28},{28,24},{1,5},{5... | collective-permute-start | bytes 1179656 | tf_op jit(solution)/shard_map/ppermute | solution.py:293
  96.9 6.4 %collective-permute-start.15 = (bf16[1,32,3072]{2,1,0:T(8,128)(2,1)}, bf16[1,32,3072]{2,1,0:T(8,128)(2,1)}, u32[]{:S(2)}, u32[]{:S(2)}) collective-permute-start(bf16[1,32,3072]{2,1,0:T(8,128)(2,1)} %get-tuple-element.60), channel_id=1, source_target_pairs={{0,8},{4,12},{8,0},{12,4},{16,24},{20,28},{24,16},{28,20},{1,9},{5... | collective-permute-start | bytes 589832 | tf_op jit(solution)/shard_map/ppermute | solution.py:293
  99.4 22.4 %collective-permute-start.1 = (bf16[896,384]{1,0:T(8,128)(2,1)}, bf16[896,384]{1,0:T(8,128)(2,1)}, u32[]{:S(2)}, u32[]{:S(2)}) collective-permute-start(bf16[896,384]{1,0:T(8,128)(2,1)} %slice.31), channel_id=1, source_target_pairs={{0,1},{1,0},{2,3},{3,2},{4,5},{5,4},{6,7},{7,6},{8,9},{9,8},{10,11... | collective-permute-start | bytes 2064392 | tf_op jit(solution)/shard_map/ppermute | solution.py:375
  99.4 7.1 %collective-permute-start.13 = (bf16[1,32,3072]{2,1,0:T(8,128)(2,1)}, bf16[1,32,3072]{2,1,0:T(8,128)(2,1)S(1)}, u32[]{:S(2)}, u32[]{:S(2)}) collective-permute-start(bf16[1,32,3072]{2,1,0:T(8,128)(2,1)} %get-tuple-element.61), channel_id=1, source_target_pairs={{0,16},{4,20},{8,24},{12,28},{16,0},{20,4},{24,8},{28,12},{1,17},{... | collective-permute-start | bytes 589832 | tf_op jit(solution)/shard_map/ppermute | solution.py:293
  105.1 16.6 %collective-permute-start.16 = (bf16[2,32,3072]{2,1,0:T(8,128)(2,1)}, bf16[2,32,3072]{2,1,0:T(8,128)(2,1)}, u32[]{:S(2)}, u32[]{:S(2)}) collective-permute-start(bf16[2,32,3072]{2,1,0:T(8,128)(2,1)} %pad_maximum_fusion.3.refs_2_), channel_id=1, source_target_pairs={{0,16},{4,20},{8,24},{12,28},{16,0},{20,4},{24,8},{28,12},{1,17},{... | collective-permute-start | bytes 1179656 | tf_op jit(solution)/shard_map/ppermute | solution.py:293
  108.2 13.6 %collective-permute-start.14 = (bf16[2,32,3072]{2,1,0:T(8,128)(2,1)}, bf16[2,32,3072]{2,1,0:T(8,128)(2,1)}, u32[]{:S(2)}, u32[]{:S(2)}) collective-permute-start(bf16[2,32,3072]{2,1,0:T(8,128)(2,1)} %pad_maximum_fusion.2.refs_0_), channel_id=1, source_target_pairs={{0,8},{4,12},{8,0},{12,4},{16,24},{20,28},{24,16},{28,20},{1,9},{5... | collective-permute-start | bytes 1179656 | tf_op jit(solution)/shard_map/ppermute | solution.py:293
  111.3 10.4 %collective-permute-start.12 = (bf16[64,384]{1,0:T(8,128)(2,1)}, bf16[64,384]{1,0:T(8,128)(2,1)}, u32[]{:S(2)}, u32[]{:S(2)}) collective-permute-start(bf16[64,384]{1,0:T(8,128)(2,1)} %broadcast_select_fusion.2), channel_id=1, source_target_pairs={{2,0},{3,1},{4,2},{5,3},{6,4},{7,5},{8,6},{9,7},{10,8},{11,9},{12,... | collective-permute-start | bytes 147464 | tf_op jit(solution)/shard_map/ppermute | solution.py:371
  121.7 7.6 %collective-permute-start.17 = (bf16[2,32,3072]{2,1,0:T(8,128)(2,1)}, bf16[2,32,3072]{2,1,0:T(8,128)(2,1)}, u32[]{:S(2)}, u32[]{:S(2)}) collective-permute-start(bf16[2,32,3072]{2,1,0:T(8,128)(2,1)} %pad_maximum_fusion.2.refs_0_), channel_id=1, source_target_pairs={{0,4},{4,0},{8,12},{12,8},{16,20},{20,16},{24,28},{28,24},{1,5},{5... | collective-permute-start | bytes 1179656 | tf_op jit(solution)/shard_map/ppermute | solution.py:293
  123.8 5.6 %collective-permute-start.18 = (bf16[2,32,3072]{2,1,0:T(8,128)(2,1)}, bf16[2,32,3072]{2,1,0:T(8,128)(2,1)}, u32[]{:S(2)}, u32[]{:S(2)}) collective-permute-start(bf16[2,32,3072]{2,1,0:T(8,128)(2,1)} %collective-permute-done.14.refs_1_), channel_id=1, source_target_pairs={{0,4},{4,0},{8,12},{12,8},{16,20},{20,16},{24,28},{28,24},{1,5},{5... | collective-permute-start | bytes 1179656 | tf_op jit(solution)/shard_map/ppermute | solution.py:293
  123.9 5.5 %collective-permute-start.19 = (bf16[2,32,3072]{2,1,0:T(8,128)(2,1)}, bf16[2,32,3072]{2,1,0:T(8,128)(2,1)}, u32[]{:S(2)}, u32[]{:S(2)}) collective-permute-start(bf16[2,32,3072]{2,1,0:T(8,128)(2,1)} %pad_maximum_fusion.3.refs_2_), channel_id=1, source_target_pairs={{0,4},{4,0},{8,12},{12,8},{16,20},{20,16},{24,28},{28,24},{1,5},{5... | collective-permute-start | bytes 1179656 | tf_op jit(solution)/shard_map/ppermute | solution.py:293
  124.3 5.1 %collective-permute-start.20 = (bf16[2,32,3072]{2,1,0:T(8,128)(2,1)}, bf16[2,32,3072]{2,1,0:T(8,128)(2,1)}, u32[]{:S(2)}, u32[]{:S(2)}) collective-permute-start(bf16[2,32,3072]{2,1,0:T(8,128)(2,1)} %collective-permute-done.16.refs_3_), channel_id=1, source_target_pairs={{0,4},{4,0},{8,12},{12,8},{16,20},{20,16},{24,28},{28,24},{1,5},{5... | collective-permute-start | bytes 1179656 | tf_op jit(solution)/shard_map/ppermute | solution.py:293
  140.1 14.2 %collective-permute-start.21 = (bf16[64,2048]{1,0:T(8,128)(2,1)S(1)}, bf16[64,2048]{1,0:T(8,128)(2,1)S(1)}, u32[]{:S(2)}, u32[]{:S(2)}) collective-permute-start(bf16[64,2048]{1,0:T(8,128)(2,1)S(1)} %correlate.2), channel_id=1, source_target_pairs={{2,0},{3,1},{0,2},{1,3},{6,4},{7,5},{4,6},{5,7},{10,8},{11,9},{8,1... | collective-permute-start | bytes 786440 | tf_op jit(solution)/shard_map/ppermute | solution.py:402
  (30 other events, 250.8 us)

commit v11 on v10

--- a/solution.py
+++ b/solution.py
@@ -354,8 +354,8 @@
     send, key, before, ahead_rows = lax.optimization_barrier((send, key, old_templates, recording))
     pairs = [(i, i ^ 1) for i in range(owners)]
     unit_rows = 16 * ROWS
-    cuts = [0, *(sub_rows * n // 16 // unit_rows * unit_rows for n in (4, 9)), sub_rows]
-    ahead_rows = lax.ppermute(ahead_rows[: cuts[1]], "unit", pairs)
+    first = sub_rows * 7 // 16 // unit_rows * unit_rows
+    ahead_rows = lax.ppermute(ahead_rows[:first], "unit", pairs)
     got = lax.all_to_all(
         send.reshape(devices, CAP * tpd, chans), AXES, split_axis=0, concat_axis=0, tiled=True
     ).reshape(devices * CAP * tpd, chans)
@@ -371,8 +371,7 @@
     beyond = lax.ppermute(
         jnp.where(odd == 1, held, head), AXES, [(i, i - 2) for i in range(2, devices)]
     )
-    early = lax.ppermute(rest[cuts[1] : cuts[2]], "unit", pairs)
-    late = lax.ppermute(rest[cuts[2] :], "unit", pairs)
+    late = lax.ppermute(rest[first:], "unit", pairs)
 
     fresh = refine(key, got, old, tpd)
     rest, fresh = lax.optimization_barrier((rest, fresh))
@@ -387,11 +386,11 @@
         back = [(j, i) for i, j in ahead]
         chunk = lax.ppermute(fresh, "unit", ahead)
         if m == 1:
-            own, chunk, mine, early = tie(across(own), chunk, mine, early)
+            own, chunk, mine = tie(across(own), chunk, mine)
             part = extract(tm_pos.astype(jnp.int32).reshape(1), own, chans, tpd, share)
             part = jnp.transpose(part[:taps, :, :share], (1, 2, 0)).reshape(panel, share * taps)
             other, late, part, beyond = tie(spread(chunk), late, part, beyond)
-            windows = (mine, fold(ahead_rows, early), fold(
+            windows = (mine, fold(ahead_rows), fold(
                 jnp.where(odd == 1, beyond, held), late, jnp.where(odd == 1, head, beyond)
             ))
         else:

time: 156 us -> 157 us (level)
  waiting for transfers between devices: 26.2 us -> 34.6 us
  local copies, waits for them, and re-layouts: 54.9 us -> 49.8 us
  starting transfers between devices: 34.1 us -> 31.2 us
    ppermute x16, waiting for transfers between devices: 7.15 us -> 13.7 us  [swap(): return lax.ppermute(value, 'tm', [(i, i ^ bit) for i in range(size)])]
    unnamed x61 -> x51, local copies, waits for them, and re-layouts: 16.5 us -> 11.2 us
    ppermute x1, waiting for transfers between devices: 1.01 us -> 3.03 us  [body(): lax.ppermute(out, 'unit', back)]
    ppermute x3 -> x2, waiting for transfers between devices: 7.67 us -> 7.12 us  [the longest x1 6.94 us: body(): ahead_rows = lax.ppermute(ahead_rows[:first], 'unit', pairs)]
  transfers between devices with their start and end apart: 24 -> 23, of which waited for: 7 -> 9; matrix products, arithmetic and copies ran while one was open for 32% -> 31% of each run, Pallas kernels for 12% -> 13%
where the time goes in v11:
time: 157 us
  local copies, waits for them, and re-layouts  49.8 us (32%)
  waiting for transfers between devices  34.6 us (22%)
  Pallas kernels  32.1 us (20%)
  starting transfers between devices  31.2 us (20%)
  other arithmetic  8.04 us (5%)
    pallas_call x2, Pallas kernels, correlate(): pl.pallas_call(functools.partial(correlate_kernel, chans, tpd, scale, mas...  21.8 us
    reshape x1, local copies, waits for them, and re-layouts, body(): cube = before.reshape(panel, chans, taps)  20.6 us
    ppermute x16, waiting for transfers between devices, swap(): return lax.ppermute(value, 'tm', [(i, i ^ bit) for i in range(size)])  13.7 us
    ppermute x16, starting transfers between devices, swap(): return lax.ppermute(value, 'tm', [(i, i ^ bit) for i in range(size)])  12.6 us
    unnamed x51, local copies, waits for them, and re-layouts  11.2 us
    ppermute x1, waiting for transfers between devices, body(): chunk = lax.ppermute(fresh, 'unit', ahead)  9.42 us
    transpose x1, local copies, waits for them, and re-layouts, body(): old = jnp.transpose(cube, (0, 2, 1)).reshape(panel, tpd * chans)  7.93 us
    all_to_all x1, starting transfers between devices, body(): tags = lax.all_to_all(tags, AXES, split_axis=0, concat_axis=0, tiled=True)  7.3 us
  transfers between devices with their start and end apart: 23, of which 9 were waited for; matrix products, arithmetic and copies ran while one was open for 31% of the time, Pallas kernels for 13%

profile of v11, /device:TPU:0, one launch (start us, length us, event | category | flops | bytes accessed | tf_op | source)
XLA Modules:
  0.0 156.7 jit_solution(13962228978166271266)
XLA Ops:
  2.4 7.3 %all-to-all-start = ((s32[32,1,8]{2,1,0:T(1,128)}), s32[32,1,8]{2,1,0:T(1,128)S(1)}, u32[]{:S(2)}, u32[]{:S(2)}) async-start(s32[32,1,8]{2,1,0:T(1,128)} %bitcast.1), calls=%async_computation | async-start | bytes 32768 | tf_op jit(solution)/shard_map/all_to_all | solution.py:352
  12.5 3.1 %pack.1 = bf16[2048,384]{1,0:T(8,128)(2,1)} custom-call(s32[32]{0:T(128)S(1)} %copy-done.24, s32[32]{0:T(128)S(1)} %copy-done.23, s32[1]{0:T(128)} %bitcast.base_ref, bf16[2048,384]{1,0:T(8,128)(2,1)S(1)} %copy-done), custom_call_target="tpu_custom_call" | custom-call | flops 100000000 | bytes 4000000 | tf_op jit(solution)/shard_map/pack/pallas_call | solution.py:66
  17.1 4.6 %all-to-all-start.1 = ((bf16[32,64,384]{2,1,0:T(8,128)(2,1)}), bf16[32,64,384]{2,1,0:T(8,128)(2,1)S(1)}, u32[]{:S(2)}, u32[]{:S(2)}) async-start(bf16[32,64,384]{2,1,0:T(8,128)(2,1)} %bitcast.3), calls=%async_computation.1 | async-start | bytes 3145728 | tf_op jit(solution)/shard_map/all_to_all | solution.py:359
  22.6 1.8 %collective-permute-start = (bf16[896,384]{1,0:T(8,128)(2,1)}, bf16[896,384]{1,0:T(8,128)(2,1)}, u32[]{:S(2)}, u32[]{:S(2)}) collective-permute-start(bf16[896,384]{1,0:T(8,128)(2,1)} %slice.27), channel_id=1, source_target_pairs={{0,1},{1,0},{2,3},{3,2},{4,5},{5,4},{6,7},{7,6},{8,9},{9,8},{10,11... | collective-permute-start | bytes 2064392 | tf_op jit(solution)/shard_map/ppermute | solution.py:358
  24.4 20.6 %reshape.74 = bf16[64,384,61]{2,1,0:T(8,128)(2,1)} reshape(bf16[64,23424]{1,0:T(8,128)(2,1)} %param.7) | data formatting | bytes 5996544 | tf_op jit(solution)/shard_map/reshape | solution.py:363
  45.0 7.9 %dynamic-slice_bitcast_fusion = bf16[64,8,384]{1,2,0:T(8,128)(2,1)} fusion(s32[]{:T(128)S(6)} %select_n.58, bf16[64,384,61]{2,1,0:T(8,128)(2,1)} %reshape.74), kind=kLoop, calls=%fused_computation | loop fusion | bytes 3391492 | tf_op jit(solution)/shard_map/transpose | solution.py:366
  52.9 5.2 %copy.13 = bf16[8,8,8,384]{3,1,2,0:T(8,128)(2,1)S(1)} copy(bf16[8,8,8,384]{2,3,1,0:T(8,128)(2,1)} %bitcast.25) | data formatting | bytes 786432
  58.1 6.9 %collective-permute-done.refs_0_ = bf16[896,384]{1,0:T(8,128)(2,1)} collective-permute-done((bf16[896,384]{1,0:T(8,128)(2,1)}, bf16[896,384]{1,0:T(8,128)(2,1)}, u32[]{:S(2)}, u32[]{:S(2)}) %collective-permute-start) | collective-permute-done | bytes 688160 | tf_op jit(solution)/shard_map/ppermute | solution.py:358
  69.0 3.9 %collective-permute-done.5 = bf16[1,32,3072]{2,1,0:T(8,128)(2,1)S(1)} collective-permute-done((bf16[1,32,3072]{2,1,0:T(8,128)(2,1)S(1)}, bf16[1,32,3072]{2,1,0:T(8,128)(2,1)S(1)}, u32[]{:S(2)}, u32[]{:S(2)}) %collective-permute-start.5) | collective-permute-done | bytes 196640 | tf_op jit(solution)/shard_map/ppermute | solution.py:293
  72.9 1.5 collective-permute-start.6
  75.7 2.4 %collective-permute-start.2 = (bf16[64,3072]{1,0:T(8,128)(2,1)S(1)}, bf16[64,3072]{1,0:T(8,128)(2,1)S(1)}, u32[]{:S(2)}, u32[]{:S(2)}) collective-permute-start(bf16[64,3072]{1,0:T(8,128)(2,1)S(1)} %refine.1), channel_id=1, source_target_pairs={{0,2},{1,3},{2,0},{3,1},{4,6},{5,7},{6,4},{7,5},{8,10},{9,11},{10,... | collective-permute-start | bytes 1179656 | tf_op jit(solution)/shard_map/ppermute | solution.py:387
  78.6 4.1 %collective-permute-done.6.refs_3_ = bf16[2,32,3072]{2,1,0:T(8,128)(2,1)S(1)} collective-permute-done((bf16[2,32,3072]{2,1,0:T(8,128)(2,1)S(1)}, bf16[2,32,3072]{2,1,0:T(8,128)(2,1)S(1)}, u32[]{:S(2)}, u32[]{:S(2)}) %collective-permute-start.6) | collective-permute-done | bytes 393248 | tf_op jit(solution)/shard_map/ppermute | solution.py:293
  84.7 9.4 %collective-permute-done.2 = bf16[64,3072]{1,0:T(8,128)(2,1)S(1)} collective-permute-done((bf16[64,3072]{1,0:T(8,128)(2,1)S(1)}, bf16[64,3072]{1,0:T(8,128)(2,1)S(1)}, u32[]{:S(2)}, u32[]{:S(2)}) %collective-permute-start.2) | collective-permute-done | bytes 393248 | tf_op jit(solution)/shard_map/ppermute | solution.py:387
  100.7 4.5 %collective-permute-done.14 = bf16[1,32,3072]{2,1,0:T(8,128)(2,1)} collective-permute-done((bf16[1,32,3072]{2,1,0:T(8,128)(2,1)}, bf16[1,32,3072]{2,1,0:T(8,128)(2,1)}, u32[]{:S(2)}, u32[]{:S(2)}) %collective-permute-start.14) | collective-permute-done | bytes 196640 | tf_op jit(solution)/shard_map/ppermute | solution.py:293
  105.1 1.8 %pad_maximum_fusion.3.refs_2_ = bf16[2,32,3072]{2,1,0:T(8,128)(2,1)} fusion(bf16[1,32,3072]{2,1,0:T(8,128)(2,1)} %collective-permute-done.14, bf16[1,32,3072]{2,1,0:T(8,128)(2,1)} %get-tuple-element.58), kind=kLoop, calls=%fused_computation.6 | loop fusion | flops 196608 | bytes 786432 | tf_op jit(solution)/shard_map/concatenate | solution.py:305
  107.5 1.7 %pad_maximum_fusion.2.refs_0_ = bf16[2,32,3072]{2,1,0:T(8,128)(2,1)} fusion(bf16[1,32,3072]{2,1,0:T(8,128)(2,1)S(1)} %collective-permute-done.12, bf16[1,32,3072]{2,1,0:T(8,128)(2,1)} %get-tuple-element.59), kind=kLoop, calls=%fused_computation.5 | loop fusion | flops 196608 | bytes 786432 | tf_op jit(solution)/shard_map/concatenate | solution.py:305
  113.2 2.3 %extract.1 = bf16[64,64,128]{2,1,0:T(8,128)(2,1)S(1)} custom-call(s32[1]{0:T(128)} %bitcast.6.place_ref, bf16[2,32,3072]{2,1,0:T(8,128)(2,1)S(1)} %copy-done.3, bf16[2,32,3072]{2,1,0:T(8,128)(2,1)S(1)} %copy-done.9, bf16[2,32,3072]{2,1,0:T(8,128)(2,1)S(1)} %pad_maximum_fusion.1.refs_2_, bf16[2,32,3072]{2,1,0:T(8,128)(2,1)S(1)} %copy-done.6, ...), custom_call_target="tpu_custom_call" | custom-call | flops 400000000 | bytes 4000000 | tf_op jit(solution)/shard_map/extract/pallas_call | solution.py:181
  116.6 3.0 %copy.12 = bf16[64,48,61]{2,1,0:T(8,128)(2,1)} copy(bf16[64,48,61]{1,0,2:T(8,128)(2,1)} %slice_bitcast_fusion) | data formatting | bytes 749568 | tf_op jit(solution)/shard_map/transpose | solution.py:391
  119.5 2.6 %reshape.77 = bf16[64,2928]{1,0:T(8,128)(2,1)} reshape(bf16[64,48,61]{2,1,0:T(8,128)(2,1)} %copy.12) | data formatting | bytes 749568 | tf_op jit(solution)/shard_map/reshape | solution.py:391
  122.3 2.9 %collective-permute-start.16 = (bf16[2,32,3072]{2,1,0:T(8,128)(2,1)}, bf16[2,32,3072]{2,1,0:T(8,128)(2,1)}, u32[]{:S(2)}, u32[]{:S(2)}) collective-permute-start(bf16[2,32,3072]{2,1,0:T(8,128)(2,1)} %pad_maximum_fusion.2.refs_0_), channel_id=1, source_target_pairs={{0,4},{4,0},{8,12},{12,8},{16,20},{20,16},{24,28},{28,24},{1,5},{5... | collective-permute-start | bytes 1179656 | tf_op jit(solution)/shard_map/ppermute | solution.py:293
  128.2 1.6 %fold.5.refs_10_ = bf16[176,3072]{1,0:T(8,128)(2,1)S(1)} custom-call(bf16[64,384]{1,0:T(8,128)(2,1)S(1)} %get-tuple-element.63.refs_0_, bf16[1152,384]{1,0:T(8,128)(2,1)} %collective-permute-done.1.refs_1_, bf16[64,384]{1,0:T(8,128)(2,1)S(1)} %get-tuple-element.62.refs_2_), custom_call_target="tpu_custom_call" | custom-call | flops 200000000 | bytes 4000000 | tf_op jit(solution)/shard_map/fold/pallas_call | solution.py:103
  129.9 10.7 %correlate.2 = bf16[64,2048]{1,0:T(8,128)(2,1)S(1)} custom-call(s32[3]{0:T(128)S(1)} %pad_add_fusion.2.place_ref, bf16[2,32,3072]{2,1,0:T(8,128)(2,1)} %pad_maximum_fusion.2.refs_0_, bf16[2,32,3072]{2,1,0:T(8,128)(2,1)} %collective-permute-done.13.refs_1_, bf16[2,32,3072]{2,1,0:T(8,128)(2,1)} %pad_maximum_fusion.3.refs_2_, ...), custom_call_target="tpu_custom_call" | custom-call | flops 8000000000 | bytes 8000000 | tf_op jit(solution)/shard_map/correlate/pallas_call | solution.py:273
  141.7 11.1 %correlate.3 = f32[64,4096]{1,0:T(8,128)} custom-call(s32[3]{0:T(128)S(1)} %pad_add_fusion.place_ref, bf16[2,32,3072]{2,1,0:T(8,128)(2,1)S(1)} %copy-done.4, bf16[2,32,3072]{2,1,0:T(8,128)(2,1)S(1)} %copy-done.10, bf16[2,32,3072]{2,1,0:T(8,128)(2,1)S(1)} %pad_maximum_fusion.1.refs_2_, bf16[2,32,3072]{2,1,0:T(8,128)(2,1)S(1)} %copy-done.7, ...), custom_call_target="tpu_custom_call" | custom-call | flops 8000000000 | bytes 8000000 | tf_op jit(solution)/shard_map/correlate/pallas_call | solution.py:273
  152.8 3.0 %collective-permute-done.20 = bf16[64,2048]{1,0:T(8,128)(2,1)S(1)} collective-permute-done((bf16[64,2048]{1,0:T(8,128)(2,1)S(1)}, bf16[64,2048]{1,0:T(8,128)(2,1)S(1)}, u32[]{:S(2)}, u32[]{:S(2)}) %collective-permute-start.20) | collective-permute-done | bytes 262176 | tf_op jit(solution)/shard_map/ppermute | solution.py:401
  (111 shorter events, 31.8 us)
Async XLA Ops:
  2.4 14.4 %all-to-all-start = ((s32[32,1,8]{2,1,0:T(1,128)}), s32[32,1,8]{2,1,0:T(1,128)S(1)}, u32[]{:S(2)}, u32[]{:S(2)}) async-start(s32[32,1,8]{2,1,0:T(1,128)} %bitcast.1), calls=%async_computation | async-start | bytes 32768 | tf_op jit(solution)/shard_map/all_to_all | solution.py:352
  17.1 47.9 %all-to-all-start.1 = ((bf16[32,64,384]{2,1,0:T(8,128)(2,1)}), bf16[32,64,384]{2,1,0:T(8,128)(2,1)S(1)}, u32[]{:S(2)}, u32[]{:S(2)}) async-start(bf16[32,64,384]{2,1,0:T(8,128)(2,1)} %bitcast.3), calls=%async_computation.1 | async-start | bytes 3145728 | tf_op jit(solution)/shard_map/all_to_all | solution.py:359
  22.6 42.4 %collective-permute-start = (bf16[896,384]{1,0:T(8,128)(2,1)}, bf16[896,384]{1,0:T(8,128)(2,1)}, u32[]{:S(2)}, u32[]{:S(2)}) collective-permute-start(bf16[896,384]{1,0:T(8,128)(2,1)} %slice.27), channel_id=1, source_target_pairs={{0,1},{1,0},{2,3},{3,2},{4,5},{5,4},{6,7},{7,6},{8,9},{9,8},{10,11... | collective-permute-start | bytes 2064392 | tf_op jit(solution)/shard_map/ppermute | solution.py:358
  66.4 6.5 %collective-permute-start.5 = (bf16[1,32,3072]{2,1,0:T(8,128)(2,1)S(1)}, bf16[1,32,3072]{2,1,0:T(8,128)(2,1)S(1)}, u32[]{:S(2)}, u32[]{:S(2)}) collective-permute-start(bf16[1,32,3072]{2,1,0:T(8,128)(2,1)S(1)} %get-tuple-element.60), channel_id=1, source_target_pairs={{0,8},{4,12},{8,0},{12,4},{16,24},{20,28},{24,16},{28,20},{1,9},{5... | collective-permute-start | bytes 589832 | tf_op jit(solution)/shard_map/ppermute | solution.py:293
  67.6 6.8 %collective-permute-start.3 = (bf16[1,32,3072]{2,1,0:T(8,128)(2,1)S(1)}, bf16[1,32,3072]{2,1,0:T(8,128)(2,1)S(1)}, u32[]{:S(2)}, u32[]{:S(2)}) collective-permute-start(bf16[1,32,3072]{2,1,0:T(8,128)(2,1)S(1)} %get-tuple-element.61), channel_id=1, source_target_pairs={{0,16},{4,20},{8,24},{12,28},{16,0},{20,4},{24,8},{28,12},{1,17},{... | collective-permute-start | bytes 589832 | tf_op jit(solution)/shard_map/ppermute | solution.py:293
  72.9 9.8 %collective-permute-start.6 = (bf16[2,32,3072]{2,1,0:T(8,128)(2,1)S(1)}, bf16[2,32,3072]{2,1,0:T(8,128)(2,1)S(1)}, u32[]{:S(2)}, u32[]{:S(2)}) collective-permute-start(bf16[2,32,3072]{2,1,0:T(8,128)(2,1)S(1)} %pad_maximum_fusion.1.refs_2_), channel_id=1, source_target_pairs={{0,16},{4,20},{8,24},{12,28},{16,0},{20,4},{24,8},{28,12},{1,17},{... | collective-permute-start | bytes 1179656 | tf_op jit(solution)/shard_map/ppermute | solution.py:293
  74.5 9.5 %collective-permute-start.4 = (bf16[2,32,3072]{2,1,0:T(8,128)(2,1)S(1)}, bf16[2,32,3072]{2,1,0:T(8,128)(2,1)S(1)}, u32[]{:S(2)}, u32[]{:S(2)}) collective-permute-start(bf16[2,32,3072]{2,1,0:T(8,128)(2,1)S(1)} %pad_maximum_fusion.refs_0_), channel_id=1, source_target_pairs={{0,8},{4,12},{8,0},{12,4},{16,24},{20,28},{24,16},{28,20},{1,9},{5... | collective-permute-start | bytes 1179656 | tf_op jit(solution)/shard_map/ppermute | solution.py:293
  75.7 18.5 %collective-permute-start.2 = (bf16[64,3072]{1,0:T(8,128)(2,1)S(1)}, bf16[64,3072]{1,0:T(8,128)(2,1)S(1)}, u32[]{:S(2)}, u32[]{:S(2)}) collective-permute-start(bf16[64,3072]{1,0:T(8,128)(2,1)S(1)} %refine.1), channel_id=1, source_target_pairs={{0,2},{1,3},{2,0},{3,1},{4,6},{5,7},{6,4},{7,5},{8,10},{9,11},{10,... | collective-permute-start | bytes 1179656 | tf_op jit(solution)/shard_map/ppermute | solution.py:387
  78.1 16.1 %collective-permute-start.9 = (bf16[2,32,3072]{2,1,0:T(8,128)(2,1)S(1)}, bf16[2,32,3072]{2,1,0:T(8,128)(2,1)S(1)}, u32[]{:S(2)}, u32[]{:S(2)}) collective-permute-start(bf16[2,32,3072]{2,1,0:T(8,128)(2,1)S(1)} %pad_maximum_fusion.1.refs_2_), channel_id=1, source_target_pairs={{0,4},{4,0},{8,12},{12,8},{16,20},{20,16},{24,28},{28,24},{1,5},{5... | collective-permute-start | bytes 1179656 | tf_op jit(solution)/shard_map/ppermute | solution.py:293
  78.1 16.8 %collective-permute-start.7 = (bf16[2,32,3072]{2,1,0:T(8,128)(2,1)S(1)}, bf16[2,32,3072]{2,1,0:T(8,128)(2,1)S(1)}, u32[]{:S(2)}, u32[]{:S(2)}) collective-permute-start(bf16[2,32,3072]{2,1,0:T(8,128)(2,1)S(1)} %pad_maximum_fusion.refs_0_), channel_id=1, source_target_pairs={{0,4},{4,0},{8,12},{12,8},{16,20},{20,16},{24,28},{28,24},{1,5},{5... | collective-permute-start | bytes 1179656 | tf_op jit(solution)/shard_map/ppermute | solution.py:293
  82.7 13.0 %collective-permute-start.10 = (bf16[2,32,3072]{2,1,0:T(8,128)(2,1)S(1)}, bf16[2,32,3072]{2,1,0:T(8,128)(2,1)S(1)}, u32[]{:S(2)}, u32[]{:S(2)}) collective-permute-start(bf16[2,32,3072]{2,1,0:T(8,128)(2,1)S(1)} %collective-permute-done.6.refs_3_), channel_id=1, source_target_pairs={{0,4},{4,0},{8,12},{12,8},{16,20},{20,16},{24,28},{28,24},{1,5},{5... | collective-permute-start | bytes 1179656 | tf_op jit(solution)/shard_map/ppermute | solution.py:293
  84.0 12.5 %collective-permute-start.8 = (bf16[2,32,3072]{2,1,0:T(8,128)(2,1)S(1)}, bf16[2,32,3072]{2,1,0:T(8,128)(2,1)S(1)}, u32[]{:S(2)}, u32[]{:S(2)}) collective-permute-start(bf16[2,32,3072]{2,1,0:T(8,128)(2,1)S(1)} %collective-permute-done.4.refs_1_), channel_id=1, source_target_pairs={{0,4},{4,0},{8,12},{12,8},{16,20},{20,16},{24,28},{28,24},{1,5},{5... | collective-permute-start | bytes 1179656 | tf_op jit(solution)/shard_map/ppermute | solution.py:293
  98.0 7.1 %collective-permute-start.14 = (bf16[1,32,3072]{2,1,0:T(8,128)(2,1)}, bf16[1,32,3072]{2,1,0:T(8,128)(2,1)}, u32[]{:S(2)}, u32[]{:S(2)}) collective-permute-start(bf16[1,32,3072]{2,1,0:T(8,128)(2,1)} %get-tuple-element.58), channel_id=1, source_target_pairs={{0,8},{4,12},{8,0},{12,4},{16,24},{20,28},{24,16},{28,20},{1,9},{5... | collective-permute-start | bytes 589832 | tf_op jit(solution)/shard_map/ppermute | solution.py:293
  98.6 14.6 %copy-start.15 = (bf16[2,32,3072]{2,1,0:T(8,128)(2,1)S(1)}, bf16[2,32,3072]{2,1,0:T(8,128)(2,1)}, u32[]{:S(2)}) copy-start(bf16[2,32,3072]{2,1,0:T(8,128)(2,1)} %copy-done.14) | copy-start | bytes 1179652
  99.6 22.7 %collective-permute-start.1 = (bf16[1152,384]{1,0:T(8,128)(2,1)}, bf16[1152,384]{1,0:T(8,128)(2,1)}, u32[]{:S(2)}, u32[]{:S(2)}) collective-permute-start(bf16[1152,384]{1,0:T(8,128)(2,1)} %slice.28), channel_id=1, source_target_pairs={{0,1},{1,0},{2,3},{3,2},{4,5},{5,4},{6,7},{7,6},{8,9},{9,8},{10,11... | collective-permute-start | bytes 2654216 | tf_op jit(solution)/shard_map/ppermute | solution.py:374
  99.6 7.9 %collective-permute-start.12 = (bf16[1,32,3072]{2,1,0:T(8,128)(2,1)}, bf16[1,32,3072]{2,1,0:T(8,128)(2,1)S(1)}, u32[]{:S(2)}, u32[]{:S(2)}) collective-permute-start(bf16[1,32,3072]{2,1,0:T(8,128)(2,1)} %get-tuple-element.59), channel_id=1, source_target_pairs={{0,16},{4,20},{8,24},{12,28},{16,0},{20,4},{24,8},{28,12},{1,17},{... | collective-permute-start | bytes 589832 | tf_op jit(solution)/shard_map/ppermute | solution.py:293
  106.9 15.3 %collective-permute-start.15 = (bf16[2,32,3072]{2,1,0:T(8,128)(2,1)}, bf16[2,32,3072]{2,1,0:T(8,128)(2,1)}, u32[]{:S(2)}, u32[]{:S(2)}) collective-permute-start(bf16[2,32,3072]{2,1,0:T(8,128)(2,1)} %pad_maximum_fusion.3.refs_2_), channel_id=1, source_target_pairs={{0,16},{4,20},{8,24},{12,28},{16,0},{20,4},{24,8},{28,12},{1,17},{... | collective-permute-start | bytes 1179656 | tf_op jit(solution)/shard_map/ppermute | solution.py:293
  109.2 13.0 %collective-permute-start.13 = (bf16[2,32,3072]{2,1,0:T(8,128)(2,1)}, bf16[2,32,3072]{2,1,0:T(8,128)(2,1)}, u32[]{:S(2)}, u32[]{:S(2)}) collective-permute-start(bf16[2,32,3072]{2,1,0:T(8,128)(2,1)} %pad_maximum_fusion.2.refs_0_), channel_id=1, source_target_pairs={{0,8},{4,12},{8,0},{12,4},{16,24},{20,28},{24,16},{28,20},{1,9},{5... | collective-permute-start | bytes 1179656 | tf_op jit(solution)/shard_map/ppermute | solution.py:293
  111.7 10.4 %collective-permute-start.11 = (bf16[64,384]{1,0:T(8,128)(2,1)}, bf16[64,384]{1,0:T(8,128)(2,1)}, u32[]{:S(2)}, u32[]{:S(2)}) collective-permute-start(bf16[64,384]{1,0:T(8,128)(2,1)} %broadcast_select_fusion.2), channel_id=1, source_target_pairs={{2,0},{3,1},{4,2},{5,3},{6,4},{7,5},{8,6},{9,7},{10,8},{11,9},{12,... | collective-permute-start | bytes 147464 | tf_op jit(solution)/shard_map/ppermute | solution.py:371
  122.3 7.6 %collective-permute-start.16 = (bf16[2,32,3072]{2,1,0:T(8,128)(2,1)}, bf16[2,32,3072]{2,1,0:T(8,128)(2,1)}, u32[]{:S(2)}, u32[]{:S(2)}) collective-permute-start(bf16[2,32,3072]{2,1,0:T(8,128)(2,1)} %pad_maximum_fusion.2.refs_0_), channel_id=1, source_target_pairs={{0,4},{4,0},{8,12},{12,8},{16,20},{20,16},{24,28},{28,24},{1,5},{5... | collective-permute-start | bytes 1179656 | tf_op jit(solution)/shard_map/ppermute | solution.py:293
  125.2 4.7 %collective-permute-start.17 = (bf16[2,32,3072]{2,1,0:T(8,128)(2,1)}, bf16[2,32,3072]{2,1,0:T(8,128)(2,1)}, u32[]{:S(2)}, u32[]{:S(2)}) collective-permute-start(bf16[2,32,3072]{2,1,0:T(8,128)(2,1)} %collective-permute-done.13.refs_1_), channel_id=1, source_target_pairs={{0,4},{4,0},{8,12},{12,8},{16,20},{20,16},{24,28},{28,24},{1,5},{5... | collective-permute-start | bytes 1179656 | tf_op jit(solution)/shard_map/ppermute | solution.py:293
  125.3 4.6 %collective-permute-start.18 = (bf16[2,32,3072]{2,1,0:T(8,128)(2,1)}, bf16[2,32,3072]{2,1,0:T(8,128)(2,1)}, u32[]{:S(2)}, u32[]{:S(2)}) collective-permute-start(bf16[2,32,3072]{2,1,0:T(8,128)(2,1)} %pad_maximum_fusion.3.refs_2_), channel_id=1, source_target_pairs={{0,4},{4,0},{8,12},{12,8},{16,20},{20,16},{24,28},{28,24},{1,5},{5... | collective-permute-start | bytes 1179656 | tf_op jit(solution)/shard_map/ppermute | solution.py:293
  125.7 4.2 %collective-permute-start.19 = (bf16[2,32,3072]{2,1,0:T(8,128)(2,1)}, bf16[2,32,3072]{2,1,0:T(8,128)(2,1)}, u32[]{:S(2)}, u32[]{:S(2)}) collective-permute-start(bf16[2,32,3072]{2,1,0:T(8,128)(2,1)} %collective-permute-done.15.refs_3_), channel_id=1, source_target_pairs={{0,4},{4,0},{8,12},{12,8},{16,20},{20,16},{24,28},{28,24},{1,5},{5... | collective-permute-start | bytes 1179656 | tf_op jit(solution)/shard_map/ppermute | solution.py:293
  140.6 15.2 %collective-permute-start.20 = (bf16[64,2048]{1,0:T(8,128)(2,1)S(1)}, bf16[64,2048]{1,0:T(8,128)(2,1)S(1)}, u32[]{:S(2)}, u32[]{:S(2)}) collective-permute-start(bf16[64,2048]{1,0:T(8,128)(2,1)S(1)} %correlate.2), channel_id=1, source_target_pairs={{2,0},{3,1},{0,2},{1,3},{6,4},{7,5},{4,6},{5,7},{10,8},{11,9},{8,1... | collective-permute-start | bytes 786440 | tf_op jit(solution)/shard_map/ppermute | solution.py:401
  (24 other events, 193.8 us)
